TPU v7x, 32 devices: a whole 2x2x4 slice. The times are simulated.
32 devices in a mesh: groups: 2 (over x), modes: 16 (over z, y, core).
Axes of the slice: x: 2, y: 2, z: 4, core: 2. Of those that a mesh axis runs over, the one named last changes fastest.
Arguments:
- rhs: float32 [64, 8, 8192], P(('groups', 'modes')), parts along dimension 0, may hold values from -6 to 6
- diffusivity: float32 [8], replicated, may hold values from 0.05 to 0.5
- jac_coef: float32 [9, 8, 8, 8192], P(None, None, None, 'modes'), may hold values from -0.3 to 0.3
- coef_index: int32 [512], replicated, may hold values from 0 to 8
- row_mode: int32 [512], replicated, may hold values from 0 to 31
- col_mode: int32 [512], replicated, may hold values from 0 to 31
- multiplicity: int32 [512], replicated, may hold values from 1 to 4
Outputs:
- update: float32 [64, 8, 8192], P(('groups', 'modes')), parts along dimension 0
- basis_next: float32 [64, 8, 8192], P(('groups', 'modes')), parts along dimension 0
There are 2 independent parts, one for each index of `groups`. A program takes and returns all parts, laid end to end along the dimension named above; an argument that names none is the same for every part. Nothing has to cross between parts.
All inputs are finite; a program needn't handle non-finite values.
Results may differ from a plain program's by a relative error of at most 0.00029.
Values sent between devices are 32-bit elements; how exact they have to be, the bound alone decides.
No kernel may reach another device: no remote copies, remote signals or barrier semaphores. Data moves between devices by JAX's collectives and lax.ppermute only.
A program may use at most 128 MiB of HBM per device.

v0:
```python
import jax
import jax.numpy as jnp
from jax import lax
from jax.sharding import PartitionSpec as P

NCOEF = 9
GY = 32


def padded_2(array, sides, width):
    for axis, dim in sides:
        size, length = (lax.axis_size(axis), array.shape[dim])
        up = [(i, (i + 1) % size) for i in range(size)]
        down = [(j, i) for i, j in up]
        last = lax.slice_in_dim(array, length - width, length, axis=dim)
        first = lax.slice_in_dim(array, 0, width, axis=dim)
        before = lax.ppermute(last, axis, up)
        after = lax.ppermute(first, axis, down)
        array = jnp.concatenate([before, array, after], axis=dim)
    return array


def build_coupling(coef_index, row_mode, col_mode, multiplicity, total_modes):
    flat = (coef_index * total_modes + row_mode) * total_modes + col_mode
    weights = 0.25 * multiplicity.astype(jnp.float32)
    dense = jax.ops.segment_sum(weights, flat, num_segments=NCOEF * total_modes * total_modes)
    dense = dense.reshape(NCOEF, total_modes, total_modes)
    return dense.at[0].add(jnp.eye(total_modes, dtype=jnp.float32))


def react_local(field, coupling, jac_coef):
    mixed = jnp.einsum("ikj,jsc->iksc", coupling, field, precision=lax.Precision.HIGHEST)
    return jnp.einsum("istc,iktc->ksc", jac_coef, mixed, precision=lax.Precision.HIGHEST)


def column_sides(field):
    column = lax.broadcasted_iota(jnp.int32, (1, 1, field.shape[2]), 2) % GY
    before = jnp.where(column == 0, jnp.roll(field, -(GY - 1), 2), jnp.roll(field, 1, 2))
    after = jnp.where(column == GY - 1, jnp.roll(field, GY - 1, 2), jnp.roll(field, -1, 2))
    return before + after


def diffuse_rows(field, diffusivity):
    padded = padded_2(field, (("modes", 2),), GY)
    beside = padded[:, :, 2 * GY :] + padded[:, :, : -2 * GY] + column_sides(field)
    return field + diffusivity[None, :, None] * (4.0 * field - beside)


def local(rhs, diffusivity, jac_coef, coef_index, row_mode, col_mode, multiplicity):
    total_modes = rhs.shape[0] * lax.axis_size("modes")
    coupling = build_coupling(coef_index, row_mode, col_mode, multiplicity, total_modes)
    vector = lax.all_to_all(rhs, "modes", split_axis=2, concat_axis=0, tiled=True)

    def apply(field):
        return diffuse_rows(field, diffusivity) - react_local(field, coupling, jac_coef)

    beta = jnp.sqrt(lax.psum(jnp.sum(vector * vector), "modes"))
    first = vector / beta
    work = apply(first)
    h11 = lax.psum(jnp.sum(first * work), "modes")
    work = work - h11 * first
    h21 = jnp.sqrt(lax.psum(jnp.sum(work * work), "modes"))
    second = work / h21
    image = apply(second)
    h12 = lax.psum(jnp.sum(first * image), "modes")
    partial_vec = image - h12 * first
    h22 = lax.psum(jnp.sum(second * partial_vec), "modes")
    third = partial_vec - h22 * second
    h32 = jnp.sqrt(lax.psum(jnp.sum(third * third), "modes"))
    basis_next = third / h32
    m11 = h11 * h11 + h21 * h21
    m12 = h11 * h12 + h21 * h22
    m22 = h12 * h12 + h22 * h22 + h32 * h32
    g1 = beta * h11
    g2 = beta * h12
    determ = m11 * m22 - m12 * m12
    coef_one = (m22 * g1 - m12 * g2) / determ
    coef_two = (m11 * g2 - m12 * g1) / determ
    update = coef_one * first + coef_two * second
    update, basis_next = (
        lax.all_to_all(update, "modes", split_axis=0, concat_axis=2, tiled=True),
        lax.all_to_all(basis_next, "modes", split_axis=0, concat_axis=2, tiled=True),
    )
    return (update, basis_next)


def solution(mesh):
    return jax.shard_map(
        local,
        mesh=mesh,
        in_specs=(
            P(("groups", "modes"), None, None),
            P(),
            P(None, None, None, "modes"),
            P(),
            P(),
            P(),
            P(),
        ),
        out_specs=(P(("groups", "modes"), None, None), P(("groups", "modes"), None, None)),
        check_vma=False,
    )
```

profile of v0, /device:TPU:0, one launch (start us, length us, event | category | flops | bytes accessed | tf_op | source)
XLA Modules:
  0.0 487.2 jit_solution(746662313661322961)
XLA Ops:
  0.7 9.3 %copy.137 = f32[2,8,8192]{1,0,2:T(2,128)} copy(f32[2,8,8192]{2,1,0:T(8,128)} %param.9) | data formatting | bytes 1048576 | tf_op args[0]
  10.0 15.6 %reshape.105 = f32[16,1,8192]{2,1,0:T(1,128)} reshape(f32[8192,2,8]{2,1,0:T(2,128)} %bitcast.68) | data formatting | bytes 1048576
  25.6 7.4 %all-to-all-start = ((f32[16,1,8192]{2,1,0:T(1,128)}), f32[16,1,8192]{2,1,0:T(1,128)S(1)}, u32[]{:S(2)}, u32[]{:S(2)}) async-start(f32[16,1,8192]{2,1,0:T(1,128)} %reshape.105), calls=%async_computation | async-start | bytes 1048576 | tf_op jit(solution)/shard_map/all_to_all | solution.py:52
  33.1 3.4 scatter_custom_fusion
  37.3 10.2 %all-to-all-done = f32[16,1,8192]{2,1,0:T(1,128)S(1)} async-done(((f32[16,1,8192]{2,1,0:T(1,128)}), f32[16,1,8192]{2,1,0:T(1,128)S(1)}, u32[]{:S(2)}, u32[]{:S(2)}) %all-to-all-start) | async-done | bytes 524320 | tf_op jit(solution)/shard_map/all_to_all | solution.py:52
  48.0 1.9 reduce.5
  49.9 14.7 %reshape.106 = f32[8192,2,8]{2,1,0:T(2,128)} reshape(f32[16,8192]{1,0:T(8,128)S(1)} %reduce.5) | data formatting | bytes 1048576
  64.6 11.0 %multiply_reduce_fusion = f32[]{:T(128)} fusion(f32[8192,2,8]{2,1,0:T(2,128)} %reshape.106), kind=kLoop, calls=%fused_computation.1 | loop fusion | flops 262143 | bytes 524292 | tf_op jit(solution)/shard_map/reduce_sum | solution.py:57
  75.6 14.1 %copy.142 = f32[9,8,8,512]{0,1,2,3:T(8,128)} copy(f32[9,8,8,512]{3,2,1,0:T(8,128)S(1)} %copy-done) | data formatting | bytes 2359296 | tf_op args[2]
  89.8 32.9 %psum.42 = f32[]{:T(128)} all-reduce(f32[]{:T(128)} %multiply_reduce_fusion), channel_id=1, replica_groups=mesh['groups'=2,'modes'=16] {'modes'}, use_global_device_ids=true, to_apply=%region_1.0 | all-reduce | flops 1 | bytes 8 | tf_op jit(solution)/shard_map/psum | solution.py:57
  123.4 9.2 %copy.138 = f32[2,8,8192]{2,1,0:T(8,128)S(1)} copy(f32[2,8,8192]{1,0,2:T(2,128)} %bitcast.67) | data formatting | bytes 1048576 | tf_op jit(solution)/shard_map/all_to_all | solution.py:52
  136.4 5.5 %fusion.16 = f32[9,32,8,512]{3,1,2,0:T(8,128)} fusion(f32[32,8,512]{2,1,0:T(8,128)S(1)} %bitcast.64, f32[9,32,32]{2,1,0:T(8,128)S(1)} %add_dynamic-update-slice_fusion), kind=kOutput, calls=%fused_computation.29 | convolution fusion | flops 452984832 | bytes 5279744 | tf_op jit(solution)/shard_map/ikj,jsc->iksc/dot_general | solution.py:32
  141.9 26.4 %copy.141 = f32[9,32,8,512]{1,0,2,3:T(8,128)} copy(f32[9,32,8,512]{3,1,2,0:T(8,128)} %fusion.16) | data formatting | bytes 9437184 | tf_op jit(solution)/shard_map/ikj,jsc->iksc/dot_general | solution.py:32
  168.8 33.8 %convolution_bitcast_fusion.1 = f32[512,32,8]{1,2,0:T(8,128)S(1)} fusion(f32[9,32,8,512]{1,0,2,3:T(8,128)} %copy.141, f32[9,8,8,512]{0,1,2,3:T(8,128)} %copy.142), kind=kOutput, calls=%fused_computation.3 | convolution fusion | flops 113246208 | bytes 6422528 | tf_op jit(solution)/shard_map/istc,iktc->ksc/dot_general | solution.py:33
  204.3 3.1 multiply_reduce_fusion.5
  207.4 34.0 %psum.43 = f32[]{:T(128)} all-reduce(f32[]{:T(128)} %get-tuple-element.18), channel_id=1, replica_groups=mesh['groups'=2,'modes'=16] {'modes'}, use_global_device_ids=true, to_apply=%region_4.5 | all-reduce | flops 1 | bytes 8 | tf_op jit(solution)/shard_map/psum | solution.py:60
  242.7 30.5 %psum.44 = f32[]{:T(128)} all-reduce(f32[]{:T(128)} %multiply_reduce_fusion.4), channel_id=1, replica_groups=mesh['groups'=2,'modes'=16] {'modes'}, use_global_device_ids=true, to_apply=%region_6.7 | all-reduce | flops 1 | bytes 8 | tf_op jit(solution)/shard_map/psum | solution.py:62
  274.5 5.5 %fusion.14 = f32[9,32,8,512]{3,1,2,0:T(8,128)} fusion(f32[32,8,512]{2,1,0:T(8,128)S(1)} %broadcast_divide_fusion.1, f32[9,32,32]{2,1,0:T(8,128)S(1)} %add_dynamic-update-slice_fusion), kind=kOutput, calls=%fused_computation.27 | convolution fusion | flops 452984832 | bytes 5279744 | tf_op jit(solution)/shard_map/ikj,jsc->iksc/dot_general | solution.py:32
  283.1 26.4 %copy.145 = f32[9,32,8,512]{1,0,2,3:T(8,128)} copy(f32[9,32,8,512]{3,1,2,0:T(8,128)} %fusion.14) | data formatting | bytes 9437184 | tf_op jit(solution)/shard_map/ikj,jsc->iksc/dot_general | solution.py:32
  309.6 33.8 %convolution_bitcast_fusion = f32[512,32,8]{1,2,0:T(8,128)S(1)} fusion(f32[9,32,8,512]{1,0,2,3:T(8,128)} %copy.145, f32[9,8,8,512]{0,1,2,3:T(8,128)} %copy.142), kind=kOutput, calls=%fused_computation.2 | convolution fusion | flops 113246208 | bytes 6422528 | tf_op jit(solution)/shard_map/istc,iktc->ksc/dot_general | solution.py:33
  344.8 1.6 copy.147
  346.4 4.7 collective-permute-done.3
  351.1 3.1 multiply_reduce_fusion.3
  354.2 30.1 %psum.45 = f32[]{:T(128)} all-reduce(f32[]{:T(128)} %get-tuple-element.16), channel_id=1, replica_groups=mesh['groups'=2,'modes'=16] {'modes'}, use_global_device_ids=true, to_apply=%region_8.9 | all-reduce | flops 1 | bytes 8 | tf_op jit(solution)/shard_map/psum | solution.py:65
  384.3 1.4 multiply_reduce_fusion.2
  385.7 30.2 %psum.46 = f32[]{:T(128)} all-reduce(f32[]{:T(128)} %multiply_reduce_fusion.2), channel_id=1, replica_groups=mesh['groups'=2,'modes'=16] {'modes'}, use_global_device_ids=true, to_apply=%region_10.11 | all-reduce | flops 1 | bytes 8 | tf_op jit(solution)/shard_map/psum | solution.py:67
  415.9 2.2 multiply_reduce_fusion.1
  418.1 30.1 %psum.47 = f32[]{:T(128)} all-reduce(f32[]{:T(128)} %get-tuple-element.14), channel_id=1, replica_groups=mesh['groups'=2,'modes'=16] {'modes'}, use_global_device_ids=true, to_apply=%region_12.13 | all-reduce | flops 1 | bytes 8 | tf_op jit(solution)/shard_map/psum | solution.py:69
  449.7 3.6 all-to-all-start.2
  461.2 6.6 %all-to-all-done.2 = f32[32,8,512]{2,1,0:T(8,128)S(1)} async-done(((f32[32,8,512]{2,1,0:T(8,128)}), f32[32,8,512]{2,1,0:T(8,128)S(1)}, u32[]{:S(2)}, u32[]{:S(2)}) %all-to-all-start.2) | async-done | bytes 524320 | tf_op jit(solution)/shard_map/all_to_all | solution.py:82
  467.7 4.0 all-to-all-start.1
  472.6 13.6 %all-to-all-done.1 = f32[32,8,512]{2,1,0:T(8,128)S(1)} async-done(((f32[32,8,512]{2,1,0:T(8,128)}), f32[32,8,512]{2,1,0:T(8,128)S(1)}, u32[]{:S(2)}, u32[]{:S(2)}) %all-to-all-start.1) | async-done | bytes 524320 | tf_op jit(solution)/shard_map/all_to_all | solution.py:81
  (51 shorter events, 17.1 us)
Async XLA Ops:
  0.6 32.4 %copy-start.4 = (s32[512]{0:T(512)S(1)}, s32[512]{0:T(512)}, u32[]{:S(2)}) copy-start(s32[512]{0:T(512)} %param.15) | copy-start | bytes 6148
  0.6 32.4 %copy-start.7 = (s32[512]{0:T(512)S(1)}, s32[512]{0:T(512)}, u32[]{:S(2)}) copy-start(s32[512]{0:T(512)} %param.12) | copy-start | bytes 6148
  0.7 32.4 %copy-start.6 = (s32[512]{0:T(512)S(1)}, s32[512]{0:T(512)}, u32[]{:S(2)}) copy-start(s32[512]{0:T(512)} %param.13) | copy-start | bytes 6148
  0.7 32.4 %copy-start.5 = (s32[512]{0:T(512)S(1)}, s32[512]{0:T(512)}, u32[]{:S(2)}) copy-start(s32[512]{0:T(512)} %param.14) | copy-start | bytes 6148
  0.7 75.0 %copy-start = (f32[9,8,8,512]{3,2,1,0:T(8,128)S(1)}, f32[9,8,8,512]{3,2,1,0:T(8,128)}, u32[]{:S(2)}) copy-start(f32[9,8,8,512]{3,2,1,0:T(8,128)} %param.11) | copy-start | bytes 3538948
  25.6 21.9 %all-to-all-start = ((f32[16,1,8192]{2,1,0:T(1,128)}), f32[16,1,8192]{2,1,0:T(1,128)S(1)}, u32[]{:S(2)}, u32[]{:S(2)}) async-start(f32[16,1,8192]{2,1,0:T(1,128)} %reshape.105), calls=%async_computation | async-start | bytes 1048576 | tf_op jit(solution)/shard_map/all_to_all | solution.py:52
  168.3 36.0 %collective-permute-start = (f32[32,8,32]{2,1,0:T(8,128)}, f32[32,8,32]{2,1,0:T(8,128)}, u32[]{:S(2)}, u32[]{:S(2)}) collective-permute-start(f32[32,8,32]{2,1,0:T(8,128)} %get-tuple-element.30), channel_id=1, source_target_pairs={{1,0},{2,1},{3,2},{4,3},{5,4},{6,5},{7,6},{8,7},{9,8},{10,9},{11,1... | collective-permute-start | bytes 98312 | tf_op jit(solution)/shard_map/ppermute | solution.py:18
  168.3 36.0 %collective-permute-start.1 = (f32[32,8,32]{2,1,0:T(8,128)}, f32[32,8,32]{2,1,0:T(8,128)}, u32[]{:S(2)}, u32[]{:S(2)}) collective-permute-start(f32[32,8,32]{2,1,0:T(8,128)} %get-tuple-element.31), channel_id=1, source_target_pairs={{0,1},{1,2},{2,3},{3,4},{4,5},{5,6},{6,7},{7,8},{8,9},{9,10},{10,1... | collective-permute-start | bytes 98312 | tf_op jit(solution)/shard_map/ppermute | solution.py:17
  309.6 41.5 %copy-start.1 = (f32[8]{0:T(128)S(1)}, f32[8]{0:T(128)}, u32[]{:S(2)}) copy-start(f32[8]{0:T(128)} %param.10) | copy-start | bytes 100
  309.6 41.5 %copy-start.2 = (pred[512]{0:T(512)(128)(4,1)S(1)}, pred[512]{0:T(512)(128)(4,1)}, u32[]{:S(2)}) copy-start(pred[512]{0:T(512)(128)(4,1)} %get-tuple-element.40) | copy-start | bytes 1540
  309.6 41.5 %copy-start.3 = (pred[512]{0:T(512)(128)(4,1)S(1)}, pred[512]{0:T(512)(128)(4,1)}, u32[]{:S(2)}) copy-start(pred[512]{0:T(512)(128)(4,1)} %get-tuple-element.41) | copy-start | bytes 1540
  343.4 3.0 collective-permute-start.2
  343.5 7.6 %collective-permute-start.3 = (f32[32,8,32]{2,1,0:T(8,128)}, f32[32,8,32]{2,1,0:T(8,128)}, u32[]{:S(2)}, u32[]{:S(2)}) collective-permute-start(f32[32,8,32]{2,1,0:T(8,128)} %get-tuple-element.21), channel_id=1, source_target_pairs={{0,1},{1,2},{2,3},{3,4},{4,5},{5,6},{6,7},{7,8},{8,9},{9,10},{10,1... | collective-permute-start | bytes 98312 | tf_op jit(solution)/shard_map/ppermute | solution.py:17
  449.7 18.0 %all-to-all-start.2 = ((f32[32,8,512]{2,1,0:T(8,128)}), f32[32,8,512]{2,1,0:T(8,128)S(1)}, u32[]{:S(2)}, u32[]{:S(2)}) async-start(f32[32,8,512]{2,1,0:T(8,128)} %broadcast_divide_fusion), calls=%async_computation.2 | async-start | bytes 1048576 | tf_op jit(solution)/shard_map/all_to_all | solution.py:82
  467.7 18.5 %all-to-all-start.1 = ((f32[32,8,512]{2,1,0:T(8,128)}), f32[32,8,512]{2,1,0:T(8,128)S(1)}, u32[]{:S(2)}, u32[]{:S(2)}) async-start(f32[32,8,512]{2,1,0:T(8,128)} %multiply_add_fusion), calls=%async_computation.1 | async-start | bytes 1048576 | tf_op jit(solution)/shard_map/all_to_all | solution.py:81
where the time goes:
time: 493 us; the launch traced here: 487 us
  blocking collectives  188 us (38%)
  local copies, waits for them, and re-layouts  129 us (26%)
  matrix products  78.7 us (16%)
  waiting for transfers between devices  35.1 us (7%)
  other arithmetic  30.4 us (6%)
  starting transfers between devices  16.2 us (3%)
  between operations  10.1 us (2%)
    dot_general x2, matrix products, react_local(): jnp.einsum('istc,iktc->ksc', jac_coef, mixed, precision=lax.Precision.HIG...  67.7 us
    unnamed x21, local copies, waits for them, and re-layouts  54.2 us
    dot_general x2, local copies, waits for them, and re-layouts, react_local(): jnp.einsum('ikj,jsc->iksc', coupling, field, precision=lax.Precision.HIGH...  52.8 us
    psum x1, blocking collectives, local(): h11 = lax.psum(jnp.sum(first * work), 'modes')  34 us
    psum x1, blocking collectives, local(): beta = jnp.sqrt(lax.psum(jnp.sum(vector * vector), 'modes'))  32.9 us
    psum x1, blocking collectives, local(): h21 = jnp.sqrt(lax.psum(jnp.sum(work * work), 'modes'))  30.5 us
    psum x1, blocking collectives, local(): h22 = lax.psum(jnp.sum(second * partial_vec), 'modes')  30.2 us
    psum x1, blocking collectives, local(): h12 = lax.psum(jnp.sum(first * image), 'modes')  30.1 us
  transfers between devices with their start and end apart: 7, of which 4 were waited for; matrix products, arithmetic and copies ran while one was open for 9% of the time, Pallas kernels for 0%

commit v1 on v0

v1 whole, which is shorter than its diff:
```python
import functools

import jax
import jax.numpy as jnp
from jax import lax
from jax.experimental import pallas as pl
from jax.experimental.pallas import tpu as pltpu
from jax.sharding import PartitionSpec as P

NCOEF = 9
GY = 32
S = 8
LANES = 128
F32 = jnp.float32
BF16 = jnp.bfloat16
VMEM = pl.BlockSpec(memory_space=pltpu.VMEM)
PARAMS = pltpu.CompilerParams(vmem_limit_bytes=40 * 1024 * 1024)


def lane_iota():
    return lax.broadcasted_iota(jnp.int32, (S, LANES), 1)


def arrange_kernel(parts, rhs_ref, out_ref):
    own, _, total = rhs_ref.shape
    cells = total // parts
    tiles = cells // LANES
    low = lane_iota() < LANES // 2
    for d in range(parts):
        after = ((d + 1) * cells) % total
        before = (d * cells - LANES) % total
        for m in range(own):
            for ct in range(tiles):
                at = d * cells + ct * LANES
                out_ref[d * own + m, ct] = rhs_ref[m, :, at : at + LANES]
            out_ref[d * own + m, tiles] = jnp.where(
                low, rhs_ref[m, :, after : after + LANES], rhs_ref[m, :, before : before + LANES]
            )


def pack_kernel(first_ref, last_ref, head_ref, tail_ref):
    piece = lane_iota() // GY
    for i in range(NCOEF):
        for q in range(S // 4):
            head = first_ref[i, q * 4]
            tail = pltpu.roll(last_ref[i, q * 4], GY, 1)
            for p in range(1, 4):
                head = jnp.where(piece == p, pltpu.roll(first_ref[i, q * 4 + p], GY * p, 1), head)
                moved = last_ref[i, q * 4 + p]
                if p < 3:
                    moved = pltpu.roll(moved, GY * (p + 1), 1)
                tail = jnp.where(piece == p, moved, tail)
            head_ref[i, q] = head
            tail_ref[i, q] = tail


def coupling_kernel(modes, coef_ref, row_ref, col_ref, mult_ref, out_ref):
    rows, cols = out_ref.shape
    triples = coef_ref.shape[1]
    key = coef_ref[...] * modes + row_ref[...]
    weight = 0.25 * mult_ref[...].astype(F32)
    row = lax.broadcasted_iota(jnp.int32, (rows, triples), 0)
    left = jnp.where(row == key, weight, 0.0).astype(BF16)
    col = lax.rem(lax.broadcasted_iota(jnp.int32, (cols, triples), 0), modes)
    right = jnp.where(col == col_ref[...], 1.0, 0.0).astype(BF16)
    dense = lax.dot_general(left, right, (((1,), (1,)), ((), ())), preferred_element_type=F32)
    r = lax.broadcasted_iota(jnp.int32, (rows, cols), 0)
    c = lax.broadcasted_iota(jnp.int32, (rows, cols), 1)
    dense = dense + jnp.where(r == lax.rem(c, modes), 1.0, 0.0)
    high = dense.astype(BF16)
    low = (dense - high.astype(F32)).astype(BF16)
    out_ref[...] = jnp.where(c < 2 * modes, high.astype(F32), low.astype(F32)).astype(BF16)


def main_kernel(
    n, tiles, dif_ref, r_ref, jac_ref, next_ref, prev_ref, coup_ref, out_ref, v_ref, w_ref, z_ref, jh_ref, vs_ref, mx_ref
):
    lane = lane_iota()
    col = lane % GY
    every = tiles + 1

    for ct in range(every):
        for s in range(S):
            v_ref[ct, s] = r_ref[pl.ds(ct * S + s, n, stride=every * S), :]

    def unpack(i, _):
        for q in range(S // 4):
            after, before = next_ref[i, q], prev_ref[i, q]
            for p in range(4):
                a = after if p == 0 else pltpu.roll(after, LANES - GY * p, 1)
                b = before if p == 3 else pltpu.roll(before, LANES - GY - GY * p, 1)
                jh_ref[i * S + q * 4 + p] = jnp.where(lane < LANES // 2, a, b)
        return 0

    lax.fori_loop(0, NCOEF, unpack, 0)

    def apply_tile(src, dst, jac, ct):
        for t in range(S):
            x = src[ct, t]
            high = x.astype(BF16)
            low = (x - high.astype(F32)).astype(BF16)
            at = slice(t * LANES, (t + 1) * LANES)
            vs_ref[0:n, at] = high
            vs_ref[n : 2 * n, at] = low
            vs_ref[2 * n : 3 * n, at] = high
        mx_ref[...] = jnp.dot(coup_ref[...], vs_ref[...], preferred_element_type=F32)
        before, after = lax.rem(ct + every - 1, every), lax.rem(ct + 1, every)
        for kb in range(0, n, 32):

            def body(i, acc):
                acc = list(acc)
                for t in range(S):
                    m = [
                        mx_ref[pl.ds(pl.multiple_of(i * n + kb + kt * 8, 8), 8), t * LANES : (t + 1) * LANES]
                        for kt in range(4)
                    ]
                    for s in range(S):
                        j = jnp.broadcast_to(jac(i * S + s, t), (8, LANES))
                        for kt in range(4):
                            acc[s * 4 + kt] = acc[s * 4 + kt] + j * m[kt]
                return tuple(acc)

            acc = lax.fori_loop(0, NCOEF, body, tuple(jnp.zeros((8, LANES), F32) for _ in range(32)))
            for s in range(S):
                for kt in range(4):
                    at = slice(kb + kt * 8, kb + kt * 8 + 8)
                    x = src[ct, s, at]
                    up, down = pltpu.roll(x, GY, 1), pltpu.roll(x, LANES - GY, 1)
                    beside = pltpu.roll(jnp.where(col == GY - 1, down, x), 1, 1)
                    beside += pltpu.roll(jnp.where(col == 0, up, x), LANES - 1, 1)
                    beside += jnp.where(lane < GY, pltpu.roll(src[before, s, at], GY, 1), up)
                    beside += jnp.where(lane >= LANES - GY, pltpu.roll(src[after, s, at], LANES - GY, 1), down)
                    dst[ct, s, at] = dif_ref[s] * (4.0 * x - beside) - acc[s * 4 + kt]

    def own_jac(ct):
        start = pl.multiple_of(ct * LANES, LANES)
        return lambda row, t: jac_ref[row, t : t + 1, pl.ds(start, LANES)]

    def first(ct, _):
        apply_tile(v_ref, w_ref, own_jac(ct), ct)
        return 0

    lax.fori_loop(0, tiles, first, 0)
    apply_tile(v_ref, w_ref, lambda row, t: jh_ref[row, t : t + 1, :], jnp.int32(tiles))

    def second(ct, _):
        apply_tile(w_ref, z_ref, own_jac(ct), ct)
        return 0

    lax.fori_loop(0, tiles, second, 0)

    def total(x):
        return jnp.sum(x)

    rr = rw = rz = jnp.zeros((n, LANES), F32)
    for ct in range(tiles):
        for s in range(S):
            v, w, z = v_ref[ct, s], w_ref[ct, s], z_ref[ct, s]
            rr, rw, rz = rr + v * v, rw + v * w, rz + v * z

    def ratio(a, b):
        return jnp.where(b > 0.0, a / jnp.where(b > 0.0, b, 1.0), 0.0)

    def full(x):
        return jnp.full((8, LANES), x, F32)

    rr, rw, rz = full(total(rr)), full(total(rw)), full(total(rz))
    c1, c2 = ratio(rw, rr), ratio(rz, rr)
    c1n, c2n = c1[:1], c2[:1]
    uu = ut = jnp.zeros((n, LANES), F32)
    per = 2 * tiles + 1
    for ct in range(tiles):
        for s in range(S):
            v, w, z = v_ref[ct, s], w_ref[ct, s], z_ref[ct, s]
            out_ref[pl.ds(ct * S + s, n, stride=per * S), :] = w
            out_ref[pl.ds((tiles + ct) * S + s, n, stride=per * S), :] = z
            u, t = w - c1n * v, z - c2n * v
            uu, ut = uu + u * u, ut + u * t
    uu, ut = full(total(uu)), full(total(ut))
    c3 = ratio(ut, uu)
    c3n = c3[:1]
    xx = jnp.zeros((n, LANES), F32)
    for ct in range(tiles):
        for s in range(S):
            v, w, z = v_ref[ct, s], w_ref[ct, s], z_ref[ct, s]
            x = (z - c2n * v) - c3n * (w - c1n * v)
            xx = xx + x * x
    xx = full(total(xx))
    stat = lax.broadcasted_iota(jnp.int32, (8, LANES), 0)
    tile = jnp.zeros((8, LANES), F32)
    for q, value in enumerate((rr, c1, uu, c2, c3, xx)):
        tile = jnp.where(stat == q, value, tile)
    for k in range(n):
        out_ref[(k * per + 2 * tiles) * S : (k * per + per) * S, :] = tile


def combine_kernel(parts, tiles, rhs_ref, got_ref, update_ref, basis_ref):
    own = rhs_ref.shape[0]
    per = 2 * tiles + 1

    def stat(q):
        return got_ref[pl.ds(2 * tiles * S + q, parts, stride=own * per * S), :]

    def add(x):
        return jnp.sum(x, axis=0, keepdims=True)

    rr, c1, uu, c2, c3, xx = (stat(q) for q in range(6))
    all_rr = add(rr)
    g1 = add(rr * c1) / all_rr
    g2 = add(rr * c2) / all_rr
    e1, e2 = c1 - g1, c2 - g2
    all_uu = add(uu + e1 * e1 * rr)
    g3 = add(c3 * uu + e1 * e2 * rr) / all_uu
    e3 = c3 - g3
    f = e2 - g3 * e1
    all_xx = add(xx + e3 * e3 * uu + f * f * rr)
    beta, nu, nx = jnp.sqrt(all_rr), jnp.sqrt(all_uu), jnp.sqrt(all_xx)
    h11 = 1.0 + g1
    h21 = nu / beta
    h12 = (g2 - g1 * g1) * beta / nu
    h22 = 1.0 + (g3 - g1)
    h32 = nx / nu
    m11 = h11 * h11 + h21 * h21
    m12 = h11 * h12 + h21 * h22
    m22 = h12 * h12 + h22 * h22 + h32 * h32
    b1, b2 = beta * h11, beta * h12
    determ = m11 * m22 - m12 * m12
    y1 = (m22 * b1 - m12 * b2) / determ
    y2 = (m11 * b2 - m12 * b1) / determ
    uw = y2 / nu
    ur = y1 / beta - uw * g1
    bz = 1.0 / nx
    bw = -g3 * bz
    br = (g3 * g1 - g2) * bz
    ur, uw, br, bw, bz = (jnp.broadcast_to(x, (S, LANES)) for x in (ur, uw, br, bw, bz))
    for d in range(parts):
        for m in range(own):
            for ct in range(tiles):
                at = slice((d * tiles + ct) * LANES, (d * tiles + ct + 1) * LANES)
                base = ((d * own + m) * per + ct) * S
                r = rhs_ref[m, :, at]
                w = got_ref[base : base + S, :]
                z = got_ref[base + tiles * S : base + tiles * S + S, :]
                update_ref[m, :, at] = ur * r + uw * w
                basis_ref[m, :, at] = br * r + bw * w + bz * z


def local(rhs, diffusivity, jac_coef, coef_index, row_mode, col_mode, multiplicity):
    parts = lax.axis_size("modes")
    own, _, total = rhs.shape
    n = own * parts
    cells = total // parts
    tiles = cells // LANES
    sds = jax.ShapeDtypeStruct

    send = pl.pallas_call(
        functools.partial(arrange_kernel, parts),
        out_shape=sds((n, tiles + 1, S, LANES), F32),
        in_specs=[VMEM],
        out_specs=VMEM,
        compiler_params=PARAMS,
        name="arrange",
    )(rhs)
    vector = lax.all_to_all(send, "modes", split_axis=0, concat_axis=0, tiled=True)

    edge = (NCOEF, S, S, LANES)
    head, tail = pl.pallas_call(
        pack_kernel,
        grid=(1,),
        out_shape=[sds((NCOEF, S // 4, S, LANES), F32)] * 2,
        in_specs=[
            pl.BlockSpec(edge, lambda g: (0, 0, 0, 0)),
            pl.BlockSpec(edge, lambda g: (0, 0, 0, tiles - 1)),
        ],
        compiler_params=PARAMS,
        name="pack",
    )(jac_coef, jac_coef)
    up = [(i, (i + 1) % parts) for i in range(parts)]
    down = [(j, i) for i, j in up]
    after = lax.ppermute(head, "modes", down)
    before = lax.ppermute(tail, "modes", up)

    coupling = pl.pallas_call(
        functools.partial(coupling_kernel, n),
        out_shape=sds((NCOEF * n, 3 * n), BF16),
        in_specs=[VMEM] * 4,
        out_specs=VMEM,
        compiler_params=PARAMS,
        name="coupling",
    )(*(x.reshape(1, -1) for x in (coef_index, row_mode, col_mode, multiplicity)))

    per = 2 * tiles + 1
    field = pltpu.VMEM((tiles + 1, S, n, LANES), F32)
    out = pl.pallas_call(
        functools.partial(main_kernel, n, tiles),
        out_shape=sds((n * per * S, LANES), F32),
        in_specs=[pl.BlockSpec(memory_space=pltpu.SMEM)] + [VMEM] * 5,
        out_specs=VMEM,
        scratch_shapes=[
            field,
            field,
            field,
            pltpu.VMEM((NCOEF * S, S, LANES), F32),
            pltpu.VMEM((3 * n, S * LANES), BF16),
            pltpu.VMEM((NCOEF * n, S * LANES), F32),
        ],
        compiler_params=PARAMS,
        name="krylov",
    )(
        diffusivity,
        vector.reshape(n * (tiles + 1) * S, LANES),
        jac_coef.reshape(NCOEF * S, S, cells),
        after,
        before,
        coupling,
    )
    got = lax.all_to_all(out.reshape(n, per, S, LANES), "modes", split_axis=0, concat_axis=0, tiled=True)
    update, basis_next = pl.pallas_call(
        functools.partial(combine_kernel, parts, tiles),
        out_shape=[sds(rhs.shape, F32)] * 2,
        in_specs=[VMEM] * 2,
        out_specs=[VMEM] * 2,
        compiler_params=PARAMS,
        name="combine",
    )(rhs, got.reshape(n * per * S, LANES))
    return (update, basis_next)


def solution(mesh):
    return jax.shard_map(
        local,
        mesh=mesh,
        in_specs=(
            P(("groups", "modes"), None, None),
            P(),
            P(None, None, None, "modes"),
            P(),
            P(),
            P(),
            P(),
        ),
        out_specs=(P(("groups", "modes"), None, None), P(("groups", "modes"), None, None)),
        check_vma=False,
    )
```

time: 493 us -> 83.3 us (0.17); the launches traced: 487 us -> 83.1 us
  blocking collectives: 188 us -> 34.2 us
  local copies, waits for them, and re-layouts: 129 us -> 1.17 us
  matrix products: 78.7 us -> 0 us
  other arithmetic: 30.4 us -> 0 us
  waiting for transfers between devices: 35.1 us -> 12.4 us
  Pallas kernels: 0 us -> 22.7 us
  between operations: 10.1 us -> 0.76 us
    psum x6 -> x0, blocking collectives: 188 us -> none  [the longest x1 34 us: local(): h11 = lax.psum(jnp.sum(first * work), 'modes')]
    dot_general x4 -> x0, matrix products: 78.7 us -> none  [the longest x2 67.7 us: react_local(): jnp.einsum('istc,iktc->ksc', jac_coef, mixed, precision=lax.Precision.HIG...]
    dot_general x4 -> x0, local copies, waits for them, and re-layouts: 55.3 us -> none  [the longest x2 52.8 us: react_local(): jnp.einsum('ikj,jsc->iksc', coupling, field, precision=lax.Precision.HIGH...]
    unnamed x21 -> x16, local copies, waits for them, and re-layouts: 54.2 us -> 1.17 us
    all_to_all x0 -> x1, blocking collectives: none -> 34.2 us  [local(): lax.all_to_all(out.reshape(n, per, S, LANES), 'modes', split_axis=0, conc...]
    all_to_all x3 -> x1, waiting for transfers between devices: 30.4 us -> 0.01 us  [local(): lax.all_to_all(send, 'modes', split_axis=0, concat_axis=0, tiled=True)]
    pallas_call x0 -> x5, Pallas kernels: none -> 22.7 us  [the longest x1 20.2 us: local(): pl.pallas_call(functools.partial(main_kernel, n, tiles), out_shape=sds((n...]
    reduce_sum x6 -> x0, other arithmetic: 22 us -> none  [the longest x1 11 us: local(): beta = jnp.sqrt(lax.psum(jnp.sum(vector * vector), 'modes'))]
  transfers between devices with their start and end apart: 7 -> 3, of which waited for: 4 -> 2; matrix products, arithmetic and copies ran while one was open for 9% -> 0% of each run, Pallas kernels for 0% -> 0%
where the time goes in v1:
time: 83.3 us; the launch traced here: 83.1 us
  blocking collectives  34.2 us (41%)
  Pallas kernels  22.7 us (27%)
  waiting for transfers between devices  12.4 us (15%)
  starting transfers between devices  11.8 us (14%)
  local copies, waits for them, and re-layouts  1.17 us (1%)
    all_to_all x1, blocking collectives, local(): lax.all_to_all(out.reshape(n, per, S, LANES), 'modes', split_axis=0, conc...  34.2 us
    pallas_call x1, Pallas kernels, local(): pl.pallas_call(functools.partial(main_kernel, n, tiles), out_shape=sds((n...  20.2 us
    ppermute x1, waiting for transfers between devices, local(): after = lax.ppermute(head, 'modes', down)  7.45 us
    all_to_all x1, starting transfers between devices, local(): lax.all_to_all(send, 'modes', split_axis=0, concat_axis=0, tiled=True)  7.39 us
    ppermute x1, waiting for transfers between devices, local(): before = lax.ppermute(tail, 'modes', up)  4.97 us
    ppermute x1, starting transfers between devices, local(): after = lax.ppermute(head, 'modes', down)  4.43 us
  transfers between devices with their start and end apart: 3, of which 2 were waited for; matrix products, arithmetic and copies ran while one was open for 0% of the time, Pallas kernels for 0%

profile of v1, /device:TPU:0, one launch (start us, length us, event | category | flops | bytes accessed | tf_op | source)
XLA Modules:
  0.0 83.1 jit_solution(17665893044957712769)
XLA Ops:
  0.6 0.0 copy-start
  0.6 0.0 copy-start.1
  0.7 1.1 %copy-done.1 = f32[2,8,8192]{2,1,0:T(8,128)S(1)} copy-done((f32[2,8,8192]{2,1,0:T(8,128)S(1)}, f32[2,8,8192]{2,1,0:T(8,128)}, u32[]{:S(2)}) %copy-start.1) | copy-done | bytes 524312
  1.8 0.9 %arrange.1 = f32[32,5,8,128]{3,2,1,0:T(8,128)} custom-call(f32[2,8,8192]{2,1,0:T(8,128)S(1)} %copy-done.1), custom_call_target="tpu_custom_call" | custom-call | tf_op jit(solution)/shard_map/arrange/pallas_call | solution.py:256
  2.7 7.4 %all-to-all-start = ((f32[32,5,8,128]{3,2,1,0:T(8,128)}), f32[32,5,8,128]{3,2,1,0:T(8,128)S(1)}, u32[]{:S(2)}, u32[]{:S(2)}) async-start(f32[32,5,8,128]{3,2,1,0:T(8,128)} %arrange.1), calls=%async_computation | async-start | bytes 1310720 | tf_op jit(solution)/shard_map/all_to_all | solution.py:264
  10.1 0.0 copy-done
  10.1 0.0 copy-start.3
  10.1 0.0 copy-start.4
  10.1 0.0 copy-start.5
  10.1 0.0 copy-start.6
  10.1 0.0 copy-start.7
  10.1 0.2 pack.1
  10.3 4.4 %collective-permute-start = (f32[9,2,8,128]{3,2,1,0:T(8,128)S(1)}, f32[9,2,8,128]{3,2,1,0:T(8,128)S(1)}, u32[]{:S(2)}, u32[]{:S(2)}) collective-permute-start(f32[9,2,8,128]{3,2,1,0:T(8,128)S(1)} %get-tuple-element.4), channel_id=1, source_target_pairs={{1,0},{2,1},{3,2},{4,3},{5,4},{6,5},{7,6},{8,7},{9,8},{10,9},{11,1... | collective-permute-start | bytes 221192 | tf_op jit(solution)/shard_map/ppermute | solution.py:280
  14.7 0.0 collective-permute-start.1
  14.7 0.0 copy-done.3
  14.8 0.0 copy-done.4
  14.8 0.0 copy-done.5
  14.8 0.0 copy-done.6
  14.8 0.2 coupling.1.coup_ref
  15.0 7.5 %collective-permute-done.next_ref = f32[9,2,8,128]{3,2,1,0:T(8,128)S(1)} collective-permute-done((f32[9,2,8,128]{3,2,1,0:T(8,128)S(1)}, f32[9,2,8,128]{3,2,1,0:T(8,128)S(1)}, u32[]{:S(2)}, u32[]{:S(2)}) %collective-permute-start) | collective-permute-done | bytes 73760 | tf_op jit(solution)/shard_map/ppermute | solution.py:280
  22.5 5.0 %collective-permute-done.1.prev_ref = f32[9,2,8,128]{3,2,1,0:T(8,128)S(1)} collective-permute-done((f32[9,2,8,128]{3,2,1,0:T(8,128)S(1)}, f32[9,2,8,128]{3,2,1,0:T(8,128)S(1)}, u32[]{:S(2)}, u32[]{:S(2)}) %collective-permute-start.1) | collective-permute-done | bytes 73760 | tf_op jit(solution)/shard_map/ppermute | solution.py:281
  27.4 0.0 all-to-all-done
  27.5 0.0 copy-done.7
  27.5 20.2 %krylov.1 = f32[2304,128]{1,0:T(8,128)S(1)} custom-call(f32[8]{0:T(128)S(1)} %copy-done.7, f32[1280,128]{1,0:T(8,128)S(1)} %bitcast.11, f32[72,8,512]{2,1,0:T(8,128)S(1)} %bitcast.8, f32[9,2,8,128]{3,2,1,0:T(8,128)S(1)} %collective-permute-done.next_ref, f32[9,2,8,128]{3,2,1,0:T(8,128)S(1)} %collective-permute-done.1.prev_ref, ...), custom_call_target="tpu_custom_call" | custom-call | tf_op jit(solution)/shard_map/krylov/pallas_call | solution.py:294
  47.7 0.0 copy-start.2
  47.7 34.2 %all_to_all.10 = f32[32,9,8,128]{3,2,1,0:T(8,128)S(1)} all-to-all(f32[32,9,8,128]{3,2,1,0:T(8,128)S(1)} %bitcast.9), channel_id=1, replica_groups=mesh['groups'=2,'modes'=16] {'modes'}, dimensions={0} | all-to-all | bytes 2359296 | tf_op jit(solution)/shard_map/all_to_all | solution.py:317
  81.9 0.0 copy-done.2
  81.9 1.2 %combine.1 = (f32[2,8,8192]{2,1,0:T(8,128)}, f32[2,8,8192]{2,1,0:T(8,128)}) custom-call(f32[2,8,8192]{2,1,0:T(8,128)S(1)} %copy-done.2, f32[2304,128]{1,0:T(8,128)S(1)} %bitcast.10), custom_call_target="tpu_custom_call" | custom-call | tf_op jit(solution)/shard_map/combine/pallas_call | solution.py:318
Async XLA Ops:
  0.6 9.4 %copy-start = (f32[9,8,8,512]{3,2,1,0:T(8,128)S(1)}, f32[9,8,8,512]{3,2,1,0:T(8,128)}, u32[]{:S(2)}) copy-start(f32[9,8,8,512]{3,2,1,0:T(8,128)} %last_ref.1) | copy-start | bytes 3538948
  0.6 1.1 %copy-start.1 = (f32[2,8,8192]{2,1,0:T(8,128)S(1)}, f32[2,8,8192]{2,1,0:T(8,128)}, u32[]{:S(2)}) copy-start(f32[2,8,8192]{2,1,0:T(8,128)} %rhs_ref.3) | copy-start | bytes 1572868
  2.7 24.8 %all-to-all-start = ((f32[32,5,8,128]{3,2,1,0:T(8,128)}), f32[32,5,8,128]{3,2,1,0:T(8,128)S(1)}, u32[]{:S(2)}, u32[]{:S(2)}) async-start(f32[32,5,8,128]{3,2,1,0:T(8,128)} %arrange.1), calls=%async_computation | async-start | bytes 1310720 | tf_op jit(solution)/shard_map/all_to_all | solution.py:264
  10.1 4.7 %copy-start.3 = (s32[512]{0:T(512)S(1)}, s32[512]{0:T(512)}, u32[]{:S(2)}) copy-start(s32[512]{0:T(512)} %param.10) | copy-start | bytes 6148
  10.1 4.7 %copy-start.4 = (s32[512]{0:T(512)S(1)}, s32[512]{0:T(512)}, u32[]{:S(2)}) copy-start(s32[512]{0:T(512)} %param.11) | copy-start | bytes 6148
  10.1 4.7 %copy-start.5 = (s32[512]{0:T(512)S(1)}, s32[512]{0:T(512)}, u32[]{:S(2)}) copy-start(s32[512]{0:T(512)} %param.12) | copy-start | bytes 6148
  10.1 4.7 %copy-start.6 = (s32[512]{0:T(512)S(1)}, s32[512]{0:T(512)}, u32[]{:S(2)}) copy-start(s32[512]{0:T(512)} %param.13) | copy-start | bytes 6148
  10.1 17.3 %copy-start.7 = (f32[8]{0:T(128)S(1)}, f32[8]{0:T(128)}, u32[]{:S(2)}) copy-start(f32[8]{0:T(128)} %dif_ref.1) | copy-start | bytes 100
  10.3 12.2 %collective-permute-start = (f32[9,2,8,128]{3,2,1,0:T(8,128)S(1)}, f32[9,2,8,128]{3,2,1,0:T(8,128)S(1)}, u32[]{:S(2)}, u32[]{:S(2)}) collective-permute-start(f32[9,2,8,128]{3,2,1,0:T(8,128)S(1)} %get-tuple-element.4), channel_id=1, source_target_pairs={{1,0},{2,1},{3,2},{4,3},{5,4},{6,5},{7,6},{8,7},{9,8},{10,9},{11,1... | collective-permute-start | bytes 221192 | tf_op jit(solution)/shard_map/ppermute | solution.py:280
  14.7 12.7 %collective-permute-start.1 = (f32[9,2,8,128]{3,2,1,0:T(8,128)S(1)}, f32[9,2,8,128]{3,2,1,0:T(8,128)S(1)}, u32[]{:S(2)}, u32[]{:S(2)}) collective-permute-start(f32[9,2,8,128]{3,2,1,0:T(8,128)S(1)} %get-tuple-element.5), channel_id=1, source_target_pairs={{0,1},{1,2},{2,3},{3,4},{4,5},{5,6},{6,7},{7,8},{8,9},{9,10},{10,1... | collective-permute-start | bytes 221192 | tf_op jit(solution)/shard_map/ppermute | solution.py:281
  47.7 34.2 %copy-start.2 = (f32[2,8,8192]{2,1,0:T(8,128)S(1)}, f32[2,8,8192]{2,1,0:T(8,128)}, u32[]{:S(2)}) copy-start(f32[2,8,8192]{2,1,0:T(8,128)} %rhs_ref.3) | copy-start | bytes 1572868

commit v2 on v1

--- a/solution.py
+++ b/solution.py
@@ -54,7 +54,7 @@
             tail_ref[i, q] = tail
 
 
-def coupling_kernel(modes, coef_ref, row_ref, col_ref, mult_ref, out_ref):
+def coupling_kernel(modes, coef_ref, row_ref, col_ref, mult_ref, out_ref, stencil_ref):
     rows, cols = out_ref.shape
     triples = coef_ref.shape[1]
     key = coef_ref[...] * modes + row_ref[...]
@@ -71,13 +71,51 @@
     low = (dense - high.astype(F32)).astype(BF16)
     out_ref[...] = jnp.where(c < 2 * modes, high.astype(F32), low.astype(F32)).astype(BF16)
 
+    a = lax.broadcasted_iota(jnp.int32, (LANES, LANES), 0)
+    b = lax.broadcasted_iota(jnp.int32, (LANES, LANES), 1)
+    step = jnp.bitwise_and(a - b, GY - 1)
+    same = (a // GY == b // GY) & ((step == 1) | (step == GY - 1))
+    apart = jnp.abs(a - b)
+    inner = jnp.where(apart == 0, 4.0, jnp.where(same | (apart == GY), -1.0, 0.0)).astype(BF16)
+    outer = jnp.where(apart == LANES - GY, -1.0, 0.0).astype(BF16)
+    stencil_ref[0:LANES] = inner
+    stencil_ref[LANES : 2 * LANES] = inner
+    stencil_ref[2 * LANES : 3 * LANES] = outer
+    stencil_ref[3 * LANES :] = outer
+
+
+def split(x):
+    high = x.astype(BF16)
+    return high, (x - high.astype(F32)).astype(BF16)
+
+
+def ratio(a, b):
+    return jnp.where(b > 0.0, a / jnp.where(b > 0.0, b, 1.0), 0.0)
+
 
 def main_kernel(
-    n, tiles, dif_ref, r_ref, jac_ref, next_ref, prev_ref, coup_ref, out_ref, v_ref, w_ref, z_ref, jh_ref, vs_ref, mx_ref
+    n,
+    tiles,
+    dif_ref,
+    r_ref,
+    jac_ref,
+    next_ref,
+    prev_ref,
+    coup_ref,
+    stencil_ref,
+    out_ref,
+    v_ref,
+    w_ref,
+    z_ref,
+    jh_ref,
+    vs_ref,
+    xs_ref,
+    mx_ref,
+    bs_ref,
 ):
     lane = lane_iota()
-    col = lane % GY
     every = tiles + 1
+    per = 2 * tiles + 1
 
     for ct in range(every):
         for s in range(S):
@@ -94,98 +132,112 @@
 
     lax.fori_loop(0, NCOEF, unpack, 0)
 
-    def apply_tile(src, dst, jac, ct):
+    def mix(src, ct, slot):
+        wide = lax.broadcasted_iota(jnp.int32, (n, LANES), 1) < LANES // 2
+        before, after = (ct - 1) % every, (ct + 1) % every
         for t in range(S):
-            x = src[ct, t]
-            high = x.astype(BF16)
-            low = (x - high.astype(F32)).astype(BF16)
             at = slice(t * LANES, (t + 1) * LANES)
-            vs_ref[0:n, at] = high
-            vs_ref[n : 2 * n, at] = low
-            vs_ref[2 * n : 3 * n, at] = high
-        mx_ref[...] = jnp.dot(coup_ref[...], vs_ref[...], preferred_element_type=F32)
-        before, after = lax.rem(ct + every - 1, every), lax.rem(ct + 1, every)
+            to = slice(t * n, (t + 1) * n)
+            high, low = split(src[ct, t])
+            vs_ref[slot, 0:n, at] = high
+            vs_ref[slot, n : 2 * n, at] = low
+            vs_ref[slot, 2 * n : 3 * n, at] = high
+            xs_ref[slot, to, 0:LANES] = high
+            xs_ref[slot, to, LANES : 2 * LANES] = low
+            high, low = split(jnp.where(wide, src[after, t], src[before, t]))
+            xs_ref[slot, to, 2 * LANES : 3 * LANES] = high
+            xs_ref[slot, to, 3 * LANES :] = low
+        mx_ref[slot] = jnp.dot(coup_ref[...], vs_ref[slot], preferred_element_type=F32)
+        bs_ref[slot] = jnp.dot(xs_ref[slot], stencil_ref[...], preferred_element_type=F32)
+
+    def react(ct, slot, finish):
         for kb in range(0, n, 32):
-
-            def body(i, acc):
-                acc = list(acc)
+            acc = [None] * 32
+            for i in range(NCOEF):
                 for t in range(S):
                     m = [
-                        mx_ref[pl.ds(pl.multiple_of(i * n + kb + kt * 8, 8), 8), t * LANES : (t + 1) * LANES]
+                        mx_ref[slot, i * n + kb + kt * 8 : i * n + kb + kt * 8 + 8, t * LANES : (t + 1) * LANES]
                         for kt in range(4)
                     ]
                     for s in range(S):
-                        j = jnp.broadcast_to(jac(i * S + s, t), (8, LANES))
+                        if ct < tiles:
+                            j = jac_ref[i * S + s, t : t + 1, ct * LANES : (ct + 1) * LANES]
+                        else:
+                            j = jh_ref[i * S + s, t : t + 1, :]
+                        j = jnp.broadcast_to(j, (8, LANES))
                         for kt in range(4):
-                            acc[s * 4 + kt] = acc[s * 4 + kt] + j * m[kt]
-                return tuple(acc)
-
-            acc = lax.fori_loop(0, NCOEF, body, tuple(jnp.zeros((8, LANES), F32) for _ in range(32)))
+                            term = j * m[kt]
+                            at = s * 4 + kt
+                            acc[at] = term if acc[at] is None else acc[at] + term
             for s in range(S):
                 for kt in range(4):
-                    at = slice(kb + kt * 8, kb + kt * 8 + 8)
-                    x = src[ct, s, at]
-                    up, down = pltpu.roll(x, GY, 1), pltpu.roll(x, LANES - GY, 1)
-                    beside = pltpu.roll(jnp.where(col == GY - 1, down, x), 1, 1)
-                    beside += pltpu.roll(jnp.where(col == 0, up, x), LANES - 1, 1)
-                    beside += jnp.where(lane < GY, pltpu.roll(src[before, s, at], GY, 1), up)
-                    beside += jnp.where(lane >= LANES - GY, pltpu.roll(src[after, s, at], LANES - GY, 1), down)
-                    dst[ct, s, at] = dif_ref[s] * (4.0 * x - beside) - acc[s * 4 + kt]
-
-    def own_jac(ct):
-        start = pl.multiple_of(ct * LANES, LANES)
-        return lambda row, t: jac_ref[row, t : t + 1, pl.ds(start, LANES)]
-
-    def first(ct, _):
-        apply_tile(v_ref, w_ref, own_jac(ct), ct)
-        return 0
-
-    lax.fori_loop(0, tiles, first, 0)
-    apply_tile(v_ref, w_ref, lambda row, t: jh_ref[row, t : t + 1, :], jnp.int32(tiles))
-
-    def second(ct, _):
-        apply_tile(w_ref, z_ref, own_jac(ct), ct)
-        return 0
-
-    lax.fori_loop(0, tiles, second, 0)
+                    k = kb + kt * 8
+                    b = bs_ref[slot, s * n + k : s * n + k + 8]
+                    finish(s, k, dif_ref[s] * b - acc[s * 4 + kt])
 
     def total(x):
-        return jnp.sum(x)
-
-    rr = rw = rz = jnp.zeros((n, LANES), F32)
+        return jnp.broadcast_to(jnp.sum(x, axis=(0, 1), keepdims=True), (8, LANES))
+
+    sums = {}
+
+    def gather(name, at, term):
+        key = (name, at % 4)
+        sums[key] = sums[key] + term if key in sums else term
+
+    def collect(name):
+        parts = [value for (key, _), value in sums.items() if key == name]
+        return total(functools.reduce(lambda a, b: a + b, parts))
+
+    def finish_first(ct):
+        def finish(s, k, w):
+            w_ref[ct, s, k : k + 8] = w
+            if ct < tiles:
+                v = v_ref[ct, s, k : k + 8]
+                out_ref[pl.ds(k * per * S + ct * S + s, 8, stride=per * S), :] = w
+                gather("rr", k // 8, v * v)
+                gather("rw", k // 8, v * w)
+
+        return finish
+
+    def finish_second(ct, c1):
+        def finish(s, k, z):
+            v, w = v_ref[ct, s, k : k + 8], w_ref[ct, s, k : k + 8]
+            z_ref[ct, s, k : k + 8] = z
+            out_ref[pl.ds(k * per * S + (tiles + ct) * S + s, 8, stride=per * S), :] = z
+            u = w - c1 * v
+            gather("uu", k // 8, u * u)
+            gather("ur", k // 8, u * v)
+            gather("uz", k // 8, u * z)
+            gather("rz", k // 8, v * z)
+
+        return finish
+
+    order = [tiles] + list(range(tiles))
+    mix(v_ref, order[0], 0)
+    for at, ct in enumerate(order):
+        if at + 1 < every:
+            mix(v_ref, order[at + 1], (at + 1) % 2)
+        elif tiles > 1:
+            mix(w_ref, 0, every % 2)
+        react(ct, at % 2, finish_first(ct))
+    if tiles == 1:
+        mix(w_ref, 0, every % 2)
+    rr, rw = collect("rr"), collect("rw")
+    c1 = ratio(rw, rr)
+    for ct in range(tiles):
+        if ct + 1 < tiles:
+            mix(w_ref, ct + 1, (every + ct + 1) % 2)
+        react(ct, (every + ct) % 2, finish_second(ct, c1))
+    uu, ur, uz, rz = (collect(name) for name in ("uu", "ur", "uz", "rz"))
+    c2 = ratio(rz, rr)
+    c3 = ratio(uz - c2 * ur, uu)
     for ct in range(tiles):
         for s in range(S):
-            v, w, z = v_ref[ct, s], w_ref[ct, s], z_ref[ct, s]
-            rr, rw, rz = rr + v * v, rw + v * w, rz + v * z
-
-    def ratio(a, b):
-        return jnp.where(b > 0.0, a / jnp.where(b > 0.0, b, 1.0), 0.0)
-
-    def full(x):
-        return jnp.full((8, LANES), x, F32)
-
-    rr, rw, rz = full(total(rr)), full(total(rw)), full(total(rz))
-    c1, c2 = ratio(rw, rr), ratio(rz, rr)
-    c1n, c2n = c1[:1], c2[:1]
-    uu = ut = jnp.zeros((n, LANES), F32)
-    per = 2 * tiles + 1
-    for ct in range(tiles):
-        for s in range(S):
-            v, w, z = v_ref[ct, s], w_ref[ct, s], z_ref[ct, s]
-            out_ref[pl.ds(ct * S + s, n, stride=per * S), :] = w
-            out_ref[pl.ds((tiles + ct) * S + s, n, stride=per * S), :] = z
-            u, t = w - c1n * v, z - c2n * v
-            uu, ut = uu + u * u, ut + u * t
-    uu, ut = full(total(uu)), full(total(ut))
-    c3 = ratio(ut, uu)
-    c3n = c3[:1]
-    xx = jnp.zeros((n, LANES), F32)
-    for ct in range(tiles):
-        for s in range(S):
-            v, w, z = v_ref[ct, s], w_ref[ct, s], z_ref[ct, s]
-            x = (z - c2n * v) - c3n * (w - c1n * v)
-            xx = xx + x * x
-    xx = full(total(xx))
+            for k in range(0, n, 8):
+                v, w, z = (ref[ct, s, k : k + 8] for ref in (v_ref, w_ref, z_ref))
+                x = (z - c2 * v) - c3 * (w - c1 * v)
+                gather("xx", k // 8, x * x)
+    xx = collect("xx")
     stat = lax.broadcasted_iota(jnp.int32, (8, LANES), 0)
     tile = jnp.zeros((8, LANES), F32)
     for q, value in enumerate((rr, c1, uu, c2, c3, xx)):
@@ -280,11 +332,11 @@
     after = lax.ppermute(head, "modes", down)
     before = lax.ppermute(tail, "modes", up)
 
-    coupling = pl.pallas_call(
+    coupling, stencil = pl.pallas_call(
         functools.partial(coupling_kernel, n),
-        out_shape=sds((NCOEF * n, 3 * n), BF16),
+        out_shape=[sds((NCOEF * n, 3 * n), BF16), sds((4 * LANES, LANES), BF16)],
         in_specs=[VMEM] * 4,
-        out_specs=VMEM,
+        out_specs=[VMEM] * 2,
         compiler_params=PARAMS,
         name="coupling",
     )(*(x.reshape(1, -1) for x in (coef_index, row_mode, col_mode, multiplicity)))
@@ -294,15 +346,17 @@
     out = pl.pallas_call(
         functools.partial(main_kernel, n, tiles),
         out_shape=sds((n * per * S, LANES), F32),
-        in_specs=[pl.BlockSpec(memory_space=pltpu.SMEM)] + [VMEM] * 5,
+        in_specs=[pl.BlockSpec(memory_space=pltpu.SMEM)] + [VMEM] * 6,
         out_specs=VMEM,
         scratch_shapes=[
             field,
             field,
             field,
             pltpu.VMEM((NCOEF * S, S, LANES), F32),
-            pltpu.VMEM((3 * n, S * LANES), BF16),
-            pltpu.VMEM((NCOEF * n, S * LANES), F32),
+            pltpu.VMEM((2, 3 * n, S * LANES), BF16),
+            pltpu.VMEM((2, S * n, 4 * LANES), BF16),
+            pltpu.VMEM((2, NCOEF * n, S * LANES), F32),
+            pltpu.VMEM((2, S * n, LANES), F32),
         ],
         compiler_params=PARAMS,
         name="krylov",
@@ -313,6 +367,7 @@
         after,
         before,
         coupling,
+        stencil,
     )
     got = lax.all_to_all(out.reshape(n, per, S, LANES), "modes", split_axis=0, concat_axis=0, tiled=True)
     update, basis_next = pl.pallas_call(

time: 83.3 us -> 74 us (0.89)
  Pallas kernels: 22.7 us -> 13.4 us
    pallas_call x1, Pallas kernels: 20.2 us -> 10.8 us  [local(): pl.pallas_call(functools.partial(main_kernel, n, tiles), out_shape=sds((n...]
  transfers between devices with their start and end apart: 3 -> 3, of which waited for: 2 -> 2; matrix products, arithmetic and copies ran while one was open for 0% -> 0% of each run, Pallas kernels for 0% -> 1%
where the time goes in v2:
time: 74 us; the launch traced here: 73.7 us
  blocking collectives  34.2 us (46%)
  Pallas kernels  13.4 us (18%)
  waiting for transfers between devices  12.4 us (17%)
  starting transfers between devices  11.8 us (16%)
  local copies, waits for them, and re-layouts  1.17 us (2%)
  between operations  0.76 us (1%)
    all_to_all x1, blocking collectives, local(): lax.all_to_all(out.reshape(n, per, S, LANES), 'modes', split_axis=0, conc...  34.2 us
    pallas_call x1, Pallas kernels, local(): pl.pallas_call(functools.partial(main_kernel, n, tiles), out_shape=sds((n...  10.8 us
    ppermute x1, waiting for transfers between devices, local(): after = lax.ppermute(head, 'modes', down)  7.42 us
    all_to_all x1, starting transfers between devices, local(): lax.all_to_all(send, 'modes', split_axis=0, concat_axis=0, tiled=True)  7.39 us
    ppermute x1, waiting for transfers between devices, local(): before = lax.ppermute(tail, 'modes', up)  4.97 us
    ppermute x1, starting transfers between devices, local(): after = lax.ppermute(head, 'modes', down)  4.43 us
  transfers between devices with their start and end apart: 3, of which 2 were waited for; matrix products, arithmetic and copies ran while one was open for 0% of the time, Pallas kernels for 1%

profile of v2, /device:TPU:0, one launch (start us, length us, event | category | flops | bytes accessed | tf_op | source)
XLA Modules:
  0.0 73.7 jit_solution(7355749583528817163)
XLA Ops:
  0.6 0.0 copy-start
  0.6 0.0 copy-start.1
  0.7 1.1 %copy-done.1 = f32[2,8,8192]{2,1,0:T(8,128)S(1)} copy-done((f32[2,8,8192]{2,1,0:T(8,128)S(1)}, f32[2,8,8192]{2,1,0:T(8,128)}, u32[]{:S(2)}) %copy-start.1) | copy-done | bytes 524312
  1.8 0.9 %arrange.1 = f32[32,5,8,128]{3,2,1,0:T(8,128)} custom-call(f32[2,8,8192]{2,1,0:T(8,128)S(1)} %copy-done.1), custom_call_target="tpu_custom_call" | custom-call | tf_op jit(solution)/shard_map/arrange/pallas_call | solution.py:308
  2.7 7.4 %all-to-all-start = ((f32[32,5,8,128]{3,2,1,0:T(8,128)}), f32[32,5,8,128]{3,2,1,0:T(8,128)S(1)}, u32[]{:S(2)}, u32[]{:S(2)}) async-start(f32[32,5,8,128]{3,2,1,0:T(8,128)} %arrange.1), calls=%async_computation | async-start | bytes 1310720 | tf_op jit(solution)/shard_map/all_to_all | solution.py:316
  10.1 0.0 copy-done
  10.1 0.0 copy-start.3
  10.1 0.0 copy-start.4
  10.1 0.0 copy-start.5
  10.1 0.0 copy-start.6
  10.1 0.0 copy-start.7
  10.1 0.2 pack.1
  10.3 4.4 %collective-permute-start = (f32[9,2,8,128]{3,2,1,0:T(8,128)S(1)}, f32[9,2,8,128]{3,2,1,0:T(8,128)S(1)}, u32[]{:S(2)}, u32[]{:S(2)}) collective-permute-start(f32[9,2,8,128]{3,2,1,0:T(8,128)S(1)} %get-tuple-element.6), channel_id=1, source_target_pairs={{1,0},{2,1},{3,2},{4,3},{5,4},{6,5},{7,6},{8,7},{9,8},{10,9},{11,1... | collective-permute-start | bytes 221192 | tf_op jit(solution)/shard_map/ppermute | solution.py:332
  14.8 0.0 collective-permute-start.1
  14.8 0.0 copy-done.3
  14.8 0.0 copy-done.4
  14.8 0.0 copy-done.5
  14.8 0.0 copy-done.6
  14.8 0.3 coupling.1
  15.1 7.4 %collective-permute-done.next_ref = f32[9,2,8,128]{3,2,1,0:T(8,128)S(1)} collective-permute-done((f32[9,2,8,128]{3,2,1,0:T(8,128)S(1)}, f32[9,2,8,128]{3,2,1,0:T(8,128)S(1)}, u32[]{:S(2)}, u32[]{:S(2)}) %collective-permute-start) | collective-permute-done | bytes 73760 | tf_op jit(solution)/shard_map/ppermute | solution.py:332
  22.5 5.0 %collective-permute-done.1.prev_ref = f32[9,2,8,128]{3,2,1,0:T(8,128)S(1)} collective-permute-done((f32[9,2,8,128]{3,2,1,0:T(8,128)S(1)}, f32[9,2,8,128]{3,2,1,0:T(8,128)S(1)}, u32[]{:S(2)}, u32[]{:S(2)}) %collective-permute-start.1) | collective-permute-done | bytes 73760 | tf_op jit(solution)/shard_map/ppermute | solution.py:333
  27.5 0.0 all-to-all-done
  27.5 0.0 copy-done.7
  27.5 10.8 %krylov.1 = f32[2304,128]{1,0:T(8,128)S(1)} custom-call(f32[8]{0:T(128)S(1)} %copy-done.7, f32[1280,128]{1,0:T(8,128)S(1)} %bitcast.11, f32[72,8,512]{2,1,0:T(8,128)S(1)} %bitcast.8, f32[9,2,8,128]{3,2,1,0:T(8,128)S(1)} %collective-permute-done.next_ref, f32[9,2,8,128]{3,2,1,0:T(8,128)S(1)} %collective-permute-done.1.prev_ref, ...), custom_call_target="tpu_custom_call" | custom-call | tf_op jit(solution)/shard_map/krylov/pallas_call | solution.py:346
  38.3 0.0 copy-start.2
  38.3 34.2 %all_to_all.10 = f32[32,9,8,128]{3,2,1,0:T(8,128)S(1)} all-to-all(f32[32,9,8,128]{3,2,1,0:T(8,128)S(1)} %bitcast.9), channel_id=1, replica_groups=mesh['groups'=2,'modes'=16] {'modes'}, dimensions={0} | all-to-all | bytes 2359296 | tf_op jit(solution)/shard_map/all_to_all | solution.py:372
  72.5 0.0 copy-done.2
  72.5 1.2 %combine.1 = (f32[2,8,8192]{2,1,0:T(8,128)}, f32[2,8,8192]{2,1,0:T(8,128)}) custom-call(f32[2,8,8192]{2,1,0:T(8,128)S(1)} %copy-done.2, f32[2304,128]{1,0:T(8,128)S(1)} %bitcast.10), custom_call_target="tpu_custom_call" | custom-call | tf_op jit(solution)/shard_map/combine/pallas_call | solution.py:373
Async XLA Ops:
  0.6 9.4 %copy-start = (f32[9,8,8,512]{3,2,1,0:T(8,128)S(1)}, f32[9,8,8,512]{3,2,1,0:T(8,128)}, u32[]{:S(2)}) copy-start(f32[9,8,8,512]{3,2,1,0:T(8,128)} %last_ref.1) | copy-start | bytes 3538948
  0.6 1.1 %copy-start.1 = (f32[2,8,8192]{2,1,0:T(8,128)S(1)}, f32[2,8,8192]{2,1,0:T(8,128)}, u32[]{:S(2)}) copy-start(f32[2,8,8192]{2,1,0:T(8,128)} %rhs_ref.3) | copy-start | bytes 1572868
  2.7 24.8 %all-to-all-start = ((f32[32,5,8,128]{3,2,1,0:T(8,128)}), f32[32,5,8,128]{3,2,1,0:T(8,128)S(1)}, u32[]{:S(2)}, u32[]{:S(2)}) async-start(f32[32,5,8,128]{3,2,1,0:T(8,128)} %arrange.1), calls=%async_computation | async-start | bytes 1310720 | tf_op jit(solution)/shard_map/all_to_all | solution.py:316
  10.1 4.7 %copy-start.3 = (s32[512]{0:T(512)S(1)}, s32[512]{0:T(512)}, u32[]{:S(2)}) copy-start(s32[512]{0:T(512)} %param.10) | copy-start | bytes 6148
  10.1 4.7 %copy-start.4 = (s32[512]{0:T(512)S(1)}, s32[512]{0:T(512)}, u32[]{:S(2)}) copy-start(s32[512]{0:T(512)} %param.11) | copy-start | bytes 6148
  10.1 4.7 %copy-start.5 = (s32[512]{0:T(512)S(1)}, s32[512]{0:T(512)}, u32[]{:S(2)}) copy-start(s32[512]{0:T(512)} %param.12) | copy-start | bytes 6148
  10.1 4.7 %copy-start.6 = (s32[512]{0:T(512)S(1)}, s32[512]{0:T(512)}, u32[]{:S(2)}) copy-start(s32[512]{0:T(512)} %param.13) | copy-start | bytes 6148
  10.1 17.3 %copy-start.7 = (f32[8]{0:T(128)S(1)}, f32[8]{0:T(128)}, u32[]{:S(2)}) copy-start(f32[8]{0:T(128)} %dif_ref.1) | copy-start | bytes 100
  10.3 12.2 %collective-permute-start = (f32[9,2,8,128]{3,2,1,0:T(8,128)S(1)}, f32[9,2,8,128]{3,2,1,0:T(8,128)S(1)}, u32[]{:S(2)}, u32[]{:S(2)}) collective-permute-start(f32[9,2,8,128]{3,2,1,0:T(8,128)S(1)} %get-tuple-element.6), channel_id=1, source_target_pairs={{1,0},{2,1},{3,2},{4,3},{5,4},{6,5},{7,6},{8,7},{9,8},{10,9},{11,1... | collective-permute-start | bytes 221192 | tf_op jit(solution)/shard_map/ppermute | solution.py:332
  14.8 12.7 %collective-permute-start.1 = (f32[9,2,8,128]{3,2,1,0:T(8,128)S(1)}, f32[9,2,8,128]{3,2,1,0:T(8,128)S(1)}, u32[]{:S(2)}, u32[]{:S(2)}) collective-permute-start(f32[9,2,8,128]{3,2,1,0:T(8,128)S(1)} %get-tuple-element.7), channel_id=1, source_target_pairs={{0,1},{1,2},{2,3},{3,4},{4,5},{5,6},{6,7},{7,8},{8,9},{9,10},{10,1... | collective-permute-start | bytes 221192 | tf_op jit(solution)/shard_map/ppermute | solution.py:333
  38.3 34.2 %copy-start.2 = (f32[2,8,8192]{2,1,0:T(8,128)S(1)}, f32[2,8,8192]{2,1,0:T(8,128)}, u32[]{:S(2)}) copy-start(f32[2,8,8192]{2,1,0:T(8,128)} %rhs_ref.3) | copy-start | bytes 1572868

commit v3 on v2

--- a/solution.py
+++ b/solution.py
@@ -93,33 +93,14 @@
     return jnp.where(b > 0.0, a / jnp.where(b > 0.0, b, 1.0), 0.0)
 
 
-def main_kernel(
-    n,
-    tiles,
-    dif_ref,
-    r_ref,
-    jac_ref,
-    next_ref,
-    prev_ref,
-    coup_ref,
-    stencil_ref,
-    out_ref,
-    v_ref,
-    w_ref,
-    z_ref,
-    jh_ref,
-    vs_ref,
-    xs_ref,
-    mx_ref,
-    bs_ref,
-):
-    lane = lane_iota()
-    every = tiles + 1
-    per = 2 * tiles + 1
-
+def transpose_in(r_ref, v_ref, n, every):
     for ct in range(every):
         for s in range(S):
             v_ref[ct, s] = r_ref[pl.ds(ct * S + s, n, stride=every * S), :]
+
+
+def unpack_edges(next_ref, prev_ref, jh_ref):
+    lane = lane_iota()
 
     def unpack(i, _):
         for q in range(S // 4):
@@ -132,103 +113,158 @@
 
     lax.fori_loop(0, NCOEF, unpack, 0)
 
-    def mix(src, ct, slot):
-        wide = lax.broadcasted_iota(jnp.int32, (n, LANES), 1) < LANES // 2
-        before, after = (ct - 1) % every, (ct + 1) % every
-        for t in range(S):
-            at = slice(t * LANES, (t + 1) * LANES)
-            to = slice(t * n, (t + 1) * n)
-            high, low = split(src[ct, t])
-            vs_ref[slot, 0:n, at] = high
-            vs_ref[slot, n : 2 * n, at] = low
-            vs_ref[slot, 2 * n : 3 * n, at] = high
-            xs_ref[slot, to, 0:LANES] = high
-            xs_ref[slot, to, LANES : 2 * LANES] = low
-            high, low = split(jnp.where(wide, src[after, t], src[before, t]))
-            xs_ref[slot, to, 2 * LANES : 3 * LANES] = high
-            xs_ref[slot, to, 3 * LANES :] = low
-        mx_ref[slot] = jnp.dot(coup_ref[...], vs_ref[slot], preferred_element_type=F32)
-        bs_ref[slot] = jnp.dot(xs_ref[slot], stencil_ref[...], preferred_element_type=F32)
-
-    def react(ct, slot, finish):
-        for kb in range(0, n, 32):
-            acc = [None] * 32
-            for i in range(NCOEF):
-                for t in range(S):
-                    m = [
-                        mx_ref[slot, i * n + kb + kt * 8 : i * n + kb + kt * 8 + 8, t * LANES : (t + 1) * LANES]
-                        for kt in range(4)
-                    ]
-                    for s in range(S):
-                        if ct < tiles:
-                            j = jac_ref[i * S + s, t : t + 1, ct * LANES : (ct + 1) * LANES]
-                        else:
-                            j = jh_ref[i * S + s, t : t + 1, :]
-                        j = jnp.broadcast_to(j, (8, LANES))
-                        for kt in range(4):
-                            term = j * m[kt]
-                            at = s * 4 + kt
-                            acc[at] = term if acc[at] is None else acc[at] + term
-            for s in range(S):
-                for kt in range(4):
-                    k = kb + kt * 8
-                    b = bs_ref[slot, s * n + k : s * n + k + 8]
-                    finish(s, k, dif_ref[s] * b - acc[s * 4 + kt])
-
-    def total(x):
+
+def mix(src, ct, slot, every, coup_ref, stencil_ref, vs_ref, xs_ref, mx_ref, bs_ref):
+    n = src.shape[2]
+    wide = lax.broadcasted_iota(jnp.int32, (n, LANES), 1) < LANES // 2
+    before, after = (ct - 1) % every, (ct + 1) % every
+    for t in range(S):
+        at = slice(t * LANES, (t + 1) * LANES)
+        to = slice(t * n, (t + 1) * n)
+        high, low = split(src[ct, t])
+        vs_ref[slot, 0:n, at] = high
+        vs_ref[slot, n : 2 * n, at] = low
+        vs_ref[slot, 2 * n : 3 * n, at] = high
+        xs_ref[slot, to, 0:LANES] = high
+        xs_ref[slot, to, LANES : 2 * LANES] = low
+        high, low = split(jnp.where(wide, src[after, t], src[before, t]))
+        xs_ref[slot, to, 2 * LANES : 3 * LANES] = high
+        xs_ref[slot, to, 3 * LANES :] = low
+    mx_ref[slot] = jnp.dot(coup_ref[...], vs_ref[slot], preferred_element_type=F32)
+    bs_ref[slot] = jnp.dot(xs_ref[slot], stencil_ref[...], preferred_element_type=F32)
+
+
+def react(n, jac, slot, dif_ref, mx_ref, bs_ref, finish):
+    for kb in range(0, n, 32):
+        acc = [None] * 32
+        for i in range(NCOEF):
+            for t in range(S):
+                m = [
+                    mx_ref[slot, i * n + kb + kt * 8 : i * n + kb + kt * 8 + 8, t * LANES : (t + 1) * LANES]
+                    for kt in range(4)
+                ]
+                for s in range(S):
+                    j = jnp.broadcast_to(jac(i * S + s, t), (8, LANES))
+                    for kt in range(4):
+                        term = j * m[kt]
+                        at = s * 4 + kt
+                        acc[at] = term if acc[at] is None else acc[at] + term
+        for s in range(S):
+            for kt in range(4):
+                k = kb + kt * 8
+                b = bs_ref[slot, s * n + k : s * n + k + 8]
+                finish(s, k, dif_ref[s] * b - acc[s * 4 + kt])
+
+
+def tile_of(jac_ref, ct):
+    return lambda row, t: jac_ref[row, t : t + 1, ct * LANES : (ct + 1) * LANES]
+
+
+class Sums:
+    def __init__(self):
+        self.parts = {}
+
+    def add(self, name, at, term):
+        mine = self.parts.setdefault(name, {})
+        mine[at % 4] = mine[at % 4] + term if at % 4 in mine else term
+
+    def total(self, name):
+        x = functools.reduce(lambda a, b: a + b, self.parts[name].values())
         return jnp.broadcast_to(jnp.sum(x, axis=(0, 1), keepdims=True), (8, LANES))
 
-    sums = {}
-
-    def gather(name, at, term):
-        key = (name, at % 4)
-        sums[key] = sums[key] + term if key in sums else term
-
-    def collect(name):
-        parts = [value for (key, _), value in sums.items() if key == name]
-        return total(functools.reduce(lambda a, b: a + b, parts))
-
-    def finish_first(ct):
+
+def first_kernel(
+    n,
+    tiles,
+    place_ref,
+    dif_ref,
+    r_ref,
+    jac_ref,
+    next_ref,
+    prev_ref,
+    coup_ref,
+    stencil_ref,
+    v_ref,
+    w_ref,
+    sum_ref,
+    *refs,
+):
+    every = tiles + 1
+    send_refs, (jh_ref, vs_ref, xs_ref, mx_ref, bs_ref) = refs[: n // 8], refs[n // 8 :]
+    work = (coup_ref, stencil_ref, vs_ref, xs_ref, mx_ref, bs_ref)
+    transpose_in(r_ref, v_ref, n, every)
+    unpack_edges(next_ref, prev_ref, jh_ref)
+    sums = Sums()
+
+    def finisher(ct):
         def finish(s, k, w):
             w_ref[ct, s, k : k + 8] = w
             if ct < tiles:
                 v = v_ref[ct, s, k : k + 8]
-                out_ref[pl.ds(k * per * S + ct * S + s, 8, stride=per * S), :] = w
-                gather("rr", k // 8, v * v)
-                gather("rw", k // 8, v * w)
+                sums.add("rr", k // 8, v * v)
+                sums.add("rw", k // 8, v * w)
 
         return finish
 
-    def finish_second(ct, c1):
+    order = list(range(tiles)) + [tiles]
+    mix(v_ref, order[0], 0, every, *work)
+    for at, ct in enumerate(order):
+        if at + 1 < every:
+            mix(v_ref, order[at + 1], (at + 1) % 2, every, *work)
+        jac = tile_of(jac_ref, ct) if ct < tiles else tile_of(jh_ref, 0)
+        react(n, jac, at % 2, dif_ref, mx_ref, bs_ref, finisher(ct))
+    for q in range(n // 8):
+        at = pl.multiple_of(jnp.bitwise_xor(place_ref[0], q) * 8, 8)
+        for ct in range(tiles):
+            for s in range(S):
+                send_refs[q][pl.ds(ct * S + s, 8, stride=tiles * S), :] = w_ref[ct, s, pl.ds(at, 8)]
+    sum_ref[0:8] = sums.total("rr")
+    sum_ref[8:16] = sums.total("rw")
+
+
+def second_kernel(
+    n,
+    tiles,
+    dif_ref,
+    v_ref,
+    w_ref,
+    sum_ref,
+    jac_ref,
+    coup_ref,
+    stencil_ref,
+    out_ref,
+    z_ref,
+    vs_ref,
+    xs_ref,
+    mx_ref,
+    bs_ref,
+):
+    every = tiles + 1
+    per = tiles * S + 1
+    work = (coup_ref, stencil_ref, vs_ref, xs_ref, mx_ref, bs_ref)
+    rr, rw = sum_ref[0:8], sum_ref[8:16]
+    c1 = ratio(rw, rr)
+    sums = Sums()
+
+    def finisher(ct):
         def finish(s, k, z):
             v, w = v_ref[ct, s, k : k + 8], w_ref[ct, s, k : k + 8]
             z_ref[ct, s, k : k + 8] = z
-            out_ref[pl.ds(k * per * S + (tiles + ct) * S + s, 8, stride=per * S), :] = z
+            out_ref[pl.ds(k * per + ct * S + s, 8, stride=per), :] = z
             u = w - c1 * v
-            gather("uu", k // 8, u * u)
-            gather("ur", k // 8, u * v)
-            gather("uz", k // 8, u * z)
-            gather("rz", k // 8, v * z)
+            sums.add("uu", k // 8, u * u)
+            sums.add("ur", k // 8, u * v)
+            sums.add("uz", k // 8, u * z)
+            sums.add("rz", k // 8, v * z)
 
         return finish
 
-    order = [tiles] + list(range(tiles))
-    mix(v_ref, order[0], 0)
-    for at, ct in enumerate(order):
-        if at + 1 < every:
-            mix(v_ref, order[at + 1], (at + 1) % 2)
-        elif tiles > 1:
-            mix(w_ref, 0, every % 2)
-        react(ct, at % 2, finish_first(ct))
-    if tiles == 1:
-        mix(w_ref, 0, every % 2)
-    rr, rw = collect("rr"), collect("rw")
-    c1 = ratio(rw, rr)
+    mix(w_ref, 0, 0, every, *work)
     for ct in range(tiles):
         if ct + 1 < tiles:
-            mix(w_ref, ct + 1, (every + ct + 1) % 2)
-        react(ct, (every + ct) % 2, finish_second(ct, c1))
-    uu, ur, uz, rz = (collect(name) for name in ("uu", "ur", "uz", "rz"))
+            mix(w_ref, ct + 1, (ct + 1) % 2, every, *work)
+        react(n, tile_of(jac_ref, ct), ct % 2, dif_ref, mx_ref, bs_ref, finisher(ct))
+    uu, ur, uz, rz = (sums.total(name) for name in ("uu", "ur", "uz", "rz"))
     c2 = ratio(rz, rr)
     c3 = ratio(uz - c2 * ur, uu)
     for ct in range(tiles):
@@ -236,22 +272,34 @@
             for k in range(0, n, 8):
                 v, w, z = (ref[ct, s, k : k + 8] for ref in (v_ref, w_ref, z_ref))
                 x = (z - c2 * v) - c3 * (w - c1 * v)
-                gather("xx", k // 8, x * x)
-    xx = collect("xx")
-    stat = lax.broadcasted_iota(jnp.int32, (8, LANES), 0)
+                sums.add("xx", k // 8, x * x)
+    xx = sums.total("xx")
+    lane = lane_iota()
     tile = jnp.zeros((8, LANES), F32)
     for q, value in enumerate((rr, c1, uu, c2, c3, xx)):
-        tile = jnp.where(stat == q, value, tile)
-    for k in range(n):
-        out_ref[(k * per + 2 * tiles) * S : (k * per + per) * S, :] = tile
-
-
-def combine_kernel(parts, tiles, rhs_ref, got_ref, update_ref, basis_ref):
+        tile = jnp.where(lane == q, value, tile)
+    for k in range(0, n, 8):
+        out_ref[pl.ds(k * per + tiles * S, 8, stride=per), :] = tile
+
+
+def relay_kernel(own, place_ref, *refs):
+    parts = 8 // own
+    count = len(refs) - parts
+    for k in range(parts):
+        at = jnp.bitwise_xor(place_ref[1], k)
+        for q in range(count):
+            refs[count + k][q] = refs[q][at]
+
+
+def combine_kernel(parts, tiles, place_ref, rhs_ref, got_ref, *refs):
     own = rhs_ref.shape[0]
-    per = 2 * tiles + 1
+    plane = 8 // own
+    w_refs, (update_ref, basis_ref) = refs[:plane], refs[plane:]
+    per = tiles * S + 1
+    stats = got_ref[pl.ds(tiles * S, parts, stride=own * per), :]
 
     def stat(q):
-        return got_ref[pl.ds(2 * tiles * S + q, parts, stride=own * per * S), :]
+        return jnp.broadcast_to(stats[:, q : q + 1], (parts, LANES))
 
     def add(x):
         return jnp.sum(x, axis=0, keepdims=True)
@@ -289,12 +337,17 @@
         for m in range(own):
             for ct in range(tiles):
                 at = slice((d * tiles + ct) * LANES, (d * tiles + ct + 1) * LANES)
-                base = ((d * own + m) * per + ct) * S
-                r = rhs_ref[m, :, at]
-                w = got_ref[base : base + S, :]
-                z = got_ref[base + tiles * S : base + tiles * S + S, :]
-                update_ref[m, :, at] = ur * r + uw * w
-                basis_ref[m, :, at] = br * r + bw * w + bz * z
+                base = (d * own + m) * per + ct * S
+                basis_ref[m, :, at] = br * rhs_ref[m, :, at] + bz * got_ref[base : base + S, :]
+    for k in range(plane):
+        for q in range(parts // plane):
+            d = jnp.bitwise_xor(place_ref[0], q) * plane + jnp.bitwise_xor(place_ref[1], k)
+            for m in range(own):
+                for ct in range(tiles):
+                    at = pl.ds(pl.multiple_of(d * (tiles * LANES) + ct * LANES, LANES), LANES)
+                    w = w_refs[k][q, m, ct * S : (ct + 1) * S, :]
+                    update_ref[m, :, at] = ur * rhs_ref[m, :, at] + uw * w
+                    basis_ref[m, :, at] += bw * w
 
 
 def local(rhs, diffusivity, jac_coef, coef_index, row_mode, col_mode, multiplicity):
@@ -303,7 +356,11 @@
     n = own * parts
     cells = total // parts
     tiles = cells // LANES
+    plane = 8 // own
     sds = jax.ShapeDtypeStruct
+    smem = pl.BlockSpec(memory_space=pltpu.SMEM)
+    index = lax.axis_index("modes")
+    place = jnp.stack([index // plane, index % plane]).astype(jnp.int32)
 
     send = pl.pallas_call(
         functools.partial(arrange_kernel, parts),
@@ -341,43 +398,62 @@
         name="coupling",
     )(*(x.reshape(1, -1) for x in (coef_index, row_mode, col_mode, multiplicity)))
 
-    per = 2 * tiles + 1
-    field = pltpu.VMEM((tiles + 1, S, n, LANES), F32)
-    out = pl.pallas_call(
-        functools.partial(main_kernel, n, tiles),
-        out_shape=sds((n * per * S, LANES), F32),
-        in_specs=[pl.BlockSpec(memory_space=pltpu.SMEM)] + [VMEM] * 6,
+    jac = jac_coef.reshape(NCOEF * S, S, cells)
+    field = (tiles + 1, S, n, LANES)
+    work = [
+        pltpu.VMEM((2, 3 * n, S * LANES), BF16),
+        pltpu.VMEM((2, S * n, 4 * LANES), BF16),
+        pltpu.VMEM((2, NCOEF * n, S * LANES), F32),
+        pltpu.VMEM((2, S * n, LANES), F32),
+    ]
+    v, w, sums, *w_send = pl.pallas_call(
+        functools.partial(first_kernel, n, tiles),
+        out_shape=[sds(field, F32)] * 2 + [sds((16, LANES), F32)] + [sds((8 * tiles * S, LANES), F32)] * (n // 8),
+        in_specs=[smem] * 2 + [VMEM] * 6,
+        out_specs=[VMEM] * (3 + n // 8),
+        scratch_shapes=[pltpu.VMEM((NCOEF * S, S, LANES), F32)] + work,
+        compiler_params=PARAMS,
+        name="first",
+    )(place, diffusivity, vector.reshape(n * (tiles + 1) * S, LANES), jac, after, before, coupling, stencil)
+
+    moved = w_send[:1]
+    for q in range(1, n // 8):
+        moved.append(lax.ppermute(w_send[q], "modes", [(i, i ^ (q * plane)) for i in range(parts)]))
+
+    z_send = pl.pallas_call(
+        functools.partial(second_kernel, n, tiles),
+        out_shape=sds((n * (tiles * S + 1), LANES), F32),
+        in_specs=[smem] + [VMEM] * 6,
         out_specs=VMEM,
-        scratch_shapes=[
-            field,
-            field,
-            field,
-            pltpu.VMEM((NCOEF * S, S, LANES), F32),
-            pltpu.VMEM((2, 3 * n, S * LANES), BF16),
-            pltpu.VMEM((2, S * n, 4 * LANES), BF16),
-            pltpu.VMEM((2, NCOEF * n, S * LANES), F32),
-            pltpu.VMEM((2, S * n, LANES), F32),
-        ],
-        compiler_params=PARAMS,
-        name="krylov",
-    )(
-        diffusivity,
-        vector.reshape(n * (tiles + 1) * S, LANES),
-        jac_coef.reshape(NCOEF * S, S, cells),
-        after,
-        before,
-        coupling,
-        stencil,
-    )
-    got = lax.all_to_all(out.reshape(n, per, S, LANES), "modes", split_axis=0, concat_axis=0, tiled=True)
+        scratch_shapes=[pltpu.VMEM(field, F32)] + work,
+        compiler_params=PARAMS,
+        cost_estimate=pl.CostEstimate(flops=2 * NCOEF * S * n * n * cells, bytes_accessed=16 << 20, transcendentals=0),
+        name="second",
+    )(diffusivity, v, w, sums, jac, coupling, stencil)
+    line = (tiles * S + 1) * LANES
+    got = lax.all_to_all(z_send.reshape(n, 1, line), "modes", split_axis=0, concat_axis=0, tiled=True)
+
+    relayed = pl.pallas_call(
+        functools.partial(relay_kernel, own),
+        out_shape=[sds((n // 8, own, tiles * S, LANES), F32)] * plane,
+        in_specs=[smem] + [VMEM] * (n // 8),
+        out_specs=[VMEM] * plane,
+        compiler_params=PARAMS,
+        cost_estimate=pl.CostEstimate(flops=10**11, bytes_accessed=1 << 20, transcendentals=0),
+        name="relay",
+    )(place, *(x.reshape(plane, own, tiles * S, LANES) for x in moved))
+    w_own = [relayed[0]]
+    for k in range(1, plane):
+        w_own.append(lax.ppermute(relayed[k], "modes", [(i, i ^ k) for i in range(parts)]))
+
     update, basis_next = pl.pallas_call(
         functools.partial(combine_kernel, parts, tiles),
         out_shape=[sds(rhs.shape, F32)] * 2,
-        in_specs=[VMEM] * 2,
+        in_specs=[smem] + [VMEM] * (2 + plane),
         out_specs=[VMEM] * 2,
         compiler_params=PARAMS,
         name="combine",
-    )(rhs, got.reshape(n * per * S, LANES))
+    )(place, rhs, got.reshape(n * (tiles * S + 1), LANES), *w_own)
     return (update, basis_next)
 
 

time: 74 us -> 66.6 us (0.90)
  blocking collectives: 34.2 us -> 0 us
  waiting for transfers between devices: 12.4 us -> 24.3 us
  starting transfers between devices: 11.8 us -> 23.2 us
  Pallas kernels: 13.4 us -> 16.7 us
    all_to_all x1 -> x0, blocking collectives: 34.2 us -> none  [local(): lax.all_to_all(out.reshape(n, per, S, LANES), 'modes', split_axis=0, conc...]
    ppermute x0 -> x6, waiting for transfers between devices: none -> 10 us  [the longest x3 10 us: local(): lax.ppermute(relayed[k], 'modes', [(i, i ^ k) for i in range(parts)])]
    ppermute x0 -> x6, starting transfers between devices: none -> 6.62 us  [the longest x3 4.47 us: local(): lax.ppermute(w_send[q], 'modes', [(i, i ^ q * plane) for i in range(parts)])]
    all_to_all x0 -> x1, starting transfers between devices: none -> 4.76 us  [local(): lax.all_to_all(z_send.reshape(n, 1, line), 'modes', split_axis=0, concat_...]
    pallas_call x1 -> x3, Pallas kernels: 10.8 us -> 13.3 us  [the longest x1 6.78 us: local(): pl.pallas_call(functools.partial(first_kernel, n, tiles), out_shape=[sds(...]
    all_to_all x0 -> x1, waiting for transfers between devices: none -> 1.93 us  [local(): lax.all_to_all(z_send.reshape(n, 1, line), 'modes', split_axis=0, concat_...]
    pallas_call x1, Pallas kernels: 1.17 us -> 2.09 us  [local(): pl.pallas_call(functools.partial(combine_kernel, parts, tiles), out_shape...]
  transfers between devices with their start and end apart: 3 -> 10, of which waited for: 2 -> 5; matrix products, arithmetic and copies ran while one was open for 0% -> 0% of each run, Pallas kernels for 1% -> 10%
where the time goes in v3:
time: 66.6 us; the launch traced here: 66.3 us
  waiting for transfers between devices  24.3 us (36%)
  starting transfers between devices  23.2 us (35%)
  Pallas kernels  16.7 us (25%)
  local copies, waits for them, and re-layouts  1.17 us (2%)
  between operations  0.8 us (1%)
    ppermute x3, waiting for transfers between devices, local(): lax.ppermute(relayed[k], 'modes', [(i, i ^ k) for i in range(parts)])  10 us
    all_to_all x1, starting transfers between devices, local(): lax.all_to_all(send, 'modes', split_axis=0, concat_axis=0, tiled=True)  7.39 us
    ppermute x1, waiting for transfers between devices, local(): after = lax.ppermute(head, 'modes', down)  7.35 us
    pallas_call x1, Pallas kernels, local(): pl.pallas_call(functools.partial(first_kernel, n, tiles), out_shape=[sds(...  6.78 us
    pallas_call x1, Pallas kernels, local(): pl.pallas_call(functools.partial(second_kernel, n, tiles), out_shape=sds(...  5.92 us
    ppermute x1, waiting for transfers between devices, local(): before = lax.ppermute(tail, 'modes', up)  4.97 us
    all_to_all x1, starting transfers between devices, local(): lax.all_to_all(z_send.reshape(n, 1, line), 'modes', split_axis=0, concat_...  4.76 us
    ppermute x3, starting transfers between devices, local(): lax.ppermute(w_send[q], 'modes', [(i, i ^ q * plane) for i in range(parts)])  4.47 us
  transfers between devices with their start and end apart: 10, of which 5 were waited for; matrix products, arithmetic and copies ran while one was open for 0% of the time, Pallas kernels for 10%

profile of v3, /device:TPU:0, one launch (start us, length us, event | category | flops | bytes accessed | tf_op | source)
XLA Modules:
  0.0 66.3 jit_solution(13320996328731024414)
XLA Ops:
  0.6 0.0 copy-start.1
  0.7 1.1 %copy-done.1 = f32[2,8,8192]{2,1,0:T(8,128)S(1)} copy-done((f32[2,8,8192]{2,1,0:T(8,128)S(1)}, f32[2,8,8192]{2,1,0:T(8,128)}, u32[]{:S(2)}) %copy-start.1) | copy-done | bytes 524312
  1.8 0.9 %arrange.1 = f32[32,5,8,128]{3,2,1,0:T(8,128)} custom-call(f32[2,8,8192]{2,1,0:T(8,128)S(1)} %copy-done.1), custom_call_target="tpu_custom_call" | custom-call | tf_op jit(solution)/shard_map/arrange/pallas_call | solution.py:365
  2.7 7.4 %all-to-all-start = ((f32[32,5,8,128]{3,2,1,0:T(8,128)}), f32[32,5,8,128]{3,2,1,0:T(8,128)S(1)}, u32[]{:S(2)}, u32[]{:S(2)}) async-start(f32[32,5,8,128]{3,2,1,0:T(8,128)} %arrange.1), calls=%async_computation | async-start | bytes 1310720 | tf_op jit(solution)/shard_map/all_to_all | solution.py:373
  10.1 0.0 copy-start.3
  10.1 0.0 copy-start.4
  10.1 0.0 copy-start.5
  10.1 0.0 copy-start.6
  10.1 0.0 copy-start.7
  10.2 0.2 pack.1
  10.3 4.4 %collective-permute-start = (f32[9,2,8,128]{3,2,1,0:T(8,128)S(1)}, f32[9,2,8,128]{3,2,1,0:T(8,128)S(1)}, u32[]{:S(2)}, u32[]{:S(2)}) collective-permute-start(f32[9,2,8,128]{3,2,1,0:T(8,128)S(1)} %get-tuple-element.17), channel_id=1, source_target_pairs={{1,0},{2,1},{3,2},{4,3},{5,4},{6,5},{7,6},{8,7},{9,8},{10,9},{11,1... | collective-permute-start | bytes 221192 | tf_op jit(solution)/shard_map/ppermute | solution.py:389
  14.8 0.0 collective-permute-start.1
  14.8 0.3 coupling.1
  15.1 0.1 pad_add_fusion.place_ref
  15.2 7.3 %collective-permute-done.next_ref = f32[9,2,8,128]{3,2,1,0:T(8,128)S(1)} collective-permute-done((f32[9,2,8,128]{3,2,1,0:T(8,128)S(1)}, f32[9,2,8,128]{3,2,1,0:T(8,128)S(1)}, u32[]{:S(2)}, u32[]{:S(2)}) %collective-permute-start) | collective-permute-done | bytes 73760 | tf_op jit(solution)/shard_map/ppermute | solution.py:389
  22.5 5.0 %collective-permute-done.1.prev_ref = f32[9,2,8,128]{3,2,1,0:T(8,128)S(1)} collective-permute-done((f32[9,2,8,128]{3,2,1,0:T(8,128)S(1)}, f32[9,2,8,128]{3,2,1,0:T(8,128)S(1)}, u32[]{:S(2)}, u32[]{:S(2)}) %collective-permute-start.1) | collective-permute-done | bytes 73760 | tf_op jit(solution)/shard_map/ppermute | solution.py:390
  27.5 0.0 all-to-all-done
  27.5 6.8 %first.1 = (f32[5,8,32,128]{3,2,1,0:T(8,128)S(1)}, f32[5,8,32,128]{3,2,1,0:T(8,128)S(1)}, f32[16,128]{1,0:T(8,128)S(1)}, f32[256,128]{1,0:T(8,128)S(1)}, f32[256...) custom-call(s32[2]{0:T(128)S(1)} %pad_add_fusion.place_ref, f32[8]{0:T(128)S(1)} %copy-done.7, ...), custom_call_target="tpu_custom_call" | custom-call | tf_op jit(solution)/shard_map/first/pallas_call | solution.py:409
  34.3 1.7 %collective-permute-start.2 = (f32[256,128]{1,0:T(8,128)S(1)}, f32[256,128]{1,0:T(8,128)S(1)}, u32[]{:S(2)}, u32[]{:S(2)}) collective-permute-start(f32[256,128]{1,0:T(8,128)S(1)} %get-tuple-element.25), channel_id=1, source_target_pairs={{0,4},{1,5},{2,6},{3,7},{4,0},{5,1},{6,2},{7,3},{8,12},{9,13},{10,... | collective-permute-start | bytes 393224 | tf_op jit(solution)/shard_map/ppermute | solution.py:421
  36.0 1.4 %collective-permute-start.3 = (f32[256,128]{1,0:T(8,128)S(1)}, f32[256,128]{1,0:T(8,128)S(1)}, u32[]{:S(2)}, u32[]{:S(2)}) collective-permute-start(f32[256,128]{1,0:T(8,128)S(1)} %get-tuple-element.26), channel_id=1, source_target_pairs={{0,8},{1,9},{2,10},{3,11},{4,12},{5,13},{6,14},{7,15},{8,0},{9,1},... | collective-permute-start | bytes 393224 | tf_op jit(solution)/shard_map/ppermute | solution.py:421
  37.3 1.4 %collective-permute-start.4 = (f32[256,128]{1,0:T(8,128)S(1)}, f32[256,128]{1,0:T(8,128)S(1)}, u32[]{:S(2)}, u32[]{:S(2)}) collective-permute-start(f32[256,128]{1,0:T(8,128)S(1)} %get-tuple-element.27), channel_id=1, source_target_pairs={{0,12},{1,13},{2,14},{3,15},{4,8},{5,9},{6,10},{7,11},{8,4},{9,5},... | collective-permute-start | bytes 393224 | tf_op jit(solution)/shard_map/ppermute | solution.py:421
  38.7 5.9 %second.1 = f32[1056,128]{1,0:T(8,128)} custom-call(f32[8]{0:T(128)S(1)} %copy-done.7, f32[5,8,32,128]{3,2,1,0:T(8,128)S(1)} %get-tuple-element.21.v_ref, f32[5,8,32,128]{3,2,1,0:T(8,128)S(1)} %get-tuple-element.22.w_ref, f32[16,128]{1,0:T(8,128)S(1)} %get-tuple-element.23.sum_ref, f32[72,8,512]{2,1,0:T(8,128)S(1)} %bitcast.15, ...), custom_call_target="tpu_custom_call" | custom-call | flops 75497472 | bytes 16777216 | tf_op jit(solution)/shard_map/second/pallas_call | solution.py:423
  44.7 4.8 %all-to-all-start.1 = ((f32[32,1,4224]{2,1,0:T(1,128)}), f32[32,1,4224]{2,1,0:T(1,128)S(1)}, u32[]{:S(2)}, u32[]{:S(2)}) async-start(f32[32,1,4224]{2,1,0:T(1,128)} %bitcast.8), calls=%async_computation.1 | async-start | bytes 1081344 | tf_op jit(solution)/shard_map/all_to_all | solution.py:434
  49.4 0.0 collective-permute-done.2
  49.4 0.0 copy-start.2
  49.5 0.6 relay.1
  50.0 0.5 collective-permute-start.5
  50.5 1.7 %collective-permute-start.6 = (f32[4,2,32,128]{3,2,1,0:T(8,128)S(1)}, f32[4,2,32,128]{3,2,1,0:T(8,128)S(1)}, u32[]{:S(2)}, u32[]{:S(2)}) collective-permute-start(f32[4,2,32,128]{3,2,1,0:T(8,128)S(1)} %get-tuple-element.30), channel_id=1, source_target_pairs={{0,2},{1,3},{2,0},{3,1},{4,6},{5,7},{6,4},{7,5},{8,10},{9,11},{10,... | collective-permute-start | bytes 393224 | tf_op jit(solution)/shard_map/ppermute | solution.py:447
  52.2 7.9 %collective-permute-done.6.refs_2_ = f32[4,2,32,128]{3,2,1,0:T(8,128)S(1)} collective-permute-done((f32[4,2,32,128]{3,2,1,0:T(8,128)S(1)}, f32[4,2,32,128]{3,2,1,0:T(8,128)S(1)}, u32[]{:S(2)}, u32[]{:S(2)}) %collective-permute-start.6) | collective-permute-done | bytes 131104 | tf_op jit(solution)/shard_map/ppermute | solution.py:447
  60.2 2.1 %collective-permute-done.7.refs_3_ = f32[4,2,32,128]{3,2,1,0:T(8,128)S(1)} collective-permute-done((f32[4,2,32,128]{3,2,1,0:T(8,128)S(1)}, f32[4,2,32,128]{3,2,1,0:T(8,128)S(1)}, u32[]{:S(2)}, u32[]{:S(2)}) %collective-permute-start.7) | collective-permute-done | bytes 131104 | tf_op jit(solution)/shard_map/ppermute | solution.py:447
  62.2 1.9 %all-to-all-done.1 = f32[32,1,4224]{2,1,0:T(1,128)S(1)} async-done(((f32[32,1,4224]{2,1,0:T(1,128)}), f32[32,1,4224]{2,1,0:T(1,128)S(1)}, u32[]{:S(2)}, u32[]{:S(2)}) %all-to-all-start.1) | async-done | bytes 540704 | tf_op jit(solution)/shard_map/all_to_all | solution.py:434
  64.2 2.1 %combine.1 = (f32[2,8,8192]{2,1,0:T(8,128)}, f32[2,8,8192]{2,1,0:T(8,128)}) custom-call(s32[2]{0:T(128)S(1)} %pad_add_fusion.place_ref, f32[2,8,8192]{2,1,0:T(8,128)S(1)} %copy-done.2, f32[1056,128]{1,0:T(8,128)S(1)} %bitcast.17, f32[4,2,32,128]{3,2,1,0:T(8,128)S(1)} %get-tuple-element.28.refs_0_, f32[4,2,32,128]{3,2,1,0:T(8,128)S(1)} %collective-permute-done.5.refs_1_, ...), custom_call_target="tpu_custom_call" | custom-call | tf_op jit(solution)/shard_map/combine/pallas_call | solution.py:449
  (12 shorter events, 0.0 us)
Async XLA Ops:
  0.6 9.5 %copy-start = (f32[9,8,8,512]{3,2,1,0:T(8,128)S(1)}, f32[9,8,8,512]{3,2,1,0:T(8,128)}, u32[]{:S(2)}) copy-start(f32[9,8,8,512]{3,2,1,0:T(8,128)} %last_ref.1) | copy-start | bytes 3538948
  0.6 1.1 %copy-start.1 = (f32[2,8,8192]{2,1,0:T(8,128)S(1)}, f32[2,8,8192]{2,1,0:T(8,128)}, u32[]{:S(2)}) copy-start(f32[2,8,8192]{2,1,0:T(8,128)} %rhs_ref.3) | copy-start | bytes 1572868
  2.7 24.8 %all-to-all-start = ((f32[32,5,8,128]{3,2,1,0:T(8,128)}), f32[32,5,8,128]{3,2,1,0:T(8,128)S(1)}, u32[]{:S(2)}, u32[]{:S(2)}) async-start(f32[32,5,8,128]{3,2,1,0:T(8,128)} %arrange.1), calls=%async_computation | async-start | bytes 1310720 | tf_op jit(solution)/shard_map/all_to_all | solution.py:373
  10.1 4.7 %copy-start.3 = (s32[512]{0:T(512)S(1)}, s32[512]{0:T(512)}, u32[]{:S(2)}) copy-start(s32[512]{0:T(512)} %param.10) | copy-start | bytes 6148
  10.1 4.7 %copy-start.4 = (s32[512]{0:T(512)S(1)}, s32[512]{0:T(512)}, u32[]{:S(2)}) copy-start(s32[512]{0:T(512)} %param.11) | copy-start | bytes 6148
  10.1 4.7 %copy-start.5 = (s32[512]{0:T(512)S(1)}, s32[512]{0:T(512)}, u32[]{:S(2)}) copy-start(s32[512]{0:T(512)} %param.12) | copy-start | bytes 6148
  10.1 4.7 %copy-start.6 = (s32[512]{0:T(512)S(1)}, s32[512]{0:T(512)}, u32[]{:S(2)}) copy-start(s32[512]{0:T(512)} %param.13) | copy-start | bytes 6148
  10.1 17.3 %copy-start.7 = (f32[8]{0:T(128)S(1)}, f32[8]{0:T(128)}, u32[]{:S(2)}) copy-start(f32[8]{0:T(128)} %dif_ref.3) | copy-start | bytes 100
  10.3 12.2 %collective-permute-start = (f32[9,2,8,128]{3,2,1,0:T(8,128)S(1)}, f32[9,2,8,128]{3,2,1,0:T(8,128)S(1)}, u32[]{:S(2)}, u32[]{:S(2)}) collective-permute-start(f32[9,2,8,128]{3,2,1,0:T(8,128)S(1)} %get-tuple-element.17), channel_id=1, source_target_pairs={{1,0},{2,1},{3,2},{4,3},{5,4},{6,5},{7,6},{8,7},{9,8},{10,9},{11,1... | collective-permute-start | bytes 221192 | tf_op jit(solution)/shard_map/ppermute | solution.py:389
  14.8 12.7 %collective-permute-start.1 = (f32[9,2,8,128]{3,2,1,0:T(8,128)S(1)}, f32[9,2,8,128]{3,2,1,0:T(8,128)S(1)}, u32[]{:S(2)}, u32[]{:S(2)}) collective-permute-start(f32[9,2,8,128]{3,2,1,0:T(8,128)S(1)} %get-tuple-element.18), channel_id=1, source_target_pairs={{0,1},{1,2},{2,3},{3,4},{4,5},{5,6},{6,7},{7,8},{8,9},{9,10},{10,1... | collective-permute-start | bytes 221192 | tf_op jit(solution)/shard_map/ppermute | solution.py:390
  34.3 15.2 %collective-permute-start.2 = (f32[256,128]{1,0:T(8,128)S(1)}, f32[256,128]{1,0:T(8,128)S(1)}, u32[]{:S(2)}, u32[]{:S(2)}) collective-permute-start(f32[256,128]{1,0:T(8,128)S(1)} %get-tuple-element.25), channel_id=1, source_target_pairs={{0,4},{1,5},{2,6},{3,7},{4,0},{5,1},{6,2},{7,3},{8,12},{9,13},{10,... | collective-permute-start | bytes 393224 | tf_op jit(solution)/shard_map/ppermute | solution.py:421
  36.0 13.5 %collective-permute-start.3 = (f32[256,128]{1,0:T(8,128)S(1)}, f32[256,128]{1,0:T(8,128)S(1)}, u32[]{:S(2)}, u32[]{:S(2)}) collective-permute-start(f32[256,128]{1,0:T(8,128)S(1)} %get-tuple-element.26), channel_id=1, source_target_pairs={{0,8},{1,9},{2,10},{3,11},{4,12},{5,13},{6,14},{7,15},{8,0},{9,1},... | collective-permute-start | bytes 393224 | tf_op jit(solution)/shard_map/ppermute | solution.py:421
  37.3 12.1 %collective-permute-start.4 = (f32[256,128]{1,0:T(8,128)S(1)}, f32[256,128]{1,0:T(8,128)S(1)}, u32[]{:S(2)}, u32[]{:S(2)}) collective-permute-start(f32[256,128]{1,0:T(8,128)S(1)} %get-tuple-element.27), channel_id=1, source_target_pairs={{0,12},{1,13},{2,14},{3,15},{4,8},{5,9},{6,10},{7,11},{8,4},{9,5},... | collective-permute-start | bytes 393224 | tf_op jit(solution)/shard_map/ppermute | solution.py:421
  44.7 19.5 %all-to-all-start.1 = ((f32[32,1,4224]{2,1,0:T(1,128)}), f32[32,1,4224]{2,1,0:T(1,128)S(1)}, u32[]{:S(2)}, u32[]{:S(2)}) async-start(f32[32,1,4224]{2,1,0:T(1,128)} %bitcast.8), calls=%async_computation.1 | async-start | bytes 1081344 | tf_op jit(solution)/shard_map/all_to_all | solution.py:434
  49.4 14.7 %copy-start.2 = (f32[2,8,8192]{2,1,0:T(8,128)S(1)}, f32[2,8,8192]{2,1,0:T(8,128)}, u32[]{:S(2)}) copy-start(f32[2,8,8192]{2,1,0:T(8,128)} %rhs_ref.3) | copy-start | bytes 1572868
  50.0 2.2 %collective-permute-start.5 = (f32[4,2,32,128]{3,2,1,0:T(8,128)S(1)}, f32[4,2,32,128]{3,2,1,0:T(8,128)S(1)}, u32[]{:S(2)}, u32[]{:S(2)}) collective-permute-start(f32[4,2,32,128]{3,2,1,0:T(8,128)S(1)} %get-tuple-element.29), channel_id=1, source_target_pairs={{0,1},{1,0},{2,3},{3,2},{4,5},{5,4},{6,7},{7,6},{8,9},{9,8},{10,11... | collective-permute-start | bytes 393224 | tf_op jit(solution)/shard_map/ppermute | solution.py:447
  50.5 9.6 %collective-permute-start.6 = (f32[4,2,32,128]{3,2,1,0:T(8,128)S(1)}, f32[4,2,32,128]{3,2,1,0:T(8,128)S(1)}, u32[]{:S(2)}, u32[]{:S(2)}) collective-permute-start(f32[4,2,32,128]{3,2,1,0:T(8,128)S(1)} %get-tuple-element.30), channel_id=1, source_target_pairs={{0,2},{1,3},{2,0},{3,1},{4,6},{5,7},{6,4},{7,5},{8,10},{9,11},{10,... | collective-permute-start | bytes 393224 | tf_op jit(solution)/shard_map/ppermute | solution.py:447
  52.2 10.0 %collective-permute-start.7 = (f32[4,2,32,128]{3,2,1,0:T(8,128)S(1)}, f32[4,2,32,128]{3,2,1,0:T(8,128)S(1)}, u32[]{:S(2)}, u32[]{:S(2)}) collective-permute-start(f32[4,2,32,128]{3,2,1,0:T(8,128)S(1)} %get-tuple-element.31), channel_id=1, source_target_pairs={{0,3},{1,2},{2,1},{3,0},{4,7},{5,6},{6,5},{7,4},{8,11},{9,10},{10,... | collective-permute-start | bytes 393224 | tf_op jit(solution)/shard_map/ppermute | solution.py:447

commit v4 on v3

--- a/solution.py
+++ b/solution.py
@@ -21,19 +21,27 @@
     return lax.broadcasted_iota(jnp.int32, (S, LANES), 1)
 
 
-def arrange_kernel(parts, rhs_ref, out_ref):
+def arrange_kernel(parts, early, place_ref, rhs_ref, out_ref, *refs):
     own, _, total = rhs_ref.shape
     cells = total // parts
     tiles = cells // LANES
+    plane = 8 // own
     low = lane_iota() < LANES // 2
+    for q in range(parts // plane):
+        base = jnp.bitwise_xor(place_ref[0], q) * plane
+        for k in range(plane):
+            for m in range(own):
+                for ct in range(early):
+                    at = pl.multiple_of((base + k) * cells + ct * LANES, LANES)
+                    refs[q][k, m, ct * S : (ct + 1) * S, :] = rhs_ref[m, :, pl.ds(at, LANES)]
     for d in range(parts):
         after = ((d + 1) * cells) % total
         before = (d * cells - LANES) % total
         for m in range(own):
-            for ct in range(tiles):
+            for ct in range(early, tiles):
                 at = d * cells + ct * LANES
-                out_ref[d * own + m, ct] = rhs_ref[m, :, at : at + LANES]
-            out_ref[d * own + m, tiles] = jnp.where(
+                out_ref[d * own + m, ct - early] = rhs_ref[m, :, at : at + LANES]
+            out_ref[d * own + m, tiles - early] = jnp.where(
                 low, rhs_ref[m, :, after : after + LANES], rhs_ref[m, :, before : before + LANES]
             )
 
@@ -93,10 +101,20 @@
     return jnp.where(b > 0.0, a / jnp.where(b > 0.0, b, 1.0), 0.0)
 
 
-def transpose_in(r_ref, v_ref, n, every):
-    for ct in range(every):
+def transpose_in(place_ref, near_refs, gather_ref, r_ref, v_ref, early):
+    every, _, n, _ = v_ref.shape
+    plane = len(near_refs)
+    for k in range(plane):
+        for q in range(near_refs[k].shape[0]):
+            d = jnp.bitwise_xor(place_ref[0], q) * plane + jnp.bitwise_xor(place_ref[1], k)
+            gather_ref[d] = near_refs[k][q]
+    flat = gather_ref.reshape(n * early * S, LANES)
+    for ct in range(early):
         for s in range(S):
-            v_ref[ct, s] = r_ref[pl.ds(ct * S + s, n, stride=every * S), :]
+            v_ref[ct, s] = flat[pl.ds(ct * S + s, n, stride=early * S), :]
+    for ct in range(early, every):
+        for s in range(S):
+            v_ref[ct, s] = r_ref[pl.ds((ct - early) * S + s, n, stride=(every - early) * S), :]
 
 
 def unpack_edges(next_ref, prev_ref, jh_ref):
@@ -176,6 +194,8 @@
 def first_kernel(
     n,
     tiles,
+    early,
+    plane,
     place_ref,
     dif_ref,
     r_ref,
@@ -184,15 +204,13 @@
     prev_ref,
     coup_ref,
     stencil_ref,
-    v_ref,
-    w_ref,
-    sum_ref,
     *refs,
 ):
     every = tiles + 1
-    send_refs, (jh_ref, vs_ref, xs_ref, mx_ref, bs_ref) = refs[: n // 8], refs[n // 8 :]
+    near_refs, (v_ref, w_ref, sum_ref), refs = refs[:plane], refs[plane : plane + 3], refs[plane + 3 :]
+    send_refs, (gather_ref, jh_ref, vs_ref, xs_ref, mx_ref, bs_ref) = refs[: n // 8], refs[n // 8 :]
     work = (coup_ref, stencil_ref, vs_ref, xs_ref, mx_ref, bs_ref)
-    transpose_in(r_ref, v_ref, n, every)
+    transpose_in(place_ref, near_refs, gather_ref, r_ref, v_ref, early)
     unpack_edges(next_ref, prev_ref, jh_ref)
     sums = Sums()
 
@@ -215,9 +233,10 @@
         react(n, jac, at % 2, dif_ref, mx_ref, bs_ref, finisher(ct))
     for q in range(n // 8):
         at = pl.multiple_of(jnp.bitwise_xor(place_ref[0], q) * 8, 8)
+        flat = send_refs[q].reshape(8 * tiles * S, LANES)
         for ct in range(tiles):
             for s in range(S):
-                send_refs[q][pl.ds(ct * S + s, 8, stride=tiles * S), :] = w_ref[ct, s, pl.ds(at, 8)]
+                flat[pl.ds(ct * S + s, 8, stride=tiles * S), :] = w_ref[ct, s, pl.ds(at, 8)]
     sum_ref[0:8] = sums.total("rr")
     sum_ref[8:16] = sums.total("rw")
 
@@ -362,15 +381,38 @@
     index = lax.axis_index("modes")
     place = jnp.stack([index // plane, index % plane]).astype(jnp.int32)
 
-    send = pl.pallas_call(
-        functools.partial(arrange_kernel, parts),
-        out_shape=sds((n, tiles + 1, S, LANES), F32),
-        in_specs=[VMEM],
-        out_specs=VMEM,
+    early = (tiles + 1) // 2
+    block = (plane, own, early * S, LANES)
+
+    def across(arrays):
+        lead, rows = len(arrays), arrays[0].shape[2]
+        come = [arrays[0]]
+        for q in range(1, lead):
+            come.append(lax.ppermute(arrays[q], "modes", [(i, i ^ (q * plane)) for i in range(parts)]))
+        relayed = pl.pallas_call(
+            functools.partial(relay_kernel, own),
+            out_shape=[sds((lead, own, rows, LANES), F32)] * plane,
+            in_specs=[smem] + [VMEM] * lead,
+            out_specs=[VMEM] * plane,
+            compiler_params=PARAMS,
+            cost_estimate=pl.CostEstimate(flops=10**11, bytes_accessed=1 << 20, transcendentals=0),
+            name="relay",
+        )(place, *come)
+        out = [relayed[0]]
+        for k in range(1, plane):
+            out.append(lax.ppermute(relayed[k], "modes", [(i, i ^ k) for i in range(parts)]))
+        return out
+
+    late_send, *early_send = pl.pallas_call(
+        functools.partial(arrange_kernel, parts, early),
+        out_shape=[sds((n, tiles + 1 - early, S, LANES), F32)] + [sds(block, F32)] * (parts // plane),
+        in_specs=[smem, VMEM],
+        out_specs=[VMEM] * (1 + parts // plane),
         compiler_params=PARAMS,
         name="arrange",
-    )(rhs)
-    vector = lax.all_to_all(send, "modes", split_axis=0, concat_axis=0, tiled=True)
+    )(place, rhs)
+    near = across(early_send)
+    vector = lax.all_to_all(late_send, "modes", split_axis=0, concat_axis=0, tiled=True)
 
     edge = (NCOEF, S, S, LANES)
     head, tail = pl.pallas_call(
@@ -407,18 +449,30 @@
         pltpu.VMEM((2, S * n, LANES), F32),
     ]
     v, w, sums, *w_send = pl.pallas_call(
-        functools.partial(first_kernel, n, tiles),
-        out_shape=[sds(field, F32)] * 2 + [sds((16, LANES), F32)] + [sds((8 * tiles * S, LANES), F32)] * (n // 8),
-        in_specs=[smem] * 2 + [VMEM] * 6,
+        functools.partial(first_kernel, n, tiles, early, plane),
+        out_shape=[sds(field, F32)] * 2 + [sds((16, LANES), F32)] + [sds((plane, own, tiles * S, LANES), F32)] * (n // 8),
+        in_specs=[smem] * 2 + [VMEM] * (6 + plane),
         out_specs=[VMEM] * (3 + n // 8),
-        scratch_shapes=[pltpu.VMEM((NCOEF * S, S, LANES), F32)] + work,
+        scratch_shapes=[
+            pltpu.VMEM((parts, own, early * S, LANES), F32),
+            pltpu.VMEM((NCOEF * S, S, LANES), F32),
+        ]
+        + work,
         compiler_params=PARAMS,
         name="first",
-    )(place, diffusivity, vector.reshape(n * (tiles + 1) * S, LANES), jac, after, before, coupling, stencil)
-
-    moved = w_send[:1]
-    for q in range(1, n // 8):
-        moved.append(lax.ppermute(w_send[q], "modes", [(i, i ^ (q * plane)) for i in range(parts)]))
+    )(
+        place,
+        diffusivity,
+        vector.reshape(n * (tiles + 1 - early) * S, LANES),
+        jac,
+        after,
+        before,
+        coupling,
+        stencil,
+        *near,
+    )
+
+    w_own = across(w_send)
 
     z_send = pl.pallas_call(
         functools.partial(second_kernel, n, tiles),
@@ -432,19 +486,6 @@
     )(diffusivity, v, w, sums, jac, coupling, stencil)
     line = (tiles * S + 1) * LANES
     got = lax.all_to_all(z_send.reshape(n, 1, line), "modes", split_axis=0, concat_axis=0, tiled=True)
-
-    relayed = pl.pallas_call(
-        functools.partial(relay_kernel, own),
-        out_shape=[sds((n // 8, own, tiles * S, LANES), F32)] * plane,
-        in_specs=[smem] + [VMEM] * (n // 8),
-        out_specs=[VMEM] * plane,
-        compiler_params=PARAMS,
-        cost_estimate=pl.CostEstimate(flops=10**11, bytes_accessed=1 << 20, transcendentals=0),
-        name="relay",
-    )(place, *(x.reshape(plane, own, tiles * S, LANES) for x in moved))
-    w_own = [relayed[0]]
-    for k in range(1, plane):
-        w_own.append(lax.ppermute(relayed[k], "modes", [(i, i ^ k) for i in range(parts)]))
 
     update, basis_next = pl.pallas_call(
         functools.partial(combine_kernel, parts, tiles),

time: 66.6 us -> 69.8 us (1.048)
  starting transfers between devices: 23.2 us -> 27.2 us
  waiting for transfers between devices: 24.3 us -> 21 us
  Pallas kernels: 16.7 us -> 18 us
  local copies, waits for them, and re-layouts: 1.17 us -> 2.36 us
    ppermute x6 -> x12, starting transfers between devices: 6.62 us -> 14.3 us  [the longest x6 10.1 us: across(): lax.ppermute(arrays[q], 'modes', [(i, i ^ q * plane) for i in range(parts)])]
    ppermute x1, waiting for transfers between devices: 7.35 us -> 0.01 us  [local(): after = lax.ppermute(head, 'modes', down)]
    ppermute x6 -> x12, waiting for transfers between devices: 10 us -> 15.6 us  [the longest x6 15.6 us: across(): lax.ppermute(relayed[k], 'modes', [(i, i ^ k) for i in range(parts)])]
    ppermute x1, waiting for transfers between devices: 4.97 us -> 0.01 us  [local(): before = lax.ppermute(tail, 'modes', up)]
    all_to_all x1, waiting for transfers between devices: 0.01 us -> 3.51 us  [local(): lax.all_to_all(late_send, 'modes', split_axis=0, concat_axis=0, tiled=True)]
    all_to_all x1, starting transfers between devices: 7.39 us -> 5.82 us  [local(): lax.all_to_all(late_send, 'modes', split_axis=0, concat_axis=0, tiled=True)]
    unnamed x16 -> x18, local copies, waits for them, and re-layouts: 1.17 us -> 2.36 us
    all_to_all x1, starting transfers between devices: 4.76 us -> 3.57 us  [local(): lax.all_to_all(z_send.reshape(n, 1, line), 'modes', split_axis=0, concat_...]
  transfers between devices with their start and end apart: 10 -> 16, of which waited for: 5 -> 6; matrix products, arithmetic and copies ran while one was open for 0% -> 0% of each run, Pallas kernels for 10% -> 11%
where the time goes in v4:
time: 69.8 us; the launch traced here: 69.4 us
  starting transfers between devices  27.2 us (39%)
  waiting for transfers between devices  21 us (30%)
  Pallas kernels  18 us (26%)
  local copies, waits for them, and re-layouts  2.36 us (3%)
  between operations  0.87 us (1%)
    ppermute x6, waiting for transfers between devices, across(): lax.ppermute(relayed[k], 'modes', [(i, i ^ k) for i in range(parts)])  15.6 us
    ppermute x6, starting transfers between devices, across(): lax.ppermute(arrays[q], 'modes', [(i, i ^ q * plane) for i in range(parts)])  10.1 us
    pallas_call x1, Pallas kernels, local(): pl.pallas_call(functools.partial(first_kernel, n, tiles, early, plane), o...  6.92 us
    pallas_call x1, Pallas kernels, local(): pl.pallas_call(functools.partial(second_kernel, n, tiles), out_shape=sds(...  6.02 us
    all_to_all x1, starting transfers between devices, local(): lax.all_to_all(late_send, 'modes', split_axis=0, concat_axis=0, tiled=True)  5.82 us
    ppermute x6, starting transfers between devices, across(): lax.ppermute(relayed[k], 'modes', [(i, i ^ k) for i in range(parts)])  4.26 us
    all_to_all x1, starting transfers between devices, local(): lax.all_to_all(z_send.reshape(n, 1, line), 'modes', split_axis=0, concat_...  3.57 us
    all_to_all x1, waiting for transfers between devices, local(): lax.all_to_all(late_send, 'modes', split_axis=0, concat_axis=0, tiled=True)  3.51 us
  transfers between devices with their start and end apart: 16, of which 6 were waited for; matrix products, arithmetic and copies ran while one was open for 0% of the time, Pallas kernels for 11%

profile of v4, /device:TPU:0, one launch (start us, length us, event | category | flops | bytes accessed | tf_op | source)
XLA Modules:
  0.0 69.4 jit_solution(3443694570317309394)
XLA Ops:
  0.6 0.1 pad_add_fusion.place_ref
  0.7 1.0 %copy-done.2 = f32[2,8,8192]{2,1,0:T(8,128)S(1)} copy-done((f32[2,8,8192]{2,1,0:T(8,128)S(1)}, f32[2,8,8192]{2,1,0:T(8,128)}, u32[]{:S(2)}) %copy-start.2) | copy-done | bytes 524312
  1.8 1.3 %arrange.1 = (f32[32,3,8,128]{3,2,1,0:T(8,128)}, f32[4,2,16,128]{3,2,1,0:T(8,128)S(1)}, f32[4,2,16,128]{3,2,1,0:T(8,128)S(1)}, f32[4,2,16,128]{3,2,1,0:T(8,128)S(1)}, f32[4,2,16,128]{3,2,1,0:T(8,128)S(1)}) custom-call(s32[2]{0:T(128)S(1)} %pad_add_fusion.place_ref, f32[2,8,8192]{2,1,0:T(8,128)S(1)} %copy-done.2), custom_call_target="tpu_custom_call" | custom-call | tf_op jit(solution)/shard_map/arrange/pallas_call | solution.py:406
  3.1 3.0 %collective-permute-start.2 = (f32[4,2,16,128]{3,2,1,0:T(8,128)S(1)}, f32[4,2,16,128]{3,2,1,0:T(8,128)S(1)}, u32[]{:S(2)}, u32[]{:S(2)}) collective-permute-start(f32[4,2,16,128]{3,2,1,0:T(8,128)S(1)} %get-tuple-element.32), channel_id=1, source_target_pairs={{0,4},{1,5},{2,6},{3,7},{4,0},{5,1},{6,2},{7,3},{8,12},{9,13},{10,... | collective-permute-start | bytes 196616 | tf_op jit(solution)/shard_map/ppermute | solution.py:391
  6.1 2.6 %collective-permute-start.3 = (f32[4,2,16,128]{3,2,1,0:T(8,128)S(1)}, f32[4,2,16,128]{3,2,1,0:T(8,128)S(1)}, u32[]{:S(2)}, u32[]{:S(2)}) collective-permute-start(f32[4,2,16,128]{3,2,1,0:T(8,128)S(1)} %get-tuple-element.33), channel_id=1, source_target_pairs={{0,8},{1,9},{2,10},{3,11},{4,12},{5,13},{6,14},{7,15},{8,0},{9,1},... | collective-permute-start | bytes 196616 | tf_op jit(solution)/shard_map/ppermute | solution.py:391
  8.7 1.3 %copy-done = f32[9,8,8,512]{3,2,1,0:T(8,128)S(1)} copy-done((f32[9,8,8,512]{3,2,1,0:T(8,128)S(1)}, f32[9,8,8,512]{3,2,1,0:T(8,128)}, u32[]{:S(2)}) %copy-start) | copy-done | bytes 1179672
  10.0 0.2 pack.1
  10.2 3.4 %collective-permute-start = (f32[9,2,8,128]{3,2,1,0:T(8,128)S(1)}, f32[9,2,8,128]{3,2,1,0:T(8,128)S(1)}, u32[]{:S(2)}, u32[]{:S(2)}) collective-permute-start(f32[9,2,8,128]{3,2,1,0:T(8,128)S(1)} %get-tuple-element.27), channel_id=1, source_target_pairs={{1,0},{2,1},{3,2},{4,3},{5,4},{6,5},{7,6},{8,7},{9,8},{10,9},{11,1... | collective-permute-start | bytes 221192 | tf_op jit(solution)/shard_map/ppermute | solution.py:431
  13.6 5.8 %all-to-all-start = ((f32[32,3,8,128]{3,2,1,0:T(8,128)}), f32[32,3,8,128]{3,2,1,0:T(8,128)S(1)}, u32[]{:S(2)}, u32[]{:S(2)}) async-start(f32[32,3,8,128]{3,2,1,0:T(8,128)} %get-tuple-element.26), calls=%async_computation | async-start | bytes 786432 | tf_op jit(solution)/shard_map/all_to_all | solution.py:415
  19.5 0.0 copy-start.4
  19.5 0.0 copy-start.5
  19.5 0.0 copy-start.1
  19.5 0.6 relay.2
  20.1 0.5 collective-permute-start.5
  20.6 1.7 %collective-permute-start.6 = (f32[4,2,16,128]{3,2,1,0:T(8,128)S(1)}, f32[4,2,16,128]{3,2,1,0:T(8,128)S(1)}, u32[]{:S(2)}, u32[]{:S(2)}) collective-permute-start(f32[4,2,16,128]{3,2,1,0:T(8,128)S(1)} %get-tuple-element.37), channel_id=1, source_target_pairs={{0,2},{1,3},{2,0},{3,1},{4,6},{5,7},{6,4},{7,5},{8,10},{9,11},{10,... | collective-permute-start | bytes 196616 | tf_op jit(solution)/shard_map/ppermute | solution.py:403
  22.3 0.3 coupling.1
  22.6 4.3 %collective-permute-done.6.refs_2_ = f32[4,2,16,128]{3,2,1,0:T(8,128)S(1)} collective-permute-done((f32[4,2,16,128]{3,2,1,0:T(8,128)S(1)}, f32[4,2,16,128]{3,2,1,0:T(8,128)S(1)}, u32[]{:S(2)}, u32[]{:S(2)}) %collective-permute-start.6) | collective-permute-done | bytes 65568 | tf_op jit(solution)/shard_map/ppermute | solution.py:403
  26.9 1.2 %collective-permute-done.7.refs_3_ = f32[4,2,16,128]{3,2,1,0:T(8,128)S(1)} collective-permute-done((f32[4,2,16,128]{3,2,1,0:T(8,128)S(1)}, f32[4,2,16,128]{3,2,1,0:T(8,128)S(1)}, u32[]{:S(2)}, u32[]{:S(2)}) %collective-permute-start.7) | collective-permute-done | bytes 65568 | tf_op jit(solution)/shard_map/ppermute | solution.py:403
  28.1 3.5 %all-to-all-done = f32[32,3,8,128]{3,2,1,0:T(8,128)S(1)} async-done(((f32[32,3,8,128]{3,2,1,0:T(8,128)}), f32[32,3,8,128]{3,2,1,0:T(8,128)S(1)}, u32[]{:S(2)}, u32[]{:S(2)}) %all-to-all-start) | async-done | bytes 393248 | tf_op jit(solution)/shard_map/all_to_all | solution.py:415
  31.6 6.9 %first.1 = (f32[5,8,32,128]{3,2,1,0:T(8,128)S(1)}, f32[5,8,32,128]{3,2,1,0:T(8,128)S(1)}, f32[16,128]{1,0:T(8,128)S(1)}, f32[4,2,32,128]{3,2,1,0:T(8,128)S(1)}, ...) custom-call(s32[2]{0:T(128)S(1)} %pad_add_fusion.place_ref, ...), custom_call_target="tpu_custom_call" | custom-call | tf_op jit(solution)/shard_map/first/pallas_call | solution.py:451
  38.6 0.8 %collective-permute-start.8 = (f32[4,2,32,128]{3,2,1,0:T(8,128)S(1)}, f32[4,2,32,128]{3,2,1,0:T(8,128)S(1)}, u32[]{:S(2)}, u32[]{:S(2)}) collective-permute-start(f32[4,2,32,128]{3,2,1,0:T(8,128)S(1)} %get-tuple-element.43), channel_id=1, source_target_pairs={{0,4},{1,5},{2,6},{3,7},{4,0},{5,1},{6,2},{7,3},{8,12},{9,13},{10,... | collective-permute-start | bytes 393224 | tf_op jit(solution)/shard_map/ppermute | solution.py:391
  39.4 1.1 %collective-permute-start.9 = (f32[4,2,32,128]{3,2,1,0:T(8,128)S(1)}, f32[4,2,32,128]{3,2,1,0:T(8,128)S(1)}, u32[]{:S(2)}, u32[]{:S(2)}) collective-permute-start(f32[4,2,32,128]{3,2,1,0:T(8,128)S(1)} %get-tuple-element.44), channel_id=1, source_target_pairs={{0,8},{1,9},{2,10},{3,11},{4,12},{5,13},{6,14},{7,15},{8,0},{9,1},... | collective-permute-start | bytes 393224 | tf_op jit(solution)/shard_map/ppermute | solution.py:391
  40.5 2.6 %collective-permute-start.10 = (f32[4,2,32,128]{3,2,1,0:T(8,128)S(1)}, f32[4,2,32,128]{3,2,1,0:T(8,128)S(1)}, u32[]{:S(2)}, u32[]{:S(2)}) collective-permute-start(f32[4,2,32,128]{3,2,1,0:T(8,128)S(1)} %get-tuple-element.45), channel_id=1, source_target_pairs={{0,12},{1,13},{2,14},{3,15},{4,8},{5,9},{6,10},{7,11},{8,4},{9,5},... | collective-permute-start | bytes 393224 | tf_op jit(solution)/shard_map/ppermute | solution.py:391
  43.0 6.0 %second.1 = f32[1056,128]{1,0:T(8,128)} custom-call(f32[8]{0:T(128)S(1)} %copy-done.8, f32[5,8,32,128]{3,2,1,0:T(8,128)S(1)} %get-tuple-element.39.v_ref, f32[5,8,32,128]{3,2,1,0:T(8,128)S(1)} %get-tuple-element.40.w_ref, f32[16,128]{1,0:T(8,128)S(1)} %get-tuple-element.41.sum_ref, f32[72,8,512]{2,1,0:T(8,128)S(1)} %bitcast.11, ...), custom_call_target="tpu_custom_call" | custom-call | flops 75497472 | bytes 16777216 | tf_op jit(solution)/shard_map/second/pallas_call | solution.py:477
  49.0 3.6 %all-to-all-start.1 = ((f32[32,1,4224]{2,1,0:T(1,128)}), f32[32,1,4224]{2,1,0:T(1,128)S(1)}, u32[]{:S(2)}, u32[]{:S(2)}) async-start(f32[32,1,4224]{2,1,0:T(1,128)} %bitcast.8), calls=%async_computation.1 | async-start | bytes 1081344 | tf_op jit(solution)/shard_map/all_to_all | solution.py:488
  52.7 0.6 relay.3
  53.3 0.4 collective-permute-start.11
  53.7 1.7 %collective-permute-start.12 = (f32[4,2,32,128]{3,2,1,0:T(8,128)S(1)}, f32[4,2,32,128]{3,2,1,0:T(8,128)S(1)}, u32[]{:S(2)}, u32[]{:S(2)}) collective-permute-start(f32[4,2,32,128]{3,2,1,0:T(8,128)S(1)} %get-tuple-element.48), channel_id=1, source_target_pairs={{0,2},{1,3},{2,0},{3,1},{4,6},{5,7},{6,4},{7,5},{8,10},{9,11},{10,... | collective-permute-start | bytes 393224 | tf_op jit(solution)/shard_map/ppermute | solution.py:403
  55.4 7.9 %collective-permute-done.12.refs_2_ = f32[4,2,32,128]{3,2,1,0:T(8,128)S(1)} collective-permute-done((f32[4,2,32,128]{3,2,1,0:T(8,128)S(1)}, f32[4,2,32,128]{3,2,1,0:T(8,128)S(1)}, u32[]{:S(2)}, u32[]{:S(2)}) %collective-permute-start.12) | collective-permute-done | bytes 131104 | tf_op jit(solution)/shard_map/ppermute | solution.py:403
  63.3 2.1 %collective-permute-done.13.refs_3_ = f32[4,2,32,128]{3,2,1,0:T(8,128)S(1)} collective-permute-done((f32[4,2,32,128]{3,2,1,0:T(8,128)S(1)}, f32[4,2,32,128]{3,2,1,0:T(8,128)S(1)}, u32[]{:S(2)}, u32[]{:S(2)}) %collective-permute-start.13) | collective-permute-done | bytes 131104 | tf_op jit(solution)/shard_map/ppermute | solution.py:403
  65.4 1.9 %all-to-all-done.1 = f32[32,1,4224]{2,1,0:T(1,128)S(1)} async-done(((f32[32,1,4224]{2,1,0:T(1,128)}), f32[32,1,4224]{2,1,0:T(1,128)S(1)}, u32[]{:S(2)}, u32[]{:S(2)}) %all-to-all-start.1) | async-done | bytes 540704 | tf_op jit(solution)/shard_map/all_to_all | solution.py:488
  67.3 2.1 %combine.1 = (f32[2,8,8192]{2,1,0:T(8,128)}, f32[2,8,8192]{2,1,0:T(8,128)}) custom-call(s32[2]{0:T(128)S(1)} %pad_add_fusion.place_ref, f32[2,8,8192]{2,1,0:T(8,128)S(1)} %copy-done.3, f32[1056,128]{1,0:T(8,128)S(1)} %bitcast.12, f32[4,2,32,128]{3,2,1,0:T(8,128)S(1)} %get-tuple-element.46.refs_0_, f32[4,2,32,128]{3,2,1,0:T(8,128)S(1)} %collective-permute-done.11.refs_1_, ...), custom_call_target="tpu_custom_call" | custom-call | tf_op jit(solution)/shard_map/combine/pallas_call | solution.py:490
  (27 shorter events, 0.1 us)
Async XLA Ops:
  0.7 1.0 %copy-start.2 = (f32[2,8,8192]{2,1,0:T(8,128)S(1)}, f32[2,8,8192]{2,1,0:T(8,128)}, u32[]{:S(2)}) copy-start(f32[2,8,8192]{2,1,0:T(8,128)} %rhs_ref.3) | copy-start | bytes 1572868
  3.1 16.3 %collective-permute-start.2 = (f32[4,2,16,128]{3,2,1,0:T(8,128)S(1)}, f32[4,2,16,128]{3,2,1,0:T(8,128)S(1)}, u32[]{:S(2)}, u32[]{:S(2)}) collective-permute-start(f32[4,2,16,128]{3,2,1,0:T(8,128)S(1)} %get-tuple-element.32), channel_id=1, source_target_pairs={{0,4},{1,5},{2,6},{3,7},{4,0},{5,1},{6,2},{7,3},{8,12},{9,13},{10,... | collective-permute-start | bytes 196616 | tf_op jit(solution)/shard_map/ppermute | solution.py:391
  6.1 13.3 %collective-permute-start.3 = (f32[4,2,16,128]{3,2,1,0:T(8,128)S(1)}, f32[4,2,16,128]{3,2,1,0:T(8,128)S(1)}, u32[]{:S(2)}, u32[]{:S(2)}) collective-permute-start(f32[4,2,16,128]{3,2,1,0:T(8,128)S(1)} %get-tuple-element.33), channel_id=1, source_target_pairs={{0,8},{1,9},{2,10},{3,11},{4,12},{5,13},{6,14},{7,15},{8,0},{9,1},... | collective-permute-start | bytes 196616 | tf_op jit(solution)/shard_map/ppermute | solution.py:391
  8.7 10.7 %collective-permute-start.4 = (f32[4,2,16,128]{3,2,1,0:T(8,128)S(1)}, f32[4,2,16,128]{3,2,1,0:T(8,128)S(1)}, u32[]{:S(2)}, u32[]{:S(2)}) collective-permute-start(f32[4,2,16,128]{3,2,1,0:T(8,128)S(1)} %get-tuple-element.34), channel_id=1, source_target_pairs={{0,12},{1,13},{2,14},{3,15},{4,8},{5,9},{6,10},{7,11},{8,4},{9,5},... | collective-permute-start | bytes 196616 | tf_op jit(solution)/shard_map/ppermute | solution.py:391
  8.7 1.3 %copy-start = (f32[9,8,8,512]{3,2,1,0:T(8,128)S(1)}, f32[9,8,8,512]{3,2,1,0:T(8,128)}, u32[]{:S(2)}) copy-start(f32[9,8,8,512]{3,2,1,0:T(8,128)} %last_ref.1) | copy-start | bytes 3538948
  10.2 12.4 %collective-permute-start = (f32[9,2,8,128]{3,2,1,0:T(8,128)S(1)}, f32[9,2,8,128]{3,2,1,0:T(8,128)S(1)}, u32[]{:S(2)}, u32[]{:S(2)}) collective-permute-start(f32[9,2,8,128]{3,2,1,0:T(8,128)S(1)} %get-tuple-element.27), channel_id=1, source_target_pairs={{1,0},{2,1},{3,2},{4,3},{5,4},{6,5},{7,6},{8,7},{9,8},{10,9},{11,1... | collective-permute-start | bytes 221192 | tf_op jit(solution)/shard_map/ppermute | solution.py:431
  13.6 9.0 %collective-permute-start.1 = (f32[9,2,8,128]{3,2,1,0:T(8,128)S(1)}, f32[9,2,8,128]{3,2,1,0:T(8,128)S(1)}, u32[]{:S(2)}, u32[]{:S(2)}) collective-permute-start(f32[9,2,8,128]{3,2,1,0:T(8,128)S(1)} %get-tuple-element.28), channel_id=1, source_target_pairs={{0,1},{1,2},{2,3},{3,4},{4,5},{5,6},{6,7},{7,8},{8,9},{9,10},{10,1... | collective-permute-start | bytes 221192 | tf_op jit(solution)/shard_map/ppermute | solution.py:432
  13.6 18.0 %all-to-all-start = ((f32[32,3,8,128]{3,2,1,0:T(8,128)}), f32[32,3,8,128]{3,2,1,0:T(8,128)S(1)}, u32[]{:S(2)}, u32[]{:S(2)}) async-start(f32[32,3,8,128]{3,2,1,0:T(8,128)} %get-tuple-element.26), calls=%async_computation | async-start | bytes 786432 | tf_op jit(solution)/shard_map/all_to_all | solution.py:415
  19.5 2.8 %copy-start.4 = (s32[512]{0:T(512)S(1)}, s32[512]{0:T(512)}, u32[]{:S(2)}) copy-start(s32[512]{0:T(512)} %param.10) | copy-start | bytes 6148
  19.5 2.8 %copy-start.5 = (s32[512]{0:T(512)S(1)}, s32[512]{0:T(512)}, u32[]{:S(2)}) copy-start(s32[512]{0:T(512)} %param.11) | copy-start | bytes 6148
  19.5 2.8 %copy-start.6 = (s32[512]{0:T(512)S(1)}, s32[512]{0:T(512)}, u32[]{:S(2)}) copy-start(s32[512]{0:T(512)} %param.12) | copy-start | bytes 6148
  19.5 2.8 %copy-start.7 = (s32[512]{0:T(512)S(1)}, s32[512]{0:T(512)}, u32[]{:S(2)}) copy-start(s32[512]{0:T(512)} %param.13) | copy-start | bytes 6148
  19.5 12.1 %copy-start.1 = (f32[9,8,8,512]{3,2,1,0:T(8,128)S(1)}, f32[9,8,8,512]{3,2,1,0:T(8,128)}, u32[]{:S(2)}) copy-start(f32[9,8,8,512]{3,2,1,0:T(8,128)} %last_ref.1) | copy-start | bytes 3538948
  19.5 12.1 %copy-start.8 = (f32[8]{0:T(128)S(1)}, f32[8]{0:T(128)}, u32[]{:S(2)}) copy-start(f32[8]{0:T(128)} %dif_ref.3) | copy-start | bytes 100
  20.1 2.5 %collective-permute-start.5 = (f32[4,2,16,128]{3,2,1,0:T(8,128)S(1)}, f32[4,2,16,128]{3,2,1,0:T(8,128)S(1)}, u32[]{:S(2)}, u32[]{:S(2)}) collective-permute-start(f32[4,2,16,128]{3,2,1,0:T(8,128)S(1)} %get-tuple-element.36), channel_id=1, source_target_pairs={{0,1},{1,0},{2,3},{3,2},{4,5},{5,4},{6,7},{7,6},{8,9},{9,8},{10,11... | collective-permute-start | bytes 196616 | tf_op jit(solution)/shard_map/ppermute | solution.py:403
  20.6 6.3 %collective-permute-start.6 = (f32[4,2,16,128]{3,2,1,0:T(8,128)S(1)}, f32[4,2,16,128]{3,2,1,0:T(8,128)S(1)}, u32[]{:S(2)}, u32[]{:S(2)}) collective-permute-start(f32[4,2,16,128]{3,2,1,0:T(8,128)S(1)} %get-tuple-element.37), channel_id=1, source_target_pairs={{0,2},{1,3},{2,0},{3,1},{4,6},{5,7},{6,4},{7,5},{8,10},{9,11},{10,... | collective-permute-start | bytes 196616 | tf_op jit(solution)/shard_map/ppermute | solution.py:403
  22.3 5.9 %collective-permute-start.7 = (f32[4,2,16,128]{3,2,1,0:T(8,128)S(1)}, f32[4,2,16,128]{3,2,1,0:T(8,128)S(1)}, u32[]{:S(2)}, u32[]{:S(2)}) collective-permute-start(f32[4,2,16,128]{3,2,1,0:T(8,128)S(1)} %get-tuple-element.38), channel_id=1, source_target_pairs={{0,3},{1,2},{2,1},{3,0},{4,7},{5,6},{6,5},{7,4},{8,11},{9,10},{10,... | collective-permute-start | bytes 196616 | tf_op jit(solution)/shard_map/ppermute | solution.py:403
  38.6 14.1 %collective-permute-start.8 = (f32[4,2,32,128]{3,2,1,0:T(8,128)S(1)}, f32[4,2,32,128]{3,2,1,0:T(8,128)S(1)}, u32[]{:S(2)}, u32[]{:S(2)}) collective-permute-start(f32[4,2,32,128]{3,2,1,0:T(8,128)S(1)} %get-tuple-element.43), channel_id=1, source_target_pairs={{0,4},{1,5},{2,6},{3,7},{4,0},{5,1},{6,2},{7,3},{8,12},{9,13},{10,... | collective-permute-start | bytes 393224 | tf_op jit(solution)/shard_map/ppermute | solution.py:391
  39.4 13.3 %collective-permute-start.9 = (f32[4,2,32,128]{3,2,1,0:T(8,128)S(1)}, f32[4,2,32,128]{3,2,1,0:T(8,128)S(1)}, u32[]{:S(2)}, u32[]{:S(2)}) collective-permute-start(f32[4,2,32,128]{3,2,1,0:T(8,128)S(1)} %get-tuple-element.44), channel_id=1, source_target_pairs={{0,8},{1,9},{2,10},{3,11},{4,12},{5,13},{6,14},{7,15},{8,0},{9,1},... | collective-permute-start | bytes 393224 | tf_op jit(solution)/shard_map/ppermute | solution.py:391
  40.5 12.2 %collective-permute-start.10 = (f32[4,2,32,128]{3,2,1,0:T(8,128)S(1)}, f32[4,2,32,128]{3,2,1,0:T(8,128)S(1)}, u32[]{:S(2)}, u32[]{:S(2)}) collective-permute-start(f32[4,2,32,128]{3,2,1,0:T(8,128)S(1)} %get-tuple-element.45), channel_id=1, source_target_pairs={{0,12},{1,13},{2,14},{3,15},{4,8},{5,9},{6,10},{7,11},{8,4},{9,5},... | collective-permute-start | bytes 393224 | tf_op jit(solution)/shard_map/ppermute | solution.py:391
  49.0 18.3 %all-to-all-start.1 = ((f32[32,1,4224]{2,1,0:T(1,128)}), f32[32,1,4224]{2,1,0:T(1,128)S(1)}, u32[]{:S(2)}, u32[]{:S(2)}) async-start(f32[32,1,4224]{2,1,0:T(1,128)} %bitcast.8), calls=%async_computation.1 | async-start | bytes 1081344 | tf_op jit(solution)/shard_map/all_to_all | solution.py:488
  52.7 14.7 %copy-start.3 = (f32[2,8,8192]{2,1,0:T(8,128)S(1)}, f32[2,8,8192]{2,1,0:T(8,128)}, u32[]{:S(2)}) copy-start(f32[2,8,8192]{2,1,0:T(8,128)} %rhs_ref.3) | copy-start | bytes 1572868
  53.3 2.1 %collective-permute-start.11 = (f32[4,2,32,128]{3,2,1,0:T(8,128)S(1)}, f32[4,2,32,128]{3,2,1,0:T(8,128)S(1)}, u32[]{:S(2)}, u32[]{:S(2)}) collective-permute-start(f32[4,2,32,128]{3,2,1,0:T(8,128)S(1)} %get-tuple-element.47), channel_id=1, source_target_pairs={{0,1},{1,0},{2,3},{3,2},{4,5},{5,4},{6,7},{7,6},{8,9},{9,8},{10,11... | collective-permute-start | bytes 393224 | tf_op jit(solution)/shard_map/ppermute | solution.py:403
  53.7 9.6 %collective-permute-start.12 = (f32[4,2,32,128]{3,2,1,0:T(8,128)S(1)}, f32[4,2,32,128]{3,2,1,0:T(8,128)S(1)}, u32[]{:S(2)}, u32[]{:S(2)}) collective-permute-start(f32[4,2,32,128]{3,2,1,0:T(8,128)S(1)} %get-tuple-element.48), channel_id=1, source_target_pairs={{0,2},{1,3},{2,0},{3,1},{4,6},{5,7},{6,4},{7,5},{8,10},{9,11},{10,... | collective-permute-start | bytes 393224 | tf_op jit(solution)/shard_map/ppermute | solution.py:403
  55.4 10.0 %collective-permute-start.13 = (f32[4,2,32,128]{3,2,1,0:T(8,128)S(1)}, f32[4,2,32,128]{3,2,1,0:T(8,128)S(1)}, u32[]{:S(2)}, u32[]{:S(2)}) collective-permute-start(f32[4,2,32,128]{3,2,1,0:T(8,128)S(1)} %get-tuple-element.49), channel_id=1, source_target_pairs={{0,3},{1,2},{2,1},{3,0},{4,7},{5,6},{6,5},{7,4},{8,11},{9,10},{10,... | collective-permute-start | bytes 393224 | tf_op jit(solution)/shard_map/ppermute | solution.py:403

commit v5 on v4

--- a/solution.py
+++ b/solution.py
@@ -46,7 +46,7 @@
             )
 
 
-def pack_kernel(first_ref, last_ref, head_ref, tail_ref):
+def pack_kernel(first_ref, last_ref, _, head_ref, tail_ref):
     piece = lane_iota() // GY
     for i in range(NCOEF):
         for q in range(S // 4):
@@ -101,58 +101,44 @@
     return jnp.where(b > 0.0, a / jnp.where(b > 0.0, b, 1.0), 0.0)
 
 
-def transpose_in(place_ref, near_refs, gather_ref, r_ref, v_ref, early):
-    every, _, n, _ = v_ref.shape
-    plane = len(near_refs)
-    for k in range(plane):
-        for q in range(near_refs[k].shape[0]):
-            d = jnp.bitwise_xor(place_ref[0], q) * plane + jnp.bitwise_xor(place_ref[1], k)
-            gather_ref[d] = near_refs[k][q]
-    flat = gather_ref.reshape(n * early * S, LANES)
-    for ct in range(early):
-        for s in range(S):
-            v_ref[ct, s] = flat[pl.ds(ct * S + s, n, stride=early * S), :]
-    for ct in range(early, every):
-        for s in range(S):
-            v_ref[ct, s] = r_ref[pl.ds((ct - early) * S + s, n, stride=(every - early) * S), :]
-
-
-def unpack_edges(next_ref, prev_ref, jh_ref):
+def unpack_kernel(next_ref, prev_ref, out_ref):
     lane = lane_iota()
-
-    def unpack(i, _):
+    for i in range(NCOEF):
         for q in range(S // 4):
             after, before = next_ref[i, q], prev_ref[i, q]
             for p in range(4):
                 a = after if p == 0 else pltpu.roll(after, LANES - GY * p, 1)
                 b = before if p == 3 else pltpu.roll(before, LANES - GY - GY * p, 1)
-                jh_ref[i * S + q * 4 + p] = jnp.where(lane < LANES // 2, a, b)
-        return 0
-
-    lax.fori_loop(0, NCOEF, unpack, 0)
-
-
-def mix(src, ct, slot, every, coup_ref, stencil_ref, vs_ref, xs_ref, mx_ref, bs_ref):
-    n = src.shape[2]
+                out_ref[i * S + q * 4 + p] = jnp.where(lane < LANES // 2, a, b)
+
+
+def mix(get, ct, slot, coup_ref, vs_ref, mx_ref):
+    n = vs_ref.shape[1] // 3
+    for t in range(S):
+        at = slice(t * LANES, (t + 1) * LANES)
+        high, low = split(get(ct, t))
+        vs_ref[slot, 0:n, at] = high
+        vs_ref[slot, n : 2 * n, at] = low
+        vs_ref[slot, 2 * n : 3 * n, at] = high
+    mx_ref[slot] = jnp.dot(coup_ref[...], vs_ref[slot], preferred_element_type=F32)
+
+
+def spread(get, ct, slot, every, stencil_ref, xs_ref, bs_ref):
+    n = bs_ref.shape[1] // S
     wide = lax.broadcasted_iota(jnp.int32, (n, LANES), 1) < LANES // 2
     before, after = (ct - 1) % every, (ct + 1) % every
     for t in range(S):
-        at = slice(t * LANES, (t + 1) * LANES)
         to = slice(t * n, (t + 1) * n)
-        high, low = split(src[ct, t])
-        vs_ref[slot, 0:n, at] = high
-        vs_ref[slot, n : 2 * n, at] = low
-        vs_ref[slot, 2 * n : 3 * n, at] = high
+        high, low = split(get(ct, t))
         xs_ref[slot, to, 0:LANES] = high
         xs_ref[slot, to, LANES : 2 * LANES] = low
-        high, low = split(jnp.where(wide, src[after, t], src[before, t]))
+        high, low = split(jnp.where(wide, get(after, t), get(before, t)))
         xs_ref[slot, to, 2 * LANES : 3 * LANES] = high
         xs_ref[slot, to, 3 * LANES :] = low
-    mx_ref[slot] = jnp.dot(coup_ref[...], vs_ref[slot], preferred_element_type=F32)
     bs_ref[slot] = jnp.dot(xs_ref[slot], stencil_ref[...], preferred_element_type=F32)
 
 
-def react(n, jac, slot, dif_ref, mx_ref, bs_ref, finish):
+def react(n, jac, slot, mx_ref, finish):
     for kb in range(0, n, 32):
         acc = [None] * 32
         for i in range(NCOEF):
@@ -169,9 +155,7 @@
                         acc[at] = term if acc[at] is None else acc[at] + term
         for s in range(S):
             for kt in range(4):
-                k = kb + kt * 8
-                b = bs_ref[slot, s * n + k : s * n + k + 8]
-                finish(s, k, dif_ref[s] * b - acc[s * 4 + kt])
+                finish(s, kb + kt * 8, acc[s * 4 + kt])
 
 
 def tile_of(jac_ref, ct):
@@ -191,46 +175,71 @@
         return jnp.broadcast_to(jnp.sum(x, axis=(0, 1), keepdims=True), (8, LANES))
 
 
-def first_kernel(
-    n,
-    tiles,
-    early,
-    plane,
-    place_ref,
-    dif_ref,
-    r_ref,
-    jac_ref,
-    next_ref,
-    prev_ref,
-    coup_ref,
-    stencil_ref,
-    *refs,
-):
+def early_kernel(n, plane, place_ref, jac_ref, coup_ref, *refs):
+    near_refs, (v_ref, a_ref, gather_ref, vs_ref, mx_ref) = refs[:plane], refs[plane:]
+    early = v_ref.shape[0]
+    for k in range(plane):
+        for q in range(near_refs[k].shape[0]):
+            d = jnp.bitwise_xor(place_ref[0], q) * plane + jnp.bitwise_xor(place_ref[1], k)
+            gather_ref[d] = near_refs[k][q]
+    flat = gather_ref.reshape(n * early * S, LANES)
+    for ct in range(early):
+        for s in range(S):
+            v_ref[ct, s] = flat[pl.ds(ct * S + s, n, stride=early * S), :]
+
+    def get(ct, t):
+        return v_ref[ct, t]
+
+    def finisher(ct):
+        def finish(s, k, acc):
+            a_ref[ct, s, k : k + 8] = acc
+
+        return finish
+
+    mix(get, 0, 0, coup_ref, vs_ref, mx_ref)
+    for ct in range(early):
+        if ct + 1 < early:
+            mix(get, ct + 1, (ct + 1) % 2, coup_ref, vs_ref, mx_ref)
+        react(n, tile_of(jac_ref, ct), ct % 2, mx_ref, finisher(ct))
+
+
+def first_kernel(n, tiles, place_ref, dif_ref, r_ref, ve_ref, ae_ref, jac_ref, coup_ref, stencil_ref, _, *refs):
     every = tiles + 1
-    near_refs, (v_ref, w_ref, sum_ref), refs = refs[:plane], refs[plane : plane + 3], refs[plane + 3 :]
-    send_refs, (gather_ref, jh_ref, vs_ref, xs_ref, mx_ref, bs_ref) = refs[: n // 8], refs[n // 8 :]
-    work = (coup_ref, stencil_ref, vs_ref, xs_ref, mx_ref, bs_ref)
-    transpose_in(place_ref, near_refs, gather_ref, r_ref, v_ref, early)
-    unpack_edges(next_ref, prev_ref, jh_ref)
+    (v_ref, w_ref, sum_ref), refs = refs[:3], refs[3:]
+    send_refs, (vs_ref, xs_ref, mx_ref, bs_ref) = refs[: n // 8], refs[n // 8 :]
+    early = ve_ref.shape[0]
+    for ct in range(early):
+        v_ref[ct] = ve_ref[ct]
+    for ct in range(early, every):
+        for s in range(S):
+            v_ref[ct, s] = r_ref[pl.ds((ct - early) * S + s, n, stride=(every - early) * S), :]
     sums = Sums()
 
+    def get(ct, t):
+        return v_ref[ct, t]
+
     def finisher(ct):
-        def finish(s, k, w):
+        def finish(s, k, acc):
+            w = dif_ref[s] * bs_ref[ct % 2, s * n + k : s * n + k + 8] - acc
             w_ref[ct, s, k : k + 8] = w
-            if ct < tiles:
-                v = v_ref[ct, s, k : k + 8]
-                sums.add("rr", k // 8, v * v)
-                sums.add("rw", k // 8, v * w)
+            v = v_ref[ct, s, k : k + 8]
+            sums.add("rr", k // 8, v * v)
+            sums.add("rw", k // 8, v * w)
 
         return finish
 
-    order = list(range(tiles)) + [tiles]
-    mix(v_ref, order[0], 0, every, *work)
-    for at, ct in enumerate(order):
-        if at + 1 < every:
-            mix(v_ref, order[at + 1], (at + 1) % 2, every, *work)
-        jac = tile_of(jac_ref, ct) if ct < tiles else tile_of(jh_ref, 0)
-        react(n, jac, at % 2, dif_ref, mx_ref, bs_ref, finisher(ct))
+    if early < tiles:
+        mix(get, early, early % 2, coup_ref, vs_ref, mx_ref)
+    for ct in range(tiles):
+        spread(get, ct, ct % 2, every, stencil_ref, xs_ref, bs_ref)
+        if early <= ct and ct + 1 < tiles:
+            mix(get, ct + 1, (ct + 1) % 2, coup_ref, vs_ref, mx_ref)
+        if ct < early:
+            for s in range(S):
+                for k in range(0, n, 8):
+                    finisher(ct)(s, k, ae_ref[ct, s, k : k + 8])
+        else:
+            react(n, tile_of(jac_ref, ct), ct % 2, mx_ref, finisher(ct))
     for q in range(n // 8):
         at = pl.multiple_of(jnp.bitwise_xor(place_ref[0], q) * 8, 8)
         flat = send_refs[q].reshape(8 * tiles * S, LANES)
@@ -249,10 +258,12 @@
     w_ref,
     sum_ref,
     jac_ref,
+    edge_ref,
     coup_ref,
     stencil_ref,
     out_ref,
     z_ref,
+    wh_ref,
     vs_ref,
     xs_ref,
     mx_ref,
@@ -260,13 +271,22 @@
 ):
     every = tiles + 1
     per = tiles * S + 1
-    work = (coup_ref, stencil_ref, vs_ref, xs_ref, mx_ref, bs_ref)
     rr, rw = sum_ref[0:8], sum_ref[8:16]
     c1 = ratio(rw, rr)
     sums = Sums()
 
+    def get_v(ct, t):
+        return v_ref[ct, t]
+
+    def get_w(ct, t):
+        return w_ref[ct, t] if ct < tiles else wh_ref[t]
+
+    def finish_edge(s, k, acc):
+        wh_ref[s, k : k + 8] = dif_ref[s] * bs_ref[tiles % 2, s * n + k : s * n + k + 8] - acc
+
     def finisher(ct):
-        def finish(s, k, z):
+        def finish(s, k, acc):
+            z = dif_ref[s] * bs_ref[ct % 2, s * n + k : s * n + k + 8] - acc
             v, w = v_ref[ct, s, k : k + 8], w_ref[ct, s, k : k + 8]
             z_ref[ct, s, k : k + 8] = z
             out_ref[pl.ds(k * per + ct * S + s, 8, stride=per), :] = z
@@ -278,11 +298,18 @@
 
         return finish
 
-    mix(w_ref, 0, 0, every, *work)
-    for ct in range(tiles):
-        if ct + 1 < tiles:
-            mix(w_ref, ct + 1, (ct + 1) % 2, every, *work)
-        react(n, tile_of(jac_ref, ct), ct % 2, dif_ref, mx_ref, bs_ref, finisher(ct))
+    slot = tiles % 2
+    mix(get_v, tiles, slot, coup_ref, vs_ref, mx_ref)
+    spread(get_v, tiles, slot, every, stencil_ref, xs_ref, bs_ref)
+    order = list(range(1, tiles)) + [0]
+    mix(get_w, order[0], 1 - slot, coup_ref, vs_ref, mx_ref)
+    react(n, tile_of(edge_ref, 0), slot, mx_ref, finish_edge)
+    for at, ct in enumerate(order):
+        now = (1 - slot + at) % 2
+        spread(get_w, ct, ct % 2, every, stencil_ref, xs_ref, bs_ref)
+        if at + 1 < tiles:
+            mix(get_w, order[at + 1], 1 - now, coup_ref, vs_ref, mx_ref)
+        react(n, tile_of(jac_ref, ct), now, mx_ref, finisher(ct))
     uu, ur, uz, rz = (sums.total(name) for name in ("uu", "ur", "uz", "rz"))
     c2 = ratio(rz, rr)
     c3 = ratio(uz - c2 * ur, uu)
@@ -401,7 +428,7 @@
         out = [relayed[0]]
         for k in range(1, plane):
             out.append(lax.ppermute(relayed[k], "modes", [(i, i ^ k) for i in range(parts)]))
-        return out
+        return out, relayed[0]
 
     late_send, *early_send = pl.pallas_call(
         functools.partial(arrange_kernel, parts, early),
@@ -411,7 +438,7 @@
         compiler_params=PARAMS,
         name="arrange",
     )(place, rhs)
-    near = across(early_send)
+    near, relayed = across(early_send)
     vector = lax.all_to_all(late_send, "modes", split_axis=0, concat_axis=0, tiled=True)
 
     edge = (NCOEF, S, S, LANES)
@@ -422,14 +449,23 @@
         in_specs=[
             pl.BlockSpec(edge, lambda g: (0, 0, 0, 0)),
             pl.BlockSpec(edge, lambda g: (0, 0, 0, tiles - 1)),
+            pl.BlockSpec(memory_space=pl.ANY),
         ],
         compiler_params=PARAMS,
         name="pack",
-    )(jac_coef, jac_coef)
+    )(jac_coef, jac_coef, relayed)
     up = [(i, (i + 1) % parts) for i in range(parts)]
     down = [(j, i) for i, j in up]
     after = lax.ppermute(head, "modes", down)
     before = lax.ppermute(tail, "modes", up)
+    edges = pl.pallas_call(
+        unpack_kernel,
+        out_shape=sds((NCOEF * S, S, LANES), F32),
+        in_specs=[VMEM] * 2,
+        out_specs=VMEM,
+        compiler_params=PARAMS,
+        name="unpack",
+    )(after, before)
 
     coupling, stencil = pl.pallas_call(
         functools.partial(coupling_kernel, n),
@@ -448,42 +484,48 @@
         pltpu.VMEM((2, NCOEF * n, S * LANES), F32),
         pltpu.VMEM((2, S * n, LANES), F32),
     ]
+    v_early, a_early = pl.pallas_call(
+        functools.partial(early_kernel, n, plane),
+        out_shape=[sds((early, S, n, LANES), F32)] * 2,
+        in_specs=[smem] + [VMEM] * (2 + plane),
+        out_specs=[VMEM] * 2,
+        scratch_shapes=[pltpu.VMEM((parts, own, early * S, LANES), F32), work[0], work[2]],
+        compiler_params=PARAMS,
+        name="early",
+    )(place, jac, coupling, *near)
     v, w, sums, *w_send = pl.pallas_call(
-        functools.partial(first_kernel, n, tiles, early, plane),
-        out_shape=[sds(field, F32)] * 2 + [sds((16, LANES), F32)] + [sds((plane, own, tiles * S, LANES), F32)] * (n // 8),
-        in_specs=[smem] * 2 + [VMEM] * (6 + plane),
+        functools.partial(first_kernel, n, tiles),
+        out_shape=[sds(field, F32), sds((tiles, S, n, LANES), F32), sds((16, LANES), F32)]
+        + [sds((plane, own, tiles * S, LANES), F32)] * (n // 8),
+        in_specs=[smem] * 2 + [VMEM] * 6 + [pl.BlockSpec(memory_space=pl.ANY)],
         out_specs=[VMEM] * (3 + n // 8),
-        scratch_shapes=[
-            pltpu.VMEM((parts, own, early * S, LANES), F32),
-            pltpu.VMEM((NCOEF * S, S, LANES), F32),
-        ]
-        + work,
+        scratch_shapes=work,
         compiler_params=PARAMS,
         name="first",
     )(
         place,
         diffusivity,
         vector.reshape(n * (tiles + 1 - early) * S, LANES),
+        v_early,
+        a_early,
         jac,
-        after,
-        before,
         coupling,
         stencil,
-        *near,
+        edges,
     )
 
-    w_own = across(w_send)
+    w_own, _ = across(w_send)
 
     z_send = pl.pallas_call(
         functools.partial(second_kernel, n, tiles),
         out_shape=sds((n * (tiles * S + 1), LANES), F32),
-        in_specs=[smem] + [VMEM] * 6,
+        in_specs=[smem] + [VMEM] * 7,
         out_specs=VMEM,
-        scratch_shapes=[pltpu.VMEM(field, F32)] + work,
+        scratch_shapes=[pltpu.VMEM((tiles, S, n, LANES), F32), pltpu.VMEM((S, n, LANES), F32)] + work,
         compiler_params=PARAMS,
         cost_estimate=pl.CostEstimate(flops=2 * NCOEF * S * n * n * cells, bytes_accessed=16 << 20, transcendentals=0),
         name="second",
-    )(diffusivity, v, w, sums, jac, coupling, stencil)
+    )(diffusivity, v, w, sums, jac, edges, coupling, stencil)
     line = (tiles * S + 1) * LANES
     got = lax.all_to_all(z_send.reshape(n, 1, line), "modes", split_axis=0, concat_axis=0, tiled=True)
 

time: 69.8 us -> 67.5 us (0.967)
  waiting for transfers between devices: 21 us -> 17.4 us
  starting transfers between devices: 27.2 us -> 28.9 us
    all_to_all x1, waiting for transfers between devices: 3.51 us -> 0.01 us  [local(): lax.all_to_all(late_send, 'modes', split_axis=0, concat_axis=0, tiled=True)]
    pallas_call x1, Pallas kernels: 6.02 us -> 7.18 us  [local(): pl.pallas_call(functools.partial(second_kernel, n, tiles), out_shape=sds(...]
    pallas_call x1 -> x3, Pallas kernels: 6.92 us -> 5.86 us  [the longest x1 3.29 us: local(): pl.pallas_call(functools.partial(first_kernel, n, tiles), out_shape=[sds(...]
    ppermute x1, starting transfers between devices: 3.43 us -> 4.43 us  [local(): after = lax.ppermute(head, 'modes', down)]
    unnamed x18 -> x16, local copies, waits for them, and re-layouts: 2.36 us -> 1.76 us
  transfers between devices with their start and end apart: 16 -> 16, of which waited for: 6 -> 5; matrix products, arithmetic and copies ran while one was open for 0% -> 0% of each run, Pallas kernels for 11% -> 17%
where the time goes in v5:
time: 67.5 us; the launch traced here: 67.1 us
  starting transfers between devices  28.9 us (43%)
  Pallas kernels  18.1 us (27%)
  waiting for transfers between devices  17.4 us (26%)
  local copies, waits for them, and re-layouts  1.76 us (3%)
  between operations  0.86 us (1%)
    ppermute x6, waiting for transfers between devices, across(): lax.ppermute(relayed[k], 'modes', [(i, i ^ k) for i in range(parts)])  15.4 us
    ppermute x6, starting transfers between devices, across(): lax.ppermute(arrays[q], 'modes', [(i, i ^ q * plane) for i in range(parts)])  10.1 us
    pallas_call x1, Pallas kernels, local(): pl.pallas_call(functools.partial(second_kernel, n, tiles), out_shape=sds(...  7.18 us
    all_to_all x1, starting transfers between devices, local(): lax.all_to_all(late_send, 'modes', split_axis=0, concat_axis=0, tiled=True)  6.16 us
    ppermute x1, starting transfers between devices, local(): after = lax.ppermute(head, 'modes', down)  4.43 us
    all_to_all x1, starting transfers between devices, local(): lax.all_to_all(z_send.reshape(n, 1, line), 'modes', split_axis=0, concat_...  4.26 us
    ppermute x6, starting transfers between devices, across(): lax.ppermute(relayed[k], 'modes', [(i, i ^ k) for i in range(parts)])  4.02 us
    pallas_call x1, Pallas kernels, local(): pl.pallas_call(functools.partial(first_kernel, n, tiles), out_shape=[sds(...  3.29 us
  transfers between devices with their start and end apart: 16, of which 5 were waited for; matrix products, arithmetic and copies ran while one was open for 0% of the time, Pallas kernels for 17%

profile of v5, /device:TPU:0, one launch (start us, length us, event | category | flops | bytes accessed | tf_op | source)
XLA Modules:
  0.0 67.1 jit_solution(7936136677767224522)
XLA Ops:
  0.6 0.1 pad_add_fusion.place_ref
  0.7 1.0 %copy-done.1 = f32[2,8,8192]{2,1,0:T(8,128)S(1)} copy-done((f32[2,8,8192]{2,1,0:T(8,128)S(1)}, f32[2,8,8192]{2,1,0:T(8,128)}, u32[]{:S(2)}) %copy-start.1) | copy-done | bytes 524312
  1.8 1.3 %arrange.1 = (f32[32,3,8,128]{3,2,1,0:T(8,128)}, f32[4,2,16,128]{3,2,1,0:T(8,128)S(1)}, f32[4,2,16,128]{3,2,1,0:T(8,128)S(1)}, f32[4,2,16,128]{3,2,1,0:T(8,128)S(1)}, f32[4,2,16,128]{3,2,1,0:T(8,128)S(1)}) custom-call(s32[2]{0:T(128)S(1)} %pad_add_fusion.place_ref, f32[2,8,8192]{2,1,0:T(8,128)S(1)} %copy-done.1), custom_call_target="tpu_custom_call" | custom-call | tf_op jit(solution)/shard_map/arrange/pallas_call | solution.py:433
  3.1 3.0 %collective-permute-start = (f32[4,2,16,128]{3,2,1,0:T(8,128)S(1)}, f32[4,2,16,128]{3,2,1,0:T(8,128)S(1)}, u32[]{:S(2)}, u32[]{:S(2)}) collective-permute-start(f32[4,2,16,128]{3,2,1,0:T(8,128)S(1)} %get-tuple-element.31), channel_id=1, source_target_pairs={{0,4},{1,5},{2,6},{3,7},{4,0},{5,1},{6,2},{7,3},{8,12},{9,13},{10,... | collective-permute-start | bytes 196616 | tf_op jit(solution)/shard_map/ppermute | solution.py:418
  6.1 2.6 %collective-permute-start.1 = (f32[4,2,16,128]{3,2,1,0:T(8,128)S(1)}, f32[4,2,16,128]{3,2,1,0:T(8,128)S(1)}, u32[]{:S(2)}, u32[]{:S(2)}) collective-permute-start(f32[4,2,16,128]{3,2,1,0:T(8,128)S(1)} %get-tuple-element.32), channel_id=1, source_target_pairs={{0,8},{1,9},{2,10},{3,11},{4,12},{5,13},{6,14},{7,15},{8,0},{9,1},... | collective-permute-start | bytes 196616 | tf_op jit(solution)/shard_map/ppermute | solution.py:418
  8.7 6.2 %all-to-all-start = ((f32[32,3,8,128]{3,2,1,0:T(8,128)}), f32[32,3,8,128]{3,2,1,0:T(8,128)S(1)}, u32[]{:S(2)}, u32[]{:S(2)}) async-start(f32[32,3,8,128]{3,2,1,0:T(8,128)} %get-tuple-element.28), calls=%async_computation | async-start | bytes 786432 | tf_op jit(solution)/shard_map/all_to_all | solution.py:442
  14.9 0.0 copy-start
  14.9 0.6 relay.2
  15.5 0.7 %copy-done = f32[9,8,8,512]{3,2,1,0:T(8,128)S(1)} copy-done((f32[9,8,8,512]{3,2,1,0:T(8,128)S(1)}, f32[9,8,8,512]{3,2,1,0:T(8,128)}, u32[]{:S(2)}) %copy-start) | copy-done | bytes 1179672
  16.2 0.2 pack.1
  16.4 0.0 copy-start.3
  16.4 4.4 %collective-permute-start.6 = (f32[9,2,8,128]{3,2,1,0:T(8,128)S(1)}, f32[9,2,8,128]{3,2,1,0:T(8,128)S(1)}, u32[]{:S(2)}, u32[]{:S(2)}) collective-permute-start(f32[9,2,8,128]{3,2,1,0:T(8,128)S(1)} %get-tuple-element.41), channel_id=1, source_target_pairs={{1,0},{2,1},{3,2},{4,3},{5,4},{6,5},{7,6},{8,7},{9,8},{10,9},{11,1... | collective-permute-start | bytes 221192 | tf_op jit(solution)/shard_map/ppermute | solution.py:459
  20.8 0.3 collective-permute-start.4
  21.2 1.5 %collective-permute-start.5 = (f32[4,2,16,128]{3,2,1,0:T(8,128)S(1)}, f32[4,2,16,128]{3,2,1,0:T(8,128)S(1)}, u32[]{:S(2)}, u32[]{:S(2)}) collective-permute-start(f32[4,2,16,128]{3,2,1,0:T(8,128)S(1)} %get-tuple-element.37), channel_id=1, source_target_pairs={{0,3},{1,2},{2,1},{3,0},{4,7},{5,6},{6,5},{7,4},{8,11},{9,10},{10,... | collective-permute-start | bytes 196616 | tf_op jit(solution)/shard_map/ppermute | solution.py:430
  22.7 0.3 coupling.1
  23.0 2.9 %collective-permute-done.4.refs_2_ = f32[4,2,16,128]{3,2,1,0:T(8,128)S(1)} collective-permute-done((f32[4,2,16,128]{3,2,1,0:T(8,128)S(1)}, f32[4,2,16,128]{3,2,1,0:T(8,128)S(1)}, u32[]{:S(2)}, u32[]{:S(2)}) %collective-permute-start.4) | collective-permute-done | bytes 65568 | tf_op jit(solution)/shard_map/ppermute | solution.py:430
  25.9 2.5 %collective-permute-done.5.refs_3_ = f32[4,2,16,128]{3,2,1,0:T(8,128)S(1)} collective-permute-done((f32[4,2,16,128]{3,2,1,0:T(8,128)S(1)}, f32[4,2,16,128]{3,2,1,0:T(8,128)S(1)}, u32[]{:S(2)}, u32[]{:S(2)}) %collective-permute-start.5) | collective-permute-done | bytes 65568 | tf_op jit(solution)/shard_map/ppermute | solution.py:430
  28.4 2.4 %early.1 = (f32[2,8,32,128]{3,2,1,0:T(8,128)S(1)}, f32[2,8,32,128]{3,2,1,0:T(8,128)S(1)}) custom-call(s32[2]{0:T(128)S(1)} %pad_add_fusion.place_ref, f32[72,8,512]{2,1,0:T(8,128)S(1)} %bitcast.10, bf16[288,96]{1,0:T(8,128)(2,1)S(1)} %get-tuple-element.29.coup_ref, f32[4,2,16,128]{3,2,1,0:T(8,128)S(1)} %get-tuple-element.34.refs_0_._, ...), custom_call_target="tpu_custom_call" | custom-call | tf_op jit(solution)/shard_map/early/pallas_call | solution.py:487
  30.8 0.2 unpack.1._.edge_ref
  31.0 3.3 %first.1 = (f32[5,8,32,128]{3,2,1,0:T(8,128)S(1)}, f32[4,8,32,128]{3,2,1,0:T(8,128)S(1)}, f32[16,128]{1,0:T(8,128)S(1)}, f32[4,2,32,128]{3,2,1,0:T(8,128)S(1)}, ...) custom-call(s32[2]{0:T(128)S(1)} %pad_add_fusion.place_ref, ...), custom_call_target="tpu_custom_call" | custom-call | tf_op jit(solution)/shard_map/first/pallas_call | solution.py:496
  34.3 0.1 collective-permute-start.8
  34.4 2.7 %collective-permute-start.9 = (f32[4,2,32,128]{3,2,1,0:T(8,128)S(1)}, f32[4,2,32,128]{3,2,1,0:T(8,128)S(1)}, u32[]{:S(2)}, u32[]{:S(2)}) collective-permute-start(f32[4,2,32,128]{3,2,1,0:T(8,128)S(1)} %get-tuple-element.48), channel_id=1, source_target_pairs={{0,8},{1,9},{2,10},{3,11},{4,12},{5,13},{6,14},{7,15},{8,0},{9,1},... | collective-permute-start | bytes 393224 | tf_op jit(solution)/shard_map/ppermute | solution.py:418
  37.1 1.7 %collective-permute-start.10 = (f32[4,2,32,128]{3,2,1,0:T(8,128)S(1)}, f32[4,2,32,128]{3,2,1,0:T(8,128)S(1)}, u32[]{:S(2)}, u32[]{:S(2)}) collective-permute-start(f32[4,2,32,128]{3,2,1,0:T(8,128)S(1)} %get-tuple-element.49), channel_id=1, source_target_pairs={{0,12},{1,13},{2,14},{3,15},{4,8},{5,9},{6,10},{7,11},{8,4},{9,5},... | collective-permute-start | bytes 393224 | tf_op jit(solution)/shard_map/ppermute | solution.py:418
  38.8 7.2 %second.1 = f32[1056,128]{1,0:T(8,128)} custom-call(f32[8]{0:T(128)S(1)} %copy-done.3, f32[5,8,32,128]{3,2,1,0:T(8,128)S(1)} %get-tuple-element.43.v_ref, f32[4,8,32,128]{3,2,1,0:T(8,128)S(1)} %get-tuple-element.44.w_ref, f32[16,128]{1,0:T(8,128)S(1)} %get-tuple-element.45.sum_ref, f32[72,8,512]{2,1,0:T(8,128)S(1)} %bitcast.12, ...), custom_call_target="tpu_custom_call" | custom-call | flops 75497472 | bytes 16777216 | tf_op jit(solution)/shard_map/second/pallas_call | solution.py:519
  46.0 4.3 %all-to-all-start.1 = ((f32[32,1,4224]{2,1,0:T(1,128)}), f32[32,1,4224]{2,1,0:T(1,128)S(1)}, u32[]{:S(2)}, u32[]{:S(2)}) async-start(f32[32,1,4224]{2,1,0:T(1,128)} %bitcast.8), calls=%async_computation.1 | async-start | bytes 1081344 | tf_op jit(solution)/shard_map/all_to_all | solution.py:530
  50.3 0.6 relay.3
  50.9 0.5 collective-permute-start.11
  51.3 1.7 %collective-permute-start.12 = (f32[4,2,32,128]{3,2,1,0:T(8,128)S(1)}, f32[4,2,32,128]{3,2,1,0:T(8,128)S(1)}, u32[]{:S(2)}, u32[]{:S(2)}) collective-permute-start(f32[4,2,32,128]{3,2,1,0:T(8,128)S(1)} %get-tuple-element.52), channel_id=1, source_target_pairs={{0,2},{1,3},{2,0},{3,1},{4,6},{5,7},{6,4},{7,5},{8,10},{9,11},{10,... | collective-permute-start | bytes 393224 | tf_op jit(solution)/shard_map/ppermute | solution.py:430
  53.0 7.9 %collective-permute-done.12.refs_2_ = f32[4,2,32,128]{3,2,1,0:T(8,128)S(1)} collective-permute-done((f32[4,2,32,128]{3,2,1,0:T(8,128)S(1)}, f32[4,2,32,128]{3,2,1,0:T(8,128)S(1)}, u32[]{:S(2)}, u32[]{:S(2)}) %collective-permute-start.12) | collective-permute-done | bytes 131104 | tf_op jit(solution)/shard_map/ppermute | solution.py:430
  61.0 2.1 %collective-permute-done.13.refs_3_ = f32[4,2,32,128]{3,2,1,0:T(8,128)S(1)} collective-permute-done((f32[4,2,32,128]{3,2,1,0:T(8,128)S(1)}, f32[4,2,32,128]{3,2,1,0:T(8,128)S(1)}, u32[]{:S(2)}, u32[]{:S(2)}) %collective-permute-start.13) | collective-permute-done | bytes 131104 | tf_op jit(solution)/shard_map/ppermute | solution.py:430
  63.1 1.9 %all-to-all-done.1 = f32[32,1,4224]{2,1,0:T(1,128)S(1)} async-done(((f32[32,1,4224]{2,1,0:T(1,128)}), f32[32,1,4224]{2,1,0:T(1,128)S(1)}, u32[]{:S(2)}, u32[]{:S(2)}) %all-to-all-start.1) | async-done | bytes 540704 | tf_op jit(solution)/shard_map/all_to_all | solution.py:530
  65.0 2.1 %combine.1 = (f32[2,8,8192]{2,1,0:T(8,128)}, f32[2,8,8192]{2,1,0:T(8,128)}) custom-call(s32[2]{0:T(128)S(1)} %pad_add_fusion.place_ref, f32[2,8,8192]{2,1,0:T(8,128)S(1)} %copy-done.2, f32[1056,128]{1,0:T(8,128)S(1)} %bitcast.13, f32[4,2,32,128]{3,2,1,0:T(8,128)S(1)} %get-tuple-element.50.refs_0_, f32[4,2,32,128]{3,2,1,0:T(8,128)S(1)} %collective-permute-done.11.refs_1_, ...), custom_call_target="tpu_custom_call" | custom-call | tf_op jit(solution)/shard_map/combine/pallas_call | solution.py:532
  (27 shorter events, 0.1 us)
Async XLA Ops:
  0.7 1.0 %copy-start.1 = (f32[2,8,8192]{2,1,0:T(8,128)S(1)}, f32[2,8,8192]{2,1,0:T(8,128)}, u32[]{:S(2)}) copy-start(f32[2,8,8192]{2,1,0:T(8,128)} %rhs_ref.3) | copy-start | bytes 1572868
  3.1 11.8 %collective-permute-start = (f32[4,2,16,128]{3,2,1,0:T(8,128)S(1)}, f32[4,2,16,128]{3,2,1,0:T(8,128)S(1)}, u32[]{:S(2)}, u32[]{:S(2)}) collective-permute-start(f32[4,2,16,128]{3,2,1,0:T(8,128)S(1)} %get-tuple-element.31), channel_id=1, source_target_pairs={{0,4},{1,5},{2,6},{3,7},{4,0},{5,1},{6,2},{7,3},{8,12},{9,13},{10,... | collective-permute-start | bytes 196616 | tf_op jit(solution)/shard_map/ppermute | solution.py:418
  6.1 8.8 %collective-permute-start.1 = (f32[4,2,16,128]{3,2,1,0:T(8,128)S(1)}, f32[4,2,16,128]{3,2,1,0:T(8,128)S(1)}, u32[]{:S(2)}, u32[]{:S(2)}) collective-permute-start(f32[4,2,16,128]{3,2,1,0:T(8,128)S(1)} %get-tuple-element.32), channel_id=1, source_target_pairs={{0,8},{1,9},{2,10},{3,11},{4,12},{5,13},{6,14},{7,15},{8,0},{9,1},... | collective-permute-start | bytes 196616 | tf_op jit(solution)/shard_map/ppermute | solution.py:418
  8.7 6.2 %collective-permute-start.2 = (f32[4,2,16,128]{3,2,1,0:T(8,128)S(1)}, f32[4,2,16,128]{3,2,1,0:T(8,128)S(1)}, u32[]{:S(2)}, u32[]{:S(2)}) collective-permute-start(f32[4,2,16,128]{3,2,1,0:T(8,128)S(1)} %get-tuple-element.33), channel_id=1, source_target_pairs={{0,12},{1,13},{2,14},{3,15},{4,8},{5,9},{6,10},{7,11},{8,4},{9,5},... | collective-permute-start | bytes 196616 | tf_op jit(solution)/shard_map/ppermute | solution.py:418
  8.7 22.3 %all-to-all-start = ((f32[32,3,8,128]{3,2,1,0:T(8,128)}), f32[32,3,8,128]{3,2,1,0:T(8,128)S(1)}, u32[]{:S(2)}, u32[]{:S(2)}) async-start(f32[32,3,8,128]{3,2,1,0:T(8,128)} %get-tuple-element.28), calls=%async_computation | async-start | bytes 786432 | tf_op jit(solution)/shard_map/all_to_all | solution.py:442
  14.9 1.3 %copy-start = (f32[9,8,8,512]{3,2,1,0:T(8,128)S(1)}, f32[9,8,8,512]{3,2,1,0:T(8,128)}, u32[]{:S(2)}) copy-start(f32[9,8,8,512]{3,2,1,0:T(8,128)} %last_ref.1) | copy-start | bytes 3538948
  16.2 6.5 %copy-start.4 = (s32[512]{0:T(512)S(1)}, s32[512]{0:T(512)}, u32[]{:S(2)}) copy-start(s32[512]{0:T(512)} %param.10) | copy-start | bytes 6148
  16.2 6.5 %copy-start.5 = (s32[512]{0:T(512)S(1)}, s32[512]{0:T(512)}, u32[]{:S(2)}) copy-start(s32[512]{0:T(512)} %param.11) | copy-start | bytes 6148
  16.2 6.5 %copy-start.6 = (s32[512]{0:T(512)S(1)}, s32[512]{0:T(512)}, u32[]{:S(2)}) copy-start(s32[512]{0:T(512)} %param.12) | copy-start | bytes 6148
  16.2 6.5 %copy-start.7 = (s32[512]{0:T(512)S(1)}, s32[512]{0:T(512)}, u32[]{:S(2)}) copy-start(s32[512]{0:T(512)} %param.13) | copy-start | bytes 6148
  16.4 14.6 %copy-start.3 = (f32[8]{0:T(128)S(1)}, f32[8]{0:T(128)}, u32[]{:S(2)}) copy-start(f32[8]{0:T(128)} %dif_ref.3) | copy-start | bytes 100
  16.4 14.4 %collective-permute-start.6 = (f32[9,2,8,128]{3,2,1,0:T(8,128)S(1)}, f32[9,2,8,128]{3,2,1,0:T(8,128)S(1)}, u32[]{:S(2)}, u32[]{:S(2)}) collective-permute-start(f32[9,2,8,128]{3,2,1,0:T(8,128)S(1)} %get-tuple-element.41), channel_id=1, source_target_pairs={{1,0},{2,1},{3,2},{4,3},{5,4},{6,5},{7,6},{8,7},{9,8},{10,9},{11,1... | collective-permute-start | bytes 221192 | tf_op jit(solution)/shard_map/ppermute | solution.py:459
  20.8 10.0 %collective-permute-start.7 = (f32[9,2,8,128]{3,2,1,0:T(8,128)S(1)}, f32[9,2,8,128]{3,2,1,0:T(8,128)S(1)}, u32[]{:S(2)}, u32[]{:S(2)}) collective-permute-start(f32[9,2,8,128]{3,2,1,0:T(8,128)S(1)} %get-tuple-element.42), channel_id=1, source_target_pairs={{0,1},{1,2},{2,3},{3,4},{4,5},{5,6},{6,7},{7,8},{8,9},{9,10},{10,1... | collective-permute-start | bytes 221192 | tf_op jit(solution)/shard_map/ppermute | solution.py:460
  20.8 2.2 %collective-permute-start.3 = (f32[4,2,16,128]{3,2,1,0:T(8,128)S(1)}, f32[4,2,16,128]{3,2,1,0:T(8,128)S(1)}, u32[]{:S(2)}, u32[]{:S(2)}) collective-permute-start(f32[4,2,16,128]{3,2,1,0:T(8,128)S(1)} %get-tuple-element.35), channel_id=1, source_target_pairs={{0,1},{1,0},{2,3},{3,2},{4,5},{5,4},{6,7},{7,6},{8,9},{9,8},{10,11... | collective-permute-start | bytes 196616 | tf_op jit(solution)/shard_map/ppermute | solution.py:430
  20.8 5.0 %collective-permute-start.4 = (f32[4,2,16,128]{3,2,1,0:T(8,128)S(1)}, f32[4,2,16,128]{3,2,1,0:T(8,128)S(1)}, u32[]{:S(2)}, u32[]{:S(2)}) collective-permute-start(f32[4,2,16,128]{3,2,1,0:T(8,128)S(1)} %get-tuple-element.36), channel_id=1, source_target_pairs={{0,2},{1,3},{2,0},{3,1},{4,6},{5,7},{6,4},{7,5},{8,10},{9,11},{10,... | collective-permute-start | bytes 196616 | tf_op jit(solution)/shard_map/ppermute | solution.py:430
  21.2 7.2 %collective-permute-start.5 = (f32[4,2,16,128]{3,2,1,0:T(8,128)S(1)}, f32[4,2,16,128]{3,2,1,0:T(8,128)S(1)}, u32[]{:S(2)}, u32[]{:S(2)}) collective-permute-start(f32[4,2,16,128]{3,2,1,0:T(8,128)S(1)} %get-tuple-element.37), channel_id=1, source_target_pairs={{0,3},{1,2},{2,1},{3,0},{4,7},{5,6},{6,5},{7,4},{8,11},{9,10},{10,... | collective-permute-start | bytes 196616 | tf_op jit(solution)/shard_map/ppermute | solution.py:430
  34.3 15.9 %collective-permute-start.8 = (f32[4,2,32,128]{3,2,1,0:T(8,128)S(1)}, f32[4,2,32,128]{3,2,1,0:T(8,128)S(1)}, u32[]{:S(2)}, u32[]{:S(2)}) collective-permute-start(f32[4,2,32,128]{3,2,1,0:T(8,128)S(1)} %get-tuple-element.47), channel_id=1, source_target_pairs={{0,4},{1,5},{2,6},{3,7},{4,0},{5,1},{6,2},{7,3},{8,12},{9,13},{10,... | collective-permute-start | bytes 393224 | tf_op jit(solution)/shard_map/ppermute | solution.py:418
  34.4 15.8 %collective-permute-start.9 = (f32[4,2,32,128]{3,2,1,0:T(8,128)S(1)}, f32[4,2,32,128]{3,2,1,0:T(8,128)S(1)}, u32[]{:S(2)}, u32[]{:S(2)}) collective-permute-start(f32[4,2,32,128]{3,2,1,0:T(8,128)S(1)} %get-tuple-element.48), channel_id=1, source_target_pairs={{0,8},{1,9},{2,10},{3,11},{4,12},{5,13},{6,14},{7,15},{8,0},{9,1},... | collective-permute-start | bytes 393224 | tf_op jit(solution)/shard_map/ppermute | solution.py:418
  37.1 13.2 %collective-permute-start.10 = (f32[4,2,32,128]{3,2,1,0:T(8,128)S(1)}, f32[4,2,32,128]{3,2,1,0:T(8,128)S(1)}, u32[]{:S(2)}, u32[]{:S(2)}) collective-permute-start(f32[4,2,32,128]{3,2,1,0:T(8,128)S(1)} %get-tuple-element.49), channel_id=1, source_target_pairs={{0,12},{1,13},{2,14},{3,15},{4,8},{5,9},{6,10},{7,11},{8,4},{9,5},... | collective-permute-start | bytes 393224 | tf_op jit(solution)/shard_map/ppermute | solution.py:418
  46.0 19.0 %all-to-all-start.1 = ((f32[32,1,4224]{2,1,0:T(1,128)}), f32[32,1,4224]{2,1,0:T(1,128)S(1)}, u32[]{:S(2)}, u32[]{:S(2)}) async-start(f32[32,1,4224]{2,1,0:T(1,128)} %bitcast.8), calls=%async_computation.1 | async-start | bytes 1081344 | tf_op jit(solution)/shard_map/all_to_all | solution.py:530
  50.3 14.7 %copy-start.2 = (f32[2,8,8192]{2,1,0:T(8,128)S(1)}, f32[2,8,8192]{2,1,0:T(8,128)}, u32[]{:S(2)}) copy-start(f32[2,8,8192]{2,1,0:T(8,128)} %rhs_ref.3) | copy-start | bytes 1572868
  50.9 2.2 %collective-permute-start.11 = (f32[4,2,32,128]{3,2,1,0:T(8,128)S(1)}, f32[4,2,32,128]{3,2,1,0:T(8,128)S(1)}, u32[]{:S(2)}, u32[]{:S(2)}) collective-permute-start(f32[4,2,32,128]{3,2,1,0:T(8,128)S(1)} %get-tuple-element.51), channel_id=1, source_target_pairs={{0,1},{1,0},{2,3},{3,2},{4,5},{5,4},{6,7},{7,6},{8,9},{9,8},{10,11... | collective-permute-start | bytes 393224 | tf_op jit(solution)/shard_map/ppermute | solution.py:430
  51.3 9.6 %collective-permute-start.12 = (f32[4,2,32,128]{3,2,1,0:T(8,128)S(1)}, f32[4,2,32,128]{3,2,1,0:T(8,128)S(1)}, u32[]{:S(2)}, u32[]{:S(2)}) collective-permute-start(f32[4,2,32,128]{3,2,1,0:T(8,128)S(1)} %get-tuple-element.52), channel_id=1, source_target_pairs={{0,2},{1,3},{2,0},{3,1},{4,6},{5,7},{6,4},{7,5},{8,10},{9,11},{10,... | collective-permute-start | bytes 393224 | tf_op jit(solution)/shard_map/ppermute | solution.py:430
  53.0 10.0 %collective-permute-start.13 = (f32[4,2,32,128]{3,2,1,0:T(8,128)S(1)}, f32[4,2,32,128]{3,2,1,0:T(8,128)S(1)}, u32[]{:S(2)}, u32[]{:S(2)}) collective-permute-start(f32[4,2,32,128]{3,2,1,0:T(8,128)S(1)} %get-tuple-element.53), channel_id=1, source_target_pairs={{0,3},{1,2},{2,1},{3,0},{4,7},{5,6},{6,5},{7,4},{8,11},{9,10},{10,... | collective-permute-start | bytes 393224 | tf_op jit(solution)/shard_map/ppermute | solution.py:430

commit v6 on v5

--- a/solution.py
+++ b/solution.py
@@ -114,34 +114,52 @@
 
 def mix(get, ct, slot, coup_ref, vs_ref, mx_ref):
     n = vs_ref.shape[1] // 3
-    for t in range(S):
-        at = slice(t * LANES, (t + 1) * LANES)
-        high, low = split(get(ct, t))
-        vs_ref[slot, 0:n, at] = high
-        vs_ref[slot, n : 2 * n, at] = low
-        vs_ref[slot, 2 * n : 3 * n, at] = high
-    mx_ref[slot] = jnp.dot(coup_ref[...], vs_ref[slot], preferred_element_type=F32)
+
+    def step(first):
+        for t in (first, first + 1):
+            at = slice(t * LANES, (t + 1) * LANES)
+            high, low = split(get(ct, t))
+            vs_ref[slot, 0:n, at] = high
+            vs_ref[slot, n : 2 * n, at] = low
+            vs_ref[slot, 2 * n : 3 * n, at] = high
+        at = slice(first * LANES, (first + 2) * LANES)
+        mx_ref[slot, :, at] = jnp.dot(coup_ref[...], vs_ref[slot, :, at], preferred_element_type=F32)
+
+    return [functools.partial(step, first) for first in range(0, S, 2)]
 
 
 def spread(get, ct, slot, every, stencil_ref, xs_ref, bs_ref):
     n = bs_ref.shape[1] // S
-    wide = lax.broadcasted_iota(jnp.int32, (n, LANES), 1) < LANES // 2
     before, after = (ct - 1) % every, (ct + 1) % every
-    for t in range(S):
-        to = slice(t * n, (t + 1) * n)
-        high, low = split(get(ct, t))
-        xs_ref[slot, to, 0:LANES] = high
-        xs_ref[slot, to, LANES : 2 * LANES] = low
-        high, low = split(jnp.where(wide, get(after, t), get(before, t)))
-        xs_ref[slot, to, 2 * LANES : 3 * LANES] = high
-        xs_ref[slot, to, 3 * LANES :] = low
-    bs_ref[slot] = jnp.dot(xs_ref[slot], stencil_ref[...], preferred_element_type=F32)
-
-
-def react(n, jac, slot, mx_ref, finish):
+
+    def fill(first):
+        wide = lax.broadcasted_iota(jnp.int32, (n, LANES), 1) < LANES // 2
+        for t in (first, first + 1):
+            to = slice(t * n, (t + 1) * n)
+            high, low = split(get(ct, t))
+            xs_ref[slot, to, 0:LANES] = high
+            xs_ref[slot, to, LANES : 2 * LANES] = low
+            high, low = split(jnp.where(wide, get(after, t), get(before, t)))
+            xs_ref[slot, to, 2 * LANES : 3 * LANES] = high
+            xs_ref[slot, to, 3 * LANES :] = low
+        if first + 2 == S:
+            bs_ref[slot] = jnp.dot(xs_ref[slot], stencil_ref[...], preferred_element_type=F32)
+
+    return [functools.partial(fill, first) for first in range(0, S, 2)]
+
+
+def run(steps):
+    for step in steps:
+        step()
+
+
+def react(n, jac, slot, mx_ref, finish, steps=()):
+    steps = list(steps)
     for kb in range(0, n, 32):
         acc = [None] * 32
         for i in range(NCOEF):
+            if steps:
+                steps.pop(0)()
             for t in range(S):
                 m = [
                     mx_ref[slot, i * n + kb + kt * 8 : i * n + kb + kt * 8 + 8, t * LANES : (t + 1) * LANES]
@@ -156,6 +174,7 @@
         for s in range(S):
             for kt in range(4):
                 finish(s, kb + kt * 8, acc[s * 4 + kt])
+    run(steps)
 
 
 def tile_of(jac_ref, ct):
@@ -196,11 +215,10 @@
 
         return finish
 
-    mix(get, 0, 0, coup_ref, vs_ref, mx_ref)
+    run(mix(get, 0, 0, coup_ref, vs_ref, mx_ref))
     for ct in range(early):
-        if ct + 1 < early:
-            mix(get, ct + 1, (ct + 1) % 2, coup_ref, vs_ref, mx_ref)
-        react(n, tile_of(jac_ref, ct), ct % 2, mx_ref, finisher(ct))
+        steps = mix(get, ct + 1, (ct + 1) % 2, coup_ref, vs_ref, mx_ref) if ct + 1 < early else []
+        react(n, tile_of(jac_ref, ct), ct % 2, mx_ref, finisher(ct), steps)
 
 
 def first_kernel(n, tiles, place_ref, dif_ref, r_ref, ve_ref, ae_ref, jac_ref, coup_ref, stencil_ref, _, *refs):
@@ -218,9 +236,9 @@
     def get(ct, t):
         return v_ref[ct, t]
 
-    def finisher(ct):
+    def finisher(ct, slot):
         def finish(s, k, acc):
-            w = dif_ref[s] * bs_ref[ct % 2, s * n + k : s * n + k + 8] - acc
+            w = dif_ref[s] * bs_ref[slot, s * n + k : s * n + k + 8] - acc
             w_ref[ct, s, k : k + 8] = w
             v = v_ref[ct, s, k : k + 8]
             sums.add("rr", k // 8, v * v)
@@ -228,18 +246,28 @@
 
         return finish
 
+    def prepare(ct):
+        return mix(get, ct, ct % 2, coup_ref, vs_ref, mx_ref) + sides(ct, ct % 2)
+
+    def sides(ct, slot):
+        return spread(get, ct, slot, every, stencil_ref, xs_ref, bs_ref)
+
+    def close(ct, slot):
+        for s in range(S):
+            for k in range(0, n, 8):
+                finisher(ct, slot)(s, k, ae_ref[ct, s, k : k + 8])
+
+    spare = tiles % 2
+    rest = []
+    for ct in range(early):
+        rest += sides(ct, spare) + [functools.partial(close, ct, spare)]
     if early < tiles:
-        mix(get, early, early % 2, coup_ref, vs_ref, mx_ref)
-    for ct in range(tiles):
-        spread(get, ct, ct % 2, every, stencil_ref, xs_ref, bs_ref)
-        if early <= ct and ct + 1 < tiles:
-            mix(get, ct + 1, (ct + 1) % 2, coup_ref, vs_ref, mx_ref)
-        if ct < early:
-            for s in range(S):
-                for k in range(0, n, 8):
-                    finisher(ct)(s, k, ae_ref[ct, s, k : k + 8])
-        else:
-            react(n, tile_of(jac_ref, ct), ct % 2, mx_ref, finisher(ct))
+        run(prepare(early))
+    for ct in range(early, tiles):
+        steps = prepare(ct + 1) if ct + 1 < tiles else rest
+        react(n, tile_of(jac_ref, ct), ct % 2, mx_ref, finisher(ct, ct % 2), steps)
+    if early == tiles:
+        run(rest)
     for q in range(n // 8):
         at = pl.multiple_of(jnp.bitwise_xor(place_ref[0], q) * 8, 8)
         flat = send_refs[q].reshape(8 * tiles * S, LANES)
@@ -282,11 +310,11 @@
         return w_ref[ct, t] if ct < tiles else wh_ref[t]
 
     def finish_edge(s, k, acc):
-        wh_ref[s, k : k + 8] = dif_ref[s] * bs_ref[tiles % 2, s * n + k : s * n + k + 8] - acc
-
-    def finisher(ct):
+        wh_ref[s, k : k + 8] = dif_ref[s] * bs_ref[0, s * n + k : s * n + k + 8] - acc
+
+    def finisher(ct, slot):
         def finish(s, k, acc):
-            z = dif_ref[s] * bs_ref[ct % 2, s * n + k : s * n + k + 8] - acc
+            z = dif_ref[s] * bs_ref[slot, s * n + k : s * n + k + 8] - acc
             v, w = v_ref[ct, s, k : k + 8], w_ref[ct, s, k : k + 8]
             z_ref[ct, s, k : k + 8] = z
             out_ref[pl.ds(k * per + ct * S + s, 8, stride=per), :] = z
@@ -298,18 +326,26 @@
 
         return finish
 
-    slot = tiles % 2
-    mix(get_v, tiles, slot, coup_ref, vs_ref, mx_ref)
-    spread(get_v, tiles, slot, every, stencil_ref, xs_ref, bs_ref)
     order = list(range(1, tiles)) + [0]
-    mix(get_w, order[0], 1 - slot, coup_ref, vs_ref, mx_ref)
-    react(n, tile_of(edge_ref, 0), slot, mx_ref, finish_edge)
+
+    def mixed(get, ct, slot):
+        return mix(get, ct, slot, coup_ref, vs_ref, mx_ref)
+
+    def sides(get, ct, slot):
+        return spread(get, ct, slot, every, stencil_ref, xs_ref, bs_ref)
+
+    run(mixed(get_v, tiles, 0) + sides(get_v, tiles, 0))
+    inside = tiles > 2
+    steps = mixed(get_w, order[0], 1) + (sides(get_w, order[0], 1) if inside else [])
+    react(n, tile_of(edge_ref, 0), 0, mx_ref, finish_edge, steps)
+    if not inside:
+        run(sides(get_w, order[0], 1))
     for at, ct in enumerate(order):
-        now = (1 - slot + at) % 2
-        spread(get_w, ct, ct % 2, every, stencil_ref, xs_ref, bs_ref)
+        slot = (at + 1) % 2
+        steps = []
         if at + 1 < tiles:
-            mix(get_w, order[at + 1], 1 - now, coup_ref, vs_ref, mx_ref)
-        react(n, tile_of(jac_ref, ct), now, mx_ref, finisher(ct))
+            steps = mixed(get_w, order[at + 1], 1 - slot) + sides(get_w, order[at + 1], 1 - slot)
+        react(n, tile_of(jac_ref, ct), slot, mx_ref, finisher(ct, slot), steps)
     uu, ur, uz, rz = (sums.total(name) for name in ("uu", "ur", "uz", "rz"))
     c2 = ratio(rz, rr)
     c3 = ratio(uz - c2 * ur, uu)
@@ -491,6 +527,7 @@
         out_specs=[VMEM] * 2,
         scratch_shapes=[pltpu.VMEM((parts, own, early * S, LANES), F32), work[0], work[2]],
         compiler_params=PARAMS,
+        cost_estimate=pl.CostEstimate(flops=2 * 10**9, bytes_accessed=1 << 20, transcendentals=0),
         name="early",
     )(place, jac, coupling, *near)
     v, w, sums, *w_send = pl.pallas_call(

time: 67.5 us -> 65 us (0.963)
  waiting for transfers between devices: 17.4 us -> 16.1 us
  local copies, waits for them, and re-layouts: 1.76 us -> 1.08 us
    ppermute x6, waiting for transfers between devices: 15.4 us -> 11.7 us  [across(): lax.ppermute(relayed[k], 'modes', [(i, i ^ k) for i in range(parts)])]
    ppermute x1, waiting for transfers between devices: 0.01 us -> 2.39 us  [local(): before = lax.ppermute(tail, 'modes', up)]
    all_to_all x1, starting transfers between devices: 4.26 us -> 3.57 us  [local(): lax.all_to_all(z_send.reshape(n, 1, line), 'modes', split_axis=0, concat_...]
    unnamed x16, local copies, waits for them, and re-layouts: 1.76 us -> 1.08 us
  transfers between devices with their start and end apart: 16 -> 16, of which waited for: 5 -> 5; matrix products, arithmetic and copies ran while one was open for 0% -> 0% of each run, Pallas kernels for 17% -> 18%
where the time goes in v6:
time: 65 us; the launch traced here: 64.6 us
  starting transfers between devices  28.5 us (44%)
  Pallas kernels  18 us (28%)
  waiting for transfers between devices  16.1 us (25%)
  local copies, waits for them, and re-layouts  1.08 us (2%)
  between operations  0.89 us (1%)
    ppermute x6, waiting for transfers between devices, across(): lax.ppermute(relayed[k], 'modes', [(i, i ^ k) for i in range(parts)])  11.7 us
    ppermute x6, starting transfers between devices, across(): lax.ppermute(arrays[q], 'modes', [(i, i ^ q * plane) for i in range(parts)])  10.1 us
    pallas_call x1, Pallas kernels, local(): pl.pallas_call(functools.partial(second_kernel, n, tiles), out_shape=sds(...  7.18 us
    all_to_all x1, starting transfers between devices, local(): lax.all_to_all(late_send, 'modes', split_axis=0, concat_axis=0, tiled=True)  6.16 us
    ppermute x1, starting transfers between devices, local(): after = lax.ppermute(head, 'modes', down)  4.48 us
    ppermute x6, starting transfers between devices, across(): lax.ppermute(relayed[k], 'modes', [(i, i ^ k) for i in range(parts)])  4.2 us
    all_to_all x1, starting transfers between devices, local(): lax.all_to_all(z_send.reshape(n, 1, line), 'modes', split_axis=0, concat_...  3.57 us
    pallas_call x1, Pallas kernels, local(): pl.pallas_call(functools.partial(first_kernel, n, tiles), out_shape=[sds(...  3.21 us
  transfers between devices with their start and end apart: 16, of which 5 were waited for; matrix products, arithmetic and copies ran while one was open for 0% of the time, Pallas kernels for 18%

profile of v6, /device:TPU:0, one launch (start us, length us, event | category | flops | bytes accessed | tf_op | source)
XLA Modules:
  0.0 64.6 jit_solution(11666649377780384365)
XLA Ops:
  0.6 0.1 pad_add_fusion.place_ref
  0.7 1.0 %copy-done.1 = f32[2,8,8192]{2,1,0:T(8,128)S(1)} copy-done((f32[2,8,8192]{2,1,0:T(8,128)S(1)}, f32[2,8,8192]{2,1,0:T(8,128)}, u32[]{:S(2)}) %copy-start.1) | copy-done | bytes 524312
  1.8 1.3 %arrange.1 = (f32[32,3,8,128]{3,2,1,0:T(8,128)}, f32[4,2,16,128]{3,2,1,0:T(8,128)S(1)}, f32[4,2,16,128]{3,2,1,0:T(8,128)S(1)}, f32[4,2,16,128]{3,2,1,0:T(8,128)S(1)}, f32[4,2,16,128]{3,2,1,0:T(8,128)S(1)}) custom-call(s32[2]{0:T(128)S(1)} %pad_add_fusion.place_ref, f32[2,8,8192]{2,1,0:T(8,128)S(1)} %copy-done.1), custom_call_target="tpu_custom_call" | custom-call | tf_op jit(solution)/shard_map/arrange/pallas_call | solution.py:469
  3.1 3.0 %collective-permute-start = (f32[4,2,16,128]{3,2,1,0:T(8,128)S(1)}, f32[4,2,16,128]{3,2,1,0:T(8,128)S(1)}, u32[]{:S(2)}, u32[]{:S(2)}) collective-permute-start(f32[4,2,16,128]{3,2,1,0:T(8,128)S(1)} %get-tuple-element.31), channel_id=1, source_target_pairs={{0,4},{1,5},{2,6},{3,7},{4,0},{5,1},{6,2},{7,3},{8,12},{9,13},{10,... | collective-permute-start | bytes 196616 | tf_op jit(solution)/shard_map/ppermute | solution.py:454
  6.1 2.6 %collective-permute-start.1 = (f32[4,2,16,128]{3,2,1,0:T(8,128)S(1)}, f32[4,2,16,128]{3,2,1,0:T(8,128)S(1)}, u32[]{:S(2)}, u32[]{:S(2)}) collective-permute-start(f32[4,2,16,128]{3,2,1,0:T(8,128)S(1)} %get-tuple-element.32), channel_id=1, source_target_pairs={{0,8},{1,9},{2,10},{3,11},{4,12},{5,13},{6,14},{7,15},{8,0},{9,1},... | collective-permute-start | bytes 196616 | tf_op jit(solution)/shard_map/ppermute | solution.py:454
  8.7 6.2 %all-to-all-start = ((f32[32,3,8,128]{3,2,1,0:T(8,128)}), f32[32,3,8,128]{3,2,1,0:T(8,128)S(1)}, u32[]{:S(2)}, u32[]{:S(2)}) async-start(f32[32,3,8,128]{3,2,1,0:T(8,128)} %get-tuple-element.28), calls=%async_computation | async-start | bytes 786432 | tf_op jit(solution)/shard_map/all_to_all | solution.py:478
  14.9 0.0 copy-start.4
  14.9 0.0 copy-start.6
  15.0 0.0 copy-start.7
  15.0 0.6 relay.2
  15.6 0.5 collective-permute-start.3
  16.0 1.7 %collective-permute-start.4 = (f32[4,2,16,128]{3,2,1,0:T(8,128)S(1)}, f32[4,2,16,128]{3,2,1,0:T(8,128)S(1)}, u32[]{:S(2)}, u32[]{:S(2)}) collective-permute-start(f32[4,2,16,128]{3,2,1,0:T(8,128)S(1)} %get-tuple-element.36), channel_id=1, source_target_pairs={{0,2},{1,3},{2,0},{3,1},{4,6},{5,7},{6,4},{7,5},{8,10},{9,11},{10,... | collective-permute-start | bytes 196616 | tf_op jit(solution)/shard_map/ppermute | solution.py:466
  17.7 0.3 coupling.1
  18.0 0.2 pack.1
  18.2 4.5 %collective-permute-start.6 = (f32[9,2,8,128]{3,2,1,0:T(8,128)S(1)}, f32[9,2,8,128]{3,2,1,0:T(8,128)S(1)}, u32[]{:S(2)}, u32[]{:S(2)}) collective-permute-start(f32[9,2,8,128]{3,2,1,0:T(8,128)S(1)} %get-tuple-element.41), channel_id=1, source_target_pairs={{1,0},{2,1},{3,2},{4,3},{5,4},{6,5},{7,6},{8,7},{9,8},{10,9},{11,1... | collective-permute-start | bytes 221192 | tf_op jit(solution)/shard_map/ppermute | solution.py:495
  22.7 1.7 %collective-permute-done.5.refs_3_ = f32[4,2,16,128]{3,2,1,0:T(8,128)S(1)} collective-permute-done((f32[4,2,16,128]{3,2,1,0:T(8,128)S(1)}, f32[4,2,16,128]{3,2,1,0:T(8,128)S(1)}, u32[]{:S(2)}, u32[]{:S(2)}) %collective-permute-start.5) | collective-permute-done | bytes 65568 | tf_op jit(solution)/shard_map/ppermute | solution.py:466
  24.4 2.4 %early.1 = (f32[2,8,32,128]{3,2,1,0:T(8,128)S(1)}, f32[2,8,32,128]{3,2,1,0:T(8,128)S(1)}) custom-call(s32[2]{0:T(128)S(1)} %pad_add_fusion.place_ref, f32[72,8,512]{2,1,0:T(8,128)S(1)} %bitcast.10, bf16[288,96]{1,0:T(8,128)(2,1)S(1)} %get-tuple-element.29.coup_ref, f32[4,2,16,128]{3,2,1,0:T(8,128)S(1)} %get-tuple-element.34.refs_0_._, ...), custom_call_target="tpu_custom_call" | custom-call | flops 2000000000 | bytes 1048576 | tf_op jit(solution)/shard_map/early/pallas_call | solution.py:523
  26.8 2.4 %collective-permute-done.7.prev_ref = f32[9,2,8,128]{3,2,1,0:T(8,128)S(1)} collective-permute-done((f32[9,2,8,128]{3,2,1,0:T(8,128)S(1)}, f32[9,2,8,128]{3,2,1,0:T(8,128)S(1)}, u32[]{:S(2)}, u32[]{:S(2)}) %collective-permute-start.7) | collective-permute-done | bytes 73760 | tf_op jit(solution)/shard_map/ppermute | solution.py:496
  29.2 0.2 unpack.1._.edge_ref
  29.4 3.2 %first.1 = (f32[5,8,32,128]{3,2,1,0:T(8,128)S(1)}, f32[4,8,32,128]{3,2,1,0:T(8,128)S(1)}, f32[16,128]{1,0:T(8,128)S(1)}, f32[4,2,32,128]{3,2,1,0:T(8,128)S(1)}, ...) custom-call(s32[2]{0:T(128)S(1)} %pad_add_fusion.place_ref, ...), custom_call_target="tpu_custom_call" | custom-call | tf_op jit(solution)/shard_map/first/pallas_call | solution.py:533
  32.6 0.1 collective-permute-start.8
  32.7 2.4 %collective-permute-start.9 = (f32[4,2,32,128]{3,2,1,0:T(8,128)S(1)}, f32[4,2,32,128]{3,2,1,0:T(8,128)S(1)}, u32[]{:S(2)}, u32[]{:S(2)}) collective-permute-start(f32[4,2,32,128]{3,2,1,0:T(8,128)S(1)} %get-tuple-element.48), channel_id=1, source_target_pairs={{0,8},{1,9},{2,10},{3,11},{4,12},{5,13},{6,14},{7,15},{8,0},{9,1},... | collective-permute-start | bytes 393224 | tf_op jit(solution)/shard_map/ppermute | solution.py:454
  35.1 1.9 %collective-permute-start.10 = (f32[4,2,32,128]{3,2,1,0:T(8,128)S(1)}, f32[4,2,32,128]{3,2,1,0:T(8,128)S(1)}, u32[]{:S(2)}, u32[]{:S(2)}) collective-permute-start(f32[4,2,32,128]{3,2,1,0:T(8,128)S(1)} %get-tuple-element.49), channel_id=1, source_target_pairs={{0,12},{1,13},{2,14},{3,15},{4,8},{5,9},{6,10},{7,11},{8,4},{9,5},... | collective-permute-start | bytes 393224 | tf_op jit(solution)/shard_map/ppermute | solution.py:454
  37.0 7.2 %second.1 = f32[1056,128]{1,0:T(8,128)} custom-call(f32[8]{0:T(128)S(1)} %copy-done.3, f32[5,8,32,128]{3,2,1,0:T(8,128)S(1)} %get-tuple-element.43.v_ref, f32[4,8,32,128]{3,2,1,0:T(8,128)S(1)} %get-tuple-element.44.w_ref, f32[16,128]{1,0:T(8,128)S(1)} %get-tuple-element.45.sum_ref, f32[72,8,512]{2,1,0:T(8,128)S(1)} %bitcast.12, ...), custom_call_target="tpu_custom_call" | custom-call | flops 75497472 | bytes 16777216 | tf_op jit(solution)/shard_map/second/pallas_call | solution.py:556
  44.2 3.6 %all-to-all-start.1 = ((f32[32,1,4224]{2,1,0:T(1,128)}), f32[32,1,4224]{2,1,0:T(1,128)S(1)}, u32[]{:S(2)}, u32[]{:S(2)}) async-start(f32[32,1,4224]{2,1,0:T(1,128)} %bitcast.8), calls=%async_computation.1 | async-start | bytes 1081344 | tf_op jit(solution)/shard_map/all_to_all | solution.py:567
  47.9 0.6 relay.3
  48.4 0.4 collective-permute-start.11
  48.8 1.7 %collective-permute-start.12 = (f32[4,2,32,128]{3,2,1,0:T(8,128)S(1)}, f32[4,2,32,128]{3,2,1,0:T(8,128)S(1)}, u32[]{:S(2)}, u32[]{:S(2)}) collective-permute-start(f32[4,2,32,128]{3,2,1,0:T(8,128)S(1)} %get-tuple-element.52), channel_id=1, source_target_pairs={{0,2},{1,3},{2,0},{3,1},{4,6},{5,7},{6,4},{7,5},{8,10},{9,11},{10,... | collective-permute-start | bytes 393224 | tf_op jit(solution)/shard_map/ppermute | solution.py:466
  50.5 7.9 %collective-permute-done.12.refs_2_ = f32[4,2,32,128]{3,2,1,0:T(8,128)S(1)} collective-permute-done((f32[4,2,32,128]{3,2,1,0:T(8,128)S(1)}, f32[4,2,32,128]{3,2,1,0:T(8,128)S(1)}, u32[]{:S(2)}, u32[]{:S(2)}) %collective-permute-start.12) | collective-permute-done | bytes 131104 | tf_op jit(solution)/shard_map/ppermute | solution.py:466
  58.4 2.1 %collective-permute-done.13.refs_3_ = f32[4,2,32,128]{3,2,1,0:T(8,128)S(1)} collective-permute-done((f32[4,2,32,128]{3,2,1,0:T(8,128)S(1)}, f32[4,2,32,128]{3,2,1,0:T(8,128)S(1)}, u32[]{:S(2)}, u32[]{:S(2)}) %collective-permute-start.13) | collective-permute-done | bytes 131104 | tf_op jit(solution)/shard_map/ppermute | solution.py:466
  60.5 2.0 %all-to-all-done.1 = f32[32,1,4224]{2,1,0:T(1,128)S(1)} async-done(((f32[32,1,4224]{2,1,0:T(1,128)}), f32[32,1,4224]{2,1,0:T(1,128)S(1)}, u32[]{:S(2)}, u32[]{:S(2)}) %all-to-all-start.1) | async-done | bytes 540704 | tf_op jit(solution)/shard_map/all_to_all | solution.py:567
  62.5 2.1 %combine.1 = (f32[2,8,8192]{2,1,0:T(8,128)}, f32[2,8,8192]{2,1,0:T(8,128)}) custom-call(s32[2]{0:T(128)S(1)} %pad_add_fusion.place_ref, f32[2,8,8192]{2,1,0:T(8,128)S(1)} %copy-done.2, f32[1056,128]{1,0:T(8,128)S(1)} %bitcast.13, f32[4,2,32,128]{3,2,1,0:T(8,128)S(1)} %get-tuple-element.50.refs_0_, f32[4,2,32,128]{3,2,1,0:T(8,128)S(1)} %collective-permute-done.11.refs_1_, ...), custom_call_target="tpu_custom_call" | custom-call | tf_op jit(solution)/shard_map/combine/pallas_call | solution.py:569
  (27 shorter events, 0.1 us)
Async XLA Ops:
  0.7 1.0 %copy-start.1 = (f32[2,8,8192]{2,1,0:T(8,128)S(1)}, f32[2,8,8192]{2,1,0:T(8,128)}, u32[]{:S(2)}) copy-start(f32[2,8,8192]{2,1,0:T(8,128)} %rhs_ref.3) | copy-start | bytes 1572868
  3.1 11.8 %collective-permute-start = (f32[4,2,16,128]{3,2,1,0:T(8,128)S(1)}, f32[4,2,16,128]{3,2,1,0:T(8,128)S(1)}, u32[]{:S(2)}, u32[]{:S(2)}) collective-permute-start(f32[4,2,16,128]{3,2,1,0:T(8,128)S(1)} %get-tuple-element.31), channel_id=1, source_target_pairs={{0,4},{1,5},{2,6},{3,7},{4,0},{5,1},{6,2},{7,3},{8,12},{9,13},{10,... | collective-permute-start | bytes 196616 | tf_op jit(solution)/shard_map/ppermute | solution.py:454
  6.1 8.8 %collective-permute-start.1 = (f32[4,2,16,128]{3,2,1,0:T(8,128)S(1)}, f32[4,2,16,128]{3,2,1,0:T(8,128)S(1)}, u32[]{:S(2)}, u32[]{:S(2)}) collective-permute-start(f32[4,2,16,128]{3,2,1,0:T(8,128)S(1)} %get-tuple-element.32), channel_id=1, source_target_pairs={{0,8},{1,9},{2,10},{3,11},{4,12},{5,13},{6,14},{7,15},{8,0},{9,1},... | collective-permute-start | bytes 196616 | tf_op jit(solution)/shard_map/ppermute | solution.py:454
  8.7 6.2 %collective-permute-start.2 = (f32[4,2,16,128]{3,2,1,0:T(8,128)S(1)}, f32[4,2,16,128]{3,2,1,0:T(8,128)S(1)}, u32[]{:S(2)}, u32[]{:S(2)}) collective-permute-start(f32[4,2,16,128]{3,2,1,0:T(8,128)S(1)} %get-tuple-element.33), channel_id=1, source_target_pairs={{0,12},{1,13},{2,14},{3,15},{4,8},{5,9},{6,10},{7,11},{8,4},{9,5},... | collective-permute-start | bytes 196616 | tf_op jit(solution)/shard_map/ppermute | solution.py:454
  8.7 20.6 %all-to-all-start = ((f32[32,3,8,128]{3,2,1,0:T(8,128)}), f32[32,3,8,128]{3,2,1,0:T(8,128)S(1)}, u32[]{:S(2)}, u32[]{:S(2)}) async-start(f32[32,3,8,128]{3,2,1,0:T(8,128)} %get-tuple-element.28), calls=%async_computation | async-start | bytes 786432 | tf_op jit(solution)/shard_map/all_to_all | solution.py:478
  14.9 2.8 %copy-start.4 = (s32[512]{0:T(512)S(1)}, s32[512]{0:T(512)}, u32[]{:S(2)}) copy-start(s32[512]{0:T(512)} %param.10) | copy-start | bytes 6148
  14.9 2.8 %copy-start.5 = (s32[512]{0:T(512)S(1)}, s32[512]{0:T(512)}, u32[]{:S(2)}) copy-start(s32[512]{0:T(512)} %param.11) | copy-start | bytes 6148
  14.9 2.8 %copy-start.6 = (s32[512]{0:T(512)S(1)}, s32[512]{0:T(512)}, u32[]{:S(2)}) copy-start(s32[512]{0:T(512)} %param.12) | copy-start | bytes 6148
  15.0 2.8 %copy-start.7 = (s32[512]{0:T(512)S(1)}, s32[512]{0:T(512)}, u32[]{:S(2)}) copy-start(s32[512]{0:T(512)} %param.13) | copy-start | bytes 6148
  15.0 3.0 %copy-start = (f32[9,8,8,512]{3,2,1,0:T(8,128)S(1)}, f32[9,8,8,512]{3,2,1,0:T(8,128)}, u32[]{:S(2)}) copy-start(f32[9,8,8,512]{3,2,1,0:T(8,128)} %last_ref.1) | copy-start | bytes 3538948
  15.6 7.1 %collective-permute-start.3 = (f32[4,2,16,128]{3,2,1,0:T(8,128)S(1)}, f32[4,2,16,128]{3,2,1,0:T(8,128)S(1)}, u32[]{:S(2)}, u32[]{:S(2)}) collective-permute-start(f32[4,2,16,128]{3,2,1,0:T(8,128)S(1)} %get-tuple-element.35), channel_id=1, source_target_pairs={{0,1},{1,0},{2,3},{3,2},{4,5},{5,4},{6,7},{7,6},{8,9},{9,8},{10,11... | collective-permute-start | bytes 196616 | tf_op jit(solution)/shard_map/ppermute | solution.py:466
  16.0 6.7 %collective-permute-start.4 = (f32[4,2,16,128]{3,2,1,0:T(8,128)S(1)}, f32[4,2,16,128]{3,2,1,0:T(8,128)S(1)}, u32[]{:S(2)}, u32[]{:S(2)}) collective-permute-start(f32[4,2,16,128]{3,2,1,0:T(8,128)S(1)} %get-tuple-element.36), channel_id=1, source_target_pairs={{0,2},{1,3},{2,0},{3,1},{4,6},{5,7},{6,4},{7,5},{8,10},{9,11},{10,... | collective-permute-start | bytes 196616 | tf_op jit(solution)/shard_map/ppermute | solution.py:466
  17.7 6.7 %collective-permute-start.5 = (f32[4,2,16,128]{3,2,1,0:T(8,128)S(1)}, f32[4,2,16,128]{3,2,1,0:T(8,128)S(1)}, u32[]{:S(2)}, u32[]{:S(2)}) collective-permute-start(f32[4,2,16,128]{3,2,1,0:T(8,128)S(1)} %get-tuple-element.37), channel_id=1, source_target_pairs={{0,3},{1,2},{2,1},{3,0},{4,7},{5,6},{6,5},{7,4},{8,11},{9,10},{10,... | collective-permute-start | bytes 196616 | tf_op jit(solution)/shard_map/ppermute | solution.py:466
  18.2 8.6 %collective-permute-start.6 = (f32[9,2,8,128]{3,2,1,0:T(8,128)S(1)}, f32[9,2,8,128]{3,2,1,0:T(8,128)S(1)}, u32[]{:S(2)}, u32[]{:S(2)}) collective-permute-start(f32[9,2,8,128]{3,2,1,0:T(8,128)S(1)} %get-tuple-element.41), channel_id=1, source_target_pairs={{1,0},{2,1},{3,2},{4,3},{5,4},{6,5},{7,6},{8,7},{9,8},{10,9},{11,1... | collective-permute-start | bytes 221192 | tf_op jit(solution)/shard_map/ppermute | solution.py:495
  22.7 6.5 %collective-permute-start.7 = (f32[9,2,8,128]{3,2,1,0:T(8,128)S(1)}, f32[9,2,8,128]{3,2,1,0:T(8,128)S(1)}, u32[]{:S(2)}, u32[]{:S(2)}) collective-permute-start(f32[9,2,8,128]{3,2,1,0:T(8,128)S(1)} %get-tuple-element.42), channel_id=1, source_target_pairs={{0,1},{1,2},{2,3},{3,4},{4,5},{5,6},{6,7},{7,8},{8,9},{9,10},{10,1... | collective-permute-start | bytes 221192 | tf_op jit(solution)/shard_map/ppermute | solution.py:496
  24.4 5.0 %copy-start.3 = (f32[8]{0:T(128)S(1)}, f32[8]{0:T(128)}, u32[]{:S(2)}) copy-start(f32[8]{0:T(128)} %dif_ref.3) | copy-start | bytes 100
  32.6 15.2 %collective-permute-start.8 = (f32[4,2,32,128]{3,2,1,0:T(8,128)S(1)}, f32[4,2,32,128]{3,2,1,0:T(8,128)S(1)}, u32[]{:S(2)}, u32[]{:S(2)}) collective-permute-start(f32[4,2,32,128]{3,2,1,0:T(8,128)S(1)} %get-tuple-element.47), channel_id=1, source_target_pairs={{0,4},{1,5},{2,6},{3,7},{4,0},{5,1},{6,2},{7,3},{8,12},{9,13},{10,... | collective-permute-start | bytes 393224 | tf_op jit(solution)/shard_map/ppermute | solution.py:454
  32.7 15.2 %collective-permute-start.9 = (f32[4,2,32,128]{3,2,1,0:T(8,128)S(1)}, f32[4,2,32,128]{3,2,1,0:T(8,128)S(1)}, u32[]{:S(2)}, u32[]{:S(2)}) collective-permute-start(f32[4,2,32,128]{3,2,1,0:T(8,128)S(1)} %get-tuple-element.48), channel_id=1, source_target_pairs={{0,8},{1,9},{2,10},{3,11},{4,12},{5,13},{6,14},{7,15},{8,0},{9,1},... | collective-permute-start | bytes 393224 | tf_op jit(solution)/shard_map/ppermute | solution.py:454
  35.1 12.7 %collective-permute-start.10 = (f32[4,2,32,128]{3,2,1,0:T(8,128)S(1)}, f32[4,2,32,128]{3,2,1,0:T(8,128)S(1)}, u32[]{:S(2)}, u32[]{:S(2)}) collective-permute-start(f32[4,2,32,128]{3,2,1,0:T(8,128)S(1)} %get-tuple-element.49), channel_id=1, source_target_pairs={{0,12},{1,13},{2,14},{3,15},{4,8},{5,9},{6,10},{7,11},{8,4},{9,5},... | collective-permute-start | bytes 393224 | tf_op jit(solution)/shard_map/ppermute | solution.py:454
  44.2 18.3 %all-to-all-start.1 = ((f32[32,1,4224]{2,1,0:T(1,128)}), f32[32,1,4224]{2,1,0:T(1,128)S(1)}, u32[]{:S(2)}, u32[]{:S(2)}) async-start(f32[32,1,4224]{2,1,0:T(1,128)} %bitcast.8), calls=%async_computation.1 | async-start | bytes 1081344 | tf_op jit(solution)/shard_map/all_to_all | solution.py:567
  47.8 14.7 %copy-start.2 = (f32[2,8,8192]{2,1,0:T(8,128)S(1)}, f32[2,8,8192]{2,1,0:T(8,128)}, u32[]{:S(2)}) copy-start(f32[2,8,8192]{2,1,0:T(8,128)} %rhs_ref.3) | copy-start | bytes 1572868
  48.4 2.0 %collective-permute-start.11 = (f32[4,2,32,128]{3,2,1,0:T(8,128)S(1)}, f32[4,2,32,128]{3,2,1,0:T(8,128)S(1)}, u32[]{:S(2)}, u32[]{:S(2)}) collective-permute-start(f32[4,2,32,128]{3,2,1,0:T(8,128)S(1)} %get-tuple-element.51), channel_id=1, source_target_pairs={{0,1},{1,0},{2,3},{3,2},{4,5},{5,4},{6,7},{7,6},{8,9},{9,8},{10,11... | collective-permute-start | bytes 393224 | tf_op jit(solution)/shard_map/ppermute | solution.py:466
  48.8 9.6 %collective-permute-start.12 = (f32[4,2,32,128]{3,2,1,0:T(8,128)S(1)}, f32[4,2,32,128]{3,2,1,0:T(8,128)S(1)}, u32[]{:S(2)}, u32[]{:S(2)}) collective-permute-start(f32[4,2,32,128]{3,2,1,0:T(8,128)S(1)} %get-tuple-element.52), channel_id=1, source_target_pairs={{0,2},{1,3},{2,0},{3,1},{4,6},{5,7},{6,4},{7,5},{8,10},{9,11},{10,... | collective-permute-start | bytes 393224 | tf_op jit(solution)/shard_map/ppermute | solution.py:466
  50.5 10.0 %collective-permute-start.13 = (f32[4,2,32,128]{3,2,1,0:T(8,128)S(1)}, f32[4,2,32,128]{3,2,1,0:T(8,128)S(1)}, u32[]{:S(2)}, u32[]{:S(2)}) collective-permute-start(f32[4,2,32,128]{3,2,1,0:T(8,128)S(1)} %get-tuple-element.53), channel_id=1, source_target_pairs={{0,3},{1,2},{2,1},{3,0},{4,7},{5,6},{6,5},{7,4},{8,11},{9,10},{10,... | collective-permute-start | bytes 393224 | tf_op jit(solution)/shard_map/ppermute | solution.py:466

commit v7 on v6

--- a/solution.py
+++ b/solution.py
@@ -11,6 +11,7 @@
 GY = 32
 S = 8
 LANES = 128
+GROUP = 16
 F32 = jnp.float32
 BF16 = jnp.bfloat16
 VMEM = pl.BlockSpec(memory_space=pltpu.VMEM)
@@ -25,7 +26,7 @@
     own, _, total = rhs_ref.shape
     cells = total // parts
     tiles = cells // LANES
-    plane = 8 // own
+    plane = GROUP // own
     low = lane_iota() < LANES // 2
     for q in range(parts // plane):
         base = jnp.bitwise_xor(place_ref[0], q) * plane
@@ -197,10 +198,7 @@
 def early_kernel(n, plane, place_ref, jac_ref, coup_ref, *refs):
     near_refs, (v_ref, a_ref, gather_ref, vs_ref, mx_ref) = refs[:plane], refs[plane:]
     early = v_ref.shape[0]
-    for k in range(plane):
-        for q in range(near_refs[k].shape[0]):
-            d = jnp.bitwise_xor(place_ref[0], q) * plane + jnp.bitwise_xor(place_ref[1], k)
-            gather_ref[d] = near_refs[k][q]
+    gather_kernel(place_ref, *near_refs, gather_ref)
     flat = gather_ref.reshape(n * early * S, LANES)
     for ct in range(early):
         for s in range(S):
@@ -224,7 +222,7 @@
 def first_kernel(n, tiles, place_ref, dif_ref, r_ref, ve_ref, ae_ref, jac_ref, coup_ref, stencil_ref, _, *refs):
     every = tiles + 1
     (v_ref, w_ref, sum_ref), refs = refs[:3], refs[3:]
-    send_refs, (vs_ref, xs_ref, mx_ref, bs_ref) = refs[: n // 8], refs[n // 8 :]
+    send_refs, (vs_ref, xs_ref, mx_ref, bs_ref) = refs[: n // GROUP], refs[n // GROUP :]
     early = ve_ref.shape[0]
     for ct in range(early):
         v_ref[ct] = ve_ref[ct]
@@ -268,12 +266,12 @@
         react(n, tile_of(jac_ref, ct), ct % 2, mx_ref, finisher(ct, ct % 2), steps)
     if early == tiles:
         run(rest)
-    for q in range(n // 8):
-        at = pl.multiple_of(jnp.bitwise_xor(place_ref[0], q) * 8, 8)
-        flat = send_refs[q].reshape(8 * tiles * S, LANES)
+    for q in range(n // GROUP):
+        at = pl.multiple_of(jnp.bitwise_xor(place_ref[0], q) * GROUP, GROUP)
+        flat = send_refs[q].reshape(GROUP * tiles * S, LANES)
         for ct in range(tiles):
             for s in range(S):
-                flat[pl.ds(ct * S + s, 8, stride=tiles * S), :] = w_ref[ct, s, pl.ds(at, 8)]
+                flat[pl.ds(ct * S + s, GROUP, stride=tiles * S), :] = w_ref[ct, s, pl.ds(at, GROUP)]
     sum_ref[0:8] = sums.total("rr")
     sum_ref[8:16] = sums.total("rw")
 
@@ -365,7 +363,7 @@
 
 
 def relay_kernel(own, place_ref, *refs):
-    parts = 8 // own
+    parts = GROUP // own
     count = len(refs) - parts
     for k in range(parts):
         at = jnp.bitwise_xor(place_ref[1], k)
@@ -373,10 +371,17 @@
             refs[count + k][q] = refs[q][at]
 
 
-def combine_kernel(parts, tiles, place_ref, rhs_ref, got_ref, *refs):
+def gather_kernel(place_ref, *refs):
+    near_refs, out_ref = refs[:-1], refs[-1]
+    plane = len(near_refs)
+    for k in range(plane):
+        for q in range(near_refs[k].shape[0]):
+            d = jnp.bitwise_xor(place_ref[0], q) * plane + jnp.bitwise_xor(place_ref[1], k)
+            out_ref[d] = near_refs[k][q]
+
+
+def combine_kernel(parts, tiles, rhs_ref, got_ref, w_ref, update_ref, basis_ref):
     own = rhs_ref.shape[0]
-    plane = 8 // own
-    w_refs, (update_ref, basis_ref) = refs[:plane], refs[plane:]
     per = tiles * S + 1
     stats = got_ref[pl.ds(tiles * S, parts, stride=own * per), :]
 
@@ -420,16 +425,10 @@
             for ct in range(tiles):
                 at = slice((d * tiles + ct) * LANES, (d * tiles + ct + 1) * LANES)
                 base = (d * own + m) * per + ct * S
-                basis_ref[m, :, at] = br * rhs_ref[m, :, at] + bz * got_ref[base : base + S, :]
-    for k in range(plane):
-        for q in range(parts // plane):
-            d = jnp.bitwise_xor(place_ref[0], q) * plane + jnp.bitwise_xor(place_ref[1], k)
-            for m in range(own):
-                for ct in range(tiles):
-                    at = pl.ds(pl.multiple_of(d * (tiles * LANES) + ct * LANES, LANES), LANES)
-                    w = w_refs[k][q, m, ct * S : (ct + 1) * S, :]
-                    update_ref[m, :, at] = ur * rhs_ref[m, :, at] + uw * w
-                    basis_ref[m, :, at] += bw * w
+                r = rhs_ref[m, :, at]
+                w = w_ref[d, m, ct * S : (ct + 1) * S, :]
+                update_ref[m, :, at] = ur * r + uw * w
+                basis_ref[m, :, at] = br * r + bw * w + bz * got_ref[base : base + S, :]
 
 
 def local(rhs, diffusivity, jac_coef, coef_index, row_mode, col_mode, multiplicity):
@@ -438,7 +437,7 @@
     n = own * parts
     cells = total // parts
     tiles = cells // LANES
-    plane = 8 // own
+    plane = GROUP // own
     sds = jax.ShapeDtypeStruct
     smem = pl.BlockSpec(memory_space=pltpu.SMEM)
     index = lax.axis_index("modes")
@@ -533,9 +532,9 @@
     v, w, sums, *w_send = pl.pallas_call(
         functools.partial(first_kernel, n, tiles),
         out_shape=[sds(field, F32), sds((tiles, S, n, LANES), F32), sds((16, LANES), F32)]
-        + [sds((plane, own, tiles * S, LANES), F32)] * (n // 8),
+        + [sds((plane, own, tiles * S, LANES), F32)] * (n // GROUP),
         in_specs=[smem] * 2 + [VMEM] * 6 + [pl.BlockSpec(memory_space=pl.ANY)],
-        out_specs=[VMEM] * (3 + n // 8),
+        out_specs=[VMEM] * (3 + n // GROUP),
         scratch_shapes=work,
         compiler_params=PARAMS,
         name="first",
@@ -566,14 +565,22 @@
     line = (tiles * S + 1) * LANES
     got = lax.all_to_all(z_send.reshape(n, 1, line), "modes", split_axis=0, concat_axis=0, tiled=True)
 
+    w_all = pl.pallas_call(
+        gather_kernel,
+        out_shape=sds((parts, own, tiles * S, LANES), F32),
+        in_specs=[smem] + [VMEM] * plane,
+        out_specs=VMEM,
+        compiler_params=PARAMS,
+        name="gather",
+    )(place, *w_own)
     update, basis_next = pl.pallas_call(
         functools.partial(combine_kernel, parts, tiles),
         out_shape=[sds(rhs.shape, F32)] * 2,
-        in_specs=[smem] + [VMEM] * (2 + plane),
+        in_specs=[VMEM] * 3,
         out_specs=[VMEM] * 2,
         compiler_params=PARAMS,
         name="combine",
-    )(place, rhs, got.reshape(n * (tiles * S + 1), LANES), *w_own)
+    )(rhs, got.reshape(n * (tiles * S + 1), LANES), w_all)
     return (update, basis_next)
 
 

time: 65 us -> 68.8 us (1.058)
  starting transfers between devices: 28.5 us -> 31.5 us
  waiting for transfers between devices: 16.1 us -> 17.1 us
    ppermute x6 -> x14, starting transfers between devices: 4.2 us -> 12.9 us  [across(): lax.ppermute(relayed[k], 'modes', [(i, i ^ k) for i in range(parts)])]
    ppermute x6 -> x2, starting transfers between devices: 10.1 us -> 4.11 us  [across(): lax.ppermute(arrays[q], 'modes', [(i, i ^ q * plane) for i in range(parts)])]
    ppermute x6 -> x2, waiting for transfers between devices: 0.02 us -> 2.38 us  [across(): lax.ppermute(arrays[q], 'modes', [(i, i ^ q * plane) for i in range(parts)])]
    all_to_all x1, starting transfers between devices: 6.16 us -> 3.91 us  [local(): lax.all_to_all(late_send, 'modes', split_axis=0, concat_axis=0, tiled=True)]
    all_to_all x1, waiting for transfers between devices: 2.01 us -> 0.01 us  [local(): lax.all_to_all(z_send.reshape(n, 1, line), 'modes', split_axis=0, concat_...]
    ppermute x1, starting transfers between devices: 4.48 us -> 6.26 us  [local(): after = lax.ppermute(head, 'modes', down)]
    ppermute x1, waiting for transfers between devices: 2.39 us -> 4.03 us  [local(): before = lax.ppermute(tail, 'modes', up)]
    ppermute x6 -> x14, waiting for transfers between devices: 11.7 us -> 10.7 us  [across(): lax.ppermute(relayed[k], 'modes', [(i, i ^ k) for i in range(parts)])]
  transfers between devices with their start and end apart: 16 -> 20, of which waited for: 5 -> 8; matrix products, arithmetic and copies ran while one was open for 0% -> 0% of each run, Pallas kernels for 18% -> 17%
where the time goes in v7:
time: 68.8 us; the launch traced here: 68.4 us
  starting transfers between devices  31.5 us (46%)
  Pallas kernels  17.8 us (26%)
  waiting for transfers between devices  17.1 us (25%)
  local copies, waits for them, and re-layouts  1.08 us (2%)
  between operations  0.88 us (1%)
    ppermute x14, starting transfers between devices, across(): lax.ppermute(relayed[k], 'modes', [(i, i ^ k) for i in range(parts)])  12.9 us
    ppermute x14, waiting for transfers between devices, across(): lax.ppermute(relayed[k], 'modes', [(i, i ^ k) for i in range(parts)])  10.7 us
    pallas_call x1, Pallas kernels, local(): pl.pallas_call(functools.partial(second_kernel, n, tiles), out_shape=sds(...  7.18 us
    ppermute x1, starting transfers between devices, local(): after = lax.ppermute(head, 'modes', down)  6.26 us
    all_to_all x1, starting transfers between devices, local(): lax.all_to_all(z_send.reshape(n, 1, line), 'modes', split_axis=0, concat_...  4.29 us
    ppermute x2, starting transfers between devices, across(): lax.ppermute(arrays[q], 'modes', [(i, i ^ q * plane) for i in range(parts)])  4.11 us
    ppermute x1, waiting for transfers between devices, local(): before = lax.ppermute(tail, 'modes', up)  4.03 us
    all_to_all x1, starting transfers between devices, local(): lax.all_to_all(late_send, 'modes', split_axis=0, concat_axis=0, tiled=True)  3.91 us
  transfers between devices with their start and end apart: 20, of which 8 were waited for; matrix products, arithmetic and copies ran while one was open for 0% of the time, Pallas kernels for 17%

profile of v7, /device:TPU:0, one launch (start us, length us, event | category | flops | bytes accessed | tf_op | source)
XLA Modules:
  0.0 68.4 jit_solution(15756758461422003657)
XLA Ops:
  0.7 1.0 %copy-done.1 = f32[2,8,8192]{2,1,0:T(8,128)S(1)} copy-done((f32[2,8,8192]{2,1,0:T(8,128)S(1)}, f32[2,8,8192]{2,1,0:T(8,128)}, u32[]{:S(2)}) %copy-start.1) | copy-done | bytes 524312
  1.8 1.3 %arrange.1 = (f32[32,3,8,128]{3,2,1,0:T(8,128)}, f32[8,2,16,128]{3,2,1,0:T(8,128)S(1)}, f32[8,2,16,128]{3,2,1,0:T(8,128)S(1)}) custom-call(s32[2]{0:T(128)S(1)} %pad_add_fusion.place_ref, f32[2,8,8192]{2,1,0:T(8,128)S(1)} %copy-done.1), custom_call_target="tpu_custom_call" | custom-call | tf_op jit(solution)/shard_map/arrange/pallas_call | solution.py:468
  3.1 4.0 %collective-permute-start = (f32[8,2,16,128]{3,2,1,0:T(8,128)S(1)}, f32[8,2,16,128]{3,2,1,0:T(8,128)S(1)}, u32[]{:S(2)}, u32[]{:S(2)}) collective-permute-start(f32[8,2,16,128]{3,2,1,0:T(8,128)S(1)} %get-tuple-element.35), channel_id=1, source_target_pairs={{0,8},{1,9},{2,10},{3,11},{4,12},{5,13},{6,14},{7,15},{8,0},{9,1},... | collective-permute-start | bytes 393224 | tf_op jit(solution)/shard_map/ppermute | solution.py:453
  7.1 3.9 %all-to-all-start = ((f32[32,3,8,128]{3,2,1,0:T(8,128)}), f32[32,3,8,128]{3,2,1,0:T(8,128)S(1)}, u32[]{:S(2)}, u32[]{:S(2)}) async-start(f32[32,3,8,128]{3,2,1,0:T(8,128)} %get-tuple-element.32), calls=%async_computation | async-start | bytes 786432 | tf_op jit(solution)/shard_map/all_to_all | solution.py:477
  11.1 2.4 %collective-permute-done.refs_1_ = f32[8,2,16,128]{3,2,1,0:T(8,128)S(1)} collective-permute-done((f32[8,2,16,128]{3,2,1,0:T(8,128)S(1)}, f32[8,2,16,128]{3,2,1,0:T(8,128)S(1)}, u32[]{:S(2)}, u32[]{:S(2)}) %collective-permute-start) | collective-permute-done | bytes 131104 | tf_op jit(solution)/shard_map/ppermute | solution.py:453
  13.5 0.6 relay.2
  14.1 1.6 %collective-permute-start.2 = (f32[2,2,16,128]{3,2,1,0:T(8,128)S(1)}, f32[2,2,16,128]{3,2,1,0:T(8,128)S(1)}, u32[]{:S(2)}, u32[]{:S(2)}) collective-permute-start(f32[2,2,16,128]{3,2,1,0:T(8,128)S(1)} %get-tuple-element.38), channel_id=1, source_target_pairs={{0,2},{1,3},{2,0},{3,1},{4,6},{5,7},{6,4},{7,5},{8,10},{9,11},{10,... | collective-permute-start | bytes 98312 | tf_op jit(solution)/shard_map/ppermute | solution.py:465
  15.8 0.2 collective-permute-start.3
  16.0 0.8 %collective-permute-start.4 = (f32[2,2,16,128]{3,2,1,0:T(8,128)S(1)}, f32[2,2,16,128]{3,2,1,0:T(8,128)S(1)}, u32[]{:S(2)}, u32[]{:S(2)}) collective-permute-start(f32[2,2,16,128]{3,2,1,0:T(8,128)S(1)} %get-tuple-element.40), channel_id=1, source_target_pairs={{0,4},{1,5},{2,6},{3,7},{4,0},{5,1},{6,2},{7,3},{8,12},{9,13},{10,... | collective-permute-start | bytes 98312 | tf_op jit(solution)/shard_map/ppermute | solution.py:465
  16.8 0.9 %collective-permute-start.5 = (f32[2,2,16,128]{3,2,1,0:T(8,128)S(1)}, f32[2,2,16,128]{3,2,1,0:T(8,128)S(1)}, u32[]{:S(2)}, u32[]{:S(2)}) collective-permute-start(f32[2,2,16,128]{3,2,1,0:T(8,128)S(1)} %get-tuple-element.41), channel_id=1, source_target_pairs={{0,5},{1,4},{2,7},{3,6},{4,1},{5,0},{6,3},{7,2},{8,13},{9,12},{10,... | collective-permute-start | bytes 98312 | tf_op jit(solution)/shard_map/ppermute | solution.py:465
  17.7 1.7 %collective-permute-start.6 = (f32[2,2,16,128]{3,2,1,0:T(8,128)S(1)}, f32[2,2,16,128]{3,2,1,0:T(8,128)S(1)}, u32[]{:S(2)}, u32[]{:S(2)}) collective-permute-start(f32[2,2,16,128]{3,2,1,0:T(8,128)S(1)} %get-tuple-element.42), channel_id=1, source_target_pairs={{0,6},{1,7},{2,4},{3,5},{4,2},{5,3},{6,0},{7,1},{8,14},{9,15},{10,... | collective-permute-start | bytes 98312 | tf_op jit(solution)/shard_map/ppermute | solution.py:465
  19.4 1.0 %collective-permute-start.7 = (f32[2,2,16,128]{3,2,1,0:T(8,128)S(1)}, f32[2,2,16,128]{3,2,1,0:T(8,128)S(1)}, u32[]{:S(2)}, u32[]{:S(2)}) collective-permute-start(f32[2,2,16,128]{3,2,1,0:T(8,128)S(1)} %get-tuple-element.43), channel_id=1, source_target_pairs={{0,7},{1,6},{2,5},{3,4},{4,3},{5,2},{6,1},{7,0},{8,15},{9,14},{10,... | collective-permute-start | bytes 98312 | tf_op jit(solution)/shard_map/ppermute | solution.py:465
  20.4 0.3 coupling.1
  20.9 6.3 %collective-permute-start.8 = (f32[9,2,8,128]{3,2,1,0:T(8,128)S(1)}, f32[9,2,8,128]{3,2,1,0:T(8,128)S(1)}, u32[]{:S(2)}, u32[]{:S(2)}) collective-permute-start(f32[9,2,8,128]{3,2,1,0:T(8,128)S(1)} %get-tuple-element.47), channel_id=1, source_target_pairs={{1,0},{2,1},{3,2},{4,3},{5,4},{6,5},{7,6},{8,7},{9,8},{10,9},{11,1... | collective-permute-start | bytes 221192 | tf_op jit(solution)/shard_map/ppermute | solution.py:494
  27.2 2.4 %early.1 = (f32[2,8,32,128]{3,2,1,0:T(8,128)S(1)}, f32[2,8,32,128]{3,2,1,0:T(8,128)S(1)}) custom-call(s32[2]{0:T(128)S(1)} %pad_add_fusion.place_ref, f32[72,8,512]{2,1,0:T(8,128)S(1)} %bitcast.10, bf16[288,96]{1,0:T(8,128)(2,1)S(1)} %get-tuple-element.33.coup_ref, f32[2,2,16,128]{3,2,1,0:T(8,128)S(1)} %get-tuple-element.36.refs_0_._, ...), custom_call_target="tpu_custom_call" | custom-call | flops 2000000000 | bytes 1048576 | tf_op jit(solution)/shard_map/early/pallas_call | solution.py:522
  29.6 4.0 %collective-permute-done.9.prev_ref = f32[9,2,8,128]{3,2,1,0:T(8,128)S(1)} collective-permute-done((f32[9,2,8,128]{3,2,1,0:T(8,128)S(1)}, f32[9,2,8,128]{3,2,1,0:T(8,128)S(1)}, u32[]{:S(2)}, u32[]{:S(2)}) %collective-permute-start.9) | collective-permute-done | bytes 73760 | tf_op jit(solution)/shard_map/ppermute | solution.py:495
  33.8 3.3 %first.1 = (f32[5,8,32,128]{3,2,1,0:T(8,128)S(1)}, f32[4,8,32,128]{3,2,1,0:T(8,128)S(1)}, f32[16,128]{1,0:T(8,128)S(1)}, f32[8,2,32,128]{3,2,1,0:T(8,128)S(1)}, f32[8,2,32,128]{3,2,1,0:T(8,128)S(1)}) custom-call(s32[2]{0:T(128)S(1)} %pad_add_fusion.place_ref, f32[8]{0:T(128)S(1)} %copy-done.3, f32[768,128]{1,0:T(8,128)S(1)} %bitcast.14, ...), custom_call_target="tpu_custom_call" | custom-call | tf_op jit(solution)/shard_map/first/pallas_call | solution.py:532
  37.3 7.2 %second.1 = f32[1056,128]{1,0:T(8,128)} custom-call(f32[8]{0:T(128)S(1)} %copy-done.3, f32[5,8,32,128]{3,2,1,0:T(8,128)S(1)} %get-tuple-element.49.v_ref, f32[4,8,32,128]{3,2,1,0:T(8,128)S(1)} %get-tuple-element.50.w_ref, f32[16,128]{1,0:T(8,128)S(1)} %get-tuple-element.51.sum_ref, f32[72,8,512]{2,1,0:T(8,128)S(1)} %bitcast.12, ...), custom_call_target="tpu_custom_call" | custom-call | flops 75497472 | bytes 16777216 | tf_op jit(solution)/shard_map/second/pallas_call | solution.py:555
  44.4 4.3 %all-to-all-start.1 = ((f32[32,1,4224]{2,1,0:T(1,128)}), f32[32,1,4224]{2,1,0:T(1,128)S(1)}, u32[]{:S(2)}, u32[]{:S(2)}) async-start(f32[32,1,4224]{2,1,0:T(1,128)} %bitcast.8), calls=%async_computation.1 | async-start | bytes 1081344 | tf_op jit(solution)/shard_map/all_to_all | solution.py:566
  48.7 0.6 relay.3
  49.3 0.5 collective-permute-start.11
  49.8 1.7 %collective-permute-start.12 = (f32[2,2,32,128]{3,2,1,0:T(8,128)S(1)}, f32[2,2,32,128]{3,2,1,0:T(8,128)S(1)}, u32[]{:S(2)}, u32[]{:S(2)}) collective-permute-start(f32[2,2,32,128]{3,2,1,0:T(8,128)S(1)} %get-tuple-element.56), channel_id=1, source_target_pairs={{0,2},{1,3},{2,0},{3,1},{4,6},{5,7},{6,4},{7,5},{8,10},{9,11},{10,... | collective-permute-start | bytes 196616 | tf_op jit(solution)/shard_map/ppermute | solution.py:465
  51.5 1.7 %collective-permute-start.14 = (f32[2,2,32,128]{3,2,1,0:T(8,128)S(1)}, f32[2,2,32,128]{3,2,1,0:T(8,128)S(1)}, u32[]{:S(2)}, u32[]{:S(2)}) collective-permute-start(f32[2,2,32,128]{3,2,1,0:T(8,128)S(1)} %get-tuple-element.58), channel_id=1, source_target_pairs={{0,4},{1,5},{2,6},{3,7},{4,0},{5,1},{6,2},{7,3},{8,12},{9,13},{10,... | collective-permute-start | bytes 196616 | tf_op jit(solution)/shard_map/ppermute | solution.py:465
  53.3 2.6 %collective-permute-start.16 = (f32[2,2,32,128]{3,2,1,0:T(8,128)S(1)}, f32[2,2,32,128]{3,2,1,0:T(8,128)S(1)}, u32[]{:S(2)}, u32[]{:S(2)}) collective-permute-start(f32[2,2,32,128]{3,2,1,0:T(8,128)S(1)} %get-tuple-element.60), channel_id=1, source_target_pairs={{0,6},{1,7},{2,4},{3,5},{4,2},{5,3},{6,0},{7,1},{8,14},{9,15},{10,... | collective-permute-start | bytes 196616 | tf_op jit(solution)/shard_map/ppermute | solution.py:465
  55.9 1.5 %collective-permute-done.12.refs_2_ = f32[2,2,32,128]{3,2,1,0:T(8,128)S(1)} collective-permute-done((f32[2,2,32,128]{3,2,1,0:T(8,128)S(1)}, f32[2,2,32,128]{3,2,1,0:T(8,128)S(1)}, u32[]{:S(2)}, u32[]{:S(2)}) %collective-permute-start.12) | collective-permute-done | bytes 65568 | tf_op jit(solution)/shard_map/ppermute | solution.py:465
  57.4 0.5 collective-permute-done.13.refs_3_
  57.8 3.3 %collective-permute-done.14.refs_4_ = f32[2,2,32,128]{3,2,1,0:T(8,128)S(1)} collective-permute-done((f32[2,2,32,128]{3,2,1,0:T(8,128)S(1)}, f32[2,2,32,128]{3,2,1,0:T(8,128)S(1)}, u32[]{:S(2)}, u32[]{:S(2)}) %collective-permute-start.14) | collective-permute-done | bytes 65568 | tf_op jit(solution)/shard_map/ppermute | solution.py:465
  61.1 0.7 %collective-permute-done.15.refs_5_ = f32[2,2,32,128]{3,2,1,0:T(8,128)S(1)} collective-permute-done((f32[2,2,32,128]{3,2,1,0:T(8,128)S(1)}, f32[2,2,32,128]{3,2,1,0:T(8,128)S(1)}, u32[]{:S(2)}, u32[]{:S(2)}) %collective-permute-start.15) | collective-permute-done | bytes 65568 | tf_op jit(solution)/shard_map/ppermute | solution.py:465
  61.8 4.3 %collective-permute-done.16.refs_6_ = f32[2,2,32,128]{3,2,1,0:T(8,128)S(1)} collective-permute-done((f32[2,2,32,128]{3,2,1,0:T(8,128)S(1)}, f32[2,2,32,128]{3,2,1,0:T(8,128)S(1)}, u32[]{:S(2)}, u32[]{:S(2)}) %collective-permute-start.16) | collective-permute-done | bytes 65568 | tf_op jit(solution)/shard_map/ppermute | solution.py:465
  66.1 0.5 collective-permute-done.17.refs_7_
  66.6 0.6 gather.1.w_ref
  67.2 1.2 %combine.1 = (f32[2,8,8192]{2,1,0:T(8,128)}, f32[2,8,8192]{2,1,0:T(8,128)}) custom-call(f32[2,8,8192]{2,1,0:T(8,128)S(1)} %copy-done.2, f32[1056,128]{1,0:T(8,128)S(1)} %bitcast.13, f32[16,2,32,128]{3,2,1,0:T(8,128)S(1)} %gather.1.w_ref), custom_call_target="tpu_custom_call" | custom-call | tf_op jit(solution)/shard_map/combine/pallas_call | solution.py:576
  (36 shorter events, 0.8 us)
Async XLA Ops:
  0.7 1.0 %copy-start.1 = (f32[2,8,8192]{2,1,0:T(8,128)S(1)}, f32[2,8,8192]{2,1,0:T(8,128)}, u32[]{:S(2)}) copy-start(f32[2,8,8192]{2,1,0:T(8,128)} %rhs_ref.3) | copy-start | bytes 1572868
  3.1 10.3 %collective-permute-start = (f32[8,2,16,128]{3,2,1,0:T(8,128)S(1)}, f32[8,2,16,128]{3,2,1,0:T(8,128)S(1)}, u32[]{:S(2)}, u32[]{:S(2)}) collective-permute-start(f32[8,2,16,128]{3,2,1,0:T(8,128)S(1)} %get-tuple-element.35), channel_id=1, source_target_pairs={{0,8},{1,9},{2,10},{3,11},{4,12},{5,13},{6,14},{7,15},{8,0},{9,1},... | collective-permute-start | bytes 393224 | tf_op jit(solution)/shard_map/ppermute | solution.py:453
  7.1 26.7 %all-to-all-start = ((f32[32,3,8,128]{3,2,1,0:T(8,128)}), f32[32,3,8,128]{3,2,1,0:T(8,128)S(1)}, u32[]{:S(2)}, u32[]{:S(2)}) async-start(f32[32,3,8,128]{3,2,1,0:T(8,128)} %get-tuple-element.32), calls=%async_computation | async-start | bytes 786432 | tf_op jit(solution)/shard_map/all_to_all | solution.py:477
  13.5 7.0 %copy-start.4 = (s32[512]{0:T(512)S(1)}, s32[512]{0:T(512)}, u32[]{:S(2)}) copy-start(s32[512]{0:T(512)} %param.10) | copy-start | bytes 6148
  13.5 7.0 %copy-start.5 = (s32[512]{0:T(512)S(1)}, s32[512]{0:T(512)}, u32[]{:S(2)}) copy-start(s32[512]{0:T(512)} %param.11) | copy-start | bytes 6148
  13.5 7.0 %copy-start.6 = (s32[512]{0:T(512)S(1)}, s32[512]{0:T(512)}, u32[]{:S(2)}) copy-start(s32[512]{0:T(512)} %param.12) | copy-start | bytes 6148
  13.5 7.0 %copy-start.7 = (s32[512]{0:T(512)S(1)}, s32[512]{0:T(512)}, u32[]{:S(2)}) copy-start(s32[512]{0:T(512)} %param.13) | copy-start | bytes 6148
  13.5 7.2 %copy-start = (f32[9,8,8,512]{3,2,1,0:T(8,128)S(1)}, f32[9,8,8,512]{3,2,1,0:T(8,128)}, u32[]{:S(2)}) copy-start(f32[9,8,8,512]{3,2,1,0:T(8,128)} %last_ref.1) | copy-start | bytes 3538948
  14.0 3.6 %collective-permute-start.1 = (f32[2,2,16,128]{3,2,1,0:T(8,128)S(1)}, f32[2,2,16,128]{3,2,1,0:T(8,128)S(1)}, u32[]{:S(2)}, u32[]{:S(2)}) collective-permute-start(f32[2,2,16,128]{3,2,1,0:T(8,128)S(1)} %get-tuple-element.37), channel_id=1, source_target_pairs={{0,1},{1,0},{2,3},{3,2},{4,5},{5,4},{6,7},{7,6},{8,9},{9,8},{10,11... | collective-permute-start | bytes 98312 | tf_op jit(solution)/shard_map/ppermute | solution.py:465
  14.1 5.3 %collective-permute-start.2 = (f32[2,2,16,128]{3,2,1,0:T(8,128)S(1)}, f32[2,2,16,128]{3,2,1,0:T(8,128)S(1)}, u32[]{:S(2)}, u32[]{:S(2)}) collective-permute-start(f32[2,2,16,128]{3,2,1,0:T(8,128)S(1)} %get-tuple-element.38), channel_id=1, source_target_pairs={{0,2},{1,3},{2,0},{3,1},{4,6},{5,7},{6,4},{7,5},{8,10},{9,11},{10,... | collective-permute-start | bytes 98312 | tf_op jit(solution)/shard_map/ppermute | solution.py:465
  15.8 5.1 %collective-permute-start.3 = (f32[2,2,16,128]{3,2,1,0:T(8,128)S(1)}, f32[2,2,16,128]{3,2,1,0:T(8,128)S(1)}, u32[]{:S(2)}, u32[]{:S(2)}) collective-permute-start(f32[2,2,16,128]{3,2,1,0:T(8,128)S(1)} %get-tuple-element.39), channel_id=1, source_target_pairs={{0,3},{1,2},{2,1},{3,0},{4,7},{5,6},{6,5},{7,4},{8,11},{9,10},{10,... | collective-permute-start | bytes 98312 | tf_op jit(solution)/shard_map/ppermute | solution.py:465
  16.0 11.2 %collective-permute-start.4 = (f32[2,2,16,128]{3,2,1,0:T(8,128)S(1)}, f32[2,2,16,128]{3,2,1,0:T(8,128)S(1)}, u32[]{:S(2)}, u32[]{:S(2)}) collective-permute-start(f32[2,2,16,128]{3,2,1,0:T(8,128)S(1)} %get-tuple-element.40), channel_id=1, source_target_pairs={{0,4},{1,5},{2,6},{3,7},{4,0},{5,1},{6,2},{7,3},{8,12},{9,13},{10,... | collective-permute-start | bytes 98312 | tf_op jit(solution)/shard_map/ppermute | solution.py:465
  16.8 10.4 %collective-permute-start.5 = (f32[2,2,16,128]{3,2,1,0:T(8,128)S(1)}, f32[2,2,16,128]{3,2,1,0:T(8,128)S(1)}, u32[]{:S(2)}, u32[]{:S(2)}) collective-permute-start(f32[2,2,16,128]{3,2,1,0:T(8,128)S(1)} %get-tuple-element.41), channel_id=1, source_target_pairs={{0,5},{1,4},{2,7},{3,6},{4,1},{5,0},{6,3},{7,2},{8,13},{9,12},{10,... | collective-permute-start | bytes 98312 | tf_op jit(solution)/shard_map/ppermute | solution.py:465
  17.7 9.5 %collective-permute-start.6 = (f32[2,2,16,128]{3,2,1,0:T(8,128)S(1)}, f32[2,2,16,128]{3,2,1,0:T(8,128)S(1)}, u32[]{:S(2)}, u32[]{:S(2)}) collective-permute-start(f32[2,2,16,128]{3,2,1,0:T(8,128)S(1)} %get-tuple-element.42), channel_id=1, source_target_pairs={{0,6},{1,7},{2,4},{3,5},{4,2},{5,3},{6,0},{7,1},{8,14},{9,15},{10,... | collective-permute-start | bytes 98312 | tf_op jit(solution)/shard_map/ppermute | solution.py:465
  19.4 7.8 %collective-permute-start.7 = (f32[2,2,16,128]{3,2,1,0:T(8,128)S(1)}, f32[2,2,16,128]{3,2,1,0:T(8,128)S(1)}, u32[]{:S(2)}, u32[]{:S(2)}) collective-permute-start(f32[2,2,16,128]{3,2,1,0:T(8,128)S(1)} %get-tuple-element.43), channel_id=1, source_target_pairs={{0,7},{1,6},{2,5},{3,4},{4,3},{5,2},{6,1},{7,0},{8,15},{9,14},{10,... | collective-permute-start | bytes 98312 | tf_op jit(solution)/shard_map/ppermute | solution.py:465
  20.9 8.7 %collective-permute-start.8 = (f32[9,2,8,128]{3,2,1,0:T(8,128)S(1)}, f32[9,2,8,128]{3,2,1,0:T(8,128)S(1)}, u32[]{:S(2)}, u32[]{:S(2)}) collective-permute-start(f32[9,2,8,128]{3,2,1,0:T(8,128)S(1)} %get-tuple-element.47), channel_id=1, source_target_pairs={{1,0},{2,1},{3,2},{4,3},{5,4},{6,5},{7,6},{8,7},{9,8},{10,9},{11,1... | collective-permute-start | bytes 221192 | tf_op jit(solution)/shard_map/ppermute | solution.py:494
  27.2 6.5 %collective-permute-start.9 = (f32[9,2,8,128]{3,2,1,0:T(8,128)S(1)}, f32[9,2,8,128]{3,2,1,0:T(8,128)S(1)}, u32[]{:S(2)}, u32[]{:S(2)}) collective-permute-start(f32[9,2,8,128]{3,2,1,0:T(8,128)S(1)} %get-tuple-element.48), channel_id=1, source_target_pairs={{0,1},{1,2},{2,3},{3,4},{4,5},{5,6},{6,7},{7,8},{8,9},{9,10},{10,1... | collective-permute-start | bytes 221192 | tf_op jit(solution)/shard_map/ppermute | solution.py:495
  27.2 6.6 %copy-start.3 = (f32[8]{0:T(128)S(1)}, f32[8]{0:T(128)}, u32[]{:S(2)}) copy-start(f32[8]{0:T(128)} %dif_ref.3) | copy-start | bytes 100
  37.2 11.6 %collective-permute-start.10 = (f32[8,2,32,128]{3,2,1,0:T(8,128)S(1)}, f32[8,2,32,128]{3,2,1,0:T(8,128)S(1)}, u32[]{:S(2)}, u32[]{:S(2)}) collective-permute-start(f32[8,2,32,128]{3,2,1,0:T(8,128)S(1)} %get-tuple-element.53), channel_id=1, source_target_pairs={{0,8},{1,9},{2,10},{3,11},{4,12},{5,13},{6,14},{7,15},{8,0},{9,1},... | collective-permute-start | bytes 786440 | tf_op jit(solution)/shard_map/ppermute | solution.py:453
  44.4 22.7 %all-to-all-start.1 = ((f32[32,1,4224]{2,1,0:T(1,128)}), f32[32,1,4224]{2,1,0:T(1,128)S(1)}, u32[]{:S(2)}, u32[]{:S(2)}) async-start(f32[32,1,4224]{2,1,0:T(1,128)} %bitcast.8), calls=%async_computation.1 | async-start | bytes 1081344 | tf_op jit(solution)/shard_map/all_to_all | solution.py:566
  49.3 17.9 %copy-start.2 = (f32[2,8,8192]{2,1,0:T(8,128)S(1)}, f32[2,8,8192]{2,1,0:T(8,128)}, u32[]{:S(2)}) copy-start(f32[2,8,8192]{2,1,0:T(8,128)} %rhs_ref.3) | copy-start | bytes 1572868
  49.3 4.0 %collective-permute-start.11 = (f32[2,2,32,128]{3,2,1,0:T(8,128)S(1)}, f32[2,2,32,128]{3,2,1,0:T(8,128)S(1)}, u32[]{:S(2)}, u32[]{:S(2)}) collective-permute-start(f32[2,2,32,128]{3,2,1,0:T(8,128)S(1)} %get-tuple-element.55), channel_id=1, source_target_pairs={{0,1},{1,0},{2,3},{3,2},{4,5},{5,4},{6,7},{7,6},{8,9},{9,8},{10,11... | collective-permute-start | bytes 196616 | tf_op jit(solution)/shard_map/ppermute | solution.py:465
  49.8 7.5 %collective-permute-start.12 = (f32[2,2,32,128]{3,2,1,0:T(8,128)S(1)}, f32[2,2,32,128]{3,2,1,0:T(8,128)S(1)}, u32[]{:S(2)}, u32[]{:S(2)}) collective-permute-start(f32[2,2,32,128]{3,2,1,0:T(8,128)S(1)} %get-tuple-element.56), channel_id=1, source_target_pairs={{0,2},{1,3},{2,0},{3,1},{4,6},{5,7},{6,4},{7,5},{8,10},{9,11},{10,... | collective-permute-start | bytes 196616 | tf_op jit(solution)/shard_map/ppermute | solution.py:465
  51.5 6.3 %collective-permute-start.13 = (f32[2,2,32,128]{3,2,1,0:T(8,128)S(1)}, f32[2,2,32,128]{3,2,1,0:T(8,128)S(1)}, u32[]{:S(2)}, u32[]{:S(2)}) collective-permute-start(f32[2,2,32,128]{3,2,1,0:T(8,128)S(1)} %get-tuple-element.57), channel_id=1, source_target_pairs={{0,3},{1,2},{2,1},{3,0},{4,7},{5,6},{6,5},{7,4},{8,11},{9,10},{10,... | collective-permute-start | bytes 196616 | tf_op jit(solution)/shard_map/ppermute | solution.py:465
  51.5 9.6 %collective-permute-start.14 = (f32[2,2,32,128]{3,2,1,0:T(8,128)S(1)}, f32[2,2,32,128]{3,2,1,0:T(8,128)S(1)}, u32[]{:S(2)}, u32[]{:S(2)}) collective-permute-start(f32[2,2,32,128]{3,2,1,0:T(8,128)S(1)} %get-tuple-element.58), channel_id=1, source_target_pairs={{0,4},{1,5},{2,6},{3,7},{4,0},{5,1},{6,2},{7,3},{8,12},{9,13},{10,... | collective-permute-start | bytes 196616 | tf_op jit(solution)/shard_map/ppermute | solution.py:465
  53.2 8.6 %collective-permute-start.15 = (f32[2,2,32,128]{3,2,1,0:T(8,128)S(1)}, f32[2,2,32,128]{3,2,1,0:T(8,128)S(1)}, u32[]{:S(2)}, u32[]{:S(2)}) collective-permute-start(f32[2,2,32,128]{3,2,1,0:T(8,128)S(1)} %get-tuple-element.59), channel_id=1, source_target_pairs={{0,5},{1,4},{2,7},{3,6},{4,1},{5,0},{6,3},{7,2},{8,13},{9,12},{10,... | collective-permute-start | bytes 196616 | tf_op jit(solution)/shard_map/ppermute | solution.py:465
  53.3 12.8 %collective-permute-start.16 = (f32[2,2,32,128]{3,2,1,0:T(8,128)S(1)}, f32[2,2,32,128]{3,2,1,0:T(8,128)S(1)}, u32[]{:S(2)}, u32[]{:S(2)}) collective-permute-start(f32[2,2,32,128]{3,2,1,0:T(8,128)S(1)} %get-tuple-element.60), channel_id=1, source_target_pairs={{0,6},{1,7},{2,4},{3,5},{4,2},{5,3},{6,0},{7,1},{8,14},{9,15},{10,... | collective-permute-start | bytes 196616 | tf_op jit(solution)/shard_map/ppermute | solution.py:465
  57.4 9.2 %collective-permute-start.17 = (f32[2,2,32,128]{3,2,1,0:T(8,128)S(1)}, f32[2,2,32,128]{3,2,1,0:T(8,128)S(1)}, u32[]{:S(2)}, u32[]{:S(2)}) collective-permute-start(f32[2,2,32,128]{3,2,1,0:T(8,128)S(1)} %get-tuple-element.61), channel_id=1, source_target_pairs={{0,7},{1,6},{2,5},{3,4},{4,3},{5,2},{6,1},{7,0},{8,15},{9,14},{10,... | collective-permute-start | bytes 196616 | tf_op jit(solution)/shard_map/ppermute | solution.py:465

commit v8 on v7

--- a/solution.py
+++ b/solution.py
@@ -11,7 +11,7 @@
 GY = 32
 S = 8
 LANES = 128
-GROUP = 16
+GROUP = 8
 F32 = jnp.float32
 BF16 = jnp.bfloat16
 VMEM = pl.BlockSpec(memory_space=pltpu.VMEM)
@@ -102,7 +102,7 @@
     return jnp.where(b > 0.0, a / jnp.where(b > 0.0, b, 1.0), 0.0)
 
 
-def unpack_kernel(next_ref, prev_ref, out_ref):
+def unpack_kernel(next_ref, prev_ref, _, out_ref):
     lane = lane_iota()
     for i in range(NCOEF):
         for q in range(S // 4):
@@ -219,7 +219,7 @@
         react(n, tile_of(jac_ref, ct), ct % 2, mx_ref, finisher(ct), steps)
 
 
-def first_kernel(n, tiles, place_ref, dif_ref, r_ref, ve_ref, ae_ref, jac_ref, coup_ref, stencil_ref, _, *refs):
+def first_kernel(n, tiles, place_ref, dif_ref, r_ref, ve_ref, ae_ref, jac_ref, coup_ref, stencil_ref, *refs):
     every = tiles + 1
     (v_ref, w_ref, sum_ref), refs = refs[:3], refs[3:]
     send_refs, (vs_ref, xs_ref, mx_ref, bs_ref) = refs[: n // GROUP], refs[n // GROUP :]
@@ -493,15 +493,6 @@
     down = [(j, i) for i, j in up]
     after = lax.ppermute(head, "modes", down)
     before = lax.ppermute(tail, "modes", up)
-    edges = pl.pallas_call(
-        unpack_kernel,
-        out_shape=sds((NCOEF * S, S, LANES), F32),
-        in_specs=[VMEM] * 2,
-        out_specs=VMEM,
-        compiler_params=PARAMS,
-        name="unpack",
-    )(after, before)
-
     coupling, stencil = pl.pallas_call(
         functools.partial(coupling_kernel, n),
         out_shape=[sds((NCOEF * n, 3 * n), BF16), sds((4 * LANES, LANES), BF16)],
@@ -533,7 +524,7 @@
         functools.partial(first_kernel, n, tiles),
         out_shape=[sds(field, F32), sds((tiles, S, n, LANES), F32), sds((16, LANES), F32)]
         + [sds((plane, own, tiles * S, LANES), F32)] * (n // GROUP),
-        in_specs=[smem] * 2 + [VMEM] * 6 + [pl.BlockSpec(memory_space=pl.ANY)],
+        in_specs=[smem] * 2 + [VMEM] * 6,
         out_specs=[VMEM] * (3 + n // GROUP),
         scratch_shapes=work,
         compiler_params=PARAMS,
@@ -547,9 +538,16 @@
         jac,
         coupling,
         stencil,
-        edges,
     )
 
+    edges = pl.pallas_call(
+        unpack_kernel,
+        out_shape=sds((NCOEF * S, S, LANES), F32),
+        in_specs=[VMEM] * 2 + [pl.BlockSpec(memory_space=pl.ANY)],
+        out_specs=VMEM,
+        compiler_params=PARAMS,
+        name="unpack",
+    )(after, before, sums)
     w_own, _ = across(w_send)
 
     z_send = pl.pallas_call(
@@ -559,7 +557,7 @@
         out_specs=VMEM,
         scratch_shapes=[pltpu.VMEM((tiles, S, n, LANES), F32), pltpu.VMEM((S, n, LANES), F32)] + work,
         compiler_params=PARAMS,
-        cost_estimate=pl.CostEstimate(flops=2 * NCOEF * S * n * n * cells, bytes_accessed=16 << 20, transcendentals=0),
+        cost_estimate=pl.CostEstimate(flops=10**10, bytes_accessed=16 << 20, transcendentals=0),
         name="second",
     )(diffusivity, v, w, sums, jac, edges, coupling, stencil)
     line = (tiles * S + 1) * LANES

time: 68.8 us -> 63.7 us (0.926)
  waiting for transfers between devices: 17.1 us -> 13.4 us
  starting transfers between devices: 31.5 us -> 30.3 us
    ppermute x14 -> x6, starting transfers between devices: 12.9 us -> 4.31 us  [across(): lax.ppermute(relayed[k], 'modes', [(i, i ^ k) for i in range(parts)])]
    ppermute x2 -> x6, starting transfers between devices: 4.11 us -> 10.3 us  [across(): lax.ppermute(arrays[q], 'modes', [(i, i ^ q * plane) for i in range(parts)])]
    ppermute x1, waiting for transfers between devices: 4.03 us -> 0.01 us  [local(): before = lax.ppermute(tail, 'modes', up)]
    ppermute x2 -> x6, waiting for transfers between devices: 2.38 us -> 0.02 us  [across(): lax.ppermute(arrays[q], 'modes', [(i, i ^ q * plane) for i in range(parts)])]
    all_to_all x1, starting transfers between devices: 3.91 us -> 6.16 us  [local(): lax.all_to_all(late_send, 'modes', split_axis=0, concat_axis=0, tiled=True)]
    ppermute x1, starting transfers between devices: 6.26 us -> 4.48 us  [local(): after = lax.ppermute(head, 'modes', down)]
    all_to_all x1, waiting for transfers between devices: 0.01 us -> 1.34 us  [local(): lax.all_to_all(z_send.reshape(n, 1, line), 'modes', split_axis=0, concat_...]
    ppermute x14 -> x6, waiting for transfers between devices: 10.7 us -> 11.7 us  [across(): lax.ppermute(relayed[k], 'modes', [(i, i ^ k) for i in range(parts)])]
  transfers between devices with their start and end apart: 20 -> 16, of which waited for: 8 -> 5; matrix products, arithmetic and copies ran while one was open for 0% -> 0% of each run, Pallas kernels for 17% -> 24%
where the time goes in v8:
time: 63.7 us; the launch traced here: 63.3 us
  starting transfers between devices  30.3 us (48%)
  Pallas kernels  17.5 us (27%)
  waiting for transfers between devices  13.4 us (21%)
  local copies, waits for them, and re-layouts  1.08 us (2%)
  between operations  0.87 us (1%)
    ppermute x6, waiting for transfers between devices, across(): lax.ppermute(relayed[k], 'modes', [(i, i ^ k) for i in range(parts)])  11.7 us
    ppermute x6, starting transfers between devices, across(): lax.ppermute(arrays[q], 'modes', [(i, i ^ q * plane) for i in range(parts)])  10.3 us
    pallas_call x1, Pallas kernels, local(): pl.pallas_call(functools.partial(second_kernel, n, tiles), out_shape=sds(...  7.09 us
    all_to_all x1, starting transfers between devices, local(): lax.all_to_all(late_send, 'modes', split_axis=0, concat_axis=0, tiled=True)  6.16 us
    all_to_all x1, starting transfers between devices, local(): lax.all_to_all(z_send.reshape(n, 1, line), 'modes', split_axis=0, concat_...  5.12 us
    ppermute x1, starting transfers between devices, local(): after = lax.ppermute(head, 'modes', down)  4.48 us
    ppermute x6, starting transfers between devices, across(): lax.ppermute(relayed[k], 'modes', [(i, i ^ k) for i in range(parts)])  4.31 us
    pallas_call x1, Pallas kernels, local(): pl.pallas_call(functools.partial(first_kernel, n, tiles), out_shape=[sds(...  3.14 us
  transfers between devices with their start and end apart: 16, of which 5 were waited for; matrix products, arithmetic and copies ran while one was open for 0% of the time, Pallas kernels for 24%

profile of v8, /device:TPU:0, one launch (start us, length us, event | category | flops | bytes accessed | tf_op | source)
XLA Modules:
  0.0 63.3 jit_solution(5065180875630588353)
XLA Ops:
  0.6 0.1 pad_add_fusion.place_ref
  0.7 1.0 %copy-done.1 = f32[2,8,8192]{2,1,0:T(8,128)S(1)} copy-done((f32[2,8,8192]{2,1,0:T(8,128)S(1)}, f32[2,8,8192]{2,1,0:T(8,128)}, u32[]{:S(2)}) %copy-start.1) | copy-done | bytes 524312
  1.8 1.3 %arrange.1 = (f32[32,3,8,128]{3,2,1,0:T(8,128)}, f32[4,2,16,128]{3,2,1,0:T(8,128)S(1)}, f32[4,2,16,128]{3,2,1,0:T(8,128)S(1)}, f32[4,2,16,128]{3,2,1,0:T(8,128)S(1)}, f32[4,2,16,128]{3,2,1,0:T(8,128)S(1)}) custom-call(s32[2]{0:T(128)S(1)} %pad_add_fusion.place_ref, f32[2,8,8192]{2,1,0:T(8,128)S(1)} %copy-done.1), custom_call_target="tpu_custom_call" | custom-call | tf_op jit(solution)/shard_map/arrange/pallas_call | solution.py:468
  3.1 3.0 %collective-permute-start = (f32[4,2,16,128]{3,2,1,0:T(8,128)S(1)}, f32[4,2,16,128]{3,2,1,0:T(8,128)S(1)}, u32[]{:S(2)}, u32[]{:S(2)}) collective-permute-start(f32[4,2,16,128]{3,2,1,0:T(8,128)S(1)} %get-tuple-element.31), channel_id=1, source_target_pairs={{0,4},{1,5},{2,6},{3,7},{4,0},{5,1},{6,2},{7,3},{8,12},{9,13},{10,... | collective-permute-start | bytes 196616 | tf_op jit(solution)/shard_map/ppermute | solution.py:453
  6.1 2.6 %collective-permute-start.1 = (f32[4,2,16,128]{3,2,1,0:T(8,128)S(1)}, f32[4,2,16,128]{3,2,1,0:T(8,128)S(1)}, u32[]{:S(2)}, u32[]{:S(2)}) collective-permute-start(f32[4,2,16,128]{3,2,1,0:T(8,128)S(1)} %get-tuple-element.32), channel_id=1, source_target_pairs={{0,8},{1,9},{2,10},{3,11},{4,12},{5,13},{6,14},{7,15},{8,0},{9,1},... | collective-permute-start | bytes 196616 | tf_op jit(solution)/shard_map/ppermute | solution.py:453
  8.7 6.2 %all-to-all-start = ((f32[32,3,8,128]{3,2,1,0:T(8,128)}), f32[32,3,8,128]{3,2,1,0:T(8,128)S(1)}, u32[]{:S(2)}, u32[]{:S(2)}) async-start(f32[32,3,8,128]{3,2,1,0:T(8,128)} %get-tuple-element.28), calls=%async_computation | async-start | bytes 786432 | tf_op jit(solution)/shard_map/all_to_all | solution.py:477
  14.9 0.0 copy-start.3
  14.9 0.0 copy-start.4
  15.0 0.0 copy-start
  15.0 0.6 relay.2
  15.6 0.5 collective-permute-start.3
  16.0 1.7 %collective-permute-start.4 = (f32[4,2,16,128]{3,2,1,0:T(8,128)S(1)}, f32[4,2,16,128]{3,2,1,0:T(8,128)S(1)}, u32[]{:S(2)}, u32[]{:S(2)}) collective-permute-start(f32[4,2,16,128]{3,2,1,0:T(8,128)S(1)} %get-tuple-element.36), channel_id=1, source_target_pairs={{0,2},{1,3},{2,0},{3,1},{4,6},{5,7},{6,4},{7,5},{8,10},{9,11},{10,... | collective-permute-start | bytes 196616 | tf_op jit(solution)/shard_map/ppermute | solution.py:465
  17.7 0.3 coupling.1
  18.0 0.2 pack.1
  18.2 4.5 %collective-permute-start.6 = (f32[9,2,8,128]{3,2,1,0:T(8,128)S(1)}, f32[9,2,8,128]{3,2,1,0:T(8,128)S(1)}, u32[]{:S(2)}, u32[]{:S(2)}) collective-permute-start(f32[9,2,8,128]{3,2,1,0:T(8,128)S(1)} %get-tuple-element.44), channel_id=1, source_target_pairs={{1,0},{2,1},{3,2},{4,3},{5,4},{6,5},{7,6},{8,7},{9,8},{10,9},{11,1... | collective-permute-start | bytes 221192 | tf_op jit(solution)/shard_map/ppermute | solution.py:494
  22.7 1.7 %collective-permute-done.5.refs_3_ = f32[4,2,16,128]{3,2,1,0:T(8,128)S(1)} collective-permute-done((f32[4,2,16,128]{3,2,1,0:T(8,128)S(1)}, f32[4,2,16,128]{3,2,1,0:T(8,128)S(1)}, u32[]{:S(2)}, u32[]{:S(2)}) %collective-permute-start.5) | collective-permute-done | bytes 65568 | tf_op jit(solution)/shard_map/ppermute | solution.py:465
  24.4 2.4 %early.1 = (f32[2,8,32,128]{3,2,1,0:T(8,128)S(1)}, f32[2,8,32,128]{3,2,1,0:T(8,128)S(1)}) custom-call(s32[2]{0:T(128)S(1)} %pad_add_fusion.place_ref, f32[72,8,512]{2,1,0:T(8,128)S(1)} %bitcast.10, bf16[288,96]{1,0:T(8,128)(2,1)S(1)} %get-tuple-element.29.coup_ref, f32[4,2,16,128]{3,2,1,0:T(8,128)S(1)} %get-tuple-element.34.refs_0_._, ...), custom_call_target="tpu_custom_call" | custom-call | flops 2000000000 | bytes 1048576 | tf_op jit(solution)/shard_map/early/pallas_call | solution.py:513
  26.8 0.3 all-to-all-done
  27.1 3.1 %first.1 = (f32[5,8,32,128]{3,2,1,0:T(8,128)S(1)}, f32[4,8,32,128]{3,2,1,0:T(8,128)S(1)}, f32[16,128]{1,0:T(8,128)S(1)}, f32[4,2,32,128]{3,2,1,0:T(8,128)S(1)}, ...) custom-call(s32[2]{0:T(128)S(1)} %pad_add_fusion.place_ref, ...), custom_call_target="tpu_custom_call" | custom-call | tf_op jit(solution)/shard_map/first/pallas_call | solution.py:523
  30.2 4.0 %collective-permute-start.10 = (f32[4,2,32,128]{3,2,1,0:T(8,128)S(1)}, f32[4,2,32,128]{3,2,1,0:T(8,128)S(1)}, u32[]{:S(2)}, u32[]{:S(2)}) collective-permute-start(f32[4,2,32,128]{3,2,1,0:T(8,128)S(1)} %get-tuple-element.49), channel_id=1, source_target_pairs={{0,12},{1,13},{2,14},{3,15},{4,8},{5,9},{6,10},{7,11},{8,4},{9,5},... | collective-permute-start | bytes 393224 | tf_op jit(solution)/shard_map/ppermute | solution.py:453
  34.3 0.6 %collective-permute-start.9 = (f32[4,2,32,128]{3,2,1,0:T(8,128)S(1)}, f32[4,2,32,128]{3,2,1,0:T(8,128)S(1)}, u32[]{:S(2)}, u32[]{:S(2)}) collective-permute-start(f32[4,2,32,128]{3,2,1,0:T(8,128)S(1)} %get-tuple-element.48), channel_id=1, source_target_pairs={{0,8},{1,9},{2,10},{3,11},{4,12},{5,13},{6,14},{7,15},{8,0},{9,1},... | collective-permute-start | bytes 393224 | tf_op jit(solution)/shard_map/ppermute | solution.py:453
  34.9 0.2 unpack.1.edge_ref
  35.1 7.1 %second.1 = f32[1056,128]{1,0:T(8,128)} custom-call(f32[8]{0:T(128)S(1)} %copy-done.7, f32[5,8,32,128]{3,2,1,0:T(8,128)S(1)} %get-tuple-element.41.v_ref, f32[4,8,32,128]{3,2,1,0:T(8,128)S(1)} %get-tuple-element.42.w_ref, f32[16,128]{1,0:T(8,128)S(1)} %get-tuple-element.43._.sum_ref, f32[72,8,512]{2,1,0:T(8,128)S(1)} %bitcast.12, ...), custom_call_target="tpu_custom_call" | custom-call | flops 10000000000 | bytes 16777216 | tf_op jit(solution)/shard_map/second/pallas_call | solution.py:553
  42.2 5.1 %all-to-all-start.1 = ((f32[32,1,4224]{2,1,0:T(1,128)}), f32[32,1,4224]{2,1,0:T(1,128)S(1)}, u32[]{:S(2)}, u32[]{:S(2)}) async-start(f32[32,1,4224]{2,1,0:T(1,128)} %bitcast.8), calls=%async_computation.1 | async-start | bytes 1081344 | tf_op jit(solution)/shard_map/all_to_all | solution.py:564
  47.3 0.6 relay.3
  48.0 0.5 collective-permute-start.11
  48.4 1.7 %collective-permute-start.12 = (f32[4,2,32,128]{3,2,1,0:T(8,128)S(1)}, f32[4,2,32,128]{3,2,1,0:T(8,128)S(1)}, u32[]{:S(2)}, u32[]{:S(2)}) collective-permute-start(f32[4,2,32,128]{3,2,1,0:T(8,128)S(1)} %get-tuple-element.52), channel_id=1, source_target_pairs={{0,2},{1,3},{2,0},{3,1},{4,6},{5,7},{6,4},{7,5},{8,10},{9,11},{10,... | collective-permute-start | bytes 393224 | tf_op jit(solution)/shard_map/ppermute | solution.py:465
  50.1 7.9 %collective-permute-done.12.refs_2_ = f32[4,2,32,128]{3,2,1,0:T(8,128)S(1)} collective-permute-done((f32[4,2,32,128]{3,2,1,0:T(8,128)S(1)}, f32[4,2,32,128]{3,2,1,0:T(8,128)S(1)}, u32[]{:S(2)}, u32[]{:S(2)}) %collective-permute-start.12) | collective-permute-done | bytes 131104 | tf_op jit(solution)/shard_map/ppermute | solution.py:465
  58.1 2.1 %collective-permute-done.13.refs_3_ = f32[4,2,32,128]{3,2,1,0:T(8,128)S(1)} collective-permute-done((f32[4,2,32,128]{3,2,1,0:T(8,128)S(1)}, f32[4,2,32,128]{3,2,1,0:T(8,128)S(1)}, u32[]{:S(2)}, u32[]{:S(2)}) %collective-permute-start.13) | collective-permute-done | bytes 131104 | tf_op jit(solution)/shard_map/ppermute | solution.py:465
  60.1 0.6 gather.1.w_ref
  60.7 1.3 %all-to-all-done.1 = f32[32,1,4224]{2,1,0:T(1,128)S(1)} async-done(((f32[32,1,4224]{2,1,0:T(1,128)}), f32[32,1,4224]{2,1,0:T(1,128)S(1)}, u32[]{:S(2)}, u32[]{:S(2)}) %all-to-all-start.1) | async-done | bytes 540704 | tf_op jit(solution)/shard_map/all_to_all | solution.py:564
  62.1 1.2 %combine.1 = (f32[2,8,8192]{2,1,0:T(8,128)}, f32[2,8,8192]{2,1,0:T(8,128)}) custom-call(f32[2,8,8192]{2,1,0:T(8,128)S(1)} %copy-done.2, f32[1056,128]{1,0:T(8,128)S(1)} %bitcast.13, f32[16,2,32,128]{3,2,1,0:T(8,128)S(1)} %gather.1.w_ref), custom_call_target="tpu_custom_call" | custom-call | tf_op jit(solution)/shard_map/combine/pallas_call | solution.py:574
  (28 shorter events, 0.1 us)
Async XLA Ops:
  0.7 1.0 %copy-start.1 = (f32[2,8,8192]{2,1,0:T(8,128)S(1)}, f32[2,8,8192]{2,1,0:T(8,128)}, u32[]{:S(2)}) copy-start(f32[2,8,8192]{2,1,0:T(8,128)} %rhs_ref.3) | copy-start | bytes 1572868
  3.1 11.8 %collective-permute-start = (f32[4,2,16,128]{3,2,1,0:T(8,128)S(1)}, f32[4,2,16,128]{3,2,1,0:T(8,128)S(1)}, u32[]{:S(2)}, u32[]{:S(2)}) collective-permute-start(f32[4,2,16,128]{3,2,1,0:T(8,128)S(1)} %get-tuple-element.31), channel_id=1, source_target_pairs={{0,4},{1,5},{2,6},{3,7},{4,0},{5,1},{6,2},{7,3},{8,12},{9,13},{10,... | collective-permute-start | bytes 196616 | tf_op jit(solution)/shard_map/ppermute | solution.py:453
  6.1 8.8 %collective-permute-start.1 = (f32[4,2,16,128]{3,2,1,0:T(8,128)S(1)}, f32[4,2,16,128]{3,2,1,0:T(8,128)S(1)}, u32[]{:S(2)}, u32[]{:S(2)}) collective-permute-start(f32[4,2,16,128]{3,2,1,0:T(8,128)S(1)} %get-tuple-element.32), channel_id=1, source_target_pairs={{0,8},{1,9},{2,10},{3,11},{4,12},{5,13},{6,14},{7,15},{8,0},{9,1},... | collective-permute-start | bytes 196616 | tf_op jit(solution)/shard_map/ppermute | solution.py:453
  8.7 6.2 %collective-permute-start.2 = (f32[4,2,16,128]{3,2,1,0:T(8,128)S(1)}, f32[4,2,16,128]{3,2,1,0:T(8,128)S(1)}, u32[]{:S(2)}, u32[]{:S(2)}) collective-permute-start(f32[4,2,16,128]{3,2,1,0:T(8,128)S(1)} %get-tuple-element.33), channel_id=1, source_target_pairs={{0,12},{1,13},{2,14},{3,15},{4,8},{5,9},{6,10},{7,11},{8,4},{9,5},... | collective-permute-start | bytes 196616 | tf_op jit(solution)/shard_map/ppermute | solution.py:453
  8.7 18.4 %all-to-all-start = ((f32[32,3,8,128]{3,2,1,0:T(8,128)}), f32[32,3,8,128]{3,2,1,0:T(8,128)S(1)}, u32[]{:S(2)}, u32[]{:S(2)}) async-start(f32[32,3,8,128]{3,2,1,0:T(8,128)} %get-tuple-element.28), calls=%async_computation | async-start | bytes 786432 | tf_op jit(solution)/shard_map/all_to_all | solution.py:477
  14.9 2.8 %copy-start.3 = (s32[512]{0:T(512)S(1)}, s32[512]{0:T(512)}, u32[]{:S(2)}) copy-start(s32[512]{0:T(512)} %param.10) | copy-start | bytes 6148
  14.9 2.8 %copy-start.4 = (s32[512]{0:T(512)S(1)}, s32[512]{0:T(512)}, u32[]{:S(2)}) copy-start(s32[512]{0:T(512)} %param.11) | copy-start | bytes 6148
  14.9 2.8 %copy-start.5 = (s32[512]{0:T(512)S(1)}, s32[512]{0:T(512)}, u32[]{:S(2)}) copy-start(s32[512]{0:T(512)} %param.12) | copy-start | bytes 6148
  15.0 2.8 %copy-start.6 = (s32[512]{0:T(512)S(1)}, s32[512]{0:T(512)}, u32[]{:S(2)}) copy-start(s32[512]{0:T(512)} %param.13) | copy-start | bytes 6148
  15.0 3.0 %copy-start = (f32[9,8,8,512]{3,2,1,0:T(8,128)S(1)}, f32[9,8,8,512]{3,2,1,0:T(8,128)}, u32[]{:S(2)}) copy-start(f32[9,8,8,512]{3,2,1,0:T(8,128)} %last_ref.1) | copy-start | bytes 3538948
  15.6 7.1 %collective-permute-start.3 = (f32[4,2,16,128]{3,2,1,0:T(8,128)S(1)}, f32[4,2,16,128]{3,2,1,0:T(8,128)S(1)}, u32[]{:S(2)}, u32[]{:S(2)}) collective-permute-start(f32[4,2,16,128]{3,2,1,0:T(8,128)S(1)} %get-tuple-element.35), channel_id=1, source_target_pairs={{0,1},{1,0},{2,3},{3,2},{4,5},{5,4},{6,7},{7,6},{8,9},{9,8},{10,11... | collective-permute-start | bytes 196616 | tf_op jit(solution)/shard_map/ppermute | solution.py:465
  16.0 6.7 %collective-permute-start.4 = (f32[4,2,16,128]{3,2,1,0:T(8,128)S(1)}, f32[4,2,16,128]{3,2,1,0:T(8,128)S(1)}, u32[]{:S(2)}, u32[]{:S(2)}) collective-permute-start(f32[4,2,16,128]{3,2,1,0:T(8,128)S(1)} %get-tuple-element.36), channel_id=1, source_target_pairs={{0,2},{1,3},{2,0},{3,1},{4,6},{5,7},{6,4},{7,5},{8,10},{9,11},{10,... | collective-permute-start | bytes 196616 | tf_op jit(solution)/shard_map/ppermute | solution.py:465
  17.7 6.7 %collective-permute-start.5 = (f32[4,2,16,128]{3,2,1,0:T(8,128)S(1)}, f32[4,2,16,128]{3,2,1,0:T(8,128)S(1)}, u32[]{:S(2)}, u32[]{:S(2)}) collective-permute-start(f32[4,2,16,128]{3,2,1,0:T(8,128)S(1)} %get-tuple-element.37), channel_id=1, source_target_pairs={{0,3},{1,2},{2,1},{3,0},{4,7},{5,6},{6,5},{7,4},{8,11},{9,10},{10,... | collective-permute-start | bytes 196616 | tf_op jit(solution)/shard_map/ppermute | solution.py:465
  18.2 16.7 %collective-permute-start.6 = (f32[9,2,8,128]{3,2,1,0:T(8,128)S(1)}, f32[9,2,8,128]{3,2,1,0:T(8,128)S(1)}, u32[]{:S(2)}, u32[]{:S(2)}) collective-permute-start(f32[9,2,8,128]{3,2,1,0:T(8,128)S(1)} %get-tuple-element.44), channel_id=1, source_target_pairs={{1,0},{2,1},{3,2},{4,3},{5,4},{6,5},{7,6},{8,7},{9,8},{10,9},{11,1... | collective-permute-start | bytes 221192 | tf_op jit(solution)/shard_map/ppermute | solution.py:494
  22.7 12.2 %collective-permute-start.7 = (f32[9,2,8,128]{3,2,1,0:T(8,128)S(1)}, f32[9,2,8,128]{3,2,1,0:T(8,128)S(1)}, u32[]{:S(2)}, u32[]{:S(2)}) collective-permute-start(f32[9,2,8,128]{3,2,1,0:T(8,128)S(1)} %get-tuple-element.45), channel_id=1, source_target_pairs={{0,1},{1,2},{2,3},{3,4},{4,5},{5,6},{6,7},{7,8},{8,9},{9,10},{10,1... | collective-permute-start | bytes 221192 | tf_op jit(solution)/shard_map/ppermute | solution.py:495
  24.4 2.7 %copy-start.7 = (f32[8]{0:T(128)S(1)}, f32[8]{0:T(128)}, u32[]{:S(2)}) copy-start(f32[8]{0:T(128)} %dif_ref.3) | copy-start | bytes 100
  30.2 17.1 %collective-permute-start.10 = (f32[4,2,32,128]{3,2,1,0:T(8,128)S(1)}, f32[4,2,32,128]{3,2,1,0:T(8,128)S(1)}, u32[]{:S(2)}, u32[]{:S(2)}) collective-permute-start(f32[4,2,32,128]{3,2,1,0:T(8,128)S(1)} %get-tuple-element.49), channel_id=1, source_target_pairs={{0,12},{1,13},{2,14},{3,15},{4,8},{5,9},{6,10},{7,11},{8,4},{9,5},... | collective-permute-start | bytes 393224 | tf_op jit(solution)/shard_map/ppermute | solution.py:453
  34.3 13.1 %collective-permute-start.8 = (f32[4,2,32,128]{3,2,1,0:T(8,128)S(1)}, f32[4,2,32,128]{3,2,1,0:T(8,128)S(1)}, u32[]{:S(2)}, u32[]{:S(2)}) collective-permute-start(f32[4,2,32,128]{3,2,1,0:T(8,128)S(1)} %get-tuple-element.47), channel_id=1, source_target_pairs={{0,4},{1,5},{2,6},{3,7},{4,0},{5,1},{6,2},{7,3},{8,12},{9,13},{10,... | collective-permute-start | bytes 393224 | tf_op jit(solution)/shard_map/ppermute | solution.py:453
  34.3 13.1 %collective-permute-start.9 = (f32[4,2,32,128]{3,2,1,0:T(8,128)S(1)}, f32[4,2,32,128]{3,2,1,0:T(8,128)S(1)}, u32[]{:S(2)}, u32[]{:S(2)}) collective-permute-start(f32[4,2,32,128]{3,2,1,0:T(8,128)S(1)} %get-tuple-element.48), channel_id=1, source_target_pairs={{0,8},{1,9},{2,10},{3,11},{4,12},{5,13},{6,14},{7,15},{8,0},{9,1},... | collective-permute-start | bytes 393224 | tf_op jit(solution)/shard_map/ppermute | solution.py:453
  42.2 19.9 %all-to-all-start.1 = ((f32[32,1,4224]{2,1,0:T(1,128)}), f32[32,1,4224]{2,1,0:T(1,128)S(1)}, u32[]{:S(2)}, u32[]{:S(2)}) async-start(f32[32,1,4224]{2,1,0:T(1,128)} %bitcast.8), calls=%async_computation.1 | async-start | bytes 1081344 | tf_op jit(solution)/shard_map/all_to_all | solution.py:564
  47.9 14.1 %copy-start.2 = (f32[2,8,8192]{2,1,0:T(8,128)S(1)}, f32[2,8,8192]{2,1,0:T(8,128)}, u32[]{:S(2)}) copy-start(f32[2,8,8192]{2,1,0:T(8,128)} %rhs_ref.3) | copy-start | bytes 1572868
  48.0 2.2 %collective-permute-start.11 = (f32[4,2,32,128]{3,2,1,0:T(8,128)S(1)}, f32[4,2,32,128]{3,2,1,0:T(8,128)S(1)}, u32[]{:S(2)}, u32[]{:S(2)}) collective-permute-start(f32[4,2,32,128]{3,2,1,0:T(8,128)S(1)} %get-tuple-element.51), channel_id=1, source_target_pairs={{0,1},{1,0},{2,3},{3,2},{4,5},{5,4},{6,7},{7,6},{8,9},{9,8},{10,11... | collective-permute-start | bytes 393224 | tf_op jit(solution)/shard_map/ppermute | solution.py:465
  48.4 9.6 %collective-permute-start.12 = (f32[4,2,32,128]{3,2,1,0:T(8,128)S(1)}, f32[4,2,32,128]{3,2,1,0:T(8,128)S(1)}, u32[]{:S(2)}, u32[]{:S(2)}) collective-permute-start(f32[4,2,32,128]{3,2,1,0:T(8,128)S(1)} %get-tuple-element.52), channel_id=1, source_target_pairs={{0,2},{1,3},{2,0},{3,1},{4,6},{5,7},{6,4},{7,5},{8,10},{9,11},{10,... | collective-permute-start | bytes 393224 | tf_op jit(solution)/shard_map/ppermute | solution.py:465
  50.1 10.0 %collective-permute-start.13 = (f32[4,2,32,128]{3,2,1,0:T(8,128)S(1)}, f32[4,2,32,128]{3,2,1,0:T(8,128)S(1)}, u32[]{:S(2)}, u32[]{:S(2)}) collective-permute-start(f32[4,2,32,128]{3,2,1,0:T(8,128)S(1)} %get-tuple-element.53), channel_id=1, source_target_pairs={{0,3},{1,2},{2,1},{3,0},{4,7},{5,6},{6,5},{7,4},{8,11},{9,10},{10,... | collective-permute-start | bytes 393224 | tf_op jit(solution)/shard_map/ppermute | solution.py:465

commit v9 on v8

--- a/solution.py
+++ b/solution.py
@@ -23,27 +23,35 @@
 
 
 def arrange_kernel(parts, early, place_ref, rhs_ref, out_ref, *refs):
-    own, _, total = rhs_ref.shape
+    refs, (buf_ref, sems) = refs[:-2], refs[-2:]
+    own, _, total = buf_ref.shape
     cells = total // parts
     tiles = cells // LANES
     plane = GROUP // own
     low = lane_iota() < LANES // 2
+    copies = []
+    for q in range(parts // plane):
+        at = pl.ds(pl.multiple_of(jnp.bitwise_xor(place_ref[0], q) * (plane * cells), LANES), plane * cells)
+        copies.append(pltpu.make_async_copy(rhs_ref.at[:, :, at], buf_ref.at[:, :, at], sems.at[q]))
+        copies[q].start()
     for q in range(parts // plane):
         base = jnp.bitwise_xor(place_ref[0], q) * plane
+        copies[q].wait()
         for k in range(plane):
             for m in range(own):
-                for ct in range(early):
+                for ct in range(tiles):
                     at = pl.multiple_of((base + k) * cells + ct * LANES, LANES)
-                    refs[q][k, m, ct * S : (ct + 1) * S, :] = rhs_ref[m, :, pl.ds(at, LANES)]
+                    tile = buf_ref[m, :, pl.ds(at, LANES)]
+                    if ct < early:
+                        refs[q][k, m, ct * S : (ct + 1) * S, :] = tile
+                    else:
+                        out_ref[(base + k) * own + m, ct - early] = tile
     for d in range(parts):
         after = ((d + 1) * cells) % total
         before = (d * cells - LANES) % total
         for m in range(own):
-            for ct in range(early, tiles):
-                at = d * cells + ct * LANES
-                out_ref[d * own + m, ct - early] = rhs_ref[m, :, at : at + LANES]
             out_ref[d * own + m, tiles - early] = jnp.where(
-                low, rhs_ref[m, :, after : after + LANES], rhs_ref[m, :, before : before + LANES]
+                low, buf_ref[m, :, after : after + LANES], buf_ref[m, :, before : before + LANES]
             )
 
 
@@ -147,6 +155,32 @@
             bs_ref[slot] = jnp.dot(xs_ref[slot], stencil_ref[...], preferred_element_type=F32)
 
     return [functools.partial(fill, first) for first in range(0, S, 2)]
+
+
+def prepare(get, ct, slot, every, coup_ref, stencil_ref, vs_ref, xs_ref, mx_ref, bs_ref):
+    n = bs_ref.shape[1] // S
+    before, after = (ct - 1) % every, (ct + 1) % every
+
+    def step(first):
+        wide = lax.broadcasted_iota(jnp.int32, (n, LANES), 1) < LANES // 2
+        for t in (first, first + 1):
+            at = slice(t * LANES, (t + 1) * LANES)
+            to = slice(t * n, (t + 1) * n)
+            high, low = split(get(ct, t))
+            vs_ref[slot, 0:n, at] = high
+            vs_ref[slot, n : 2 * n, at] = low
+            vs_ref[slot, 2 * n : 3 * n, at] = high
+            xs_ref[slot, to, 0:LANES] = high
+            xs_ref[slot, to, LANES : 2 * LANES] = low
+            high, low = split(jnp.where(wide, get(after, t), get(before, t)))
+            xs_ref[slot, to, 2 * LANES : 3 * LANES] = high
+            xs_ref[slot, to, 3 * LANES :] = low
+        at = slice(first * LANES, (first + 2) * LANES)
+        mx_ref[slot, :, at] = jnp.dot(coup_ref[...], vs_ref[slot, :, at], preferred_element_type=F32)
+        if first + 2 == S:
+            bs_ref[slot] = jnp.dot(xs_ref[slot], stencil_ref[...], preferred_element_type=F32)
+
+    return [functools.partial(step, first) for first in range(0, S, 2)]
 
 
 def run(steps):
@@ -244,8 +278,8 @@
 
         return finish
 
-    def prepare(ct):
-        return mix(get, ct, ct % 2, coup_ref, vs_ref, mx_ref) + sides(ct, ct % 2)
+    def ready(ct):
+        return prepare(get, ct, ct % 2, every, coup_ref, stencil_ref, vs_ref, xs_ref, mx_ref, bs_ref)
 
     def sides(ct, slot):
         return spread(get, ct, slot, every, stencil_ref, xs_ref, bs_ref)
@@ -260,9 +294,9 @@
     for ct in range(early):
         rest += sides(ct, spare) + [functools.partial(close, ct, spare)]
     if early < tiles:
-        run(prepare(early))
+        run(ready(early))
     for ct in range(early, tiles):
-        steps = prepare(ct + 1) if ct + 1 < tiles else rest
+        steps = ready(ct + 1) if ct + 1 < tiles else rest
         react(n, tile_of(jac_ref, ct), ct % 2, mx_ref, finisher(ct, ct % 2), steps)
     if early == tiles:
         run(rest)
@@ -326,23 +360,18 @@
 
     order = list(range(1, tiles)) + [0]
 
-    def mixed(get, ct, slot):
-        return mix(get, ct, slot, coup_ref, vs_ref, mx_ref)
-
-    def sides(get, ct, slot):
-        return spread(get, ct, slot, every, stencil_ref, xs_ref, bs_ref)
-
-    run(mixed(get_v, tiles, 0) + sides(get_v, tiles, 0))
+    def ready(get, ct, slot):
+        return prepare(get, ct, slot, every, coup_ref, stencil_ref, vs_ref, xs_ref, mx_ref, bs_ref)
+
+    run(ready(get_v, tiles, 0))
     inside = tiles > 2
-    steps = mixed(get_w, order[0], 1) + (sides(get_w, order[0], 1) if inside else [])
+    steps = ready(get_w, order[0], 1) if inside else []
     react(n, tile_of(edge_ref, 0), 0, mx_ref, finish_edge, steps)
     if not inside:
-        run(sides(get_w, order[0], 1))
+        run(ready(get_w, order[0], 1))
     for at, ct in enumerate(order):
         slot = (at + 1) % 2
-        steps = []
-        if at + 1 < tiles:
-            steps = mixed(get_w, order[at + 1], 1 - slot) + sides(get_w, order[at + 1], 1 - slot)
+        steps = ready(get_w, order[at + 1], 1 - slot) if at + 1 < tiles else []
         react(n, tile_of(jac_ref, ct), slot, mx_ref, finisher(ct, slot), steps)
     uu, ur, uz, rz = (sums.total(name) for name in ("uu", "ur", "uz", "rz"))
     c2 = ratio(rz, rr)
@@ -468,9 +497,10 @@
     late_send, *early_send = pl.pallas_call(
         functools.partial(arrange_kernel, parts, early),
         out_shape=[sds((n, tiles + 1 - early, S, LANES), F32)] + [sds(block, F32)] * (parts // plane),
-        in_specs=[smem, VMEM],
+        in_specs=[smem, pl.BlockSpec(memory_space=pltpu.HBM)],
         out_specs=[VMEM] * (1 + parts // plane),
-        compiler_params=PARAMS,
+        scratch_shapes=[pltpu.VMEM(rhs.shape, F32), pltpu.SemaphoreType.DMA((parts // plane,))],
+        compiler_params=pltpu.CompilerParams(vmem_limit_bytes=60 * 1024 * 1024),
         name="arrange",
     )(place, rhs)
     near, relayed = across(early_send)

time: 63.7 us -> 64.7 us (1.016)
  Pallas kernels: 17.5 us -> 19.2 us
    pallas_call x1, Pallas kernels: 1.34 us -> 2.72 us  [local(): pl.pallas_call(functools.partial(arrange_kernel, parts, early), out_shape...]
where the time goes in v9:
time: 64.7 us; the launch traced here: 64.3 us
  starting transfers between devices  29.7 us (46%)
  Pallas kernels  19.2 us (30%)
  waiting for transfers between devices  13 us (20%)
  local copies, waits for them, and re-layouts  0.87 us (1%)
  between operations  0.86 us (1%)
  other arithmetic  0.65 us (1%)
    ppermute x6, waiting for transfers between devices, across(): lax.ppermute(relayed[k], 'modes', [(i, i ^ k) for i in range(parts)])  11.6 us
    ppermute x6, starting transfers between devices, across(): lax.ppermute(arrays[q], 'modes', [(i, i ^ q * plane) for i in range(parts)])  10.1 us
    pallas_call x1, Pallas kernels, local(): pl.pallas_call(functools.partial(second_kernel, n, tiles), out_shape=sds(...  7.23 us
    all_to_all x1, starting transfers between devices, local(): lax.all_to_all(late_send, 'modes', split_axis=0, concat_axis=0, tiled=True)  6.16 us
    all_to_all x1, starting transfers between devices, local(): lax.all_to_all(z_send.reshape(n, 1, line), 'modes', split_axis=0, concat_...  4.73 us
    ppermute x1, starting transfers between devices, local(): after = lax.ppermute(head, 'modes', down)  4.48 us
    ppermute x6, starting transfers between devices, across(): lax.ppermute(relayed[k], 'modes', [(i, i ^ k) for i in range(parts)])  4.24 us
    pallas_call x1, Pallas kernels, local(): pl.pallas_call(functools.partial(first_kernel, n, tiles), out_shape=[sds(...  3.2 us
  transfers between devices with their start and end apart: 16, of which 5 were waited for; matrix products, arithmetic and copies ran while one was open for 0% of the time, Pallas kernels for 24%

profile of v9, /device:TPU:0, one launch (start us, length us, event | category | flops | bytes accessed | tf_op | source)
XLA Modules:
  0.0 64.3 jit_solution(9199408493663151070)
XLA Ops:
  0.6 0.6 %pad_add_fusion.place_ref = s32[2]{0:T(128)} fusion(s32[1]{0:T(128)} %bitcast.1, s32[1]{0:T(128)} %bitcast), kind=kLoop, calls=%fused_computation | loop fusion | flops 2 | bytes 16 | tf_op jit(solution)/shard_map/stack | solution.py:473
  1.3 2.7 %arrange.1 = (f32[32,3,8,128]{3,2,1,0:T(8,128)}, f32[4,2,16,128]{3,2,1,0:T(8,128)}, f32[4,2,16,128]{3,2,1,0:T(8,128)}, f32[4,2,16,128]{3,2,1,0:T(8,128)}, f32[4,2,16,128]{3,2,1,0:T(8,128)}) custom-call(s32[2]{0:T(128)} %pad_add_fusion.place_ref, f32[2,8,8192]{2,1,0:T(8,128)} %rhs_ref.3), custom_call_target="tpu_custom_call" | custom-call | tf_op jit(solution)/shard_map/arrange/pallas_call | solution.py:497
  4.0 3.1 %collective-permute-start = (f32[4,2,16,128]{3,2,1,0:T(8,128)}, f32[4,2,16,128]{3,2,1,0:T(8,128)S(1)}, u32[]{:S(2)}, u32[]{:S(2)}) collective-permute-start(f32[4,2,16,128]{3,2,1,0:T(8,128)} %get-tuple-element.31), channel_id=1, source_target_pairs={{0,4},{1,5},{2,6},{3,7},{4,0},{5,1},{6,2},{7,3},{8,12},{9,13},{10,... | collective-permute-start | bytes 196616 | tf_op jit(solution)/shard_map/ppermute | solution.py:482
  7.1 2.6 %collective-permute-start.1 = (f32[4,2,16,128]{3,2,1,0:T(8,128)}, f32[4,2,16,128]{3,2,1,0:T(8,128)S(1)}, u32[]{:S(2)}, u32[]{:S(2)}) collective-permute-start(f32[4,2,16,128]{3,2,1,0:T(8,128)} %get-tuple-element.32), channel_id=1, source_target_pairs={{0,8},{1,9},{2,10},{3,11},{4,12},{5,13},{6,14},{7,15},{8,0},{9,1},... | collective-permute-start | bytes 196616 | tf_op jit(solution)/shard_map/ppermute | solution.py:482
  9.7 6.2 %all-to-all-start = ((f32[32,3,8,128]{3,2,1,0:T(8,128)}), f32[32,3,8,128]{3,2,1,0:T(8,128)S(1)}, u32[]{:S(2)}, u32[]{:S(2)}) async-start(f32[32,3,8,128]{3,2,1,0:T(8,128)} %get-tuple-element.28), calls=%async_computation | async-start | bytes 786432 | tf_op jit(solution)/shard_map/all_to_all | solution.py:507
  15.9 0.1 collective-permute-done.2.refs_3_
  16.0 0.8 %copy-done.8 = f32[4,2,16,128]{3,2,1,0:T(8,128)S(1)} copy-done((f32[4,2,16,128]{3,2,1,0:T(8,128)S(1)}, f32[4,2,16,128]{3,2,1,0:T(8,128)}, u32[]{:S(2)}) %copy-start.8) | copy-done | bytes 65560
  16.8 0.0 copy-start
  16.9 0.6 relay.2
  17.4 0.4 collective-permute-start.3
  17.8 1.7 %collective-permute-start.4 = (f32[4,2,16,128]{3,2,1,0:T(8,128)S(1)}, f32[4,2,16,128]{3,2,1,0:T(8,128)S(1)}, u32[]{:S(2)}, u32[]{:S(2)}) collective-permute-start(f32[4,2,16,128]{3,2,1,0:T(8,128)S(1)} %get-tuple-element.36), channel_id=1, source_target_pairs={{0,2},{1,3},{2,0},{3,1},{4,6},{5,7},{6,4},{7,5},{8,10},{9,11},{10,... | collective-permute-start | bytes 196616 | tf_op jit(solution)/shard_map/ppermute | solution.py:494
  19.5 0.3 coupling.1
  19.8 0.2 pack.1
  20.0 4.5 %collective-permute-start.6 = (f32[9,2,8,128]{3,2,1,0:T(8,128)S(1)}, f32[9,2,8,128]{3,2,1,0:T(8,128)S(1)}, u32[]{:S(2)}, u32[]{:S(2)}) collective-permute-start(f32[9,2,8,128]{3,2,1,0:T(8,128)S(1)} %get-tuple-element.44), channel_id=1, source_target_pairs={{1,0},{2,1},{3,2},{4,3},{5,4},{6,5},{7,6},{8,7},{9,8},{10,9},{11,1... | collective-permute-start | bytes 221192 | tf_op jit(solution)/shard_map/ppermute | solution.py:524
  24.5 1.5 %collective-permute-done.5.refs_3_ = f32[4,2,16,128]{3,2,1,0:T(8,128)S(1)} collective-permute-done((f32[4,2,16,128]{3,2,1,0:T(8,128)S(1)}, f32[4,2,16,128]{3,2,1,0:T(8,128)S(1)}, u32[]{:S(2)}, u32[]{:S(2)}) %collective-permute-start.5) | collective-permute-done | bytes 65568 | tf_op jit(solution)/shard_map/ppermute | solution.py:494
  26.0 2.5 %early.1 = (f32[2,8,32,128]{3,2,1,0:T(8,128)S(1)}, f32[2,8,32,128]{3,2,1,0:T(8,128)S(1)}) custom-call(s32[2]{0:T(128)S(1)} %copy-done.2, f32[72,8,512]{2,1,0:T(8,128)S(1)} %bitcast.10, bf16[288,96]{1,0:T(8,128)(2,1)S(1)} %get-tuple-element.29.coup_ref, f32[4,2,16,128]{3,2,1,0:T(8,128)S(1)} %get-tuple-element.34.refs_0_._, ...), custom_call_target="tpu_custom_call" | custom-call | flops 2000000000 | bytes 1048576 | tf_op jit(solution)/shard_map/early/pallas_call | solution.py:543
  28.5 3.2 %first.1 = (f32[5,8,32,128]{3,2,1,0:T(8,128)S(1)}, f32[4,8,32,128]{3,2,1,0:T(8,128)S(1)}, f32[16,128]{1,0:T(8,128)S(1)}, f32[4,2,32,128]{3,2,1,0:T(8,128)S(1)}, ...) custom-call(s32[2]{0:T(128)S(1)} %copy-done.2, f32[8]{0:T(128)S(1)} %copy-done.7, ...), custom_call_target="tpu_custom_call" | custom-call | tf_op jit(solution)/shard_map/first/pallas_call | solution.py:553
  31.7 2.7 %collective-permute-start.10 = (f32[4,2,32,128]{3,2,1,0:T(8,128)S(1)}, f32[4,2,32,128]{3,2,1,0:T(8,128)S(1)}, u32[]{:S(2)}, u32[]{:S(2)}) collective-permute-start(f32[4,2,32,128]{3,2,1,0:T(8,128)S(1)} %get-tuple-element.49), channel_id=1, source_target_pairs={{0,12},{1,13},{2,14},{3,15},{4,8},{5,9},{6,10},{7,11},{8,4},{9,5},... | collective-permute-start | bytes 393224 | tf_op jit(solution)/shard_map/ppermute | solution.py:482
  34.5 0.3 collective-permute-start.8
  34.8 1.4 %collective-permute-start.9 = (f32[4,2,32,128]{3,2,1,0:T(8,128)S(1)}, f32[4,2,32,128]{3,2,1,0:T(8,128)S(1)}, u32[]{:S(2)}, u32[]{:S(2)}) collective-permute-start(f32[4,2,32,128]{3,2,1,0:T(8,128)S(1)} %get-tuple-element.48), channel_id=1, source_target_pairs={{0,8},{1,9},{2,10},{3,11},{4,12},{5,13},{6,14},{7,15},{8,0},{9,1},... | collective-permute-start | bytes 393224 | tf_op jit(solution)/shard_map/ppermute | solution.py:482
  36.2 0.2 unpack.1.edge_ref
  36.4 7.2 %second.1 = f32[1056,128]{1,0:T(8,128)} custom-call(f32[8]{0:T(128)S(1)} %copy-done.7, f32[5,8,32,128]{3,2,1,0:T(8,128)S(1)} %get-tuple-element.41.v_ref, f32[4,8,32,128]{3,2,1,0:T(8,128)S(1)} %get-tuple-element.42.w_ref, f32[16,128]{1,0:T(8,128)S(1)} %get-tuple-element.43._.sum_ref, f32[72,8,512]{2,1,0:T(8,128)S(1)} %bitcast.12, ...), custom_call_target="tpu_custom_call" | custom-call | flops 10000000000 | bytes 16777216 | tf_op jit(solution)/shard_map/second/pallas_call | solution.py:583
  43.6 4.7 %all-to-all-start.1 = ((f32[32,1,4224]{2,1,0:T(1,128)}), f32[32,1,4224]{2,1,0:T(1,128)S(1)}, u32[]{:S(2)}, u32[]{:S(2)}) async-start(f32[32,1,4224]{2,1,0:T(1,128)} %bitcast.8), calls=%async_computation.1 | async-start | bytes 1081344 | tf_op jit(solution)/shard_map/all_to_all | solution.py:594
  48.4 0.6 relay.3
  49.0 0.0 copy-start.1
  49.0 0.5 collective-permute-start.11
  49.4 1.7 %collective-permute-start.12 = (f32[4,2,32,128]{3,2,1,0:T(8,128)S(1)}, f32[4,2,32,128]{3,2,1,0:T(8,128)S(1)}, u32[]{:S(2)}, u32[]{:S(2)}) collective-permute-start(f32[4,2,32,128]{3,2,1,0:T(8,128)S(1)} %get-tuple-element.52), channel_id=1, source_target_pairs={{0,2},{1,3},{2,0},{3,1},{4,6},{5,7},{6,4},{7,5},{8,10},{9,11},{10,... | collective-permute-start | bytes 393224 | tf_op jit(solution)/shard_map/ppermute | solution.py:494
  51.1 7.9 %collective-permute-done.12.refs_2_ = f32[4,2,32,128]{3,2,1,0:T(8,128)S(1)} collective-permute-done((f32[4,2,32,128]{3,2,1,0:T(8,128)S(1)}, f32[4,2,32,128]{3,2,1,0:T(8,128)S(1)}, u32[]{:S(2)}, u32[]{:S(2)}) %collective-permute-start.12) | collective-permute-done | bytes 131104 | tf_op jit(solution)/shard_map/ppermute | solution.py:494
  59.1 2.1 %collective-permute-done.13.refs_3_ = f32[4,2,32,128]{3,2,1,0:T(8,128)S(1)} collective-permute-done((f32[4,2,32,128]{3,2,1,0:T(8,128)S(1)}, f32[4,2,32,128]{3,2,1,0:T(8,128)S(1)}, u32[]{:S(2)}, u32[]{:S(2)}) %collective-permute-start.13) | collective-permute-done | bytes 131104 | tf_op jit(solution)/shard_map/ppermute | solution.py:494
  61.2 0.6 gather.1.w_ref
  61.7 1.3 %all-to-all-done.1 = f32[32,1,4224]{2,1,0:T(1,128)S(1)} async-done(((f32[32,1,4224]{2,1,0:T(1,128)}), f32[32,1,4224]{2,1,0:T(1,128)S(1)}, u32[]{:S(2)}, u32[]{:S(2)}) %all-to-all-start.1) | async-done | bytes 540704 | tf_op jit(solution)/shard_map/all_to_all | solution.py:594
  63.1 1.2 %combine.1 = (f32[2,8,8192]{2,1,0:T(8,128)}, f32[2,8,8192]{2,1,0:T(8,128)}) custom-call(f32[2,8,8192]{2,1,0:T(8,128)S(1)} %copy-done.1, f32[1056,128]{1,0:T(8,128)S(1)} %bitcast.13, f32[16,2,32,128]{3,2,1,0:T(8,128)S(1)} %gather.1.w_ref), custom_call_target="tpu_custom_call" | custom-call | tf_op jit(solution)/shard_map/combine/pallas_call | solution.py:604
  (30 shorter events, 0.1 us)
Async XLA Ops:
  1.3 14.7 %copy-start.2 = (s32[2]{0:T(128)S(1)}, s32[2]{0:T(128)}, u32[]{:S(2)}) copy-start(s32[2]{0:T(128)} %pad_add_fusion.place_ref) | copy-start | bytes 28
  4.0 11.8 %collective-permute-start = (f32[4,2,16,128]{3,2,1,0:T(8,128)}, f32[4,2,16,128]{3,2,1,0:T(8,128)S(1)}, u32[]{:S(2)}, u32[]{:S(2)}) collective-permute-start(f32[4,2,16,128]{3,2,1,0:T(8,128)} %get-tuple-element.31), channel_id=1, source_target_pairs={{0,4},{1,5},{2,6},{3,7},{4,0},{5,1},{6,2},{7,3},{8,12},{9,13},{10,... | collective-permute-start | bytes 196616 | tf_op jit(solution)/shard_map/ppermute | solution.py:482
  7.1 8.8 %collective-permute-start.1 = (f32[4,2,16,128]{3,2,1,0:T(8,128)}, f32[4,2,16,128]{3,2,1,0:T(8,128)S(1)}, u32[]{:S(2)}, u32[]{:S(2)}) collective-permute-start(f32[4,2,16,128]{3,2,1,0:T(8,128)} %get-tuple-element.32), channel_id=1, source_target_pairs={{0,8},{1,9},{2,10},{3,11},{4,12},{5,13},{6,14},{7,15},{8,0},{9,1},... | collective-permute-start | bytes 196616 | tf_op jit(solution)/shard_map/ppermute | solution.py:482
  9.7 6.3 %collective-permute-start.2 = (f32[4,2,16,128]{3,2,1,0:T(8,128)}, f32[4,2,16,128]{3,2,1,0:T(8,128)S(1)}, u32[]{:S(2)}, u32[]{:S(2)}) collective-permute-start(f32[4,2,16,128]{3,2,1,0:T(8,128)} %get-tuple-element.33), channel_id=1, source_target_pairs={{0,12},{1,13},{2,14},{3,15},{4,8},{5,9},{6,10},{7,11},{8,4},{9,5},... | collective-permute-start | bytes 196616 | tf_op jit(solution)/shard_map/ppermute | solution.py:482
  9.7 18.8 %all-to-all-start = ((f32[32,3,8,128]{3,2,1,0:T(8,128)}), f32[32,3,8,128]{3,2,1,0:T(8,128)S(1)}, u32[]{:S(2)}, u32[]{:S(2)}) async-start(f32[32,3,8,128]{3,2,1,0:T(8,128)} %get-tuple-element.28), calls=%async_computation | async-start | bytes 786432 | tf_op jit(solution)/shard_map/all_to_all | solution.py:507
  16.0 0.8 %copy-start.8 = (f32[4,2,16,128]{3,2,1,0:T(8,128)S(1)}, f32[4,2,16,128]{3,2,1,0:T(8,128)}, u32[]{:S(2)}) copy-start(f32[4,2,16,128]{3,2,1,0:T(8,128)} %get-tuple-element.30.refs_0_) | copy-start | bytes 196612
  16.8 2.7 %copy-start.3 = (s32[512]{0:T(512)S(1)}, s32[512]{0:T(512)}, u32[]{:S(2)}) copy-start(s32[512]{0:T(512)} %param.10) | copy-start | bytes 6148
  16.8 2.7 %copy-start.4 = (s32[512]{0:T(512)S(1)}, s32[512]{0:T(512)}, u32[]{:S(2)}) copy-start(s32[512]{0:T(512)} %param.11) | copy-start | bytes 6148
  16.8 2.7 %copy-start.5 = (s32[512]{0:T(512)S(1)}, s32[512]{0:T(512)}, u32[]{:S(2)}) copy-start(s32[512]{0:T(512)} %param.12) | copy-start | bytes 6148
  16.8 2.7 %copy-start.6 = (s32[512]{0:T(512)S(1)}, s32[512]{0:T(512)}, u32[]{:S(2)}) copy-start(s32[512]{0:T(512)} %param.13) | copy-start | bytes 6148
  16.8 3.0 %copy-start = (f32[9,8,8,512]{3,2,1,0:T(8,128)S(1)}, f32[9,8,8,512]{3,2,1,0:T(8,128)}, u32[]{:S(2)}) copy-start(f32[9,8,8,512]{3,2,1,0:T(8,128)} %last_ref.1) | copy-start | bytes 3538948
  17.4 7.1 %collective-permute-start.3 = (f32[4,2,16,128]{3,2,1,0:T(8,128)S(1)}, f32[4,2,16,128]{3,2,1,0:T(8,128)S(1)}, u32[]{:S(2)}, u32[]{:S(2)}) collective-permute-start(f32[4,2,16,128]{3,2,1,0:T(8,128)S(1)} %get-tuple-element.35), channel_id=1, source_target_pairs={{0,1},{1,0},{2,3},{3,2},{4,5},{5,4},{6,7},{7,6},{8,9},{9,8},{10,11... | collective-permute-start | bytes 196616 | tf_op jit(solution)/shard_map/ppermute | solution.py:494
  17.8 6.7 %collective-permute-start.4 = (f32[4,2,16,128]{3,2,1,0:T(8,128)S(1)}, f32[4,2,16,128]{3,2,1,0:T(8,128)S(1)}, u32[]{:S(2)}, u32[]{:S(2)}) collective-permute-start(f32[4,2,16,128]{3,2,1,0:T(8,128)S(1)} %get-tuple-element.36), channel_id=1, source_target_pairs={{0,2},{1,3},{2,0},{3,1},{4,6},{5,7},{6,4},{7,5},{8,10},{9,11},{10,... | collective-permute-start | bytes 196616 | tf_op jit(solution)/shard_map/ppermute | solution.py:494
  19.5 6.5 %collective-permute-start.5 = (f32[4,2,16,128]{3,2,1,0:T(8,128)S(1)}, f32[4,2,16,128]{3,2,1,0:T(8,128)S(1)}, u32[]{:S(2)}, u32[]{:S(2)}) collective-permute-start(f32[4,2,16,128]{3,2,1,0:T(8,128)S(1)} %get-tuple-element.37), channel_id=1, source_target_pairs={{0,3},{1,2},{2,1},{3,0},{4,7},{5,6},{6,5},{7,4},{8,11},{9,10},{10,... | collective-permute-start | bytes 196616 | tf_op jit(solution)/shard_map/ppermute | solution.py:494
  20.0 16.2 %collective-permute-start.6 = (f32[9,2,8,128]{3,2,1,0:T(8,128)S(1)}, f32[9,2,8,128]{3,2,1,0:T(8,128)S(1)}, u32[]{:S(2)}, u32[]{:S(2)}) collective-permute-start(f32[9,2,8,128]{3,2,1,0:T(8,128)S(1)} %get-tuple-element.44), channel_id=1, source_target_pairs={{1,0},{2,1},{3,2},{4,3},{5,4},{6,5},{7,6},{8,7},{9,8},{10,9},{11,1... | collective-permute-start | bytes 221192 | tf_op jit(solution)/shard_map/ppermute | solution.py:524
  24.5 11.7 %collective-permute-start.7 = (f32[9,2,8,128]{3,2,1,0:T(8,128)S(1)}, f32[9,2,8,128]{3,2,1,0:T(8,128)S(1)}, u32[]{:S(2)}, u32[]{:S(2)}) collective-permute-start(f32[9,2,8,128]{3,2,1,0:T(8,128)S(1)} %get-tuple-element.45), channel_id=1, source_target_pairs={{0,1},{1,2},{2,3},{3,4},{4,5},{5,6},{6,7},{7,8},{8,9},{9,10},{10,1... | collective-permute-start | bytes 221192 | tf_op jit(solution)/shard_map/ppermute | solution.py:525
  26.0 2.5 %copy-start.7 = (f32[8]{0:T(128)S(1)}, f32[8]{0:T(128)}, u32[]{:S(2)}) copy-start(f32[8]{0:T(128)} %dif_ref.3) | copy-start | bytes 100
  31.7 16.6 %collective-permute-start.10 = (f32[4,2,32,128]{3,2,1,0:T(8,128)S(1)}, f32[4,2,32,128]{3,2,1,0:T(8,128)S(1)}, u32[]{:S(2)}, u32[]{:S(2)}) collective-permute-start(f32[4,2,32,128]{3,2,1,0:T(8,128)S(1)} %get-tuple-element.49), channel_id=1, source_target_pairs={{0,12},{1,13},{2,14},{3,15},{4,8},{5,9},{6,10},{7,11},{8,4},{9,5},... | collective-permute-start | bytes 393224 | tf_op jit(solution)/shard_map/ppermute | solution.py:482
  34.5 13.9 %collective-permute-start.8 = (f32[4,2,32,128]{3,2,1,0:T(8,128)S(1)}, f32[4,2,32,128]{3,2,1,0:T(8,128)S(1)}, u32[]{:S(2)}, u32[]{:S(2)}) collective-permute-start(f32[4,2,32,128]{3,2,1,0:T(8,128)S(1)} %get-tuple-element.47), channel_id=1, source_target_pairs={{0,4},{1,5},{2,6},{3,7},{4,0},{5,1},{6,2},{7,3},{8,12},{9,13},{10,... | collective-permute-start | bytes 393224 | tf_op jit(solution)/shard_map/ppermute | solution.py:482
  34.8 13.6 %collective-permute-start.9 = (f32[4,2,32,128]{3,2,1,0:T(8,128)S(1)}, f32[4,2,32,128]{3,2,1,0:T(8,128)S(1)}, u32[]{:S(2)}, u32[]{:S(2)}) collective-permute-start(f32[4,2,32,128]{3,2,1,0:T(8,128)S(1)} %get-tuple-element.48), channel_id=1, source_target_pairs={{0,8},{1,9},{2,10},{3,11},{4,12},{5,13},{6,14},{7,15},{8,0},{9,1},... | collective-permute-start | bytes 393224 | tf_op jit(solution)/shard_map/ppermute | solution.py:482
  43.6 19.5 %all-to-all-start.1 = ((f32[32,1,4224]{2,1,0:T(1,128)}), f32[32,1,4224]{2,1,0:T(1,128)S(1)}, u32[]{:S(2)}, u32[]{:S(2)}) async-start(f32[32,1,4224]{2,1,0:T(1,128)} %bitcast.8), calls=%async_computation.1 | async-start | bytes 1081344 | tf_op jit(solution)/shard_map/all_to_all | solution.py:594
  49.0 14.1 %copy-start.1 = (f32[2,8,8192]{2,1,0:T(8,128)S(1)}, f32[2,8,8192]{2,1,0:T(8,128)}, u32[]{:S(2)}) copy-start(f32[2,8,8192]{2,1,0:T(8,128)} %rhs_ref.3) | copy-start | bytes 1572868
  49.0 2.2 %collective-permute-start.11 = (f32[4,2,32,128]{3,2,1,0:T(8,128)S(1)}, f32[4,2,32,128]{3,2,1,0:T(8,128)S(1)}, u32[]{:S(2)}, u32[]{:S(2)}) collective-permute-start(f32[4,2,32,128]{3,2,1,0:T(8,128)S(1)} %get-tuple-element.51), channel_id=1, source_target_pairs={{0,1},{1,0},{2,3},{3,2},{4,5},{5,4},{6,7},{7,6},{8,9},{9,8},{10,11... | collective-permute-start | bytes 393224 | tf_op jit(solution)/shard_map/ppermute | solution.py:494
  49.4 9.6 %collective-permute-start.12 = (f32[4,2,32,128]{3,2,1,0:T(8,128)S(1)}, f32[4,2,32,128]{3,2,1,0:T(8,128)S(1)}, u32[]{:S(2)}, u32[]{:S(2)}) collective-permute-start(f32[4,2,32,128]{3,2,1,0:T(8,128)S(1)} %get-tuple-element.52), channel_id=1, source_target_pairs={{0,2},{1,3},{2,0},{3,1},{4,6},{5,7},{6,4},{7,5},{8,10},{9,11},{10,... | collective-permute-start | bytes 393224 | tf_op jit(solution)/shard_map/ppermute | solution.py:494
  51.1 10.0 %collective-permute-start.13 = (f32[4,2,32,128]{3,2,1,0:T(8,128)S(1)}, f32[4,2,32,128]{3,2,1,0:T(8,128)S(1)}, u32[]{:S(2)}, u32[]{:S(2)}) collective-permute-start(f32[4,2,32,128]{3,2,1,0:T(8,128)S(1)} %get-tuple-element.53), channel_id=1, source_target_pairs={{0,3},{1,2},{2,1},{3,0},{4,7},{5,6},{6,5},{7,4},{8,11},{9,10},{10,... | collective-permute-start | bytes 393224 | tf_op jit(solution)/shard_map/ppermute | solution.py:494

commit v10 on v8

--- a/solution.py
+++ b/solution.py
@@ -63,7 +63,7 @@
             tail_ref[i, q] = tail
 
 
-def coupling_kernel(modes, coef_ref, row_ref, col_ref, mult_ref, out_ref, stencil_ref):
+def coupling_kernel(modes, coef_ref, row_ref, col_ref, mult_ref, _, out_ref, stencil_ref):
     rows, cols = out_ref.shape
     triples = coef_ref.shape[1]
     key = coef_ref[...] * modes + row_ref[...]
@@ -195,40 +195,40 @@
         return jnp.broadcast_to(jnp.sum(x, axis=(0, 1), keepdims=True), (8, LANES))
 
 
-def early_kernel(n, plane, place_ref, jac_ref, coup_ref, *refs):
-    near_refs, (v_ref, a_ref, gather_ref, vs_ref, mx_ref) = refs[:plane], refs[plane:]
-    early = v_ref.shape[0]
+def late_kernel(n, early, jac_ref, coup_ref, r_ref, v_ref, a_ref, vs_ref, mx_ref):
+    late = v_ref.shape[0]
+    for ct in range(late):
+        for s in range(S):
+            v_ref[ct, s] = r_ref[pl.ds(ct * S + s, n, stride=late * S), :]
+
+    def get(ct, t):
+        return v_ref[ct, t]
+
+    def finisher(ct):
+        def finish(s, k, acc):
+            a_ref[ct, s, k : k + 8] = acc
+
+        return finish
+
+    if late > 1:
+        run(mix(get, 0, 0, coup_ref, vs_ref, mx_ref))
+    for ct in range(late - 1):
+        steps = mix(get, ct + 1, (ct + 1) % 2, coup_ref, vs_ref, mx_ref) if ct + 2 < late else []
+        react(n, tile_of(jac_ref, early + ct), ct % 2, mx_ref, finisher(ct), steps)
+
+
+def first_kernel(n, tiles, plane, place_ref, dif_ref, vl_ref, al_ref, jac_ref, coup_ref, stencil_ref, *refs):
+    every = tiles + 1
+    near_refs, (v_ref, w_ref, sum_ref), refs = refs[:plane], refs[plane : plane + 3], refs[plane + 3 :]
+    send_refs, (gather_ref, vs_ref, xs_ref, mx_ref, bs_ref) = refs[: n // GROUP], refs[n // GROUP :]
+    early = every - vl_ref.shape[0]
     gather_kernel(place_ref, *near_refs, gather_ref)
     flat = gather_ref.reshape(n * early * S, LANES)
     for ct in range(early):
         for s in range(S):
             v_ref[ct, s] = flat[pl.ds(ct * S + s, n, stride=early * S), :]
-
-    def get(ct, t):
-        return v_ref[ct, t]
-
-    def finisher(ct):
-        def finish(s, k, acc):
-            a_ref[ct, s, k : k + 8] = acc
-
-        return finish
-
-    run(mix(get, 0, 0, coup_ref, vs_ref, mx_ref))
-    for ct in range(early):
-        steps = mix(get, ct + 1, (ct + 1) % 2, coup_ref, vs_ref, mx_ref) if ct + 1 < early else []
-        react(n, tile_of(jac_ref, ct), ct % 2, mx_ref, finisher(ct), steps)
-
-
-def first_kernel(n, tiles, place_ref, dif_ref, r_ref, ve_ref, ae_ref, jac_ref, coup_ref, stencil_ref, *refs):
-    every = tiles + 1
-    (v_ref, w_ref, sum_ref), refs = refs[:3], refs[3:]
-    send_refs, (vs_ref, xs_ref, mx_ref, bs_ref) = refs[: n // GROUP], refs[n // GROUP :]
-    early = ve_ref.shape[0]
-    for ct in range(early):
-        v_ref[ct] = ve_ref[ct]
     for ct in range(early, every):
-        for s in range(S):
-            v_ref[ct, s] = r_ref[pl.ds((ct - early) * S + s, n, stride=(every - early) * S), :]
+        v_ref[ct] = vl_ref[ct - early]
     sums = Sums()
 
     def get(ct, t):
@@ -253,19 +253,16 @@
     def close(ct, slot):
         for s in range(S):
             for k in range(0, n, 8):
-                finisher(ct, slot)(s, k, ae_ref[ct, s, k : k + 8])
-
-    spare = tiles % 2
+                finisher(ct, slot)(s, k, al_ref[ct - early, s, k : k + 8])
+
+    spare = early % 2
     rest = []
+    for ct in range(early, tiles):
+        rest += sides(ct, spare) + [functools.partial(close, ct, spare)]
+    run(prepare(0))
     for ct in range(early):
-        rest += sides(ct, spare) + [functools.partial(close, ct, spare)]
-    if early < tiles:
-        run(prepare(early))
-    for ct in range(early, tiles):
-        steps = prepare(ct + 1) if ct + 1 < tiles else rest
+        steps = prepare(ct + 1) if ct + 1 < early else rest
         react(n, tile_of(jac_ref, ct), ct % 2, mx_ref, finisher(ct, ct % 2), steps)
-    if early == tiles:
-        run(rest)
     for q in range(n // GROUP):
         at = pl.multiple_of(jnp.bitwise_xor(place_ref[0], q) * GROUP, GROUP)
         flat = send_refs[q].reshape(GROUP * tiles * S, LANES)
@@ -443,7 +440,7 @@
     index = lax.axis_index("modes")
     place = jnp.stack([index // plane, index % plane]).astype(jnp.int32)
 
-    early = (tiles + 1) // 2
+    early = (3 * tiles + 3) // 4
     block = (plane, own, early * S, LANES)
 
     def across(arrays):
@@ -496,11 +493,11 @@
     coupling, stencil = pl.pallas_call(
         functools.partial(coupling_kernel, n),
         out_shape=[sds((NCOEF * n, 3 * n), BF16), sds((4 * LANES, LANES), BF16)],
-        in_specs=[VMEM] * 4,
+        in_specs=[VMEM] * 4 + [pl.BlockSpec(memory_space=pl.ANY)],
         out_specs=[VMEM] * 2,
         compiler_params=PARAMS,
         name="coupling",
-    )(*(x.reshape(1, -1) for x in (coef_index, row_mode, col_mode, multiplicity)))
+    )(*(x.reshape(1, -1) for x in (coef_index, row_mode, col_mode, multiplicity)), relayed)
 
     jac = jac_coef.reshape(NCOEF * S, S, cells)
     field = (tiles + 1, S, n, LANES)
@@ -510,36 +507,27 @@
         pltpu.VMEM((2, NCOEF * n, S * LANES), F32),
         pltpu.VMEM((2, S * n, LANES), F32),
     ]
-    v_early, a_early = pl.pallas_call(
-        functools.partial(early_kernel, n, plane),
-        out_shape=[sds((early, S, n, LANES), F32)] * 2,
-        in_specs=[smem] + [VMEM] * (2 + plane),
+    late = tiles + 1 - early
+    v_late, a_late = pl.pallas_call(
+        functools.partial(late_kernel, n, early),
+        out_shape=[sds((late, S, n, LANES), F32), sds((max(late - 1, 1), S, n, LANES), F32)],
+        in_specs=[VMEM] * 3,
         out_specs=[VMEM] * 2,
-        scratch_shapes=[pltpu.VMEM((parts, own, early * S, LANES), F32), work[0], work[2]],
+        scratch_shapes=[work[0], work[2]],
         compiler_params=PARAMS,
         cost_estimate=pl.CostEstimate(flops=2 * 10**9, bytes_accessed=1 << 20, transcendentals=0),
-        name="early",
-    )(place, jac, coupling, *near)
+        name="late",
+    )(jac, coupling, vector.reshape(n * late * S, LANES))
     v, w, sums, *w_send = pl.pallas_call(
-        functools.partial(first_kernel, n, tiles),
+        functools.partial(first_kernel, n, tiles, plane),
         out_shape=[sds(field, F32), sds((tiles, S, n, LANES), F32), sds((16, LANES), F32)]
         + [sds((plane, own, tiles * S, LANES), F32)] * (n // GROUP),
-        in_specs=[smem] * 2 + [VMEM] * 6,
+        in_specs=[smem] * 2 + [VMEM] * (5 + plane),
         out_specs=[VMEM] * (3 + n // GROUP),
-        scratch_shapes=work,
+        scratch_shapes=[pltpu.VMEM((parts, own, early * S, LANES), F32)] + work,
         compiler_params=PARAMS,
         name="first",
-    )(
-        place,
-        diffusivity,
-        vector.reshape(n * (tiles + 1 - early) * S, LANES),
-        v_early,
-        a_early,
-        jac,
-        coupling,
-        stencil,
-    )
-
+    )(place, diffusivity, v_late, a_late, jac, coupling, stencil, *near)
     edges = pl.pallas_call(
         unpack_kernel,
         out_shape=sds((NCOEF * S, S, LANES), F32),

time: 63.7 us -> 62.8 us (0.986)
  starting transfers between devices: 30.3 us -> 28 us
  waiting for transfers between devices: 13.4 us -> 15 us
    ppermute x6, waiting for transfers between devices: 11.7 us -> 10 us  [across(): lax.ppermute(relayed[k], 'modes', [(i, i ^ k) for i in range(parts)])]
    ppermute x6, waiting for transfers between devices: 0.02 us -> 1.67 us  [across(): lax.ppermute(arrays[q], 'modes', [(i, i ^ q * plane) for i in range(parts)])]
    all_to_all x1, waiting for transfers between devices: 0.32 us -> 1.93 us  [local(): lax.all_to_all(late_send, 'modes', split_axis=0, concat_axis=0, tiled=True)]
    ppermute x1, starting transfers between devices: 4.48 us -> 3.43 us  [local(): after = lax.ppermute(head, 'modes', down)]
    all_to_all x1, starting transfers between devices: 5.12 us -> 4.29 us  [local(): lax.all_to_all(z_send.reshape(n, 1, line), 'modes', split_axis=0, concat_...]
where the time goes in v10:
time: 62.8 us; the launch traced here: 62.4 us
  starting transfers between devices  28 us (45%)
  Pallas kernels  17.4 us (28%)
  waiting for transfers between devices  15 us (24%)
  local copies, waits for them, and re-layouts  1.07 us (2%)
  between operations  0.85 us (1%)
    ppermute x6, starting transfers between devices, across(): lax.ppermute(arrays[q], 'modes', [(i, i ^ q * plane) for i in range(parts)])  10.1 us
    ppermute x6, waiting for transfers between devices, across(): lax.ppermute(relayed[k], 'modes', [(i, i ^ k) for i in range(parts)])  10 us
    pallas_call x1, Pallas kernels, local(): pl.pallas_call(functools.partial(second_kernel, n, tiles), out_shape=sds(...  7.22 us
    all_to_all x1, starting transfers between devices, local(): lax.all_to_all(late_send, 'modes', split_axis=0, concat_axis=0, tiled=True)  6.16 us
    all_to_all x1, starting transfers between devices, local(): lax.all_to_all(z_send.reshape(n, 1, line), 'modes', split_axis=0, concat_...  4.29 us
    pallas_call x1, Pallas kernels, local(): pl.pallas_call(functools.partial(first_kernel, n, tiles, plane), out_shap...  4.25 us
    ppermute x6, starting transfers between devices, across(): lax.ppermute(relayed[k], 'modes', [(i, i ^ k) for i in range(parts)])  4.09 us
    ppermute x1, starting transfers between devices, local(): after = lax.ppermute(head, 'modes', down)  3.43 us
  transfers between devices with their start and end apart: 16, of which 5 were waited for; matrix products, arithmetic and copies ran while one was open for 0% of the time, Pallas kernels for 24%

profile of v10, /device:TPU:0, one launch (start us, length us, event | category | flops | bytes accessed | tf_op | source)
XLA Modules:
  0.0 62.4 jit_solution(1800162442874182576)
XLA Ops:
  0.6 0.1 pad_add_fusion.place_ref
  0.7 1.0 %copy-done.1 = f32[2,8,8192]{2,1,0:T(8,128)S(1)} copy-done((f32[2,8,8192]{2,1,0:T(8,128)S(1)}, f32[2,8,8192]{2,1,0:T(8,128)}, u32[]{:S(2)}) %copy-start.1) | copy-done | bytes 524312
  1.8 1.3 %arrange.1 = (f32[32,2,8,128]{3,2,1,0:T(8,128)}, f32[4,2,24,128]{3,2,1,0:T(8,128)S(1)}, f32[4,2,24,128]{3,2,1,0:T(8,128)S(1)}, f32[4,2,24,128]{3,2,1,0:T(8,128)S(1)}, f32[4,2,24,128]{3,2,1,0:T(8,128)S(1)}) custom-call(s32[2]{0:T(128)S(1)} %pad_add_fusion.place_ref, f32[2,8,8192]{2,1,0:T(8,128)S(1)} %copy-done.1), custom_call_target="tpu_custom_call" | custom-call | tf_op jit(solution)/shard_map/arrange/pallas_call | solution.py:465
  3.1 3.0 %collective-permute-start = (f32[4,2,24,128]{3,2,1,0:T(8,128)S(1)}, f32[4,2,24,128]{3,2,1,0:T(8,128)S(1)}, u32[]{:S(2)}, u32[]{:S(2)}) collective-permute-start(f32[4,2,24,128]{3,2,1,0:T(8,128)S(1)} %get-tuple-element.29), channel_id=1, source_target_pairs={{0,4},{1,5},{2,6},{3,7},{4,0},{5,1},{6,2},{7,3},{8,12},{9,13},{10,... | collective-permute-start | bytes 294920 | tf_op jit(solution)/shard_map/ppermute | solution.py:450
  6.1 2.6 %collective-permute-start.1 = (f32[4,2,24,128]{3,2,1,0:T(8,128)S(1)}, f32[4,2,24,128]{3,2,1,0:T(8,128)S(1)}, u32[]{:S(2)}, u32[]{:S(2)}) collective-permute-start(f32[4,2,24,128]{3,2,1,0:T(8,128)S(1)} %get-tuple-element.30), channel_id=1, source_target_pairs={{0,8},{1,9},{2,10},{3,11},{4,12},{5,13},{6,14},{7,15},{8,0},{9,1},... | collective-permute-start | bytes 294920 | tf_op jit(solution)/shard_map/ppermute | solution.py:450
  8.7 6.2 %all-to-all-start = ((f32[32,2,8,128]{3,2,1,0:T(8,128)}), f32[32,2,8,128]{3,2,1,0:T(8,128)S(1)}, u32[]{:S(2)}, u32[]{:S(2)}) async-start(f32[32,2,8,128]{3,2,1,0:T(8,128)} %get-tuple-element.34), calls=%async_computation | async-start | bytes 524288 | tf_op jit(solution)/shard_map/all_to_all | solution.py:474
  14.9 1.7 %collective-permute-done.1.refs_2_ = f32[4,2,24,128]{3,2,1,0:T(8,128)S(1)} collective-permute-done((f32[4,2,24,128]{3,2,1,0:T(8,128)S(1)}, f32[4,2,24,128]{3,2,1,0:T(8,128)S(1)}, u32[]{:S(2)}, u32[]{:S(2)}) %collective-permute-start.1) | collective-permute-done | bytes 98336 | tf_op jit(solution)/shard_map/ppermute | solution.py:450
  16.5 0.6 relay.2
  17.1 0.1 collective-permute-start.3
  17.2 1.6 %collective-permute-start.4 = (f32[4,2,24,128]{3,2,1,0:T(8,128)S(1)}, f32[4,2,24,128]{3,2,1,0:T(8,128)S(1)}, u32[]{:S(2)}, u32[]{:S(2)}) collective-permute-start(f32[4,2,24,128]{3,2,1,0:T(8,128)S(1)} %get-tuple-element.39), channel_id=1, source_target_pairs={{0,2},{1,3},{2,0},{3,1},{4,6},{5,7},{6,4},{7,5},{8,10},{9,11},{10,... | collective-permute-start | bytes 294920 | tf_op jit(solution)/shard_map/ppermute | solution.py:462
  18.8 0.3 collective-permute-start.5
  19.1 0.0 copy-start.6
  19.1 0.2 pack.1
  19.3 3.4 %collective-permute-start.6 = (f32[9,2,8,128]{3,2,1,0:T(8,128)S(1)}, f32[9,2,8,128]{3,2,1,0:T(8,128)S(1)}, u32[]{:S(2)}, u32[]{:S(2)}) collective-permute-start(f32[9,2,8,128]{3,2,1,0:T(8,128)S(1)} %get-tuple-element.44), channel_id=1, source_target_pairs={{1,0},{2,1},{3,2},{4,3},{5,4},{6,5},{7,6},{8,7},{9,8},{10,9},{11,1... | collective-permute-start | bytes 221192 | tf_op jit(solution)/shard_map/ppermute | solution.py:491
  22.7 0.3 coupling.1
  23.0 1.9 %all-to-all-done = f32[32,2,8,128]{3,2,1,0:T(8,128)S(1)} async-done(((f32[32,2,8,128]{3,2,1,0:T(8,128)}), f32[32,2,8,128]{3,2,1,0:T(8,128)S(1)}, u32[]{:S(2)}, u32[]{:S(2)}) %all-to-all-start) | async-done | bytes 262176 | tf_op jit(solution)/shard_map/all_to_all | solution.py:474
  24.9 1.0 %late.1 = (f32[2,8,32,128]{3,2,1,0:T(8,128)S(1)}, f32[1,8,32,128]{3,2,1,0:T(8,128)S(1)}) custom-call(f32[72,8,512]{2,1,0:T(8,128)S(1)} %bitcast.10, bf16[288,96]{1,0:T(8,128)(2,1)S(1)} %get-tuple-element.33.coup_ref, f32[512,128]{1,0:T(8,128)S(1)} %bitcast.14), custom_call_target="tpu_custom_call" | custom-call | flops 2000000000 | bytes 1048576 | tf_op jit(solution)/shard_map/late/pallas_call | solution.py:511
  26.0 4.3 %first.1 = (f32[5,8,32,128]{3,2,1,0:T(8,128)S(1)}, f32[4,8,32,128]{3,2,1,0:T(8,128)S(1)}, f32[16,128]{1,0:T(8,128)S(1)}, f32[4,2,32,128]{3,2,1,0:T(8,128)S(1)}, ...) custom-call(s32[2]{0:T(128)S(1)} %pad_add_fusion.place_ref, ...), custom_call_target="tpu_custom_call" | custom-call | tf_op jit(solution)/shard_map/first/pallas_call | solution.py:521
  30.3 2.1 %collective-permute-start.10 = (f32[4,2,32,128]{3,2,1,0:T(8,128)S(1)}, f32[4,2,32,128]{3,2,1,0:T(8,128)S(1)}, u32[]{:S(2)}, u32[]{:S(2)}) collective-permute-start(f32[4,2,32,128]{3,2,1,0:T(8,128)S(1)} %get-tuple-element.49), channel_id=1, source_target_pairs={{0,12},{1,13},{2,14},{3,15},{4,8},{5,9},{6,10},{7,11},{8,4},{9,5},... | collective-permute-start | bytes 393224 | tf_op jit(solution)/shard_map/ppermute | solution.py:450
  32.4 1.5 %collective-permute-start.8 = (f32[4,2,32,128]{3,2,1,0:T(8,128)S(1)}, f32[4,2,32,128]{3,2,1,0:T(8,128)S(1)}, u32[]{:S(2)}, u32[]{:S(2)}) collective-permute-start(f32[4,2,32,128]{3,2,1,0:T(8,128)S(1)} %get-tuple-element.47), channel_id=1, source_target_pairs={{0,4},{1,5},{2,6},{3,7},{4,0},{5,1},{6,2},{7,3},{8,12},{9,13},{10,... | collective-permute-start | bytes 393224 | tf_op jit(solution)/shard_map/ppermute | solution.py:450
  33.8 0.9 %collective-permute-start.9 = (f32[4,2,32,128]{3,2,1,0:T(8,128)S(1)}, f32[4,2,32,128]{3,2,1,0:T(8,128)S(1)}, u32[]{:S(2)}, u32[]{:S(2)}) collective-permute-start(f32[4,2,32,128]{3,2,1,0:T(8,128)S(1)} %get-tuple-element.48), channel_id=1, source_target_pairs={{0,8},{1,9},{2,10},{3,11},{4,12},{5,13},{6,14},{7,15},{8,0},{9,1},... | collective-permute-start | bytes 393224 | tf_op jit(solution)/shard_map/ppermute | solution.py:450
  34.7 0.2 unpack.1.edge_ref
  34.9 7.2 %second.1 = f32[1056,128]{1,0:T(8,128)} custom-call(f32[8]{0:T(128)S(1)} %copy-done.7, f32[5,8,32,128]{3,2,1,0:T(8,128)S(1)} %get-tuple-element.41.v_ref, f32[4,8,32,128]{3,2,1,0:T(8,128)S(1)} %get-tuple-element.42.w_ref, f32[16,128]{1,0:T(8,128)S(1)} %get-tuple-element.43._.sum_ref, f32[72,8,512]{2,1,0:T(8,128)S(1)} %bitcast.12, ...), custom_call_target="tpu_custom_call" | custom-call | flops 10000000000 | bytes 16777216 | tf_op jit(solution)/shard_map/second/pallas_call | solution.py:541
  42.1 4.3 %all-to-all-start.1 = ((f32[32,1,4224]{2,1,0:T(1,128)}), f32[32,1,4224]{2,1,0:T(1,128)S(1)}, u32[]{:S(2)}, u32[]{:S(2)}) async-start(f32[32,1,4224]{2,1,0:T(1,128)} %bitcast.8), calls=%async_computation.1 | async-start | bytes 1081344 | tf_op jit(solution)/shard_map/all_to_all | solution.py:552
  46.5 0.6 relay.3
  47.1 0.5 collective-permute-start.11
  47.5 1.7 %collective-permute-start.12 = (f32[4,2,32,128]{3,2,1,0:T(8,128)S(1)}, f32[4,2,32,128]{3,2,1,0:T(8,128)S(1)}, u32[]{:S(2)}, u32[]{:S(2)}) collective-permute-start(f32[4,2,32,128]{3,2,1,0:T(8,128)S(1)} %get-tuple-element.52), channel_id=1, source_target_pairs={{0,2},{1,3},{2,0},{3,1},{4,6},{5,7},{6,4},{7,5},{8,10},{9,11},{10,... | collective-permute-start | bytes 393224 | tf_op jit(solution)/shard_map/ppermute | solution.py:462
  49.2 7.9 %collective-permute-done.12.refs_2_ = f32[4,2,32,128]{3,2,1,0:T(8,128)S(1)} collective-permute-done((f32[4,2,32,128]{3,2,1,0:T(8,128)S(1)}, f32[4,2,32,128]{3,2,1,0:T(8,128)S(1)}, u32[]{:S(2)}, u32[]{:S(2)}) %collective-permute-start.12) | collective-permute-done | bytes 131104 | tf_op jit(solution)/shard_map/ppermute | solution.py:462
  57.2 2.1 %collective-permute-done.13.refs_3_ = f32[4,2,32,128]{3,2,1,0:T(8,128)S(1)} collective-permute-done((f32[4,2,32,128]{3,2,1,0:T(8,128)S(1)}, f32[4,2,32,128]{3,2,1,0:T(8,128)S(1)}, u32[]{:S(2)}, u32[]{:S(2)}) %collective-permute-start.13) | collective-permute-done | bytes 131104 | tf_op jit(solution)/shard_map/ppermute | solution.py:462
  59.3 0.6 gather.1.w_ref
  59.9 1.3 %all-to-all-done.1 = f32[32,1,4224]{2,1,0:T(1,128)S(1)} async-done(((f32[32,1,4224]{2,1,0:T(1,128)}), f32[32,1,4224]{2,1,0:T(1,128)S(1)}, u32[]{:S(2)}, u32[]{:S(2)}) %all-to-all-start.1) | async-done | bytes 540704 | tf_op jit(solution)/shard_map/all_to_all | solution.py:552
  61.2 1.2 %combine.1 = (f32[2,8,8192]{2,1,0:T(8,128)}, f32[2,8,8192]{2,1,0:T(8,128)}) custom-call(f32[2,8,8192]{2,1,0:T(8,128)S(1)} %copy-done.2, f32[1056,128]{1,0:T(8,128)S(1)} %bitcast.13, f32[16,2,32,128]{3,2,1,0:T(8,128)S(1)} %gather.1.w_ref), custom_call_target="tpu_custom_call" | custom-call | tf_op jit(solution)/shard_map/combine/pallas_call | solution.py:562
  (28 shorter events, 0.1 us)
Async XLA Ops:
  0.7 1.0 %copy-start.1 = (f32[2,8,8192]{2,1,0:T(8,128)S(1)}, f32[2,8,8192]{2,1,0:T(8,128)}, u32[]{:S(2)}) copy-start(f32[2,8,8192]{2,1,0:T(8,128)} %rhs_ref.3) | copy-start | bytes 1572868
  3.1 11.8 %collective-permute-start = (f32[4,2,24,128]{3,2,1,0:T(8,128)S(1)}, f32[4,2,24,128]{3,2,1,0:T(8,128)S(1)}, u32[]{:S(2)}, u32[]{:S(2)}) collective-permute-start(f32[4,2,24,128]{3,2,1,0:T(8,128)S(1)} %get-tuple-element.29), channel_id=1, source_target_pairs={{0,4},{1,5},{2,6},{3,7},{4,0},{5,1},{6,2},{7,3},{8,12},{9,13},{10,... | collective-permute-start | bytes 294920 | tf_op jit(solution)/shard_map/ppermute | solution.py:450
  6.1 10.4 %collective-permute-start.1 = (f32[4,2,24,128]{3,2,1,0:T(8,128)S(1)}, f32[4,2,24,128]{3,2,1,0:T(8,128)S(1)}, u32[]{:S(2)}, u32[]{:S(2)}) collective-permute-start(f32[4,2,24,128]{3,2,1,0:T(8,128)S(1)} %get-tuple-element.30), channel_id=1, source_target_pairs={{0,8},{1,9},{2,10},{3,11},{4,12},{5,13},{6,14},{7,15},{8,0},{9,1},... | collective-permute-start | bytes 294920 | tf_op jit(solution)/shard_map/ppermute | solution.py:450
  8.7 7.8 %collective-permute-start.2 = (f32[4,2,24,128]{3,2,1,0:T(8,128)S(1)}, f32[4,2,24,128]{3,2,1,0:T(8,128)S(1)}, u32[]{:S(2)}, u32[]{:S(2)}) collective-permute-start(f32[4,2,24,128]{3,2,1,0:T(8,128)S(1)} %get-tuple-element.31), channel_id=1, source_target_pairs={{0,12},{1,13},{2,14},{3,15},{4,8},{5,9},{6,10},{7,11},{8,4},{9,5},... | collective-permute-start | bytes 294920 | tf_op jit(solution)/shard_map/ppermute | solution.py:450
  8.7 16.2 %all-to-all-start = ((f32[32,2,8,128]{3,2,1,0:T(8,128)}), f32[32,2,8,128]{3,2,1,0:T(8,128)S(1)}, u32[]{:S(2)}, u32[]{:S(2)}) async-start(f32[32,2,8,128]{3,2,1,0:T(8,128)} %get-tuple-element.34), calls=%async_computation | async-start | bytes 524288 | tf_op jit(solution)/shard_map/all_to_all | solution.py:474
  16.5 2.5 %copy-start = (f32[9,8,8,512]{3,2,1,0:T(8,128)S(1)}, f32[9,8,8,512]{3,2,1,0:T(8,128)}, u32[]{:S(2)}) copy-start(f32[9,8,8,512]{3,2,1,0:T(8,128)} %last_ref.1) | copy-start | bytes 3538948
  17.1 8.9 %collective-permute-start.3 = (f32[4,2,24,128]{3,2,1,0:T(8,128)S(1)}, f32[4,2,24,128]{3,2,1,0:T(8,128)S(1)}, u32[]{:S(2)}, u32[]{:S(2)}) collective-permute-start(f32[4,2,24,128]{3,2,1,0:T(8,128)S(1)} %get-tuple-element.38), channel_id=1, source_target_pairs={{0,1},{1,0},{2,3},{3,2},{4,5},{5,4},{6,7},{7,6},{8,9},{9,8},{10,11... | collective-permute-start | bytes 294920 | tf_op jit(solution)/shard_map/ppermute | solution.py:462
  17.2 8.8 %collective-permute-start.4 = (f32[4,2,24,128]{3,2,1,0:T(8,128)S(1)}, f32[4,2,24,128]{3,2,1,0:T(8,128)S(1)}, u32[]{:S(2)}, u32[]{:S(2)}) collective-permute-start(f32[4,2,24,128]{3,2,1,0:T(8,128)S(1)} %get-tuple-element.39), channel_id=1, source_target_pairs={{0,2},{1,3},{2,0},{3,1},{4,6},{5,7},{6,4},{7,5},{8,10},{9,11},{10,... | collective-permute-start | bytes 294920 | tf_op jit(solution)/shard_map/ppermute | solution.py:462
  18.8 7.2 %collective-permute-start.5 = (f32[4,2,24,128]{3,2,1,0:T(8,128)S(1)}, f32[4,2,24,128]{3,2,1,0:T(8,128)S(1)}, u32[]{:S(2)}, u32[]{:S(2)}) collective-permute-start(f32[4,2,24,128]{3,2,1,0:T(8,128)S(1)} %get-tuple-element.40), channel_id=1, source_target_pairs={{0,3},{1,2},{2,1},{3,0},{4,7},{5,6},{6,5},{7,4},{8,11},{9,10},{10,... | collective-permute-start | bytes 294920 | tf_op jit(solution)/shard_map/ppermute | solution.py:462
  19.1 3.6 %copy-start.3 = (s32[512]{0:T(512)S(1)}, s32[512]{0:T(512)}, u32[]{:S(2)}) copy-start(s32[512]{0:T(512)} %param.10) | copy-start | bytes 6148
  19.1 3.6 %copy-start.4 = (s32[512]{0:T(512)S(1)}, s32[512]{0:T(512)}, u32[]{:S(2)}) copy-start(s32[512]{0:T(512)} %param.11) | copy-start | bytes 6148
  19.1 3.7 %copy-start.5 = (s32[512]{0:T(512)S(1)}, s32[512]{0:T(512)}, u32[]{:S(2)}) copy-start(s32[512]{0:T(512)} %param.12) | copy-start | bytes 6148
  19.1 3.7 %copy-start.6 = (s32[512]{0:T(512)S(1)}, s32[512]{0:T(512)}, u32[]{:S(2)}) copy-start(s32[512]{0:T(512)} %param.13) | copy-start | bytes 6148
  19.3 15.5 %collective-permute-start.6 = (f32[9,2,8,128]{3,2,1,0:T(8,128)S(1)}, f32[9,2,8,128]{3,2,1,0:T(8,128)S(1)}, u32[]{:S(2)}, u32[]{:S(2)}) collective-permute-start(f32[9,2,8,128]{3,2,1,0:T(8,128)S(1)} %get-tuple-element.44), channel_id=1, source_target_pairs={{1,0},{2,1},{3,2},{4,3},{5,4},{6,5},{7,6},{8,7},{9,8},{10,9},{11,1... | collective-permute-start | bytes 221192 | tf_op jit(solution)/shard_map/ppermute | solution.py:491
  22.7 12.0 %collective-permute-start.7 = (f32[9,2,8,128]{3,2,1,0:T(8,128)S(1)}, f32[9,2,8,128]{3,2,1,0:T(8,128)S(1)}, u32[]{:S(2)}, u32[]{:S(2)}) collective-permute-start(f32[9,2,8,128]{3,2,1,0:T(8,128)S(1)} %get-tuple-element.45), channel_id=1, source_target_pairs={{0,1},{1,2},{2,3},{3,4},{4,5},{5,6},{6,7},{7,8},{8,9},{9,10},{10,1... | collective-permute-start | bytes 221192 | tf_op jit(solution)/shard_map/ppermute | solution.py:492
  24.9 1.1 %copy-start.7 = (f32[8]{0:T(128)S(1)}, f32[8]{0:T(128)}, u32[]{:S(2)}) copy-start(f32[8]{0:T(128)} %dif_ref.3) | copy-start | bytes 100
  30.3 16.2 %collective-permute-start.10 = (f32[4,2,32,128]{3,2,1,0:T(8,128)S(1)}, f32[4,2,32,128]{3,2,1,0:T(8,128)S(1)}, u32[]{:S(2)}, u32[]{:S(2)}) collective-permute-start(f32[4,2,32,128]{3,2,1,0:T(8,128)S(1)} %get-tuple-element.49), channel_id=1, source_target_pairs={{0,12},{1,13},{2,14},{3,15},{4,8},{5,9},{6,10},{7,11},{8,4},{9,5},... | collective-permute-start | bytes 393224 | tf_op jit(solution)/shard_map/ppermute | solution.py:450
  32.4 14.1 %collective-permute-start.8 = (f32[4,2,32,128]{3,2,1,0:T(8,128)S(1)}, f32[4,2,32,128]{3,2,1,0:T(8,128)S(1)}, u32[]{:S(2)}, u32[]{:S(2)}) collective-permute-start(f32[4,2,32,128]{3,2,1,0:T(8,128)S(1)} %get-tuple-element.47), channel_id=1, source_target_pairs={{0,4},{1,5},{2,6},{3,7},{4,0},{5,1},{6,2},{7,3},{8,12},{9,13},{10,... | collective-permute-start | bytes 393224 | tf_op jit(solution)/shard_map/ppermute | solution.py:450
  33.8 12.6 %collective-permute-start.9 = (f32[4,2,32,128]{3,2,1,0:T(8,128)S(1)}, f32[4,2,32,128]{3,2,1,0:T(8,128)S(1)}, u32[]{:S(2)}, u32[]{:S(2)}) collective-permute-start(f32[4,2,32,128]{3,2,1,0:T(8,128)S(1)} %get-tuple-element.48), channel_id=1, source_target_pairs={{0,8},{1,9},{2,10},{3,11},{4,12},{5,13},{6,14},{7,15},{8,0},{9,1},... | collective-permute-start | bytes 393224 | tf_op jit(solution)/shard_map/ppermute | solution.py:450
  42.1 19.1 %all-to-all-start.1 = ((f32[32,1,4224]{2,1,0:T(1,128)}), f32[32,1,4224]{2,1,0:T(1,128)S(1)}, u32[]{:S(2)}, u32[]{:S(2)}) async-start(f32[32,1,4224]{2,1,0:T(1,128)} %bitcast.8), calls=%async_computation.1 | async-start | bytes 1081344 | tf_op jit(solution)/shard_map/all_to_all | solution.py:552
  47.1 14.1 %copy-start.2 = (f32[2,8,8192]{2,1,0:T(8,128)S(1)}, f32[2,8,8192]{2,1,0:T(8,128)}, u32[]{:S(2)}) copy-start(f32[2,8,8192]{2,1,0:T(8,128)} %rhs_ref.3) | copy-start | bytes 1572868
  47.1 2.2 %collective-permute-start.11 = (f32[4,2,32,128]{3,2,1,0:T(8,128)S(1)}, f32[4,2,32,128]{3,2,1,0:T(8,128)S(1)}, u32[]{:S(2)}, u32[]{:S(2)}) collective-permute-start(f32[4,2,32,128]{3,2,1,0:T(8,128)S(1)} %get-tuple-element.51), channel_id=1, source_target_pairs={{0,1},{1,0},{2,3},{3,2},{4,5},{5,4},{6,7},{7,6},{8,9},{9,8},{10,11... | collective-permute-start | bytes 393224 | tf_op jit(solution)/shard_map/ppermute | solution.py:462
  47.5 9.6 %collective-permute-start.12 = (f32[4,2,32,128]{3,2,1,0:T(8,128)S(1)}, f32[4,2,32,128]{3,2,1,0:T(8,128)S(1)}, u32[]{:S(2)}, u32[]{:S(2)}) collective-permute-start(f32[4,2,32,128]{3,2,1,0:T(8,128)S(1)} %get-tuple-element.52), channel_id=1, source_target_pairs={{0,2},{1,3},{2,0},{3,1},{4,6},{5,7},{6,4},{7,5},{8,10},{9,11},{10,... | collective-permute-start | bytes 393224 | tf_op jit(solution)/shard_map/ppermute | solution.py:462
  49.2 10.0 %collective-permute-start.13 = (f32[4,2,32,128]{3,2,1,0:T(8,128)S(1)}, f32[4,2,32,128]{3,2,1,0:T(8,128)S(1)}, u32[]{:S(2)}, u32[]{:S(2)}) collective-permute-start(f32[4,2,32,128]{3,2,1,0:T(8,128)S(1)} %get-tuple-element.53), channel_id=1, source_target_pairs={{0,3},{1,2},{2,1},{3,0},{4,7},{5,6},{6,5},{7,4},{8,11},{9,10},{10,... | collective-permute-start | bytes 393224 | tf_op jit(solution)/shard_map/ppermute | solution.py:462

commit v11 on v10

--- a/solution.py
+++ b/solution.py
@@ -182,6 +182,10 @@
     return lambda row, t: jac_ref[row, t : t + 1, ct * LANES : (ct + 1) * LANES]
 
 
+def spread_sum(x):
+    return jnp.broadcast_to(jnp.sum(x, axis=(0, 1), keepdims=True), (8, LANES))
+
+
 class Sums:
     def __init__(self):
         self.parts = {}
@@ -190,9 +194,11 @@
         mine = self.parts.setdefault(name, {})
         mine[at % 4] = mine[at % 4] + term if at % 4 in mine else term
 
+    def partial(self, name):
+        return functools.reduce(lambda a, b: a + b, self.parts[name].values())
+
     def total(self, name):
-        x = functools.reduce(lambda a, b: a + b, self.parts[name].values())
-        return jnp.broadcast_to(jnp.sum(x, axis=(0, 1), keepdims=True), (8, LANES))
+        return spread_sum(self.partial(name))
 
 
 def late_kernel(n, early, jac_ref, coup_ref, r_ref, v_ref, a_ref, vs_ref, mx_ref):
@@ -255,22 +261,24 @@
             for k in range(0, n, 8):
                 finisher(ct, slot)(s, k, al_ref[ct - early, s, k : k + 8])
 
+    def pack(ct):
+        for q in range(n // GROUP):
+            at = pl.multiple_of(jnp.bitwise_xor(place_ref[0], q) * GROUP, GROUP)
+            flat = send_refs[q].reshape(GROUP * tiles * S, LANES)
+            for s in range(S):
+                flat[pl.ds(ct * S + s, GROUP, stride=tiles * S), :] = w_ref[ct, s, pl.ds(at, GROUP)]
+
     spare = early % 2
     rest = []
     for ct in range(early, tiles):
-        rest += sides(ct, spare) + [functools.partial(close, ct, spare)]
+        rest += sides(ct, spare) + [functools.partial(close, ct, spare), functools.partial(pack, ct)]
     run(prepare(0))
     for ct in range(early):
         steps = prepare(ct + 1) if ct + 1 < early else rest
         react(n, tile_of(jac_ref, ct), ct % 2, mx_ref, finisher(ct, ct % 2), steps)
-    for q in range(n // GROUP):
-        at = pl.multiple_of(jnp.bitwise_xor(place_ref[0], q) * GROUP, GROUP)
-        flat = send_refs[q].reshape(GROUP * tiles * S, LANES)
-        for ct in range(tiles):
-            for s in range(S):
-                flat[pl.ds(ct * S + s, GROUP, stride=tiles * S), :] = w_ref[ct, s, pl.ds(at, GROUP)]
-    sum_ref[0:8] = sums.total("rr")
-    sum_ref[8:16] = sums.total("rw")
+        pack(ct)
+    sum_ref[0:8] = sums.partial("rr")
+    sum_ref[8:16] = sums.partial("rw")
 
 
 def second_kernel(
@@ -294,7 +302,7 @@
 ):
     every = tiles + 1
     per = tiles * S + 1
-    rr, rw = sum_ref[0:8], sum_ref[8:16]
+    rr, rw = spread_sum(sum_ref[0:8]), spread_sum(sum_ref[8:16])
     c1 = ratio(rw, rr)
     sums = Sums()
 

time: 62.8 us -> 62.8 us (level)
  no operation moved by 1% of the time
where the time goes in v11:
time: 62.8 us; the launch traced here: 62.4 us
  starting transfers between devices  28 us (45%)
  Pallas kernels  17.4 us (28%)
  waiting for transfers between devices  15 us (24%)
  local copies, waits for them, and re-layouts  1.07 us (2%)
  between operations  0.85 us (1%)
    ppermute x6, starting transfers between devices, across(): lax.ppermute(arrays[q], 'modes', [(i, i ^ q * plane) for i in range(parts)])  10.1 us
    ppermute x6, waiting for transfers between devices, across(): lax.ppermute(relayed[k], 'modes', [(i, i ^ k) for i in range(parts)])  10 us
    pallas_call x1, Pallas kernels, local(): pl.pallas_call(functools.partial(second_kernel, n, tiles), out_shape=sds(...  7.18 us
    all_to_all x1, starting transfers between devices, local(): lax.all_to_all(late_send, 'modes', split_axis=0, concat_axis=0, tiled=True)  6.16 us
    all_to_all x1, starting transfers between devices, local(): lax.all_to_all(z_send.reshape(n, 1, line), 'modes', split_axis=0, concat_...  4.29 us
    pallas_call x1, Pallas kernels, local(): pl.pallas_call(functools.partial(first_kernel, n, tiles, plane), out_shap...  4.25 us
    ppermute x6, starting transfers between devices, across(): lax.ppermute(relayed[k], 'modes', [(i, i ^ k) for i in range(parts)])  4.09 us
    ppermute x1, starting transfers between devices, local(): after = lax.ppermute(head, 'modes', down)  3.43 us
  transfers between devices with their start and end apart: 16, of which 5 were waited for; matrix products, arithmetic and copies ran while one was open for 0% of the time, Pallas kernels for 24%

profile of v11, /device:TPU:0, one launch (start us, length us, event | category | flops | bytes accessed | tf_op | source)
XLA Modules:
  0.0 62.4 jit_solution(13344133026693541743)
XLA Ops:
  0.6 0.1 pad_add_fusion.place_ref
  0.7 1.0 %copy-done.1 = f32[2,8,8192]{2,1,0:T(8,128)S(1)} copy-done((f32[2,8,8192]{2,1,0:T(8,128)S(1)}, f32[2,8,8192]{2,1,0:T(8,128)}, u32[]{:S(2)}) %copy-start.1) | copy-done | bytes 524312
  1.8 1.3 %arrange.1 = (f32[32,2,8,128]{3,2,1,0:T(8,128)}, f32[4,2,24,128]{3,2,1,0:T(8,128)S(1)}, f32[4,2,24,128]{3,2,1,0:T(8,128)S(1)}, f32[4,2,24,128]{3,2,1,0:T(8,128)S(1)}, f32[4,2,24,128]{3,2,1,0:T(8,128)S(1)}) custom-call(s32[2]{0:T(128)S(1)} %pad_add_fusion.place_ref, f32[2,8,8192]{2,1,0:T(8,128)S(1)} %copy-done.1), custom_call_target="tpu_custom_call" | custom-call | tf_op jit(solution)/shard_map/arrange/pallas_call | solution.py:473
  3.1 3.0 %collective-permute-start = (f32[4,2,24,128]{3,2,1,0:T(8,128)S(1)}, f32[4,2,24,128]{3,2,1,0:T(8,128)S(1)}, u32[]{:S(2)}, u32[]{:S(2)}) collective-permute-start(f32[4,2,24,128]{3,2,1,0:T(8,128)S(1)} %get-tuple-element.29), channel_id=1, source_target_pairs={{0,4},{1,5},{2,6},{3,7},{4,0},{5,1},{6,2},{7,3},{8,12},{9,13},{10,... | collective-permute-start | bytes 294920 | tf_op jit(solution)/shard_map/ppermute | solution.py:458
  6.1 2.6 %collective-permute-start.1 = (f32[4,2,24,128]{3,2,1,0:T(8,128)S(1)}, f32[4,2,24,128]{3,2,1,0:T(8,128)S(1)}, u32[]{:S(2)}, u32[]{:S(2)}) collective-permute-start(f32[4,2,24,128]{3,2,1,0:T(8,128)S(1)} %get-tuple-element.30), channel_id=1, source_target_pairs={{0,8},{1,9},{2,10},{3,11},{4,12},{5,13},{6,14},{7,15},{8,0},{9,1},... | collective-permute-start | bytes 294920 | tf_op jit(solution)/shard_map/ppermute | solution.py:458
  8.7 6.2 %all-to-all-start = ((f32[32,2,8,128]{3,2,1,0:T(8,128)}), f32[32,2,8,128]{3,2,1,0:T(8,128)S(1)}, u32[]{:S(2)}, u32[]{:S(2)}) async-start(f32[32,2,8,128]{3,2,1,0:T(8,128)} %get-tuple-element.34), calls=%async_computation | async-start | bytes 524288 | tf_op jit(solution)/shard_map/all_to_all | solution.py:482
  14.9 1.7 %collective-permute-done.1.refs_2_ = f32[4,2,24,128]{3,2,1,0:T(8,128)S(1)} collective-permute-done((f32[4,2,24,128]{3,2,1,0:T(8,128)S(1)}, f32[4,2,24,128]{3,2,1,0:T(8,128)S(1)}, u32[]{:S(2)}, u32[]{:S(2)}) %collective-permute-start.1) | collective-permute-done | bytes 98336 | tf_op jit(solution)/shard_map/ppermute | solution.py:458
  16.5 0.6 relay.2
  17.1 0.1 collective-permute-start.3
  17.2 1.6 %collective-permute-start.4 = (f32[4,2,24,128]{3,2,1,0:T(8,128)S(1)}, f32[4,2,24,128]{3,2,1,0:T(8,128)S(1)}, u32[]{:S(2)}, u32[]{:S(2)}) collective-permute-start(f32[4,2,24,128]{3,2,1,0:T(8,128)S(1)} %get-tuple-element.39), channel_id=1, source_target_pairs={{0,2},{1,3},{2,0},{3,1},{4,6},{5,7},{6,4},{7,5},{8,10},{9,11},{10,... | collective-permute-start | bytes 294920 | tf_op jit(solution)/shard_map/ppermute | solution.py:470
  18.8 0.3 collective-permute-start.5
  19.1 0.2 pack.1
  19.3 3.4 %collective-permute-start.6 = (f32[9,2,8,128]{3,2,1,0:T(8,128)S(1)}, f32[9,2,8,128]{3,2,1,0:T(8,128)S(1)}, u32[]{:S(2)}, u32[]{:S(2)}) collective-permute-start(f32[9,2,8,128]{3,2,1,0:T(8,128)S(1)} %get-tuple-element.44), channel_id=1, source_target_pairs={{1,0},{2,1},{3,2},{4,3},{5,4},{6,5},{7,6},{8,7},{9,8},{10,9},{11,1... | collective-permute-start | bytes 221192 | tf_op jit(solution)/shard_map/ppermute | solution.py:499
  22.7 0.3 coupling.1
  23.0 1.9 %all-to-all-done = f32[32,2,8,128]{3,2,1,0:T(8,128)S(1)} async-done(((f32[32,2,8,128]{3,2,1,0:T(8,128)}), f32[32,2,8,128]{3,2,1,0:T(8,128)S(1)}, u32[]{:S(2)}, u32[]{:S(2)}) %all-to-all-start) | async-done | bytes 262176 | tf_op jit(solution)/shard_map/all_to_all | solution.py:482
  24.9 1.0 %late.1 = (f32[2,8,32,128]{3,2,1,0:T(8,128)S(1)}, f32[1,8,32,128]{3,2,1,0:T(8,128)S(1)}) custom-call(f32[72,8,512]{2,1,0:T(8,128)S(1)} %bitcast.10, bf16[288,96]{1,0:T(8,128)(2,1)S(1)} %get-tuple-element.33.coup_ref, f32[512,128]{1,0:T(8,128)S(1)} %bitcast.14), custom_call_target="tpu_custom_call" | custom-call | flops 2000000000 | bytes 1048576 | tf_op jit(solution)/shard_map/late/pallas_call | solution.py:519
  26.0 4.3 %first.1 = (f32[5,8,32,128]{3,2,1,0:T(8,128)S(1)}, f32[4,8,32,128]{3,2,1,0:T(8,128)S(1)}, f32[16,128]{1,0:T(8,128)S(1)}, f32[4,2,32,128]{3,2,1,0:T(8,128)S(1)}, ...) custom-call(s32[2]{0:T(128)S(1)} %pad_add_fusion.place_ref, ...), custom_call_target="tpu_custom_call" | custom-call | tf_op jit(solution)/shard_map/first/pallas_call | solution.py:529
  30.3 2.1 %collective-permute-start.10 = (f32[4,2,32,128]{3,2,1,0:T(8,128)S(1)}, f32[4,2,32,128]{3,2,1,0:T(8,128)S(1)}, u32[]{:S(2)}, u32[]{:S(2)}) collective-permute-start(f32[4,2,32,128]{3,2,1,0:T(8,128)S(1)} %get-tuple-element.49), channel_id=1, source_target_pairs={{0,12},{1,13},{2,14},{3,15},{4,8},{5,9},{6,10},{7,11},{8,4},{9,5},... | collective-permute-start | bytes 393224 | tf_op jit(solution)/shard_map/ppermute | solution.py:458
  32.4 1.5 %collective-permute-start.8 = (f32[4,2,32,128]{3,2,1,0:T(8,128)S(1)}, f32[4,2,32,128]{3,2,1,0:T(8,128)S(1)}, u32[]{:S(2)}, u32[]{:S(2)}) collective-permute-start(f32[4,2,32,128]{3,2,1,0:T(8,128)S(1)} %get-tuple-element.47), channel_id=1, source_target_pairs={{0,4},{1,5},{2,6},{3,7},{4,0},{5,1},{6,2},{7,3},{8,12},{9,13},{10,... | collective-permute-start | bytes 393224 | tf_op jit(solution)/shard_map/ppermute | solution.py:458
  33.8 0.9 %collective-permute-start.9 = (f32[4,2,32,128]{3,2,1,0:T(8,128)S(1)}, f32[4,2,32,128]{3,2,1,0:T(8,128)S(1)}, u32[]{:S(2)}, u32[]{:S(2)}) collective-permute-start(f32[4,2,32,128]{3,2,1,0:T(8,128)S(1)} %get-tuple-element.48), channel_id=1, source_target_pairs={{0,8},{1,9},{2,10},{3,11},{4,12},{5,13},{6,14},{7,15},{8,0},{9,1},... | collective-permute-start | bytes 393224 | tf_op jit(solution)/shard_map/ppermute | solution.py:458
  34.7 0.2 unpack.1.edge_ref
  34.9 7.2 %second.1 = f32[1056,128]{1,0:T(8,128)} custom-call(f32[8]{0:T(128)S(1)} %copy-done.7, f32[5,8,32,128]{3,2,1,0:T(8,128)S(1)} %get-tuple-element.41.v_ref, f32[4,8,32,128]{3,2,1,0:T(8,128)S(1)} %get-tuple-element.42.w_ref, f32[16,128]{1,0:T(8,128)S(1)} %get-tuple-element.43._.sum_ref, f32[72,8,512]{2,1,0:T(8,128)S(1)} %bitcast.12, ...), custom_call_target="tpu_custom_call" | custom-call | flops 10000000000 | bytes 16777216 | tf_op jit(solution)/shard_map/second/pallas_call | solution.py:549
  42.1 4.3 %all-to-all-start.1 = ((f32[32,1,4224]{2,1,0:T(1,128)}), f32[32,1,4224]{2,1,0:T(1,128)S(1)}, u32[]{:S(2)}, u32[]{:S(2)}) async-start(f32[32,1,4224]{2,1,0:T(1,128)} %bitcast.8), calls=%async_computation.1 | async-start | bytes 1081344 | tf_op jit(solution)/shard_map/all_to_all | solution.py:560
  46.4 0.6 relay.3
  47.0 0.0 copy-start.2
  47.0 0.5 collective-permute-start.11
  47.5 1.7 %collective-permute-start.12 = (f32[4,2,32,128]{3,2,1,0:T(8,128)S(1)}, f32[4,2,32,128]{3,2,1,0:T(8,128)S(1)}, u32[]{:S(2)}, u32[]{:S(2)}) collective-permute-start(f32[4,2,32,128]{3,2,1,0:T(8,128)S(1)} %get-tuple-element.52), channel_id=1, source_target_pairs={{0,2},{1,3},{2,0},{3,1},{4,6},{5,7},{6,4},{7,5},{8,10},{9,11},{10,... | collective-permute-start | bytes 393224 | tf_op jit(solution)/shard_map/ppermute | solution.py:470
  49.2 7.9 %collective-permute-done.12.refs_2_ = f32[4,2,32,128]{3,2,1,0:T(8,128)S(1)} collective-permute-done((f32[4,2,32,128]{3,2,1,0:T(8,128)S(1)}, f32[4,2,32,128]{3,2,1,0:T(8,128)S(1)}, u32[]{:S(2)}, u32[]{:S(2)}) %collective-permute-start.12) | collective-permute-done | bytes 131104 | tf_op jit(solution)/shard_map/ppermute | solution.py:470
  57.1 2.1 %collective-permute-done.13.refs_3_ = f32[4,2,32,128]{3,2,1,0:T(8,128)S(1)} collective-permute-done((f32[4,2,32,128]{3,2,1,0:T(8,128)S(1)}, f32[4,2,32,128]{3,2,1,0:T(8,128)S(1)}, u32[]{:S(2)}, u32[]{:S(2)}) %collective-permute-start.13) | collective-permute-done | bytes 131104 | tf_op jit(solution)/shard_map/ppermute | solution.py:470
  59.2 0.6 gather.1.w_ref
  59.8 1.3 %all-to-all-done.1 = f32[32,1,4224]{2,1,0:T(1,128)S(1)} async-done(((f32[32,1,4224]{2,1,0:T(1,128)}), f32[32,1,4224]{2,1,0:T(1,128)S(1)}, u32[]{:S(2)}, u32[]{:S(2)}) %all-to-all-start.1) | async-done | bytes 540704 | tf_op jit(solution)/shard_map/all_to_all | solution.py:560
  61.2 1.2 %combine.1 = (f32[2,8,8192]{2,1,0:T(8,128)}, f32[2,8,8192]{2,1,0:T(8,128)}) custom-call(f32[2,8,8192]{2,1,0:T(8,128)S(1)} %copy-done.2, f32[1056,128]{1,0:T(8,128)S(1)} %bitcast.13, f32[16,2,32,128]{3,2,1,0:T(8,128)S(1)} %gather.1.w_ref), custom_call_target="tpu_custom_call" | custom-call | tf_op jit(solution)/shard_map/combine/pallas_call | solution.py:570
  (28 shorter events, 0.1 us)
Async XLA Ops:
  0.7 1.0 %copy-start.1 = (f32[2,8,8192]{2,1,0:T(8,128)S(1)}, f32[2,8,8192]{2,1,0:T(8,128)}, u32[]{:S(2)}) copy-start(f32[2,8,8192]{2,1,0:T(8,128)} %rhs_ref.3) | copy-start | bytes 1572868
  3.1 11.8 %collective-permute-start = (f32[4,2,24,128]{3,2,1,0:T(8,128)S(1)}, f32[4,2,24,128]{3,2,1,0:T(8,128)S(1)}, u32[]{:S(2)}, u32[]{:S(2)}) collective-permute-start(f32[4,2,24,128]{3,2,1,0:T(8,128)S(1)} %get-tuple-element.29), channel_id=1, source_target_pairs={{0,4},{1,5},{2,6},{3,7},{4,0},{5,1},{6,2},{7,3},{8,12},{9,13},{10,... | collective-permute-start | bytes 294920 | tf_op jit(solution)/shard_map/ppermute | solution.py:458
  6.1 10.4 %collective-permute-start.1 = (f32[4,2,24,128]{3,2,1,0:T(8,128)S(1)}, f32[4,2,24,128]{3,2,1,0:T(8,128)S(1)}, u32[]{:S(2)}, u32[]{:S(2)}) collective-permute-start(f32[4,2,24,128]{3,2,1,0:T(8,128)S(1)} %get-tuple-element.30), channel_id=1, source_target_pairs={{0,8},{1,9},{2,10},{3,11},{4,12},{5,13},{6,14},{7,15},{8,0},{9,1},... | collective-permute-start | bytes 294920 | tf_op jit(solution)/shard_map/ppermute | solution.py:458
  8.7 7.8 %collective-permute-start.2 = (f32[4,2,24,128]{3,2,1,0:T(8,128)S(1)}, f32[4,2,24,128]{3,2,1,0:T(8,128)S(1)}, u32[]{:S(2)}, u32[]{:S(2)}) collective-permute-start(f32[4,2,24,128]{3,2,1,0:T(8,128)S(1)} %get-tuple-element.31), channel_id=1, source_target_pairs={{0,12},{1,13},{2,14},{3,15},{4,8},{5,9},{6,10},{7,11},{8,4},{9,5},... | collective-permute-start | bytes 294920 | tf_op jit(solution)/shard_map/ppermute | solution.py:458
  8.7 16.2 %all-to-all-start = ((f32[32,2,8,128]{3,2,1,0:T(8,128)}), f32[32,2,8,128]{3,2,1,0:T(8,128)S(1)}, u32[]{:S(2)}, u32[]{:S(2)}) async-start(f32[32,2,8,128]{3,2,1,0:T(8,128)} %get-tuple-element.34), calls=%async_computation | async-start | bytes 524288 | tf_op jit(solution)/shard_map/all_to_all | solution.py:482
  16.5 2.5 %copy-start = (f32[9,8,8,512]{3,2,1,0:T(8,128)S(1)}, f32[9,8,8,512]{3,2,1,0:T(8,128)}, u32[]{:S(2)}) copy-start(f32[9,8,8,512]{3,2,1,0:T(8,128)} %last_ref.1) | copy-start | bytes 3538948
  17.1 8.9 %collective-permute-start.3 = (f32[4,2,24,128]{3,2,1,0:T(8,128)S(1)}, f32[4,2,24,128]{3,2,1,0:T(8,128)S(1)}, u32[]{:S(2)}, u32[]{:S(2)}) collective-permute-start(f32[4,2,24,128]{3,2,1,0:T(8,128)S(1)} %get-tuple-element.38), channel_id=1, source_target_pairs={{0,1},{1,0},{2,3},{3,2},{4,5},{5,4},{6,7},{7,6},{8,9},{9,8},{10,11... | collective-permute-start | bytes 294920 | tf_op jit(solution)/shard_map/ppermute | solution.py:470
  17.2 8.8 %collective-permute-start.4 = (f32[4,2,24,128]{3,2,1,0:T(8,128)S(1)}, f32[4,2,24,128]{3,2,1,0:T(8,128)S(1)}, u32[]{:S(2)}, u32[]{:S(2)}) collective-permute-start(f32[4,2,24,128]{3,2,1,0:T(8,128)S(1)} %get-tuple-element.39), channel_id=1, source_target_pairs={{0,2},{1,3},{2,0},{3,1},{4,6},{5,7},{6,4},{7,5},{8,10},{9,11},{10,... | collective-permute-start | bytes 294920 | tf_op jit(solution)/shard_map/ppermute | solution.py:470
  18.8 7.2 %collective-permute-start.5 = (f32[4,2,24,128]{3,2,1,0:T(8,128)S(1)}, f32[4,2,24,128]{3,2,1,0:T(8,128)S(1)}, u32[]{:S(2)}, u32[]{:S(2)}) collective-permute-start(f32[4,2,24,128]{3,2,1,0:T(8,128)S(1)} %get-tuple-element.40), channel_id=1, source_target_pairs={{0,3},{1,2},{2,1},{3,0},{4,7},{5,6},{6,5},{7,4},{8,11},{9,10},{10,... | collective-permute-start | bytes 294920 | tf_op jit(solution)/shard_map/ppermute | solution.py:470
  19.1 3.6 %copy-start.3 = (s32[512]{0:T(512)S(1)}, s32[512]{0:T(512)}, u32[]{:S(2)}) copy-start(s32[512]{0:T(512)} %param.10) | copy-start | bytes 6148
  19.1 3.6 %copy-start.4 = (s32[512]{0:T(512)S(1)}, s32[512]{0:T(512)}, u32[]{:S(2)}) copy-start(s32[512]{0:T(512)} %param.11) | copy-start | bytes 6148
  19.1 3.7 %copy-start.5 = (s32[512]{0:T(512)S(1)}, s32[512]{0:T(512)}, u32[]{:S(2)}) copy-start(s32[512]{0:T(512)} %param.12) | copy-start | bytes 6148
  19.1 3.7 %copy-start.6 = (s32[512]{0:T(512)S(1)}, s32[512]{0:T(512)}, u32[]{:S(2)}) copy-start(s32[512]{0:T(512)} %param.13) | copy-start | bytes 6148
  19.3 15.5 %collective-permute-start.6 = (f32[9,2,8,128]{3,2,1,0:T(8,128)S(1)}, f32[9,2,8,128]{3,2,1,0:T(8,128)S(1)}, u32[]{:S(2)}, u32[]{:S(2)}) collective-permute-start(f32[9,2,8,128]{3,2,1,0:T(8,128)S(1)} %get-tuple-element.44), channel_id=1, source_target_pairs={{1,0},{2,1},{3,2},{4,3},{5,4},{6,5},{7,6},{8,7},{9,8},{10,9},{11,1... | collective-permute-start | bytes 221192 | tf_op jit(solution)/shard_map/ppermute | solution.py:499
  22.7 12.0 %collective-permute-start.7 = (f32[9,2,8,128]{3,2,1,0:T(8,128)S(1)}, f32[9,2,8,128]{3,2,1,0:T(8,128)S(1)}, u32[]{:S(2)}, u32[]{:S(2)}) collective-permute-start(f32[9,2,8,128]{3,2,1,0:T(8,128)S(1)} %get-tuple-element.45), channel_id=1, source_target_pairs={{0,1},{1,2},{2,3},{3,4},{4,5},{5,6},{6,7},{7,8},{8,9},{9,10},{10,1... | collective-permute-start | bytes 221192 | tf_op jit(solution)/shard_map/ppermute | solution.py:500
  24.9 1.1 %copy-start.7 = (f32[8]{0:T(128)S(1)}, f32[8]{0:T(128)}, u32[]{:S(2)}) copy-start(f32[8]{0:T(128)} %dif_ref.3) | copy-start | bytes 100
  30.3 16.1 %collective-permute-start.10 = (f32[4,2,32,128]{3,2,1,0:T(8,128)S(1)}, f32[4,2,32,128]{3,2,1,0:T(8,128)S(1)}, u32[]{:S(2)}, u32[]{:S(2)}) collective-permute-start(f32[4,2,32,128]{3,2,1,0:T(8,128)S(1)} %get-tuple-element.49), channel_id=1, source_target_pairs={{0,12},{1,13},{2,14},{3,15},{4,8},{5,9},{6,10},{7,11},{8,4},{9,5},... | collective-permute-start | bytes 393224 | tf_op jit(solution)/shard_map/ppermute | solution.py:458
  32.4 14.0 %collective-permute-start.8 = (f32[4,2,32,128]{3,2,1,0:T(8,128)S(1)}, f32[4,2,32,128]{3,2,1,0:T(8,128)S(1)}, u32[]{:S(2)}, u32[]{:S(2)}) collective-permute-start(f32[4,2,32,128]{3,2,1,0:T(8,128)S(1)} %get-tuple-element.47), channel_id=1, source_target_pairs={{0,4},{1,5},{2,6},{3,7},{4,0},{5,1},{6,2},{7,3},{8,12},{9,13},{10,... | collective-permute-start | bytes 393224 | tf_op jit(solution)/shard_map/ppermute | solution.py:458
  33.8 12.6 %collective-permute-start.9 = (f32[4,2,32,128]{3,2,1,0:T(8,128)S(1)}, f32[4,2,32,128]{3,2,1,0:T(8,128)S(1)}, u32[]{:S(2)}, u32[]{:S(2)}) collective-permute-start(f32[4,2,32,128]{3,2,1,0:T(8,128)S(1)} %get-tuple-element.48), channel_id=1, source_target_pairs={{0,8},{1,9},{2,10},{3,11},{4,12},{5,13},{6,14},{7,15},{8,0},{9,1},... | collective-permute-start | bytes 393224 | tf_op jit(solution)/shard_map/ppermute | solution.py:458
  42.1 19.1 %all-to-all-start.1 = ((f32[32,1,4224]{2,1,0:T(1,128)}), f32[32,1,4224]{2,1,0:T(1,128)S(1)}, u32[]{:S(2)}, u32[]{:S(2)}) async-start(f32[32,1,4224]{2,1,0:T(1,128)} %bitcast.8), calls=%async_computation.1 | async-start | bytes 1081344 | tf_op jit(solution)/shard_map/all_to_all | solution.py:560
  47.0 14.1 %copy-start.2 = (f32[2,8,8192]{2,1,0:T(8,128)S(1)}, f32[2,8,8192]{2,1,0:T(8,128)}, u32[]{:S(2)}) copy-start(f32[2,8,8192]{2,1,0:T(8,128)} %rhs_ref.3) | copy-start | bytes 1572868
  47.0 2.2 %collective-permute-start.11 = (f32[4,2,32,128]{3,2,1,0:T(8,128)S(1)}, f32[4,2,32,128]{3,2,1,0:T(8,128)S(1)}, u32[]{:S(2)}, u32[]{:S(2)}) collective-permute-start(f32[4,2,32,128]{3,2,1,0:T(8,128)S(1)} %get-tuple-element.51), channel_id=1, source_target_pairs={{0,1},{1,0},{2,3},{3,2},{4,5},{5,4},{6,7},{7,6},{8,9},{9,8},{10,11... | collective-permute-start | bytes 393224 | tf_op jit(solution)/shard_map/ppermute | solution.py:470
  47.5 9.6 %collective-permute-start.12 = (f32[4,2,32,128]{3,2,1,0:T(8,128)S(1)}, f32[4,2,32,128]{3,2,1,0:T(8,128)S(1)}, u32[]{:S(2)}, u32[]{:S(2)}) collective-permute-start(f32[4,2,32,128]{3,2,1,0:T(8,128)S(1)} %get-tuple-element.52), channel_id=1, source_target_pairs={{0,2},{1,3},{2,0},{3,1},{4,6},{5,7},{6,4},{7,5},{8,10},{9,11},{10,... | collective-permute-start | bytes 393224 | tf_op jit(solution)/shard_map/ppermute | solution.py:470
  49.2 10.0 %collective-permute-start.13 = (f32[4,2,32,128]{3,2,1,0:T(8,128)S(1)}, f32[4,2,32,128]{3,2,1,0:T(8,128)S(1)}, u32[]{:S(2)}, u32[]{:S(2)}) collective-permute-start(f32[4,2,32,128]{3,2,1,0:T(8,128)S(1)} %get-tuple-element.53), channel_id=1, source_target_pairs={{0,3},{1,2},{2,1},{3,0},{4,7},{5,6},{6,5},{7,4},{8,11},{9,10},{10,... | collective-permute-start | bytes 393224 | tf_op jit(solution)/shard_map/ppermute | solution.py:470

commit v12 on v11

--- a/solution.py
+++ b/solution.py
@@ -367,9 +367,14 @@
         out_ref[pl.ds(k * per + tiles * S, 8, stride=per), :] = tile
 
 
+def flip(arrays):
+    return list(arrays[:1]) + list(arrays[1:])[::-1]
+
+
 def relay_kernel(own, place_ref, *refs):
     parts = GROUP // own
     count = len(refs) - parts
+    refs = flip(refs[:count]) + list(refs[count:])
     for k in range(parts):
         at = jnp.bitwise_xor(place_ref[1], k)
         for q in range(count):
@@ -377,7 +382,7 @@
 
 
 def gather_kernel(place_ref, *refs):
-    near_refs, out_ref = refs[:-1], refs[-1]
+    near_refs, out_ref = flip(refs[:-1]), refs[-1]
     plane = len(near_refs)
     for k in range(plane):
         for q in range(near_refs[k].shape[0]):
@@ -453,9 +458,9 @@
 
     def across(arrays):
         lead, rows = len(arrays), arrays[0].shape[2]
-        come = [arrays[0]]
-        for q in range(1, lead):
-            come.append(lax.ppermute(arrays[q], "modes", [(i, i ^ (q * plane)) for i in range(parts)]))
+        come = [arrays[0]] * lead
+        for q in reversed(range(1, lead)):
+            come[q] = lax.ppermute(arrays[q], "modes", [(i, i ^ (q * plane)) for i in range(parts)])
         relayed = pl.pallas_call(
             functools.partial(relay_kernel, own),
             out_shape=[sds((lead, own, rows, LANES), F32)] * plane,
@@ -464,10 +469,10 @@
             compiler_params=PARAMS,
             cost_estimate=pl.CostEstimate(flops=10**11, bytes_accessed=1 << 20, transcendentals=0),
             name="relay",
-        )(place, *come)
-        out = [relayed[0]]
-        for k in range(1, plane):
-            out.append(lax.ppermute(relayed[k], "modes", [(i, i ^ k) for i in range(parts)]))
+        )(place, *flip(come))
+        out = [relayed[0]] * plane
+        for k in reversed(range(1, plane)):
+            out[k] = lax.ppermute(relayed[k], "modes", [(i, i ^ k) for i in range(parts)])
         return out, relayed[0]
 
     late_send, *early_send = pl.pallas_call(
@@ -535,7 +540,7 @@
         scratch_shapes=[pltpu.VMEM((parts, own, early * S, LANES), F32)] + work,
         compiler_params=PARAMS,
         name="first",
-    )(place, diffusivity, v_late, a_late, jac, coupling, stencil, *near)
+    )(place, diffusivity, v_late, a_late, jac, coupling, stencil, *flip(near))
     edges = pl.pallas_call(
         unpack_kernel,
         out_shape=sds((NCOEF * S, S, LANES), F32),
@@ -566,7 +571,7 @@
         out_specs=VMEM,
         compiler_params=PARAMS,
         name="gather",
-    )(place, *w_own)
+    )(place, *flip(w_own))
     update, basis_next = pl.pallas_call(
         functools.partial(combine_kernel, parts, tiles),
         out_shape=[sds(rhs.shape, F32)] * 2,

time: 62.8 us -> 62.9 us (level)
    all_to_all x1, starting transfers between devices: 4.29 us -> 5.21 us  [local(): lax.all_to_all(z_send.reshape(n, 1, line), 'modes', split_axis=0, concat_...]
    ppermute x6, starting transfers between devices: 10.1 us -> 9.33 us  [across(): lax.ppermute(arrays[q], 'modes', [(i, i ^ q * plane) for i in range(parts)])]
    ppermute x6, waiting for transfers between devices: 10 us -> 10.7 us  [across(): lax.ppermute(relayed[k], 'modes', [(i, i ^ k) for i in range(parts)])]
    all_to_all x1, waiting for transfers between devices: 1.34 us -> 0.68 us  [local(): lax.all_to_all(z_send.reshape(n, 1, line), 'modes', split_axis=0, concat_...]
where the time goes in v12:
time: 62.9 us; the launch traced here: 62.6 us
  starting transfers between devices  28 us (45%)
  Pallas kernels  17.4 us (28%)
  waiting for transfers between devices  15.2 us (24%)
  local copies, waits for them, and re-layouts  1.07 us (2%)
  between operations  0.85 us (1%)
    ppermute x6, waiting for transfers between devices, across(): lax.ppermute(relayed[k], 'modes', [(i, i ^ k) for i in range(parts)])  10.7 us
    ppermute x6, starting transfers between devices, across(): lax.ppermute(arrays[q], 'modes', [(i, i ^ q * plane) for i in range(parts)])  9.33 us
    pallas_call x1, Pallas kernels, local(): pl.pallas_call(functools.partial(second_kernel, n, tiles), out_shape=sds(...  7.19 us
    all_to_all x1, starting transfers between devices, local(): lax.all_to_all(late_send, 'modes', split_axis=0, concat_axis=0, tiled=True)  6.16 us
    all_to_all x1, starting transfers between devices, local(): lax.all_to_all(z_send.reshape(n, 1, line), 'modes', split_axis=0, concat_...  5.21 us
    pallas_call x1, Pallas kernels, local(): pl.pallas_call(functools.partial(first_kernel, n, tiles, plane), out_shap...  4.25 us
    ppermute x6, starting transfers between devices, across(): lax.ppermute(relayed[k], 'modes', [(i, i ^ k) for i in range(parts)])  4.05 us
    ppermute x1, starting transfers between devices, local(): after = lax.ppermute(head, 'modes', down)  3.22 us
  transfers between devices with their start and end apart: 16, of which 5 were waited for; matrix products, arithmetic and copies ran while one was open for 0% of the time, Pallas kernels for 24%

profile of v12, /device:TPU:0, one launch (start us, length us, event | category | flops | bytes accessed | tf_op | source)
XLA Modules:
  0.0 62.6 jit_solution(2366232652374088153)
XLA Ops:
  0.6 0.1 pad_add_fusion.place_ref
  0.7 1.0 %copy-done.1 = f32[2,8,8192]{2,1,0:T(8,128)S(1)} copy-done((f32[2,8,8192]{2,1,0:T(8,128)S(1)}, f32[2,8,8192]{2,1,0:T(8,128)}, u32[]{:S(2)}) %copy-start.1) | copy-done | bytes 524312
  1.8 1.3 %arrange.1 = (f32[32,2,8,128]{3,2,1,0:T(8,128)}, f32[4,2,24,128]{3,2,1,0:T(8,128)S(1)}, f32[4,2,24,128]{3,2,1,0:T(8,128)S(1)}, f32[4,2,24,128]{3,2,1,0:T(8,128)S(1)}, f32[4,2,24,128]{3,2,1,0:T(8,128)S(1)}) custom-call(s32[2]{0:T(128)S(1)} %pad_add_fusion.place_ref, f32[2,8,8192]{2,1,0:T(8,128)S(1)} %copy-done.1), custom_call_target="tpu_custom_call" | custom-call | tf_op jit(solution)/shard_map/arrange/pallas_call | solution.py:478
  3.1 5.0 %collective-permute-start = (f32[4,2,24,128]{3,2,1,0:T(8,128)S(1)}, f32[4,2,24,128]{3,2,1,0:T(8,128)S(1)}, u32[]{:S(2)}, u32[]{:S(2)}) collective-permute-start(f32[4,2,24,128]{3,2,1,0:T(8,128)S(1)} %get-tuple-element.29), channel_id=1, source_target_pairs={{0,12},{1,13},{2,14},{3,15},{4,8},{5,9},{6,10},{7,11},{8,4},{9,5},... | collective-permute-start | bytes 294920 | tf_op jit(solution)/shard_map/ppermute | solution.py:463
  8.1 0.6 collective-permute-start.2
  8.7 6.2 %all-to-all-start = ((f32[32,2,8,128]{3,2,1,0:T(8,128)}), f32[32,2,8,128]{3,2,1,0:T(8,128)S(1)}, u32[]{:S(2)}, u32[]{:S(2)}) async-start(f32[32,2,8,128]{3,2,1,0:T(8,128)} %get-tuple-element.34), calls=%async_computation | async-start | bytes 524288 | tf_op jit(solution)/shard_map/all_to_all | solution.py:487
  14.9 1.5 %collective-permute-done.1.refs_2_ = f32[4,2,24,128]{3,2,1,0:T(8,128)S(1)} collective-permute-done((f32[4,2,24,128]{3,2,1,0:T(8,128)S(1)}, f32[4,2,24,128]{3,2,1,0:T(8,128)S(1)}, u32[]{:S(2)}, u32[]{:S(2)}) %collective-permute-start.1) | collective-permute-done | bytes 98336 | tf_op jit(solution)/shard_map/ppermute | solution.py:463
  16.4 0.6 relay.2
  17.0 0.3 collective-permute-start.3
  17.3 1.3 %collective-permute-start.4 = (f32[4,2,24,128]{3,2,1,0:T(8,128)S(1)}, f32[4,2,24,128]{3,2,1,0:T(8,128)S(1)}, u32[]{:S(2)}, u32[]{:S(2)}) collective-permute-start(f32[4,2,24,128]{3,2,1,0:T(8,128)S(1)} %get-tuple-element.39), channel_id=1, source_target_pairs={{0,2},{1,3},{2,0},{3,1},{4,6},{5,7},{6,4},{7,5},{8,10},{9,11},{10,... | collective-permute-start | bytes 294920 | tf_op jit(solution)/shard_map/ppermute | solution.py:475
  18.6 0.3 collective-permute-start.5
  18.9 0.0 copy-start.6
  18.9 0.2 pack.1
  19.1 3.2 %collective-permute-start.6 = (f32[9,2,8,128]{3,2,1,0:T(8,128)S(1)}, f32[9,2,8,128]{3,2,1,0:T(8,128)S(1)}, u32[]{:S(2)}, u32[]{:S(2)}) collective-permute-start(f32[9,2,8,128]{3,2,1,0:T(8,128)S(1)} %get-tuple-element.44), channel_id=1, source_target_pairs={{1,0},{2,1},{3,2},{4,3},{5,4},{6,5},{7,6},{8,7},{9,8},{10,9},{11,1... | collective-permute-start | bytes 221192 | tf_op jit(solution)/shard_map/ppermute | solution.py:504
  22.4 0.3 coupling.1
  22.6 2.3 %all-to-all-done = f32[32,2,8,128]{3,2,1,0:T(8,128)S(1)} async-done(((f32[32,2,8,128]{3,2,1,0:T(8,128)}), f32[32,2,8,128]{3,2,1,0:T(8,128)S(1)}, u32[]{:S(2)}, u32[]{:S(2)}) %all-to-all-start) | async-done | bytes 262176 | tf_op jit(solution)/shard_map/all_to_all | solution.py:487
  24.9 1.0 %late.1 = (f32[2,8,32,128]{3,2,1,0:T(8,128)S(1)}, f32[1,8,32,128]{3,2,1,0:T(8,128)S(1)}) custom-call(f32[72,8,512]{2,1,0:T(8,128)S(1)} %bitcast.10, bf16[288,96]{1,0:T(8,128)(2,1)S(1)} %get-tuple-element.33.coup_ref, f32[512,128]{1,0:T(8,128)S(1)} %bitcast.14), custom_call_target="tpu_custom_call" | custom-call | flops 2000000000 | bytes 1048576 | tf_op jit(solution)/shard_map/late/pallas_call | solution.py:524
  26.0 4.3 %first.1 = (f32[5,8,32,128]{3,2,1,0:T(8,128)S(1)}, f32[4,8,32,128]{3,2,1,0:T(8,128)S(1)}, f32[16,128]{1,0:T(8,128)S(1)}, f32[4,2,32,128]{3,2,1,0:T(8,128)S(1)}, ...) custom-call(s32[2]{0:T(128)S(1)} %pad_add_fusion.place_ref, ...), custom_call_target="tpu_custom_call" | custom-call | tf_op jit(solution)/shard_map/first/pallas_call | solution.py:534
  30.3 1.7 %collective-permute-start.10 = (f32[4,2,32,128]{3,2,1,0:T(8,128)S(1)}, f32[4,2,32,128]{3,2,1,0:T(8,128)S(1)}, u32[]{:S(2)}, u32[]{:S(2)}) collective-permute-start(f32[4,2,32,128]{3,2,1,0:T(8,128)S(1)} %get-tuple-element.49), channel_id=1, source_target_pairs={{0,4},{1,5},{2,6},{3,7},{4,0},{5,1},{6,2},{7,3},{8,12},{9,13},{10,... | collective-permute-start | bytes 393224 | tf_op jit(solution)/shard_map/ppermute | solution.py:463
  32.0 2.0 %collective-permute-start.8 = (f32[4,2,32,128]{3,2,1,0:T(8,128)S(1)}, f32[4,2,32,128]{3,2,1,0:T(8,128)S(1)}, u32[]{:S(2)}, u32[]{:S(2)}) collective-permute-start(f32[4,2,32,128]{3,2,1,0:T(8,128)S(1)} %get-tuple-element.47), channel_id=1, source_target_pairs={{0,12},{1,13},{2,14},{3,15},{4,8},{5,9},{6,10},{7,11},{8,4},{9,5},... | collective-permute-start | bytes 393224 | tf_op jit(solution)/shard_map/ppermute | solution.py:463
  34.0 0.2 unpack.1.edge_ref
  34.2 7.2 %second.1 = f32[1056,128]{1,0:T(8,128)} custom-call(f32[8]{0:T(128)S(1)} %copy-done.7, f32[5,8,32,128]{3,2,1,0:T(8,128)S(1)} %get-tuple-element.41.v_ref, f32[4,8,32,128]{3,2,1,0:T(8,128)S(1)} %get-tuple-element.42.w_ref, f32[16,128]{1,0:T(8,128)S(1)} %get-tuple-element.43._.sum_ref, f32[72,8,512]{2,1,0:T(8,128)S(1)} %bitcast.12, ...), custom_call_target="tpu_custom_call" | custom-call | flops 10000000000 | bytes 16777216 | tf_op jit(solution)/shard_map/second/pallas_call | solution.py:554
  41.4 5.2 %all-to-all-start.1 = ((f32[32,1,4224]{2,1,0:T(1,128)}), f32[32,1,4224]{2,1,0:T(1,128)S(1)}, u32[]{:S(2)}, u32[]{:S(2)}) async-start(f32[32,1,4224]{2,1,0:T(1,128)} %bitcast.8), calls=%async_computation.1 | async-start | bytes 1081344 | tf_op jit(solution)/shard_map/all_to_all | solution.py:565
  46.6 0.6 relay.3
  47.2 0.0 copy-start.2
  47.2 1.7 %collective-permute-start.11 = (f32[4,2,32,128]{3,2,1,0:T(8,128)S(1)}, f32[4,2,32,128]{3,2,1,0:T(8,128)S(1)}, u32[]{:S(2)}, u32[]{:S(2)}) collective-permute-start(f32[4,2,32,128]{3,2,1,0:T(8,128)S(1)} %get-tuple-element.51), channel_id=1, source_target_pairs={{0,3},{1,2},{2,1},{3,0},{4,7},{5,6},{6,5},{7,4},{8,11},{9,10},{10,... | collective-permute-start | bytes 393224 | tf_op jit(solution)/shard_map/ppermute | solution.py:475
  49.0 0.4 collective-permute-start.12
  49.4 6.3 %collective-permute-done.11.refs_1_ = f32[4,2,32,128]{3,2,1,0:T(8,128)S(1)} collective-permute-done((f32[4,2,32,128]{3,2,1,0:T(8,128)S(1)}, f32[4,2,32,128]{3,2,1,0:T(8,128)S(1)}, u32[]{:S(2)}, u32[]{:S(2)}) %collective-permute-start.11) | collective-permute-done | bytes 131104 | tf_op jit(solution)/shard_map/ppermute | solution.py:475
  55.7 4.4 %collective-permute-done.12.refs_2_ = f32[4,2,32,128]{3,2,1,0:T(8,128)S(1)} collective-permute-done((f32[4,2,32,128]{3,2,1,0:T(8,128)S(1)}, f32[4,2,32,128]{3,2,1,0:T(8,128)S(1)}, u32[]{:S(2)}, u32[]{:S(2)}) %collective-permute-start.12) | collective-permute-done | bytes 131104 | tf_op jit(solution)/shard_map/ppermute | solution.py:475
  60.1 0.6 gather.1.w_ref
  60.7 0.7 %all-to-all-done.1 = f32[32,1,4224]{2,1,0:T(1,128)S(1)} async-done(((f32[32,1,4224]{2,1,0:T(1,128)}), f32[32,1,4224]{2,1,0:T(1,128)S(1)}, u32[]{:S(2)}, u32[]{:S(2)}) %all-to-all-start.1) | async-done | bytes 540704 | tf_op jit(solution)/shard_map/all_to_all | solution.py:565
  61.4 1.2 %combine.1 = (f32[2,8,8192]{2,1,0:T(8,128)}, f32[2,8,8192]{2,1,0:T(8,128)}) custom-call(f32[2,8,8192]{2,1,0:T(8,128)S(1)} %copy-done.2, f32[1056,128]{1,0:T(8,128)S(1)} %bitcast.13, f32[16,2,32,128]{3,2,1,0:T(8,128)S(1)} %gather.1.w_ref), custom_call_target="tpu_custom_call" | custom-call | tf_op jit(solution)/shard_map/combine/pallas_call | solution.py:575
  (28 shorter events, 0.1 us)
Async XLA Ops:
  0.7 1.0 %copy-start.1 = (f32[2,8,8192]{2,1,0:T(8,128)S(1)}, f32[2,8,8192]{2,1,0:T(8,128)}, u32[]{:S(2)}) copy-start(f32[2,8,8192]{2,1,0:T(8,128)} %rhs_ref.3) | copy-start | bytes 1572868
  3.1 11.8 %collective-permute-start = (f32[4,2,24,128]{3,2,1,0:T(8,128)S(1)}, f32[4,2,24,128]{3,2,1,0:T(8,128)S(1)}, u32[]{:S(2)}, u32[]{:S(2)}) collective-permute-start(f32[4,2,24,128]{3,2,1,0:T(8,128)S(1)} %get-tuple-element.29), channel_id=1, source_target_pairs={{0,12},{1,13},{2,14},{3,15},{4,8},{5,9},{6,10},{7,11},{8,4},{9,5},... | collective-permute-start | bytes 294920 | tf_op jit(solution)/shard_map/ppermute | solution.py:463
  8.1 8.3 %collective-permute-start.1 = (f32[4,2,24,128]{3,2,1,0:T(8,128)S(1)}, f32[4,2,24,128]{3,2,1,0:T(8,128)S(1)}, u32[]{:S(2)}, u32[]{:S(2)}) collective-permute-start(f32[4,2,24,128]{3,2,1,0:T(8,128)S(1)} %get-tuple-element.30), channel_id=1, source_target_pairs={{0,8},{1,9},{2,10},{3,11},{4,12},{5,13},{6,14},{7,15},{8,0},{9,1},... | collective-permute-start | bytes 294920 | tf_op jit(solution)/shard_map/ppermute | solution.py:463
  8.1 8.3 %collective-permute-start.2 = (f32[4,2,24,128]{3,2,1,0:T(8,128)S(1)}, f32[4,2,24,128]{3,2,1,0:T(8,128)S(1)}, u32[]{:S(2)}, u32[]{:S(2)}) collective-permute-start(f32[4,2,24,128]{3,2,1,0:T(8,128)S(1)} %get-tuple-element.31), channel_id=1, source_target_pairs={{0,4},{1,5},{2,6},{3,7},{4,0},{5,1},{6,2},{7,3},{8,12},{9,13},{10,... | collective-permute-start | bytes 294920 | tf_op jit(solution)/shard_map/ppermute | solution.py:463
  8.7 16.2 %all-to-all-start = ((f32[32,2,8,128]{3,2,1,0:T(8,128)}), f32[32,2,8,128]{3,2,1,0:T(8,128)S(1)}, u32[]{:S(2)}, u32[]{:S(2)}) async-start(f32[32,2,8,128]{3,2,1,0:T(8,128)} %get-tuple-element.34), calls=%async_computation | async-start | bytes 524288 | tf_op jit(solution)/shard_map/all_to_all | solution.py:487
  16.4 2.5 %copy-start = (f32[9,8,8,512]{3,2,1,0:T(8,128)S(1)}, f32[9,8,8,512]{3,2,1,0:T(8,128)}, u32[]{:S(2)}) copy-start(f32[9,8,8,512]{3,2,1,0:T(8,128)} %last_ref.1) | copy-start | bytes 3538948
  17.0 9.0 %collective-permute-start.3 = (f32[4,2,24,128]{3,2,1,0:T(8,128)S(1)}, f32[4,2,24,128]{3,2,1,0:T(8,128)S(1)}, u32[]{:S(2)}, u32[]{:S(2)}) collective-permute-start(f32[4,2,24,128]{3,2,1,0:T(8,128)S(1)} %get-tuple-element.38), channel_id=1, source_target_pairs={{0,3},{1,2},{2,1},{3,0},{4,7},{5,6},{6,5},{7,4},{8,11},{9,10},{10,... | collective-permute-start | bytes 294920 | tf_op jit(solution)/shard_map/ppermute | solution.py:475
  17.3 8.7 %collective-permute-start.4 = (f32[4,2,24,128]{3,2,1,0:T(8,128)S(1)}, f32[4,2,24,128]{3,2,1,0:T(8,128)S(1)}, u32[]{:S(2)}, u32[]{:S(2)}) collective-permute-start(f32[4,2,24,128]{3,2,1,0:T(8,128)S(1)} %get-tuple-element.39), channel_id=1, source_target_pairs={{0,2},{1,3},{2,0},{3,1},{4,6},{5,7},{6,4},{7,5},{8,10},{9,11},{10,... | collective-permute-start | bytes 294920 | tf_op jit(solution)/shard_map/ppermute | solution.py:475
  18.6 7.4 %collective-permute-start.5 = (f32[4,2,24,128]{3,2,1,0:T(8,128)S(1)}, f32[4,2,24,128]{3,2,1,0:T(8,128)S(1)}, u32[]{:S(2)}, u32[]{:S(2)}) collective-permute-start(f32[4,2,24,128]{3,2,1,0:T(8,128)S(1)} %get-tuple-element.40), channel_id=1, source_target_pairs={{0,1},{1,0},{2,3},{3,2},{4,5},{5,4},{6,7},{7,6},{8,9},{9,8},{10,11... | collective-permute-start | bytes 294920 | tf_op jit(solution)/shard_map/ppermute | solution.py:475
  18.9 3.4 %copy-start.3 = (s32[512]{0:T(512)S(1)}, s32[512]{0:T(512)}, u32[]{:S(2)}) copy-start(s32[512]{0:T(512)} %param.10) | copy-start | bytes 6148
  18.9 3.4 %copy-start.4 = (s32[512]{0:T(512)S(1)}, s32[512]{0:T(512)}, u32[]{:S(2)}) copy-start(s32[512]{0:T(512)} %param.11) | copy-start | bytes 6148
  18.9 3.4 %copy-start.5 = (s32[512]{0:T(512)S(1)}, s32[512]{0:T(512)}, u32[]{:S(2)}) copy-start(s32[512]{0:T(512)} %param.12) | copy-start | bytes 6148
  18.9 3.4 %copy-start.6 = (s32[512]{0:T(512)S(1)}, s32[512]{0:T(512)}, u32[]{:S(2)}) copy-start(s32[512]{0:T(512)} %param.13) | copy-start | bytes 6148
  19.1 14.9 %collective-permute-start.6 = (f32[9,2,8,128]{3,2,1,0:T(8,128)S(1)}, f32[9,2,8,128]{3,2,1,0:T(8,128)S(1)}, u32[]{:S(2)}, u32[]{:S(2)}) collective-permute-start(f32[9,2,8,128]{3,2,1,0:T(8,128)S(1)} %get-tuple-element.44), channel_id=1, source_target_pairs={{1,0},{2,1},{3,2},{4,3},{5,4},{6,5},{7,6},{8,7},{9,8},{10,9},{11,1... | collective-permute-start | bytes 221192 | tf_op jit(solution)/shard_map/ppermute | solution.py:504
  22.3 11.7 %collective-permute-start.7 = (f32[9,2,8,128]{3,2,1,0:T(8,128)S(1)}, f32[9,2,8,128]{3,2,1,0:T(8,128)S(1)}, u32[]{:S(2)}, u32[]{:S(2)}) collective-permute-start(f32[9,2,8,128]{3,2,1,0:T(8,128)S(1)} %get-tuple-element.45), channel_id=1, source_target_pairs={{0,1},{1,2},{2,3},{3,4},{4,5},{5,6},{6,7},{7,8},{8,9},{9,10},{10,1... | collective-permute-start | bytes 221192 | tf_op jit(solution)/shard_map/ppermute | solution.py:505
  24.9 1.1 %copy-start.7 = (f32[8]{0:T(128)S(1)}, f32[8]{0:T(128)}, u32[]{:S(2)}) copy-start(f32[8]{0:T(128)} %dif_ref.3) | copy-start | bytes 100
  30.3 16.3 %collective-permute-start.10 = (f32[4,2,32,128]{3,2,1,0:T(8,128)S(1)}, f32[4,2,32,128]{3,2,1,0:T(8,128)S(1)}, u32[]{:S(2)}, u32[]{:S(2)}) collective-permute-start(f32[4,2,32,128]{3,2,1,0:T(8,128)S(1)} %get-tuple-element.49), channel_id=1, source_target_pairs={{0,4},{1,5},{2,6},{3,7},{4,0},{5,1},{6,2},{7,3},{8,12},{9,13},{10,... | collective-permute-start | bytes 393224 | tf_op jit(solution)/shard_map/ppermute | solution.py:463
  32.0 14.6 %collective-permute-start.8 = (f32[4,2,32,128]{3,2,1,0:T(8,128)S(1)}, f32[4,2,32,128]{3,2,1,0:T(8,128)S(1)}, u32[]{:S(2)}, u32[]{:S(2)}) collective-permute-start(f32[4,2,32,128]{3,2,1,0:T(8,128)S(1)} %get-tuple-element.47), channel_id=1, source_target_pairs={{0,12},{1,13},{2,14},{3,15},{4,8},{5,9},{6,10},{7,11},{8,4},{9,5},... | collective-permute-start | bytes 393224 | tf_op jit(solution)/shard_map/ppermute | solution.py:463
  34.0 12.6 %collective-permute-start.9 = (f32[4,2,32,128]{3,2,1,0:T(8,128)S(1)}, f32[4,2,32,128]{3,2,1,0:T(8,128)S(1)}, u32[]{:S(2)}, u32[]{:S(2)}) collective-permute-start(f32[4,2,32,128]{3,2,1,0:T(8,128)S(1)} %get-tuple-element.48), channel_id=1, source_target_pairs={{0,8},{1,9},{2,10},{3,11},{4,12},{5,13},{6,14},{7,15},{8,0},{9,1},... | collective-permute-start | bytes 393224 | tf_op jit(solution)/shard_map/ppermute | solution.py:463
  41.4 20.0 %all-to-all-start.1 = ((f32[32,1,4224]{2,1,0:T(1,128)}), f32[32,1,4224]{2,1,0:T(1,128)S(1)}, u32[]{:S(2)}, u32[]{:S(2)}) async-start(f32[32,1,4224]{2,1,0:T(1,128)} %bitcast.8), calls=%async_computation.1 | async-start | bytes 1081344 | tf_op jit(solution)/shard_map/all_to_all | solution.py:565
  47.2 14.1 %copy-start.2 = (f32[2,8,8192]{2,1,0:T(8,128)S(1)}, f32[2,8,8192]{2,1,0:T(8,128)}, u32[]{:S(2)}) copy-start(f32[2,8,8192]{2,1,0:T(8,128)} %rhs_ref.3) | copy-start | bytes 1572868
  47.2 8.4 %collective-permute-start.11 = (f32[4,2,32,128]{3,2,1,0:T(8,128)S(1)}, f32[4,2,32,128]{3,2,1,0:T(8,128)S(1)}, u32[]{:S(2)}, u32[]{:S(2)}) collective-permute-start(f32[4,2,32,128]{3,2,1,0:T(8,128)S(1)} %get-tuple-element.51), channel_id=1, source_target_pairs={{0,3},{1,2},{2,1},{3,0},{4,7},{5,6},{6,5},{7,4},{8,11},{9,10},{10,... | collective-permute-start | bytes 393224 | tf_op jit(solution)/shard_map/ppermute | solution.py:475
  49.0 11.1 %collective-permute-start.12 = (f32[4,2,32,128]{3,2,1,0:T(8,128)S(1)}, f32[4,2,32,128]{3,2,1,0:T(8,128)S(1)}, u32[]{:S(2)}, u32[]{:S(2)}) collective-permute-start(f32[4,2,32,128]{3,2,1,0:T(8,128)S(1)} %get-tuple-element.52), channel_id=1, source_target_pairs={{0,2},{1,3},{2,0},{3,1},{4,6},{5,7},{6,4},{7,5},{8,10},{9,11},{10,... | collective-permute-start | bytes 393224 | tf_op jit(solution)/shard_map/ppermute | solution.py:475
  49.4 10.7 %collective-permute-start.13 = (f32[4,2,32,128]{3,2,1,0:T(8,128)S(1)}, f32[4,2,32,128]{3,2,1,0:T(8,128)S(1)}, u32[]{:S(2)}, u32[]{:S(2)}) collective-permute-start(f32[4,2,32,128]{3,2,1,0:T(8,128)S(1)} %get-tuple-element.53), channel_id=1, source_target_pairs={{0,1},{1,0},{2,3},{3,2},{4,5},{5,4},{6,7},{7,6},{8,9},{9,8},{10,11... | collective-permute-start | bytes 393224 | tf_op jit(solution)/shard_map/ppermute | solution.py:475

commit v13 on v12

--- a/solution.py
+++ b/solution.py
@@ -149,6 +149,32 @@
     return [functools.partial(fill, first) for first in range(0, S, 2)]
 
 
+def prepare(get, ct, slot, every, coup_ref, stencil_ref, vs_ref, xs_ref, mx_ref, bs_ref):
+    n = bs_ref.shape[1] // S
+    before, after = (ct - 1) % every, (ct + 1) % every
+
+    def step(first):
+        wide = lax.broadcasted_iota(jnp.int32, (n, LANES), 1) < LANES // 2
+        for t in (first, first + 1):
+            at = slice(t * LANES, (t + 1) * LANES)
+            to = slice(t * n, (t + 1) * n)
+            high, low = split(get(ct, t))
+            vs_ref[slot, 0:n, at] = high
+            vs_ref[slot, n : 2 * n, at] = low
+            vs_ref[slot, 2 * n : 3 * n, at] = high
+            xs_ref[slot, to, 0:LANES] = high
+            xs_ref[slot, to, LANES : 2 * LANES] = low
+            high, low = split(jnp.where(wide, get(after, t), get(before, t)))
+            xs_ref[slot, to, 2 * LANES : 3 * LANES] = high
+            xs_ref[slot, to, 3 * LANES :] = low
+        at = slice(first * LANES, (first + 2) * LANES)
+        mx_ref[slot, :, at] = jnp.dot(coup_ref[...], vs_ref[slot, :, at], preferred_element_type=F32)
+        if first + 2 == S:
+            bs_ref[slot] = jnp.dot(xs_ref[slot], stencil_ref[...], preferred_element_type=F32)
+
+    return [functools.partial(step, first) for first in range(0, S, 2)]
+
+
 def run(steps):
     for step in steps:
         step()
@@ -250,8 +276,8 @@
 
         return finish
 
-    def prepare(ct):
-        return mix(get, ct, ct % 2, coup_ref, vs_ref, mx_ref) + sides(ct, ct % 2)
+    def ready(ct):
+        return prepare(get, ct, ct % 2, every, coup_ref, stencil_ref, vs_ref, xs_ref, mx_ref, bs_ref)
 
     def sides(ct, slot):
         return spread(get, ct, slot, every, stencil_ref, xs_ref, bs_ref)
@@ -272,9 +298,9 @@
     rest = []
     for ct in range(early, tiles):
         rest += sides(ct, spare) + [functools.partial(close, ct, spare), functools.partial(pack, ct)]
-    run(prepare(0))
+    run(ready(0))
     for ct in range(early):
-        steps = prepare(ct + 1) if ct + 1 < early else rest
+        steps = ready(ct + 1) if ct + 1 < early else rest
         react(n, tile_of(jac_ref, ct), ct % 2, mx_ref, finisher(ct, ct % 2), steps)
         pack(ct)
     sum_ref[0:8] = sums.partial("rr")
@@ -331,23 +357,18 @@
 
     order = list(range(1, tiles)) + [0]
 
-    def mixed(get, ct, slot):
-        return mix(get, ct, slot, coup_ref, vs_ref, mx_ref)
-
-    def sides(get, ct, slot):
-        return spread(get, ct, slot, every, stencil_ref, xs_ref, bs_ref)
-
-    run(mixed(get_v, tiles, 0) + sides(get_v, tiles, 0))
+    def ready(get, ct, slot):
+        return prepare(get, ct, slot, every, coup_ref, stencil_ref, vs_ref, xs_ref, mx_ref, bs_ref)
+
+    run(ready(get_v, tiles, 0))
     inside = tiles > 2
-    steps = mixed(get_w, order[0], 1) + (sides(get_w, order[0], 1) if inside else [])
+    steps = ready(get_w, order[0], 1) if inside else []
     react(n, tile_of(edge_ref, 0), 0, mx_ref, finish_edge, steps)
     if not inside:
-        run(sides(get_w, order[0], 1))
+        run(ready(get_w, order[0], 1))
     for at, ct in enumerate(order):
         slot = (at + 1) % 2
-        steps = []
-        if at + 1 < tiles:
-            steps = mixed(get_w, order[at + 1], 1 - slot) + sides(get_w, order[at + 1], 1 - slot)
+        steps = ready(get_w, order[at + 1], 1 - slot) if at + 1 < tiles else []
         react(n, tile_of(jac_ref, ct), slot, mx_ref, finisher(ct, slot), steps)
     uu, ur, uz, rz = (sums.total(name) for name in ("uu", "ur", "uz", "rz"))
     c2 = ratio(rz, rr)

time: 62.9 us -> 62.8 us (level)
  no operation moved by 1% of the time
where the time goes in v13:
time: 62.8 us; the launch traced here: 62.5 us
  starting transfers between devices  28 us (45%)
  Pallas kernels  17.3 us (28%)
  waiting for transfers between devices  15.2 us (24%)
  local copies, waits for them, and re-layouts  1.07 us (2%)
  between operations  0.85 us (1%)
    ppermute x6, waiting for transfers between devices, across(): lax.ppermute(relayed[k], 'modes', [(i, i ^ k) for i in range(parts)])  10.7 us
    ppermute x6, starting transfers between devices, across(): lax.ppermute(arrays[q], 'modes', [(i, i ^ q * plane) for i in range(parts)])  9.33 us
    pallas_call x1, Pallas kernels, local(): pl.pallas_call(functools.partial(second_kernel, n, tiles), out_shape=sds(...  7.11 us
    all_to_all x1, starting transfers between devices, local(): lax.all_to_all(late_send, 'modes', split_axis=0, concat_axis=0, tiled=True)  6.16 us
    all_to_all x1, starting transfers between devices, local(): lax.all_to_all(z_send.reshape(n, 1, line), 'modes', split_axis=0, concat_...  5.22 us
    pallas_call x1, Pallas kernels, local(): pl.pallas_call(functools.partial(first_kernel, n, tiles, plane), out_shap...  4.22 us
    ppermute x6, starting transfers between devices, across(): lax.ppermute(relayed[k], 'modes', [(i, i ^ k) for i in range(parts)])  4.05 us
    ppermute x1, starting transfers between devices, local(): after = lax.ppermute(head, 'modes', down)  3.22 us
  transfers between devices with their start and end apart: 16, of which 5 were waited for; matrix products, arithmetic and copies ran while one was open for 0% of the time, Pallas kernels for 24%

profile of v13, /device:TPU:0, one launch (start us, length us, event | category | flops | bytes accessed | tf_op | source)
XLA Modules:
  0.0 62.5 jit_solution(17536407059480786289)
XLA Ops:
  0.6 0.1 pad_add_fusion.place_ref
  0.7 1.0 %copy-done.1 = f32[2,8,8192]{2,1,0:T(8,128)S(1)} copy-done((f32[2,8,8192]{2,1,0:T(8,128)S(1)}, f32[2,8,8192]{2,1,0:T(8,128)}, u32[]{:S(2)}) %copy-start.1) | copy-done | bytes 524312
  1.8 1.3 %arrange.1 = (f32[32,2,8,128]{3,2,1,0:T(8,128)}, f32[4,2,24,128]{3,2,1,0:T(8,128)S(1)}, f32[4,2,24,128]{3,2,1,0:T(8,128)S(1)}, f32[4,2,24,128]{3,2,1,0:T(8,128)S(1)}, f32[4,2,24,128]{3,2,1,0:T(8,128)S(1)}) custom-call(s32[2]{0:T(128)S(1)} %pad_add_fusion.place_ref, f32[2,8,8192]{2,1,0:T(8,128)S(1)} %copy-done.1), custom_call_target="tpu_custom_call" | custom-call | tf_op jit(solution)/shard_map/arrange/pallas_call | solution.py:499
  3.1 5.0 %collective-permute-start = (f32[4,2,24,128]{3,2,1,0:T(8,128)S(1)}, f32[4,2,24,128]{3,2,1,0:T(8,128)S(1)}, u32[]{:S(2)}, u32[]{:S(2)}) collective-permute-start(f32[4,2,24,128]{3,2,1,0:T(8,128)S(1)} %get-tuple-element.29), channel_id=1, source_target_pairs={{0,12},{1,13},{2,14},{3,15},{4,8},{5,9},{6,10},{7,11},{8,4},{9,5},... | collective-permute-start | bytes 294920 | tf_op jit(solution)/shard_map/ppermute | solution.py:484
  8.1 0.6 collective-permute-start.2
  8.7 6.2 %all-to-all-start = ((f32[32,2,8,128]{3,2,1,0:T(8,128)}), f32[32,2,8,128]{3,2,1,0:T(8,128)S(1)}, u32[]{:S(2)}, u32[]{:S(2)}) async-start(f32[32,2,8,128]{3,2,1,0:T(8,128)} %get-tuple-element.34), calls=%async_computation | async-start | bytes 524288 | tf_op jit(solution)/shard_map/all_to_all | solution.py:508
  14.9 1.5 %collective-permute-done.1.refs_2_ = f32[4,2,24,128]{3,2,1,0:T(8,128)S(1)} collective-permute-done((f32[4,2,24,128]{3,2,1,0:T(8,128)S(1)}, f32[4,2,24,128]{3,2,1,0:T(8,128)S(1)}, u32[]{:S(2)}, u32[]{:S(2)}) %collective-permute-start.1) | collective-permute-done | bytes 98336 | tf_op jit(solution)/shard_map/ppermute | solution.py:484
  16.4 0.6 relay.2
  17.0 0.3 collective-permute-start.3
  17.3 1.3 %collective-permute-start.4 = (f32[4,2,24,128]{3,2,1,0:T(8,128)S(1)}, f32[4,2,24,128]{3,2,1,0:T(8,128)S(1)}, u32[]{:S(2)}, u32[]{:S(2)}) collective-permute-start(f32[4,2,24,128]{3,2,1,0:T(8,128)S(1)} %get-tuple-element.39), channel_id=1, source_target_pairs={{0,2},{1,3},{2,0},{3,1},{4,6},{5,7},{6,4},{7,5},{8,10},{9,11},{10,... | collective-permute-start | bytes 294920 | tf_op jit(solution)/shard_map/ppermute | solution.py:496
  18.6 0.3 collective-permute-start.5
  18.9 0.0 copy-start.6
  18.9 0.2 pack.1
  19.1 3.2 %collective-permute-start.6 = (f32[9,2,8,128]{3,2,1,0:T(8,128)S(1)}, f32[9,2,8,128]{3,2,1,0:T(8,128)S(1)}, u32[]{:S(2)}, u32[]{:S(2)}) collective-permute-start(f32[9,2,8,128]{3,2,1,0:T(8,128)S(1)} %get-tuple-element.44), channel_id=1, source_target_pairs={{1,0},{2,1},{3,2},{4,3},{5,4},{6,5},{7,6},{8,7},{9,8},{10,9},{11,1... | collective-permute-start | bytes 221192 | tf_op jit(solution)/shard_map/ppermute | solution.py:525
  22.4 0.3 coupling.1
  22.6 2.3 %all-to-all-done = f32[32,2,8,128]{3,2,1,0:T(8,128)S(1)} async-done(((f32[32,2,8,128]{3,2,1,0:T(8,128)}), f32[32,2,8,128]{3,2,1,0:T(8,128)S(1)}, u32[]{:S(2)}, u32[]{:S(2)}) %all-to-all-start) | async-done | bytes 262176 | tf_op jit(solution)/shard_map/all_to_all | solution.py:508
  24.9 1.0 %late.1 = (f32[2,8,32,128]{3,2,1,0:T(8,128)S(1)}, f32[1,8,32,128]{3,2,1,0:T(8,128)S(1)}) custom-call(f32[72,8,512]{2,1,0:T(8,128)S(1)} %bitcast.10, bf16[288,96]{1,0:T(8,128)(2,1)S(1)} %get-tuple-element.33.coup_ref, f32[512,128]{1,0:T(8,128)S(1)} %bitcast.14), custom_call_target="tpu_custom_call" | custom-call | flops 2000000000 | bytes 1048576 | tf_op jit(solution)/shard_map/late/pallas_call | solution.py:545
  26.0 4.2 %first.1 = (f32[5,8,32,128]{3,2,1,0:T(8,128)S(1)}, f32[4,8,32,128]{3,2,1,0:T(8,128)S(1)}, f32[16,128]{1,0:T(8,128)S(1)}, f32[4,2,32,128]{3,2,1,0:T(8,128)S(1)}, ...) custom-call(s32[2]{0:T(128)S(1)} %pad_add_fusion.place_ref, ...), custom_call_target="tpu_custom_call" | custom-call | tf_op jit(solution)/shard_map/first/pallas_call | solution.py:555
  30.2 1.7 %collective-permute-start.10 = (f32[4,2,32,128]{3,2,1,0:T(8,128)S(1)}, f32[4,2,32,128]{3,2,1,0:T(8,128)S(1)}, u32[]{:S(2)}, u32[]{:S(2)}) collective-permute-start(f32[4,2,32,128]{3,2,1,0:T(8,128)S(1)} %get-tuple-element.49), channel_id=1, source_target_pairs={{0,4},{1,5},{2,6},{3,7},{4,0},{5,1},{6,2},{7,3},{8,12},{9,13},{10,... | collective-permute-start | bytes 393224 | tf_op jit(solution)/shard_map/ppermute | solution.py:484
  32.0 2.0 %collective-permute-start.8 = (f32[4,2,32,128]{3,2,1,0:T(8,128)S(1)}, f32[4,2,32,128]{3,2,1,0:T(8,128)S(1)}, u32[]{:S(2)}, u32[]{:S(2)}) collective-permute-start(f32[4,2,32,128]{3,2,1,0:T(8,128)S(1)} %get-tuple-element.47), channel_id=1, source_target_pairs={{0,12},{1,13},{2,14},{3,15},{4,8},{5,9},{6,10},{7,11},{8,4},{9,5},... | collective-permute-start | bytes 393224 | tf_op jit(solution)/shard_map/ppermute | solution.py:484
  34.0 0.2 unpack.1.edge_ref
  34.2 7.1 %second.1 = f32[1056,128]{1,0:T(8,128)} custom-call(f32[8]{0:T(128)S(1)} %copy-done.7, f32[5,8,32,128]{3,2,1,0:T(8,128)S(1)} %get-tuple-element.41.v_ref, f32[4,8,32,128]{3,2,1,0:T(8,128)S(1)} %get-tuple-element.42.w_ref, f32[16,128]{1,0:T(8,128)S(1)} %get-tuple-element.43._.sum_ref, f32[72,8,512]{2,1,0:T(8,128)S(1)} %bitcast.12, ...), custom_call_target="tpu_custom_call" | custom-call | flops 10000000000 | bytes 16777216 | tf_op jit(solution)/shard_map/second/pallas_call | solution.py:575
  41.3 5.2 %all-to-all-start.1 = ((f32[32,1,4224]{2,1,0:T(1,128)}), f32[32,1,4224]{2,1,0:T(1,128)S(1)}, u32[]{:S(2)}, u32[]{:S(2)}) async-start(f32[32,1,4224]{2,1,0:T(1,128)} %bitcast.8), calls=%async_computation.1 | async-start | bytes 1081344 | tf_op jit(solution)/shard_map/all_to_all | solution.py:586
  46.5 0.6 relay.3
  47.1 0.0 copy-start.2
  47.1 1.7 %collective-permute-start.11 = (f32[4,2,32,128]{3,2,1,0:T(8,128)S(1)}, f32[4,2,32,128]{3,2,1,0:T(8,128)S(1)}, u32[]{:S(2)}, u32[]{:S(2)}) collective-permute-start(f32[4,2,32,128]{3,2,1,0:T(8,128)S(1)} %get-tuple-element.51), channel_id=1, source_target_pairs={{0,3},{1,2},{2,1},{3,0},{4,7},{5,6},{6,5},{7,4},{8,11},{9,10},{10,... | collective-permute-start | bytes 393224 | tf_op jit(solution)/shard_map/ppermute | solution.py:496
  48.9 0.4 collective-permute-start.12
  49.3 6.3 %collective-permute-done.11.refs_1_ = f32[4,2,32,128]{3,2,1,0:T(8,128)S(1)} collective-permute-done((f32[4,2,32,128]{3,2,1,0:T(8,128)S(1)}, f32[4,2,32,128]{3,2,1,0:T(8,128)S(1)}, u32[]{:S(2)}, u32[]{:S(2)}) %collective-permute-start.11) | collective-permute-done | bytes 131104 | tf_op jit(solution)/shard_map/ppermute | solution.py:496
  55.6 4.4 %collective-permute-done.12.refs_2_ = f32[4,2,32,128]{3,2,1,0:T(8,128)S(1)} collective-permute-done((f32[4,2,32,128]{3,2,1,0:T(8,128)S(1)}, f32[4,2,32,128]{3,2,1,0:T(8,128)S(1)}, u32[]{:S(2)}, u32[]{:S(2)}) %collective-permute-start.12) | collective-permute-done | bytes 131104 | tf_op jit(solution)/shard_map/ppermute | solution.py:496
  60.0 0.6 gather.1.w_ref
  60.6 0.7 %all-to-all-done.1 = f32[32,1,4224]{2,1,0:T(1,128)S(1)} async-done(((f32[32,1,4224]{2,1,0:T(1,128)}), f32[32,1,4224]{2,1,0:T(1,128)S(1)}, u32[]{:S(2)}, u32[]{:S(2)}) %all-to-all-start.1) | async-done | bytes 540704 | tf_op jit(solution)/shard_map/all_to_all | solution.py:586
  61.2 1.2 %combine.1 = (f32[2,8,8192]{2,1,0:T(8,128)}, f32[2,8,8192]{2,1,0:T(8,128)}) custom-call(f32[2,8,8192]{2,1,0:T(8,128)S(1)} %copy-done.2, f32[1056,128]{1,0:T(8,128)S(1)} %bitcast.13, f32[16,2,32,128]{3,2,1,0:T(8,128)S(1)} %gather.1.w_ref), custom_call_target="tpu_custom_call" | custom-call | tf_op jit(solution)/shard_map/combine/pallas_call | solution.py:596
  (28 shorter events, 0.1 us)
Async XLA Ops:
  0.7 1.0 %copy-start.1 = (f32[2,8,8192]{2,1,0:T(8,128)S(1)}, f32[2,8,8192]{2,1,0:T(8,128)}, u32[]{:S(2)}) copy-start(f32[2,8,8192]{2,1,0:T(8,128)} %rhs_ref.3) | copy-start | bytes 1572868
  3.1 11.8 %collective-permute-start = (f32[4,2,24,128]{3,2,1,0:T(8,128)S(1)}, f32[4,2,24,128]{3,2,1,0:T(8,128)S(1)}, u32[]{:S(2)}, u32[]{:S(2)}) collective-permute-start(f32[4,2,24,128]{3,2,1,0:T(8,128)S(1)} %get-tuple-element.29), channel_id=1, source_target_pairs={{0,12},{1,13},{2,14},{3,15},{4,8},{5,9},{6,10},{7,11},{8,4},{9,5},... | collective-permute-start | bytes 294920 | tf_op jit(solution)/shard_map/ppermute | solution.py:484
  8.1 8.3 %collective-permute-start.1 = (f32[4,2,24,128]{3,2,1,0:T(8,128)S(1)}, f32[4,2,24,128]{3,2,1,0:T(8,128)S(1)}, u32[]{:S(2)}, u32[]{:S(2)}) collective-permute-start(f32[4,2,24,128]{3,2,1,0:T(8,128)S(1)} %get-tuple-element.30), channel_id=1, source_target_pairs={{0,8},{1,9},{2,10},{3,11},{4,12},{5,13},{6,14},{7,15},{8,0},{9,1},... | collective-permute-start | bytes 294920 | tf_op jit(solution)/shard_map/ppermute | solution.py:484
  8.1 8.3 %collective-permute-start.2 = (f32[4,2,24,128]{3,2,1,0:T(8,128)S(1)}, f32[4,2,24,128]{3,2,1,0:T(8,128)S(1)}, u32[]{:S(2)}, u32[]{:S(2)}) collective-permute-start(f32[4,2,24,128]{3,2,1,0:T(8,128)S(1)} %get-tuple-element.31), channel_id=1, source_target_pairs={{0,4},{1,5},{2,6},{3,7},{4,0},{5,1},{6,2},{7,3},{8,12},{9,13},{10,... | collective-permute-start | bytes 294920 | tf_op jit(solution)/shard_map/ppermute | solution.py:484
  8.7 16.2 %all-to-all-start = ((f32[32,2,8,128]{3,2,1,0:T(8,128)}), f32[32,2,8,128]{3,2,1,0:T(8,128)S(1)}, u32[]{:S(2)}, u32[]{:S(2)}) async-start(f32[32,2,8,128]{3,2,1,0:T(8,128)} %get-tuple-element.34), calls=%async_computation | async-start | bytes 524288 | tf_op jit(solution)/shard_map/all_to_all | solution.py:508
  16.4 2.5 %copy-start = (f32[9,8,8,512]{3,2,1,0:T(8,128)S(1)}, f32[9,8,8,512]{3,2,1,0:T(8,128)}, u32[]{:S(2)}) copy-start(f32[9,8,8,512]{3,2,1,0:T(8,128)} %last_ref.1) | copy-start | bytes 3538948
  17.0 9.0 %collective-permute-start.3 = (f32[4,2,24,128]{3,2,1,0:T(8,128)S(1)}, f32[4,2,24,128]{3,2,1,0:T(8,128)S(1)}, u32[]{:S(2)}, u32[]{:S(2)}) collective-permute-start(f32[4,2,24,128]{3,2,1,0:T(8,128)S(1)} %get-tuple-element.38), channel_id=1, source_target_pairs={{0,3},{1,2},{2,1},{3,0},{4,7},{5,6},{6,5},{7,4},{8,11},{9,10},{10,... | collective-permute-start | bytes 294920 | tf_op jit(solution)/shard_map/ppermute | solution.py:496
  17.3 8.7 %collective-permute-start.4 = (f32[4,2,24,128]{3,2,1,0:T(8,128)S(1)}, f32[4,2,24,128]{3,2,1,0:T(8,128)S(1)}, u32[]{:S(2)}, u32[]{:S(2)}) collective-permute-start(f32[4,2,24,128]{3,2,1,0:T(8,128)S(1)} %get-tuple-element.39), channel_id=1, source_target_pairs={{0,2},{1,3},{2,0},{3,1},{4,6},{5,7},{6,4},{7,5},{8,10},{9,11},{10,... | collective-permute-start | bytes 294920 | tf_op jit(solution)/shard_map/ppermute | solution.py:496
  18.6 7.4 %collective-permute-start.5 = (f32[4,2,24,128]{3,2,1,0:T(8,128)S(1)}, f32[4,2,24,128]{3,2,1,0:T(8,128)S(1)}, u32[]{:S(2)}, u32[]{:S(2)}) collective-permute-start(f32[4,2,24,128]{3,2,1,0:T(8,128)S(1)} %get-tuple-element.40), channel_id=1, source_target_pairs={{0,1},{1,0},{2,3},{3,2},{4,5},{5,4},{6,7},{7,6},{8,9},{9,8},{10,11... | collective-permute-start | bytes 294920 | tf_op jit(solution)/shard_map/ppermute | solution.py:496
  18.9 3.4 %copy-start.3 = (s32[512]{0:T(512)S(1)}, s32[512]{0:T(512)}, u32[]{:S(2)}) copy-start(s32[512]{0:T(512)} %param.10) | copy-start | bytes 6148
  18.9 3.4 %copy-start.4 = (s32[512]{0:T(512)S(1)}, s32[512]{0:T(512)}, u32[]{:S(2)}) copy-start(s32[512]{0:T(512)} %param.11) | copy-start | bytes 6148
  18.9 3.4 %copy-start.5 = (s32[512]{0:T(512)S(1)}, s32[512]{0:T(512)}, u32[]{:S(2)}) copy-start(s32[512]{0:T(512)} %param.12) | copy-start | bytes 6148
  18.9 3.4 %copy-start.6 = (s32[512]{0:T(512)S(1)}, s32[512]{0:T(512)}, u32[]{:S(2)}) copy-start(s32[512]{0:T(512)} %param.13) | copy-start | bytes 6148
  19.1 14.8 %collective-permute-start.6 = (f32[9,2,8,128]{3,2,1,0:T(8,128)S(1)}, f32[9,2,8,128]{3,2,1,0:T(8,128)S(1)}, u32[]{:S(2)}, u32[]{:S(2)}) collective-permute-start(f32[9,2,8,128]{3,2,1,0:T(8,128)S(1)} %get-tuple-element.44), channel_id=1, source_target_pairs={{1,0},{2,1},{3,2},{4,3},{5,4},{6,5},{7,6},{8,7},{9,8},{10,9},{11,1... | collective-permute-start | bytes 221192 | tf_op jit(solution)/shard_map/ppermute | solution.py:525
  22.3 11.6 %collective-permute-start.7 = (f32[9,2,8,128]{3,2,1,0:T(8,128)S(1)}, f32[9,2,8,128]{3,2,1,0:T(8,128)S(1)}, u32[]{:S(2)}, u32[]{:S(2)}) collective-permute-start(f32[9,2,8,128]{3,2,1,0:T(8,128)S(1)} %get-tuple-element.45), channel_id=1, source_target_pairs={{0,1},{1,2},{2,3},{3,4},{4,5},{5,6},{6,7},{7,8},{8,9},{9,10},{10,1... | collective-permute-start | bytes 221192 | tf_op jit(solution)/shard_map/ppermute | solution.py:526
  24.9 1.1 %copy-start.7 = (f32[8]{0:T(128)S(1)}, f32[8]{0:T(128)}, u32[]{:S(2)}) copy-start(f32[8]{0:T(128)} %dif_ref.3) | copy-start | bytes 100
  30.2 16.2 %collective-permute-start.10 = (f32[4,2,32,128]{3,2,1,0:T(8,128)S(1)}, f32[4,2,32,128]{3,2,1,0:T(8,128)S(1)}, u32[]{:S(2)}, u32[]{:S(2)}) collective-permute-start(f32[4,2,32,128]{3,2,1,0:T(8,128)S(1)} %get-tuple-element.49), channel_id=1, source_target_pairs={{0,4},{1,5},{2,6},{3,7},{4,0},{5,1},{6,2},{7,3},{8,12},{9,13},{10,... | collective-permute-start | bytes 393224 | tf_op jit(solution)/shard_map/ppermute | solution.py:484
  32.0 14.6 %collective-permute-start.8 = (f32[4,2,32,128]{3,2,1,0:T(8,128)S(1)}, f32[4,2,32,128]{3,2,1,0:T(8,128)S(1)}, u32[]{:S(2)}, u32[]{:S(2)}) collective-permute-start(f32[4,2,32,128]{3,2,1,0:T(8,128)S(1)} %get-tuple-element.47), channel_id=1, source_target_pairs={{0,12},{1,13},{2,14},{3,15},{4,8},{5,9},{6,10},{7,11},{8,4},{9,5},... | collective-permute-start | bytes 393224 | tf_op jit(solution)/shard_map/ppermute | solution.py:484
  34.0 12.6 %collective-permute-start.9 = (f32[4,2,32,128]{3,2,1,0:T(8,128)S(1)}, f32[4,2,32,128]{3,2,1,0:T(8,128)S(1)}, u32[]{:S(2)}, u32[]{:S(2)}) collective-permute-start(f32[4,2,32,128]{3,2,1,0:T(8,128)S(1)} %get-tuple-element.48), channel_id=1, source_target_pairs={{0,8},{1,9},{2,10},{3,11},{4,12},{5,13},{6,14},{7,15},{8,0},{9,1},... | collective-permute-start | bytes 393224 | tf_op jit(solution)/shard_map/ppermute | solution.py:484
  41.3 20.0 %all-to-all-start.1 = ((f32[32,1,4224]{2,1,0:T(1,128)}), f32[32,1,4224]{2,1,0:T(1,128)S(1)}, u32[]{:S(2)}, u32[]{:S(2)}) async-start(f32[32,1,4224]{2,1,0:T(1,128)} %bitcast.8), calls=%async_computation.1 | async-start | bytes 1081344 | tf_op jit(solution)/shard_map/all_to_all | solution.py:586
  47.1 14.1 %copy-start.2 = (f32[2,8,8192]{2,1,0:T(8,128)S(1)}, f32[2,8,8192]{2,1,0:T(8,128)}, u32[]{:S(2)}) copy-start(f32[2,8,8192]{2,1,0:T(8,128)} %rhs_ref.3) | copy-start | bytes 1572868
  47.1 8.4 %collective-permute-start.11 = (f32[4,2,32,128]{3,2,1,0:T(8,128)S(1)}, f32[4,2,32,128]{3,2,1,0:T(8,128)S(1)}, u32[]{:S(2)}, u32[]{:S(2)}) collective-permute-start(f32[4,2,32,128]{3,2,1,0:T(8,128)S(1)} %get-tuple-element.51), channel_id=1, source_target_pairs={{0,3},{1,2},{2,1},{3,0},{4,7},{5,6},{6,5},{7,4},{8,11},{9,10},{10,... | collective-permute-start | bytes 393224 | tf_op jit(solution)/shard_map/ppermute | solution.py:496
  48.9 11.1 %collective-permute-start.12 = (f32[4,2,32,128]{3,2,1,0:T(8,128)S(1)}, f32[4,2,32,128]{3,2,1,0:T(8,128)S(1)}, u32[]{:S(2)}, u32[]{:S(2)}) collective-permute-start(f32[4,2,32,128]{3,2,1,0:T(8,128)S(1)} %get-tuple-element.52), channel_id=1, source_target_pairs={{0,2},{1,3},{2,0},{3,1},{4,6},{5,7},{6,4},{7,5},{8,10},{9,11},{10,... | collective-permute-start | bytes 393224 | tf_op jit(solution)/shard_map/ppermute | solution.py:496
  49.2 10.7 %collective-permute-start.13 = (f32[4,2,32,128]{3,2,1,0:T(8,128)S(1)}, f32[4,2,32,128]{3,2,1,0:T(8,128)S(1)}, u32[]{:S(2)}, u32[]{:S(2)}) collective-permute-start(f32[4,2,32,128]{3,2,1,0:T(8,128)S(1)} %get-tuple-element.53), channel_id=1, source_target_pairs={{0,1},{1,0},{2,3},{3,2},{4,5},{5,4},{6,7},{7,6},{8,9},{9,8},{10,11... | collective-permute-start | bytes 393224 | tf_op jit(solution)/shard_map/ppermute | solution.py:496
